TPU v7x, 32 devices: a whole 2x2x4 slice. The times are simulated.
32 devices in a mesh: dp: 4 (over y, x), seq: 8 (over z, core).
Axes of the slice: x: 2, y: 2, z: 4, core: 2. Of those that a mesh axis runs over, the one named last changes fastest.
Arguments:
- tokens: bfloat16 [8, 512, 512], P('dp', 'seq'), may hold values from -6 to 6
- memory: bfloat16 [8, 20, 512], P('dp'), may hold values from -6 to 6
- lengths: int32 [8], P('dp'), may hold values from 128 to 512, as said below
- w_qkv: bfloat16 [512, 1536], P(('dp', 'seq')), may hold values from -0.25 to 0.25
- b_query: bfloat16 [512], P(('dp', 'seq')), may hold values from -0.59765625 to 0.59765625
- b_value: bfloat16 [512], P(('dp', 'seq')), may hold values from -0.29882812 to 0.29882812
- w_out: bfloat16 [512, 512], P(('dp', 'seq')), may hold values from -1 to 1
- b_out: bfloat16 [512], P(('dp', 'seq')), may hold values from -3 to 3
- gain_one: bfloat16 [512], P(('dp', 'seq')), may hold values from 0.25 to 1.75
- shift_one: bfloat16 [512], P(('dp', 'seq')), may hold values from -3 to 3
- w_up: bfloat16 [512, 2048], P(('dp', 'seq')), may hold values from -0.25 to 0.25
- b_up: bfloat16 [2048], P(('dp', 'seq')), may hold values from -1.5 to 1.5
- w_down: bfloat16 [2048, 512], P(('dp', 'seq')), may hold values from -0.25 to 0.25
- b_down: bfloat16 [512], P(('dp', 'seq')), may hold values from -3 to 3
- gain_two: bfloat16 [512], P(('dp', 'seq')), may hold values from 0.25 to 1.75
- shift_two: bfloat16 [512], P(('dp', 'seq')), may hold values from -3 to 3
- cot_tokens: bfloat16 [8, 512, 512], P('dp', 'seq'), may hold values from -6 to 6
- cot_memory: bfloat16 [8, 20, 512], P('dp'), may hold values from -6 to 6
Outputs:
- layer_tokens: bfloat16 [8, 512, 512], P('dp', 'seq')
- layer_memory: bfloat16 [8, 20, 512], P('dp')
- input_grad_tokens: bfloat16 [8, 512, 512], P('dp', 'seq')
- input_grad_memory: bfloat16 [8, 20, 512], P('dp')
- grad_w_qkv: float32 [512, 1536], P(('dp', 'seq'))
- grad_b_query: float32 [512], P(('dp', 'seq'))
- grad_b_value: float32 [512], P(('dp', 'seq'))
- grad_w_out: float32 [512, 512], P(('dp', 'seq'))
- grad_b_out: float32 [512], P(('dp', 'seq'))
- grad_gain_one: float32 [512], P(('dp', 'seq'))
- grad_shift_one: float32 [512], P(('dp', 'seq'))
- grad_w_up: float32 [512, 2048], P(('dp', 'seq'))
- grad_b_up: float32 [2048], P(('dp', 'seq'))
- grad_w_down: float32 [2048, 512], P(('dp', 'seq'))
- grad_b_down: float32 [512], P(('dp', 'seq'))
- grad_gain_two: float32 [512], P(('dp', 'seq'))
- grad_shift_two: float32 [512], P(('dp', 'seq'))
- token_rms: float32 [8, 512], P('dp')
Inputs may be any that keep to these rules, and one draw needn't show every extreme that they name: `lengths`: token positions below a slot's length are valid, the rest padding. Some slot has length 512 and some 512 // 4.
All inputs are finite; a program needn't handle non-finite values.
Results may differ from a plain program's by a relative error of at most 0.025.
Values may be sent and summed in bfloat16 or wider, within the bound.
No kernel may reach another device: no remote copies, remote signals or barrier semaphores. Data moves between devices by JAX's collectives and lax.ppermute only.
A program may use at most 128 MiB of HBM per device.

v0:
```python
import jax
import jax.numpy as jnp
from jax import lax
from jax.sharding import PartitionSpec as P

HEADS = 8
HEAD_DIM = 64


masked_score = -1e30


def joined(shard, axis, join):
    gathered = jax.tree.map(
        lambda a, kind: lax.all_gather(a.astype(kind), axis),
        shard,
        jax.tree.map(lambda a: jnp.bfloat16 if a.dtype == jnp.float32 else a.dtype, shard),
    )

    def take(source):
        return jax.tree.map(
            lambda a, own: lax.dynamic_index_in_dim(a, source, 0, False).astype(own.dtype),
            gathered,
            shard,
        )

    return lax.fori_loop(
        1, lax.axis_size(axis), lambda source, state: join(state, take(source)), take(0)
    )


def block_size():
    return 512


def smooth_unit(values):
    return (
        0.5
        * values
        * (1.0 + jnp.tanh(0.7978845608 * (values + 0.044715 * values * values * values)))
    )


def split_heads(matrix):
    return matrix.reshape(matrix.shape[0], HEADS, HEAD_DIM)


def partial_softmax(queries, key_heads, value_heads, keep_mask):
    scores = (
        jnp.einsum("qhd,khd->hqk", queries, key_heads, preferred_element_type=jnp.float32) * 0.125
    )
    scores = jnp.where(keep_mask[None, None, :], scores, masked_score)
    highest = jnp.max(scores, axis=-1)
    weights = jnp.where(keep_mask[None, None, :], jnp.exp(scores - highest[..., None]), 0.0)
    denominator = jnp.sum(weights, axis=-1)
    weighted = jnp.einsum(
        "hqk,khd->hqd",
        weights.astype(jnp.bfloat16),
        value_heads,
        preferred_element_type=jnp.float32,
    )
    return (highest, denominator, weighted)


def combine(earlier, later):
    highest = jnp.maximum(earlier[0], later[0])
    scale_earlier = jnp.exp(earlier[0] - highest)
    scale_later = jnp.exp(later[0] - highest)
    return (
        highest,
        earlier[1] * scale_earlier + later[1] * scale_later,
        earlier[2] * scale_earlier[..., None] + later[2] * scale_later[..., None],
    )


def attend_blocks(queries, key_rows, value_rows, length, totals):
    row_count = key_rows.shape[0]
    step_rows = block_size()
    blocks = row_count // step_rows
    key_blocks = key_rows.reshape(blocks, step_rows, HEADS, HEAD_DIM)
    value_blocks = value_rows.reshape(blocks, step_rows, HEADS, HEAD_DIM)

    def visit_block(running, inputs):
        key_block, value_block, block_index = inputs
        places = block_index * step_rows + jnp.arange(step_rows, dtype=jnp.int32)
        return (
            combine(running, partial_softmax(queries, key_block, value_block, places < length)),
            None,
        )

    folded, unused_rest = lax.scan(
        visit_block, totals, (key_blocks, value_blocks, jnp.arange(blocks, dtype=jnp.int32))
    )
    return folded


def backward_block(queries, grad_heads, log_total, row_delta, key_heads, value_heads, keep_mask):
    scores = (
        jnp.einsum("qhd,khd->hqk", queries, key_heads, preferred_element_type=jnp.float32) * 0.125
    )
    weights = jnp.where(keep_mask[None, None, :], jnp.exp(scores - log_total[..., None]), 0.0)
    grad_value = jnp.einsum(
        "hqk,qhd->khd", weights.astype(jnp.bfloat16), grad_heads, preferred_element_type=jnp.float32
    )
    grad_weights = jnp.einsum(
        "qhd,khd->hqk", grad_heads, value_heads, preferred_element_type=jnp.float32
    )
    grad_scores = (weights * (grad_weights - row_delta[..., None])).astype(jnp.bfloat16)
    grad_query = (
        jnp.einsum("hqk,khd->qhd", grad_scores, key_heads, preferred_element_type=jnp.float32)
        * 0.125
    )
    grad_key = (
        jnp.einsum("hqk,qhd->khd", grad_scores, queries, preferred_element_type=jnp.float32) * 0.125
    )
    return (grad_query, grad_key, grad_value)


def normalize(hidden):
    center = hidden - jnp.mean(hidden, axis=-1, keepdims=True)
    inverse = lax.rsqrt(jnp.mean(center * center, axis=-1, keepdims=True) + 1e-05)
    return (center * inverse, inverse)


def norm_back(grad_normed, normed, inverse):
    mean_grad = jnp.mean(grad_normed, axis=-1, keepdims=True)
    mean_cross = jnp.mean(grad_normed * normed, axis=-1, keepdims=True)
    return inverse * (grad_normed - mean_grad - normed * mean_cross)


def local(
    tokens,
    memory,
    lengths,
    w_qkv,
    b_query,
    b_value,
    w_out,
    b_out,
    gain_one,
    shift_one,
    w_up,
    b_up,
    w_down,
    b_down,
    gain_two,
    shift_two,
    cot_tokens,
    cot_memory,
):
    shards = (
        w_qkv,
        b_query,
        b_value,
        w_out,
        b_out,
        gain_one,
        shift_one,
        w_up,
        b_up,
        w_down,
        b_down,
        gain_two,
        shift_two,
    )
    gathered = (
        lax.all_gather(shards[0], ("dp", "seq"), axis=0, tiled=True),
        lax.all_gather(shards[1], ("dp", "seq"), axis=0, tiled=True),
        lax.all_gather(shards[2], ("dp", "seq"), axis=0, tiled=True),
        lax.all_gather(shards[3], ("dp", "seq"), axis=0, tiled=True),
        lax.all_gather(shards[4], ("dp", "seq"), axis=0, tiled=True),
        lax.all_gather(shards[5], ("dp", "seq"), axis=0, tiled=True),
        lax.all_gather(shards[6], ("dp", "seq"), axis=0, tiled=True),
        lax.all_gather(shards[7], ("dp", "seq"), axis=0, tiled=True),
        lax.all_gather(shards[8], ("dp", "seq"), axis=0, tiled=True),
        lax.all_gather(shards[9], ("dp", "seq"), axis=0, tiled=True),
        lax.all_gather(shards[10], ("dp", "seq"), axis=0, tiled=True),
        lax.all_gather(shards[11], ("dp", "seq"), axis=0, tiled=True),
        lax.all_gather(shards[12], ("dp", "seq"), axis=0, tiled=True),
    )
    (
        qkv_weight,
        query_bias,
        value_bias,
        out_weight,
        out_bias,
        norm_gain_one,
        norm_shift_one,
        up_weight,
        up_bias,
        down_weight,
        down_bias,
        norm_gain_two,
        norm_shift_two,
    ) = gathered
    seq_count = lax.axis_size("seq")
    mem_rows = memory.shape[1]
    tok_rows = tokens.shape[1]
    model_width = tokens.shape[2]
    slot_len = tok_rows * seq_count
    local_places = lax.axis_index("seq") * tok_rows + jnp.arange(tok_rows, dtype=jnp.int32)
    qkv_shift = jnp.concatenate(
        [
            query_bias.astype(jnp.float32),
            jnp.zeros((model_width,), jnp.float32),
            value_bias.astype(jnp.float32),
        ]
    )
    row_weight = jnp.concatenate(
        [jnp.full((mem_rows,), 1.0 / seq_count, jnp.float32), jnp.ones((tok_rows,), jnp.float32)]
    )
    row_weight_low = row_weight.astype(jnp.bfloat16)[:, None]
    memory_keep = jnp.ones((mem_rows,), bool)
    gain_one_f = norm_gain_one.astype(jnp.float32)
    gain_two_f = norm_gain_two.astype(jnp.float32)

    def one_slot(totals, inputs):
        token_in, memory_in, length, token_cot, memory_cot = inputs
        token_keep = local_places < length
        stacked = jnp.concatenate([memory_in, token_in], axis=0)
        packed = (
            jnp.dot(stacked, qkv_weight, preferred_element_type=jnp.float32) + qkv_shift
        ).astype(jnp.bfloat16)
        query_all = split_heads(packed[:, :model_width])
        key_flat = packed[:, model_width : 2 * model_width]
        value_flat = packed[:, 2 * model_width :]
        query_mem = query_all[:mem_rows]
        query_tok = query_all[mem_rows:]
        key_mem = split_heads(key_flat[:mem_rows])
        value_mem = split_heads(value_flat[:mem_rows])
        key_tok_flat = key_flat[mem_rows:]
        value_tok_flat = value_flat[mem_rows:]
        key_tok = split_heads(key_tok_flat)
        value_tok = split_heads(value_tok_flat)
        start_state = partial_softmax(query_tok, key_mem, value_mem, memory_keep)
        token_state = attend_blocks(
            query_tok,
            lax.all_gather(key_tok_flat, "seq", axis=0, tiled=True),
            lax.all_gather(value_tok_flat, "seq", axis=0, tiled=True),
            length,
            start_state,
        )
        local_state = partial_softmax(query_mem, key_tok, value_tok, token_keep)
        merged = joined(local_state, "seq", combine)
        memory_state = combine(partial_softmax(query_mem, key_mem, value_mem, memory_keep), merged)
        highest = jnp.concatenate([memory_state[0], token_state[0]], axis=1)
        denominator = jnp.concatenate([memory_state[1], token_state[1]], axis=1)
        weighted = jnp.concatenate([memory_state[2], token_state[2]], axis=1)
        heads_out = weighted / denominator[..., None]
        log_total = highest + jnp.log(denominator)
        attn_float = jnp.transpose(heads_out, (1, 0, 2)).reshape(-1, model_width)
        attn_low = attn_float.astype(jnp.bfloat16)
        branch = jnp.dot(
            attn_low, out_weight, preferred_element_type=jnp.float32
        ) + out_bias.astype(jnp.float32)
        normed_one, inverse_one = normalize(stacked.astype(jnp.float32) + branch)
        hidden_one = normed_one * gain_one_f + norm_shift_one.astype(jnp.float32)
        hidden_low = hidden_one.astype(jnp.bfloat16)
        up_linear = jnp.dot(
            hidden_low, up_weight, preferred_element_type=jnp.float32
        ) + up_bias.astype(jnp.float32)
        smooth_value, smooth_back = jax.vjp(smooth_unit, up_linear)
        active = smooth_value.astype(jnp.bfloat16)
        feed_branch = jnp.dot(
            active, down_weight, preferred_element_type=jnp.float32
        ) + down_bias.astype(jnp.float32)
        normed_two, inverse_two = normalize(hidden_one + feed_branch)
        valid_rows = jnp.concatenate(
            [jnp.ones((mem_rows,), jnp.float32), token_keep.astype(jnp.float32)]
        )
        output = (normed_two * gain_two_f + norm_shift_two.astype(jnp.float32)) * valid_rows[
            :, None
        ]
        token_feed = feed_branch[mem_rows:]
        squares = jnp.sum(token_feed * token_feed * token_keep.astype(jnp.float32)[:, None], axis=0)
        cotangent = (
            jnp.concatenate([memory_cot, token_cot], axis=0).astype(jnp.float32)
            * valid_rows[:, None]
        )
        weighted_cot = cotangent * row_weight[:, None]
        grad_gain_two = jnp.sum(weighted_cot * normed_two, axis=0)
        grad_shift_two = jnp.sum(weighted_cot, axis=0)
        grad_second = norm_back(cotangent * gain_two_f, normed_two, inverse_two)
        grad_feed = grad_second.astype(jnp.bfloat16)
        feed_scaled = grad_feed * row_weight_low
        grad_down = jnp.einsum("rf,rd->fd", active, feed_scaled, preferred_element_type=jnp.float32)
        grad_down_bias = jnp.sum(feed_scaled.astype(jnp.float32), axis=0)
        grad_active = jnp.einsum(
            "rd,fd->rf", grad_feed, down_weight, preferred_element_type=jnp.float32
        )
        grad_linear = smooth_back(grad_active)[0].astype(jnp.bfloat16)
        linear_scaled = grad_linear * row_weight_low
        grad_up = jnp.einsum(
            "rd,rf->df", hidden_low, linear_scaled, preferred_element_type=jnp.float32
        )
        grad_up_bias = jnp.sum(linear_scaled.astype(jnp.float32), axis=0)
        grad_hidden = grad_second + jnp.einsum(
            "rf,df->rd", grad_linear, up_weight, preferred_element_type=jnp.float32
        )
        grad_gain_one = jnp.sum(grad_hidden * normed_one * row_weight[:, None], axis=0)
        grad_shift_one = jnp.sum(grad_hidden * row_weight[:, None], axis=0)
        grad_first = norm_back(grad_hidden * gain_one_f, normed_one, inverse_one)
        grad_branch = grad_first.astype(jnp.bfloat16)
        branch_scaled = grad_branch * row_weight_low
        grad_out = jnp.einsum(
            "rd,re->de", attn_low, branch_scaled, preferred_element_type=jnp.float32
        )
        grad_out_bias = jnp.sum(branch_scaled.astype(jnp.float32), axis=0)
        grad_attn = jnp.einsum(
            "re,de->rd", grad_branch, out_weight, preferred_element_type=jnp.float32
        ).astype(jnp.bfloat16)
        grad_heads = split_heads(grad_attn)
        row_delta = jnp.transpose(
            jnp.sum(grad_heads.astype(jnp.float32) * split_heads(attn_float), axis=-1)
        )
        grad_heads_mem = grad_heads[:mem_rows]
        grad_heads_tok = grad_heads[mem_rows:]
        log_mem = log_total[:, :mem_rows]
        log_tok = log_total[:, mem_rows:]
        delta_mem = row_delta[:, :mem_rows]
        delta_tok = row_delta[:, mem_rows:]
        key_whole, value_whole = (
            lax.all_gather(key_tok_flat, "seq", axis=0, tiled=True),
            lax.all_gather(value_tok_flat, "seq", axis=0, tiled=True),
        )
        step_rows = block_size()
        blocks = slot_len // step_rows
        key_blocks = key_whole.reshape(blocks, step_rows, HEADS, HEAD_DIM)
        value_blocks = value_whole.reshape(blocks, step_rows, HEADS, HEAD_DIM)

        def back_visit(running, inputs):
            key_block, value_block, block_index = inputs
            places = block_index * step_rows + jnp.arange(step_rows, dtype=jnp.int32)
            grad_query, grad_key, grad_value = backward_block(
                query_tok,
                grad_heads_tok,
                log_tok,
                delta_tok,
                key_block,
                value_block,
                places < length,
            )
            return (
                running + grad_query,
                (
                    grad_key.reshape(step_rows, model_width),
                    grad_value.reshape(step_rows, model_width),
                ),
            )

        query_start = jnp.zeros((tok_rows, HEADS, HEAD_DIM), jnp.float32)
        grad_query_tok, key_terms = lax.scan(
            back_visit, query_start, (key_blocks, value_blocks, jnp.arange(blocks, dtype=jnp.int32))
        )
        key_grad_all = key_terms[0].reshape(slot_len, model_width)
        value_grad_all = key_terms[1].reshape(slot_len, model_width)
        grad_key_tok, grad_value_tok = (
            lax.psum_scatter(key_grad_all, "seq", scatter_dimension=0, tiled=True),
            lax.psum_scatter(value_grad_all, "seq", scatter_dimension=0, tiled=True),
        )
        tokens_on_memory = backward_block(
            query_tok, grad_heads_tok, log_tok, delta_tok, key_mem, value_mem, memory_keep
        )
        memory_on_tokens = backward_block(
            query_mem, grad_heads_mem, log_mem, delta_mem, key_tok, value_tok, token_keep
        )
        memory_on_memory = backward_block(
            query_mem, grad_heads_mem, log_mem, delta_mem, key_mem, value_mem, memory_keep
        )
        shared = lax.psum(
            (
                memory_on_tokens[0].reshape(mem_rows, model_width),
                tokens_on_memory[1].reshape(mem_rows, model_width),
                tokens_on_memory[2].reshape(mem_rows, model_width),
            ),
            "seq",
        )
        grad_query_mem = shared[0] + memory_on_memory[0].reshape(mem_rows, model_width)
        grad_key_mem = shared[1] + memory_on_memory[1].reshape(mem_rows, model_width)
        grad_value_mem = shared[2] + memory_on_memory[2].reshape(mem_rows, model_width)
        grad_query_all = jnp.concatenate(
            [grad_query_mem, (grad_query_tok + tokens_on_memory[0]).reshape(tok_rows, model_width)],
            axis=0,
        )
        grad_key_all = jnp.concatenate(
            [grad_key_mem, grad_key_tok + memory_on_tokens[1].reshape(tok_rows, model_width)],
            axis=0,
        )
        grad_value_all = jnp.concatenate(
            [grad_value_mem, grad_value_tok + memory_on_tokens[2].reshape(tok_rows, model_width)],
            axis=0,
        )
        grad_packed = jnp.concatenate(
            [grad_query_all, grad_key_all, grad_value_all], axis=1
        ).astype(jnp.bfloat16)
        packed_scaled = grad_packed * row_weight_low
        grad_qkv = jnp.einsum(
            "rd,re->de", stacked, packed_scaled, preferred_element_type=jnp.float32
        )
        grad_query_bias = jnp.sum(packed_scaled[:, :model_width].astype(jnp.float32), axis=0)
        grad_value_bias = jnp.sum(packed_scaled[:, 2 * model_width :].astype(jnp.float32), axis=0)
        grad_rows = grad_first + jnp.einsum(
            "re,de->rd", grad_packed, qkv_weight, preferred_element_type=jnp.float32
        )
        grad_set = (
            grad_qkv,
            grad_query_bias,
            grad_value_bias,
            grad_out,
            grad_out_bias,
            grad_gain_one,
            grad_shift_one,
            grad_up,
            grad_up_bias,
            grad_down,
            grad_down_bias,
            grad_gain_two,
            grad_shift_two,
        )
        totals = tuple((running + update for running, update in zip(totals, grad_set)))
        output_low = output.astype(jnp.bfloat16)
        grad_low = grad_rows.astype(jnp.bfloat16)
        return (
            totals,
            (
                output_low[mem_rows:],
                output_low[:mem_rows],
                grad_low[mem_rows:],
                grad_low[:mem_rows],
                squares,
            ),
        )

    initial = tuple((jnp.zeros(whole.shape, jnp.float32) for whole in gathered))
    totals, emitted = lax.scan(one_slot, initial, (tokens, memory, lengths, cot_tokens, cot_memory))
    owned = lax.psum_scatter(totals, ("dp", "seq"), scatter_dimension=0, tiled=True)
    square_sums = lax.psum(emitted[4], "seq")
    token_rms = jnp.sqrt(square_sums / lengths.astype(jnp.float32)[:, None])
    return (
        emitted[0],
        emitted[1],
        emitted[2],
        emitted[3],
        owned[0],
        owned[1],
        owned[2],
        owned[3],
        owned[4],
        owned[5],
        owned[6],
        owned[7],
        owned[8],
        owned[9],
        owned[10],
        owned[11],
        owned[12],
        token_rms,
    )


def solution(mesh):
    in_specs = (
        P("dp", "seq", None),
        P("dp", None, None),
        P("dp"),
        P(("dp", "seq"), None),
        P(("dp", "seq")),
        P(("dp", "seq")),
        P(("dp", "seq"), None),
        P(("dp", "seq")),
        P(("dp", "seq")),
        P(("dp", "seq")),
        P(("dp", "seq"), None),
        P(("dp", "seq")),
        P(("dp", "seq"), None),
        P(("dp", "seq")),
        P(("dp", "seq")),
        P(("dp", "seq")),
        P("dp", "seq", None),
        P("dp", None, None),
    )
    out_specs = (
        P("dp", "seq", None),
        P("dp", None, None),
        P("dp", "seq", None),
        P("dp", None, None),
        P(("dp", "seq"), None),
        P(("dp", "seq")),
        P(("dp", "seq")),
        P(("dp", "seq"), None),
        P(("dp", "seq")),
        P(("dp", "seq")),
        P(("dp", "seq")),
        P(("dp", "seq"), None),
        P(("dp", "seq")),
        P(("dp", "seq"), None),
        P(("dp", "seq")),
        P(("dp", "seq")),
        P(("dp", "seq")),
        P("dp", None),
    )
    return jax.shard_map(local, mesh=mesh, in_specs=in_specs, out_specs=out_specs, check_vma=False)
```

profile of v0, /device:TPU:0, one launch (start us, length us, event | category | flops | bytes accessed | tf_op | source)
XLA Modules:
  0.0 1164.9 jit_solution(18292380273451569531)
XLA Ops:
  17.3 42.2 %all-reduce.21 = (bf16[512]{0:T(512)(128)(2,1)S(1)}, bf16[512]{0:T(512)(128)(2,1)S(1)}, bf16[512]{0:T(512)(128)(2,1)}, bf16[512]{0:T(512)(128)(2,1)S(1)}, bf16[5...) all-reduce(bf16[512]{0:T(512)(128)(2,1)S(1)} %dynamic-update-slice., ...), channel_id=1, replica_groups=mesh['dp'=4,'seq'=8] {'dp','seq'}, use_global_device_ids=true, to_apply=%add.2 | all-reduce | flops 6144 | bytes 24576
  62.9 43.6 %all_gather.100 = bf16[512,512]{1,0:T(8,128)(2,1)S(1)} all-gather(bf16[16,512]{1,0:T(8,128)(2,1)} %param.28), channel_id=1, replica_groups=mesh['dp'=4,'seq'=8] {'dp','seq'}, dimensions={0}, use_global_device_ids=true | all-gather | bytes 540672 | tf_op jit(solution)/shard_map/all_gather | solution.py:170
  106.4 21.4 %all-gather.18.cloned.1.call-done = bf16[512,2048]{1,0:T(8,128)(2,1)} async-done(((bf16[16,2048]{1,0:T(8,128)(2,1)}), bf16[512,2048]{1,0:T(8,128)(2,1)}) %all-gather.18.cloned.1.call-update) | async-done | bytes 2097168 | tf_op jit(solution)/shard_map/all_gather | solution.py:174
  127.8 58.4 %all-gather.20.cloned.1.call-done = bf16[2048,512]{1,0:T(8,128)(2,1)} async-done(((bf16[64,512]{1,0:T(8,128)(2,1)}), bf16[2048,512]{1,0:T(8,128)(2,1)}) %all-gather.20.cloned.1.call-update) | async-done | bytes 2097168 | tf_op jit(solution)/shard_map/all_gather | solution.py:176
  186.1 444.4 %while.107 = (s32[]{:T(128)}, f32[512,1536]{1,0:T(8,128)}, f32[512]{0:T(512)}, f32[512]{0:T(512)}, f32[512,512]{1,0:T(8,128)}, /*index=5*/f32[512]{0:T(512)}, f3...) while((s32[]{:T(128)}, f32[512,1536]{1,0:T(8,128)}, ...), condition=%wide.region_35.36_spmd.clone, body=%wide.region_0.35_spmd.clone.sunk | while | flops 1832945792 | bytes 165956592 | solution.py:435
  189.2 14.6 %all_gather.114 = bf16[512,512]{1,0:T(8,128)(2,1)S(1)} all-gather(bf16[64,512]{1,0:T(8,128)(2,1)S(1)} %get-tuple-element.1836), channel_id=1, replica_groups=mesh['dp'=4,'seq'=8] {'seq'}, dimensions={0}, use_global_device_ids=true | all-gather | bytes 589824 | tf_op jit(solution)/shard_map/while/body/eval_jaxpr/all_gather | solution.py:238
  204.0 14.8 %all_gather.115 = bf16[512,512]{1,0:T(8,128)(2,1)S(1)} all-gather(bf16[64,512]{1,0:T(8,128)(2,1)S(1)} %get-tuple-element.1847), channel_id=1, replica_groups=mesh['dp'=4,'seq'=8] {'seq'}, dimensions={0}, use_global_device_ids=true | all-gather | bytes 589824 | tf_op jit(solution)/shard_map/while/body/eval_jaxpr/all_gather | solution.py:239
  222.3 13.2 %all-gather.11 = bf16[64,20,64]{2,0,1:T(8,128)(2,1)S(1)} all-gather(bf16[8,20,64]{2,0,1:T(8,128)(2,1)S(1)} %copy.303), channel_id=4, replica_groups=mesh['dp'=4,'seq'=8] {'seq'}, dimensions={0}, use_global_device_ids=true | all-gather | bytes 184320 | tf_op jit(solution)/shard_map/while/body/eval_jaxpr/all_gather | solution.py:15
  235.5 12.7 %all-gather.10 = bf16[64,20]{1,0:T(8,128)(2,1)S(1)} all-gather(bf16[8,20]{1,0:T(8,128)(2,1)S(1)} %fusion.335), channel_id=3, replica_groups=mesh['dp'=4,'seq'=8] {'seq'}, dimensions={0}, use_global_device_ids=true | all-gather | bytes 2880 | tf_op jit(solution)/shard_map/while/body/eval_jaxpr/all_gather | solution.py:15
  248.3 12.7 %all-gather.9 = bf16[64,20]{1,0:T(8,128)(2,1)S(1)} all-gather(bf16[8,20]{1,0:T(8,128)(2,1)S(1)} %convert_element_type.720), channel_id=2, replica_groups=mesh['dp'=4,'seq'=8] {'seq'}, dimensions={0}, use_global_device_ids=true | all-gather | bytes 2880 | tf_op jit(solution)/shard_map/while/body/eval_jaxpr/all_gather | solution.py:15
  303.5 2.8 select_add_fusion.21
  306.3 2.8 select_add_fusion.23
  309.2 23.5 %all-reduce.26.cloned.1.call-done = (f32[20,512]{1,0:T(8,128)}, f32[20,512]{1,0:T(8,128)}, f32[20,512]{1,0:T(8,128)}) async-done(((f32[20,512]{1,0:T(8,128)}, f32[20,512]{1,0:T(8,128)}, f32[20,512]{1,0:T(8,128)}), (f32[20,512]{1,0:T(8,128)}, f32[20,512]{1,0:T(8,128)}, f32[20,512]{1,0:T(8,128)})) %all-reduce.26.cloned.1.call-update) | async-done | bytes 122896 | tf_op jit(solution)/shard_map/while/body/eval_jaxpr/psum | solution.py:370
  335.5 33.1 %reduce-scatter.25.cloned.1.call-done = f32[64,512]{1,0:T(8,128)} async-done(((f32[512,512]{1,0:T(8,128)}), f32[64,512]{1,0:T(8,128)}) %reduce-scatter.25.cloned.1.call-update) | async-done | bytes 131088 | tf_op jit(solution)/shard_map/while
  369.7 31.9 %reduce-scatter.23.cloned.1.call-done = f32[64,512]{1,0:T(8,128)} async-done(((f32[512,512]{1,0:T(8,128)}), f32[64,512]{1,0:T(8,128)}) %reduce-scatter.23.cloned.1.call-update) | async-done | bytes 131088 | tf_op jit(solution)/shard_map/while
  408.4 1.8 fusion.328
  410.5 15.0 %all_gather.114 = bf16[512,512]{1,0:T(8,128)(2,1)S(1)} all-gather(bf16[64,512]{1,0:T(8,128)(2,1)S(1)} %get-tuple-element.1836), channel_id=1, replica_groups=mesh['dp'=4,'seq'=8] {'seq'}, dimensions={0}, use_global_device_ids=true | all-gather | bytes 589824 | tf_op jit(solution)/shard_map/while/body/eval_jaxpr/all_gather | solution.py:238
  425.7 15.0 %all_gather.115 = bf16[512,512]{1,0:T(8,128)(2,1)S(1)} all-gather(bf16[64,512]{1,0:T(8,128)(2,1)S(1)} %get-tuple-element.1847), channel_id=1, replica_groups=mesh['dp'=4,'seq'=8] {'seq'}, dimensions={0}, use_global_device_ids=true | all-gather | bytes 589824 | tf_op jit(solution)/shard_map/while/body/eval_jaxpr/all_gather | solution.py:239
  444.1 13.2 %all-gather.11 = bf16[64,20,64]{2,0,1:T(8,128)(2,1)S(1)} all-gather(bf16[8,20,64]{2,0,1:T(8,128)(2,1)S(1)} %copy.303), channel_id=4, replica_groups=mesh['dp'=4,'seq'=8] {'seq'}, dimensions={0}, use_global_device_ids=true | all-gather | bytes 184320 | tf_op jit(solution)/shard_map/while/body/eval_jaxpr/all_gather | solution.py:15
  457.4 12.7 %all-gather.10 = bf16[64,20]{1,0:T(8,128)(2,1)S(1)} all-gather(bf16[8,20]{1,0:T(8,128)(2,1)S(1)} %fusion.335), channel_id=3, replica_groups=mesh['dp'=4,'seq'=8] {'seq'}, dimensions={0}, use_global_device_ids=true | all-gather | bytes 2880 | tf_op jit(solution)/shard_map/while/body/eval_jaxpr/all_gather | solution.py:15
  470.1 12.7 %all-gather.9 = bf16[64,20]{1,0:T(8,128)(2,1)S(1)} all-gather(bf16[8,20]{1,0:T(8,128)(2,1)S(1)} %convert_element_type.720), channel_id=2, replica_groups=mesh['dp'=4,'seq'=8] {'seq'}, dimensions={0}, use_global_device_ids=true | all-gather | bytes 2880 | tf_op jit(solution)/shard_map/while/body/eval_jaxpr/all_gather | solution.py:15
  526.0 5.4 select_add_fusion.21
  531.4 5.1 select_add_fusion.23
  536.5 19.0 %all-reduce.26.cloned.1.call-done = (f32[20,512]{1,0:T(8,128)}, f32[20,512]{1,0:T(8,128)}, f32[20,512]{1,0:T(8,128)}) async-done(((f32[20,512]{1,0:T(8,128)}, f32[20,512]{1,0:T(8,128)}, f32[20,512]{1,0:T(8,128)}), (f32[20,512]{1,0:T(8,128)}, f32[20,512]{1,0:T(8,128)}, f32[20,512]{1,0:T(8,128)})) %all-reduce.26.cloned.1.call-update) | async-done | bytes 122896 | tf_op jit(solution)/shard_map/while/body/eval_jaxpr/psum | solution.py:370
  558.4 33.3 %reduce-scatter.25.cloned.1.call-done = f32[64,512]{1,0:T(8,128)} async-done(((f32[512,512]{1,0:T(8,128)}), f32[64,512]{1,0:T(8,128)}) %reduce-scatter.25.cloned.1.call-update) | async-done | bytes 131088 | tf_op jit(solution)/shard_map/while
  592.8 32.0 %reduce-scatter.23.cloned.1.call-done = f32[64,512]{1,0:T(8,128)} async-done(((f32[512,512]{1,0:T(8,128)}), f32[64,512]{1,0:T(8,128)}) %reduce-scatter.23.cloned.1.call-update) | async-done | bytes 131088 | tf_op jit(solution)/shard_map/while
  633.4 38.4 %all-reduce.20 = (f32[512]{0:T(512)S(1)}, f32[512]{0:T(512)S(1)}, f32[512]{0:T(512)S(1)}, f32[512]{0:T(512)S(1)}, f32[512]{0:T(512)S(1)}, /*index=5*/f32[2048]{0...) all-reduce(f32[512]{0:T(512)S(1)} %copy-done.74, ...), channel_id=8, replica_groups=mesh['dp'=4,'seq'=8] {'dp','seq'}, use_global_device_ids=true, to_apply=%region_37.38.clone | all-reduce | flops 6144 | bytes 49152
  678.4 14.8 %psum.46 = f32[2,512]{1,0:T(2,128)S(1)} all-reduce(f32[2,512]{1,0:T(2,128)S(1)} %copy-done.95), channel_id=1, replica_groups=mesh['dp'=4,'seq'=8] {'seq'}, use_global_device_ids=true, to_apply=%region_49.50 | all-reduce | flops 1024 | bytes 8192 | tf_op jit(solution)/shard_map/psum | solution.py:437
  693.9 73.2 %reduce-scatter.17.cloned.1.call-done = f32[16,512]{1,0:T(8,128)} async-done(((f32[512,512]{1,0:T(8,128)}), f32[16,512]{1,0:T(8,128)}) %reduce-scatter.17.cloned.1.call-update) | async-done | bytes 32784 | tf_op jit(solution)/shard_map/reduce_scatter | solution.py:436
  767.1 104.8 %reduce-scatter.15.cloned.1.call-done = f32[16,1536]{1,0:T(8,128)} async-done(((f32[512,1536]{1,0:T(8,128)}), f32[16,1536]{1,0:T(8,128)}) %reduce-scatter.15.cloned.1.call-update) | async-done | bytes 98320 | tf_op jit(solution)/shard_map/reduce_scatter | solution.py:436
  871.9 144.3 %reduce-scatter.19.cloned.1.call-done = f32[16,2048]{1,0:T(8,128)} async-done(((f32[512,2048]{1,0:T(8,128)}), f32[16,2048]{1,0:T(8,128)}) %reduce-scatter.19.cloned.1.call-update) | async-done | bytes 131088 | tf_op jit(solution)/shard_map/reduce_scatter | solution.py:436
  1016.2 142.2 %reduce-scatter.21.cloned.1.call-done = f32[64,512]{1,0:T(8,128)} async-done(((f32[2048,512]{1,0:T(8,128)}), f32[64,512]{1,0:T(8,128)}) %reduce-scatter.21.cloned.1.call-update) | async-done | bytes 131088 | tf_op jit(solution)/shard_map/reduce_scatter | solution.py:436
  (769 shorter events, 139.4 us)
Async XLA Ops:
  7.2 99.2 %all-gather.16.cloned.1.call-start = ((), (), s32[]{:S(2)}) async-start(), calls=%async_computation.6 | async-start | bytes 1622016 | tf_op jit(solution)/shard_map/all_gather | solution.py:167
  7.9 119.8 %all-gather.18.cloned.1.call-start = ((), (), s32[]{:S(2)}) async-start(), calls=%async_computation.7 | async-start | bytes 2162688 | tf_op jit(solution)/shard_map/all_gather | solution.py:174
  8.7 177.4 %all-gather.20.cloned.1.call-start = ((), (), s32[]{:S(2)}) async-start(), calls=%async_computation.8 | async-start | bytes 2162688 | tf_op jit(solution)/shard_map/all_gather | solution.py:176
  186.1 88.9 %copy-start.11 = (bf16[512,512]{1,0:T(8,128)(2,1)}, bf16[512,512]{1,0:T(8,128)(2,1)S(1)}, u32[]{:S(2)}) copy-start(bf16[512,512]{1,0:T(8,128)(2,1)S(1)} %get-tuple-element.2060) | copy-start | bytes 1572868 | tf_op jit(solution)/shard_map/while
  186.1 146.5 %all-reduce.26.cloned.1.call-start = ((), (), s32[]{:S(2)}) async-start(), calls=%async_computation.14 | async-start | bytes 294912 | tf_op jit(solution)/shard_map/while/body/eval_jaxpr/psum | solution.py:370
  187.1 79.4 %copy-start.33 = (bf16[20,512]{1,0:T(8,128)(2,1)}, bf16[20,512]{1,0:T(8,128)(2,1)S(1)}, u32[]{:S(2)}) copy-start(bf16[20,512]{1,0:T(8,128)(2,1)S(1)} %dynamic-slice_bitcast_fusion.9) | copy-start | bytes 61444 | tf_op jit(solution)/shard_map/while
  189.2 46.3 %copy-start.30 = (bf16[64,8,64]{2,1,0:T(8,128)(2,1)}, bf16[64,8,64]{2,1,0:T(8,128)(2,1)S(1)}, u32[]{:S(2)}) copy-start(bf16[64,8,64]{2,1,0:T(8,128)(2,1)S(1)} %reshape.460) | copy-start | bytes 196612 | tf_op jit(solution)/shard_map/while
  220.2 45.4 %copy-start.62 = (pred[512]{0:T(512)(128)(4,1)}, pred[512]{0:T(512)(128)(4,1)S(1)}, u32[]{:S(2)}) copy-start(pred[512]{0:T(512)(128)(4,1)S(1)} %iota_compare_fusion.2) | copy-start | bytes 1540 | tf_op jit(solution)/shard_map/while
  282.3 86.3 %reduce-scatter.25.cloned.1.call-start = ((), (), s32[]{:S(2)}) async-start(), calls=%async_computation.15 | async-start | bytes 1179648 | tf_op jit(solution)/shard_map/while
  286.4 115.2 %reduce-scatter.23.cloned.1.call-start = ((), (), s32[]{:S(2)}) async-start(), calls=%async_computation.13 | async-start | bytes 1179648 | tf_op jit(solution)/shard_map/while
  306.3 96.4 %copy-start.31 = (bf16[8,64,64]{2,1,0:T(8,128)(2,1)S(1)}, bf16[8,64,64]{2,1,0:T(8,128)(2,1)}, u32[]{:S(2)}) copy-start(bf16[8,64,64]{2,1,0:T(8,128)(2,1)} %fusion.355) | copy-start | bytes 196612 | tf_op jit(solution)/shard_map/while
  306.3 96.4 %copy-start.51 = (bf16[84]{0:T(256)(128)(2,1)S(1)}, bf16[84]{0:T(256)(128)(2,1)}, u32[]{:S(2)}) copy-start(bf16[84]{0:T(256)(128)(2,1)} %get-tuple-element.2075) | copy-start | bytes 508 | tf_op jit(solution)/shard_map/while
  309.2 93.8 %copy-start.1 = (bf16[512,1536]{1,0:T(8,128)(2,1)S(1)}, bf16[512,1536]{1,0:T(8,128)(2,1)}, u32[]{:S(2)}) copy-start(bf16[512,1536]{1,0:T(8,128)(2,1)} %get-tuple-element.2057) | copy-start | bytes 4718596 | tf_op jit(solution)/shard_map/while
  335.4 68.4 %copy-start.26 = (bf16[64,512]{1,0:T(8,128)(2,1)S(1)}, bf16[64,512]{1,0:T(8,128)(2,1)}, u32[]{:S(2)}) copy-start(bf16[64,512]{1,0:T(8,128)(2,1)} %copy-done.24) | copy-start | bytes 196612 | tf_op jit(solution)/shard_map/while
  335.4 68.4 %copy-start.34 = (bf16[20,512]{1,0:T(8,128)(2,1)S(1)}, bf16[20,512]{1,0:T(8,128)(2,1)}, u32[]{:S(2)}) copy-start(bf16[20,512]{1,0:T(8,128)(2,1)} %copy-done.33) | copy-start | bytes 61444 | tf_op jit(solution)/shard_map/while
  407.4 89.5 %copy-start.11 = (bf16[512,512]{1,0:T(8,128)(2,1)}, bf16[512,512]{1,0:T(8,128)(2,1)S(1)}, u32[]{:S(2)}) copy-start(bf16[512,512]{1,0:T(8,128)(2,1)S(1)} %get-tuple-element.2060) | copy-start | bytes 1572868 | tf_op jit(solution)/shard_map/while
  407.4 148.1 %all-reduce.26.cloned.1.call-start = ((), (), s32[]{:S(2)}) async-start(), calls=%async_computation.14 | async-start | bytes 294912 | tf_op jit(solution)/shard_map/while/body/eval_jaxpr/psum | solution.py:370
  408.4 79.9 %copy-start.33 = (bf16[20,512]{1,0:T(8,128)(2,1)}, bf16[20,512]{1,0:T(8,128)(2,1)S(1)}, u32[]{:S(2)}) copy-start(bf16[20,512]{1,0:T(8,128)(2,1)S(1)} %dynamic-slice_bitcast_fusion.9) | copy-start | bytes 61444 | tf_op jit(solution)/shard_map/while
  410.5 46.8 %copy-start.30 = (bf16[64,8,64]{2,1,0:T(8,128)(2,1)}, bf16[64,8,64]{2,1,0:T(8,128)(2,1)S(1)}, u32[]{:S(2)}) copy-start(bf16[64,8,64]{2,1,0:T(8,128)(2,1)S(1)} %reshape.460) | copy-start | bytes 196612 | tf_op jit(solution)/shard_map/while
  442.0 45.4 %copy-start.62 = (pred[512]{0:T(512)(128)(4,1)}, pred[512]{0:T(512)(128)(4,1)S(1)}, u32[]{:S(2)}) copy-start(pred[512]{0:T(512)(128)(4,1)S(1)} %iota_compare_fusion.2) | copy-start | bytes 1540 | tf_op jit(solution)/shard_map/while
  504.2 87.5 %reduce-scatter.25.cloned.1.call-start = ((), (), s32[]{:S(2)}) async-start(), calls=%async_computation.15 | async-start | bytes 1179648 | tf_op jit(solution)/shard_map/while
  508.2 116.5 %reduce-scatter.23.cloned.1.call-start = ((), (), s32[]{:S(2)}) async-start(), calls=%async_computation.13 | async-start | bytes 1179648 | tf_op jit(solution)/shard_map/while
  531.4 94.4 %copy-start.31 = (bf16[8,64,64]{2,1,0:T(8,128)(2,1)S(1)}, bf16[8,64,64]{2,1,0:T(8,128)(2,1)}, u32[]{:S(2)}) copy-start(bf16[8,64,64]{2,1,0:T(8,128)(2,1)} %fusion.355) | copy-start | bytes 196612 | tf_op jit(solution)/shard_map/while
  531.4 94.4 %copy-start.51 = (bf16[84]{0:T(256)(128)(2,1)S(1)}, bf16[84]{0:T(256)(128)(2,1)}, u32[]{:S(2)}) copy-start(bf16[84]{0:T(256)(128)(2,1)} %get-tuple-element.2075) | copy-start | bytes 508 | tf_op jit(solution)/shard_map/while
  536.5 89.7 %copy-start.1 = (bf16[512,1536]{1,0:T(8,128)(2,1)S(1)}, bf16[512,1536]{1,0:T(8,128)(2,1)}, u32[]{:S(2)}) copy-start(bf16[512,1536]{1,0:T(8,128)(2,1)} %get-tuple-element.2057) | copy-start | bytes 4718596 | tf_op jit(solution)/shard_map/while
  558.2 68.7 %copy-start.26 = (bf16[64,512]{1,0:T(8,128)(2,1)S(1)}, bf16[64,512]{1,0:T(8,128)(2,1)}, u32[]{:S(2)}) copy-start(bf16[64,512]{1,0:T(8,128)(2,1)} %copy-done.24) | copy-start | bytes 196612 | tf_op jit(solution)/shard_map/while
  558.2 68.7 %copy-start.34 = (bf16[20,512]{1,0:T(8,128)(2,1)S(1)}, bf16[20,512]{1,0:T(8,128)(2,1)}, u32[]{:S(2)}) copy-start(bf16[20,512]{1,0:T(8,128)(2,1)} %copy-done.33) | copy-start | bytes 61444 | tf_op jit(solution)/shard_map/while
  630.5 136.6 %reduce-scatter.17.cloned.1.call-start = ((), (), s32[]{:S(2)}) async-start(), calls=%async_computation.10 | async-start | bytes 1081344 | tf_op jit(solution)/shard_map/reduce_scatter | solution.py:436
  631.1 240.8 %reduce-scatter.15.cloned.1.call-start = ((), (), s32[]{:S(2)}) async-start(), calls=%async_computation.9 | async-start | bytes 3244032 | tf_op jit(solution)/shard_map/reduce_scatter | solution.py:436
  631.8 384.3 %reduce-scatter.19.cloned.1.call-start = ((), (), s32[]{:S(2)}) async-start(), calls=%async_computation.11 | async-start | bytes 4325376 | tf_op jit(solution)/shard_map/reduce_scatter | solution.py:436
  632.5 45.9 %copy-start.95 = (f32[2,512]{1,0:T(2,128)S(1)}, f32[2,512]{1,0:T(2,128)}, u32[]{:S(2)}) copy-start(f32[2,512]{1,0:T(2,128)} %get-tuple-element.1020) | copy-start | bytes 12292
  632.5 525.9 %reduce-scatter.21.cloned.1.call-start = ((), (), s32[]{:S(2)}) async-start(), calls=%async_computation.12 | async-start | bytes 4325376 | tf_op jit(solution)/shard_map/reduce_scatter | solution.py:436
  (174 other events, 1126.3 us)
Sparse Core Ops, SparseCore 0:
  11.0 58.0 all-gather.15
  72.1 55.6 all-gather.17
  130.7 55.3 all-gather.19
  282.5 50.1 all-reduce.25
  334.8 33.8 reduce-scatter.24
  370.8 30.7 reduce-scatter.22
  504.3 51.1 all-reduce.25
  557.8 33.8 reduce-scatter.24
  594.0 30.7 reduce-scatter.22
  633.8 133.1 reduce-scatter.16
  774.0 97.8 reduce-scatter.14
  874.7 141.4 reduce-scatter.18
  1019.1 139.2 reduce-scatter.20
where the time goes:
time: 1170 us; the launch traced here: 1160 us
  waiting for transfers between devices  722 us (62%)
  blocking collectives  276 us (24%)
  matrix products  66.6 us (6%)
  local copies, waits for them, and re-layouts  49.9 us (4%)
  other arithmetic  32.7 us (3%)
  between operations  14.2 us (1%)
    reduce_scatter x4, waiting for transfers between devices, local(): lax.psum_scatter(totals, ('dp', 'seq'), scatter_dimension=0, tiled=True)  465 us
    while x10, waiting for transfers between devices  130 us
    unnamed x2, blocking collectives  80.6 us
    all_gather x6, blocking collectives, joined(): lax.all_gather(a.astype(kind), axis)  77.3 us
    all_gather x1, waiting for transfers between devices, local(): lax.all_gather(shards[9], ('dp', 'seq'), axis=0, tiled=True)  58.4 us
    all_gather x1, blocking collectives, local(): lax.all_gather(shards[3], ('dp', 'seq'), axis=0, tiled=True)  43.6 us
    psum x2, waiting for transfers between devices, one_slot(): lax.psum((memory_on_tokens[0].reshape(mem_rows, model_width), tokens_on_m...  42.5 us
    all_gather x2, blocking collectives, one_slot(): lax.all_gather(value_tok_flat, 'seq', axis=0, tiled=True)  29.8 us
  transfers between devices with their start and end apart: 13, of which 12 were waited for; matrix products, arithmetic and copies ran while one was open for 7% of the time, Pallas kernels for 0%

commit v1 on v0

v1 whole, which is shorter than its diff:
```python
import functools

import jax
import jax.numpy as jnp
from jax import lax
from jax.experimental import pallas as pl
from jax.experimental.pallas import tpu as pltpu
from jax.sharding import PartitionSpec as P

HEADS = 8
HEAD_DIM = 64
WIDTH = 512
FF = 2048
BLOCKS = 32
ROWS = 128
MEM_PAD = 32
OWN = ROWS + MEM_PAD
MEM_KEYS = 128
LANES = 128
MIB = 1 << 20

BF = jnp.bfloat16
F32 = jnp.float32
NN = (((1,), (0,)), ((), ()))
NT = (((1,), (1,)), ((), ()))
TN = (((0,), (0,)), ((), ()))

GATHER_QKV = (2, 3, 4, 1, 0)
GATHER_UP = (2, 4, 1, 3, 0)
GATHER_DOWN = (2, 1, 3, 4, 0)
REDUCE_UP = (0, 1, 4, 3, 2)
REDUCE_DOWN = (0, 3, 1, 4, 2)
REDUCE_QKV = (0, 4, 3, 1, 2)


def dot(a, b, dims=NN):
    return lax.dot_general(a, b, dims, preferred_element_type=F32)


def low(v):
    return v.astype(BF)


def high(v):
    return v.astype(F32)


def split_three(v):
    first = high(low(v))
    second = high(low(v - first))
    return first, second, high(low(v - first - second))


def aligned(index, size):
    return pl.ds(pl.multiple_of(index * size, size), size)


class Layout:
    def __init__(self, mesh):
        self.dp = mesh.shape["dp"]
        self.seq = mesh.shape["seq"]
        self.devices = self.dp * self.seq
        self.low_bits = (self.devices // BLOCKS).bit_length() - 1
        self.group = self.seq // 2
        self.seq_bits = self.seq.bit_length() - 1

    def dim(self, bit):
        if bit < self.seq_bits:
            return "seq", 1 << bit
        return "dp", 1 << (bit - self.seq_bits)

    def swap(self, x, bit):
        axis, mask = self.dim(bit)
        size = self.seq if axis == "seq" else self.dp
        return lax.ppermute(x, axis, [(i, i ^ mask) for i in range(size)])

    def block_swap(self, x, bit):
        return self.swap(x, bit + self.low_bits)

    def device(self):
        return lax.axis_index("dp") * self.seq + lax.axis_index("seq")

    def block(self):
        return self.device() >> self.low_bits

    def join_low(self, x, axis):
        for bit in range(self.low_bits):
            other = self.swap(x, bit)
            first = (self.device() >> bit) % 2 == 0
            x = jnp.where(
                first, jnp.concatenate([x, other], axis), jnp.concatenate([other, x], axis)
            )
        return x

    def reduce_low(self, x, axis):
        for bit in reversed(range(self.low_bits)):
            first = (self.device() >> bit) % 2 == 0
            lower, upper = jnp.split(x, 2, axis)
            other = self.swap(jnp.where(first, upper, lower), bit)
            x = jnp.where(first, lower, upper) + other
        return x

    def gather(self, x, order):
        held = x
        for bit in order[:3]:
            held = jnp.concatenate([held, self.block_swap(held, bit)], 0)
        last = self.block_swap(held, order[3])
        return held, last, self.block_swap(held, order[4]), self.block_swap(last, order[4])

    def reduce(self, keep, send, order, fold):
        other = self.block_swap(send, order[0])
        for bit in order[1:]:
            keep, send = fold(keep, other)
            other = self.block_swap(send, bit)
        return keep, other

    def gather_group(self, x):
        near = x
        mask = self.group // 2
        while mask > 1:
            near = jnp.concatenate([near, self.swap(near, mask.bit_length() - 1)], 0)
            mask //= 2
        return near, self.swap(near, 0)

    def group_masks(self):
        near = [0]
        mask = self.group // 2
        while mask > 1:
            near += [m ^ mask for m in near]
            mask //= 2
        return near, [m ^ 1 for m in near]


def gather_masks(order):
    held = [0]
    for bit in order[:3]:
        held = held + [m ^ (1 << bit) for m in held]
    last = [m ^ (1 << order[3]) for m in held]
    swapped = [[m ^ (1 << order[4]) for m in part] for part in (held, last)]
    return held, last, swapped[0], swapped[1]


def reduce_masks(order):
    return [
        sum(((place >> (4 - k)) & 1) << bit for k, bit in enumerate(order))
        for place in range(BLOCKS)
    ]


def place_blocks(target, parts, order, block, unit, lanes):
    for part, masks in zip(parts, gather_masks(order)):
        for place, mask in enumerate(masks):
            target[aligned(block ^ mask, unit), :] = part[place, :, lanes]


def emit_blocks(source, keep, send, order, block, unit, at, lanes):
    for place, mask in enumerate(reduce_masks(order)):
        target = keep if place < BLOCKS // 2 else send
        target[place % (BLOCKS // 2), at, lanes] = source[aligned(block ^ mask, unit), :]


def roll_lanes(v, shift):
    return pltpu.roll(v, shift % LANES, 1) if shift % LANES else v


def lane_index(shape):
    return lax.broadcasted_iota(jnp.int32, shape, 1)


def normalize(hidden):
    center = hidden - jnp.mean(hidden, axis=-1, keepdims=True)
    inverse = lax.rsqrt(jnp.mean(center * center, axis=-1, keepdims=True) + 1e-05)
    return center * inverse, inverse


def norm_back(grad_normed, normed, inverse):
    mean_grad = jnp.mean(grad_normed, axis=-1, keepdims=True)
    mean_cross = jnp.mean(grad_normed * normed, axis=-1, keepdims=True)
    return inverse * (grad_normed - mean_grad - normed * mean_cross)


def half_masks():
    first = lane_index((1, LANES)) < HEAD_DIM
    return low(jnp.where(first, 1.0, 0.0)), low(jnp.where(first, 0.0, 1.0))


def both_heads(pair, scale=1.0):
    first, second = half_masks()
    return jnp.concatenate([pair * (first * scale), pair * (second * scale)], 0)


def join_heads(pair):
    half = pair.shape[0] // 2
    return jnp.where(lane_index((half, LANES)) < HEAD_DIM, pair[:half], pair[half:])


def head_column(columns, pair):
    lanes = lane_index(columns.shape)
    picked = [
        jnp.sum(jnp.where(lanes == 2 * pair + k, columns, 0.0), axis=1, keepdims=True)
        for k in range(2)
    ]
    return jnp.concatenate(picked, 0)


def key_valid(shape, axis, slot, group, length, slot_len, mem_rows):
    place = lax.broadcasted_iota(jnp.int32, shape, axis)
    half = (place >> 6) & 1
    position = ((half ^ slot) * group + (place >> 7)) * HEAD_DIM + (place & 63)
    token = jnp.logical_and(place < slot_len, position < length)
    mem = jnp.logical_and(place >= slot_len, place < slot_len + mem_rows)
    return jnp.logical_or(token, mem)


def own_valid(shape, slot, group, rank, length, mem_rows):
    place = lax.broadcasted_iota(jnp.int32, shape, 0)
    half = (place >> 6) & 1
    position = ((half ^ slot) * group + rank) * HEAD_DIM + (place & 63)
    token = jnp.logical_and(place < ROWS, position < length)
    mem = jnp.logical_and(place >= ROWS, place < ROWS + mem_rows)
    return jnp.logical_or(token, mem)


def forward_kernel(layout, mem_rows, slot_len, *refs):
    lengths, near, far, memory, w0, w1, w2, w3 = refs[:8]
    qkv, attn, lse_col, vectors, up_bias = refs[8:13]
    rows, weight, extra = refs[13:]
    group = layout.group
    place = lax.axis_index("seq")
    slot, rank = place // group, place % group
    block = layout.block()
    length = lengths[slot]
    parts = (w0, w1, w2, w3)
    place_blocks(weight, parts, GATHER_QKV, block, 16, slice(0, 3 * WIDTH))
    place_blocks(extra, parts, GATHER_QKV, block, 16, slice(4 * WIDTH, 4 * WIDTH + LANES))
    for part, masks in zip((near, far), layout.group_masks()):
        for k, mask in enumerate(masks):
            rows[aligned(rank ^ mask, ROWS), :] = part[k]
    rows[slot_len : slot_len + MEM_PAD, :] = memory[slot]

    pieces, ups = [], []
    for g in range(4):
        total = jnp.zeros((8, LANES), F32)
        for p in range(8):
            total += roll_lanes(high(extra[(8 * g + p) * 16 : (8 * g + p + 1) * 16, :])[:8], 16 * p)
        pieces.append(total)
    for g in range(16):
        total = jnp.zeros((8, LANES), F32)
        for p in range(2):
            at = (2 * g + p) * 16
            total += roll_lanes(high(extra[at : at + 16, :])[8:], 64 * p)
        ups.append(total)
    vector_rows = jnp.concatenate(pieces, 1)
    vectors[...] = vector_rows
    up_bias[...] = jnp.concatenate(ups, 1)

    key_rows = slot_len + MEM_KEYS
    filled = slot_len + MEM_PAD
    qkv[filled:key_rows, :] = jnp.zeros((key_rows - filled, 3 * WIDTH), BF)
    shifts = (vector_rows[0:1], None, vector_rows[1:2])
    step = 544 if filled == 544 else 512
    for start in range(0, filled, step):
        size = min(step, filled - start)
        for part, shift in enumerate(shifts):
            lanes = slice(part * WIDTH, (part + 1) * WIDTH)
            value = dot(rows[start : start + size, :], weight[:, lanes])
            qkv[start : start + size, lanes] = low(value if shift is None else value + shift)

    keep = key_valid((1, key_rows), 1, slot, group, length, slot_len, mem_rows)
    bias = jnp.where(keep, 0.0, -1e30)
    log_columns = jnp.zeros((OWN, LANES), F32)
    for pair in range(HEADS // 2):
        at = pair * LANES
        own = jnp.concatenate(
            [qkv[aligned(rank, ROWS), at : at + LANES], qkv[slot_len:filled, at : at + LANES]], 0
        )
        keys = qkv[:, WIDTH + at : WIDTH + at + LANES]
        values = qkv[:, 2 * WIDTH + at : 2 * WIDTH + at + LANES]
        scores = dot(both_heads(own, 0.125), keys, NT) + bias
        highest = jnp.max(scores, axis=1, keepdims=True)
        expos = jnp.exp(scores - highest)
        total = jnp.sum(expos, axis=1, keepdims=True)
        attn[:, at : at + LANES] = join_heads(dot(low(expos), values) / total)
        log_total = highest + jnp.log(total)
        lanes = lane_index((OWN, LANES))
        log_columns = jnp.where(lanes == 2 * pair, log_total[:OWN], log_columns)
        log_columns = jnp.where(lanes == 2 * pair + 1, log_total[OWN:], log_columns)
    lse_col[...] = log_columns


def feed_kernel(layout, mem_rows, *refs):
    lengths, tokens, arrived, memory, cots, cot_arrived, cot_memory = refs[:7]
    attn, lse_col, vectors, up_bias = refs[7:11]
    outs, ups, downs = refs[11:15], refs[15:19], refs[19:23]
    pack, grad_mem, lse_mem, delta_mem, delta_col, first_grad, out_own, out_send = refs[23:31]
    attn_low, branch_low, hidden_low, grad_linear, active, feed_low, vector_grads, up_grads = refs[
        31:39
    ]
    w_out, w_up, w_down, slope = refs[39:]
    group = layout.group
    place = lax.axis_index("seq")
    slot, rank = place // group, place % group
    block = layout.block()
    length = lengths[slot]
    place_blocks(w_out, outs, GATHER_QKV, block, 16, slice(3 * WIDTH, 4 * WIDTH))
    place_blocks(w_up, ups, GATHER_UP, block, 16, slice(0, FF))
    place_blocks(w_down, downs, GATHER_DOWN, block, 64, slice(0, WIDTH))

    vec = vectors[...]
    out_bias, gain_one, shift_one, down_bias, gain_two, shift_two = [
        vec[k : k + 1] for k in range(2, 8)
    ]
    rows = jnp.concatenate([high(tokens[slot]), high(arrived[...]), high(memory[slot])], 0)
    cot = jnp.concatenate([high(cots[slot]), high(cot_arrived[...]), high(cot_memory[slot])], 0)
    valid = jnp.where(own_valid((OWN, 1), slot, group, rank, length, mem_rows), 1.0, 0.0)
    share = 1.0 / group
    row = lax.broadcasted_iota(jnp.int32, (OWN, 1), 0)
    weight = jnp.where(row < ROWS, 1.0, share)
    weight_low = low(weight)

    def total(v):
        return jnp.sum(v * weight, axis=0, keepdims=True)

    heads_out = attn[...]
    attn_low[...] = low(heads_out)
    branch = dot(attn_low[...], w_out[...]) + out_bias
    normed_one, inverse_one = normalize(rows + branch)
    hidden_one = normed_one * gain_one + shift_one
    hidden_low[...] = low(hidden_one)
    feed = jnp.zeros((OWN, WIDTH), F32) + down_bias
    for at in range(0, FF, WIDTH):
        cols = slice(at, at + WIDTH)
        t = dot(hidden_low[...], w_up[:, cols]) + up_bias[0:1, cols]
        square = t * t
        bent = jnp.tanh(0.7978845608 * (t + 0.044715 * (square * t)))
        half = 0.5 * (1.0 + bent)
        slope[:, cols] = half + (0.5 * 0.7978845608) * t * (1.0 - bent * bent) * (
            1.0 + (3 * 0.044715) * square
        )
        act = low(t * half)
        active[:, cols] = act
        feed += dot(act, w_down[cols, :])
    normed_two, inverse_two = normalize(hidden_one + feed)
    output = (normed_two * gain_two + shift_two) * valid
    out_own[:HEAD_DIM, :] = low(output[:HEAD_DIM])
    out_own[HEAD_DIM:, :] = low(output[ROWS:])
    out_send[...] = low(output[HEAD_DIM:])
    token_valid = jnp.where(row < ROWS, valid, 0.0)
    squares = jnp.sum(feed * feed * token_valid, axis=0, keepdims=True)

    g = cot * valid
    grads = [None] * 8
    grads[6] = total(g * normed_two)
    grads[7] = total(g)
    second = norm_back(g * gain_two, normed_two, inverse_two)
    grad_feed = low(second)
    feed_low[...] = grad_feed * weight_low
    grads[5] = total(high(grad_feed))
    grad_hidden = second
    for at in range(0, FF, WIDTH):
        cols = slice(at, at + WIDTH)
        linear = low(dot(grad_feed, w_down[cols, :], NT) * slope[:, cols])
        grad_linear[:, cols] = linear * weight_low
        up_grads[:, cols] = jnp.broadcast_to(total(high(linear)), (8, WIDTH))
        grad_hidden += dot(linear, w_up[:, cols], NT)
    grads[3] = total(grad_hidden * normed_one)
    grads[4] = total(grad_hidden)
    first = norm_back(grad_hidden * gain_one, normed_one, inverse_one)
    first_grad[...] = first
    grad_branch = low(first)
    branch_low[...] = grad_branch * weight_low
    grads[2] = total(high(grad_branch))
    grads[0] = grads[1] = jnp.zeros((1, WIDTH), F32)
    vector_grads[...] = jnp.concatenate(grads, 0)

    grad_attn = low(dot(grad_branch, w_out[...], NT))
    product = high(grad_attn) * heads_out
    chosen = lax.broadcasted_iota(jnp.int32, (16, WIDTH), 0)
    head = lax.broadcasted_iota(jnp.int32, (16, WIDTH), 1) // HEAD_DIM
    pick = low(jnp.where(chosen == head, 1.0, 0.0))
    down = lax.broadcasted_iota(jnp.int32, (WIDTH, LANES), 0) // HEAD_DIM
    pick_col = low(jnp.where(down == lane_index((WIDTH, LANES)), 1.0, 0.0))
    identity = low(
        jnp.where(
            lax.broadcasted_iota(jnp.int32, (16, LANES), 0) == lane_index((16, LANES)), 1.0, 0.0
        )
    )
    terms = [low(v) for v in split_three(product)]
    delta_col[...] = sum(dot(v, pick_col) for v in terms)
    delta_row = sum(dot(pick, v, NT) for v in terms)[:8]
    log_row = sum(dot(identity, low(v), NT) for v in split_three(lse_col[...]))[:8]
    log_terms = split_three(log_row[:, :ROWS])
    delta_terms = split_three(delta_row[:, :ROWS])
    square_terms = split_three(squares)
    square_rows = jnp.concatenate(
        [v[:, k * LANES : (k + 1) * LANES] for v in square_terms[:2] for k in range(4)], 0
    )
    pack[0, :ROWS, :] = grad_attn[:ROWS]
    pack[0, ROWS:, :] = low(
        jnp.concatenate(
            [
                jnp.concatenate([*log_terms, delta_terms[0]], 1),
                jnp.concatenate(
                    [delta_terms[1], delta_terms[2], square_rows, jnp.zeros((8, LANES), F32)], 1
                ),
            ],
            0,
        )
    )
    grad_mem[...] = grad_attn[ROWS:]
    blank = jnp.zeros((8, LANES - MEM_PAD), F32)
    lse_mem[...] = jnp.concatenate([log_row[:, ROWS:], blank], 1)
    delta_mem[...] = jnp.concatenate([delta_row[:, ROWS:], blank], 1)


def weight_kernel(layout, *refs):
    attn_low, branch_low, hidden_low, grad_linear, active, feed_low = refs[:6]
    up_keep, up_send, down_keep, down_send = refs[6:10]
    up, down, out = refs[10:]
    block = layout.block()
    for at in range(0, FF, WIDTH):
        cols = slice(at, at + WIDTH)
        down[cols, :] = low(dot(active[:, cols], feed_low[...], TN))
    out[...] = low(dot(attn_low[...], branch_low[...], TN))
    every = slice(0, WIDTH)
    emit_blocks(down, down_keep, down_send, REDUCE_DOWN, block, 64, slice(0, 64), every)
    emit_blocks(out, down_keep, down_send, REDUCE_DOWN, block, 16, slice(64, 80), every)
    for at in range(0, FF, WIDTH):
        cols = slice(at, at + WIDTH)
        up[:, cols] = low(dot(hidden_low[...], grad_linear[:, cols], TN))
    emit_blocks(up, up_keep, up_send, REDUCE_UP, block, 16, slice(0, 16), slice(0, FF))


def backward_kernel(layout, mem_rows, slot_len, *refs):
    lengths, tokens, arrived, memory, qkv, near, far, grad_mem, lse_mem, delta_mem = refs[:10]
    lse_col, delta_col, first_grad, vector_grads, up_grads = refs[10:15]
    parts = refs[15:19]
    keep_out, send_out, own_out, give_out = refs[19:23]
    weight, grad_rows, log_row, delta_row, squares, packed, grad_weight, extra = refs[23:]
    group = layout.group
    place = lax.axis_index("seq")
    slot, rank = place // group, place % group
    block = layout.block()
    length = lengths[slot]
    filled = slot_len + MEM_PAD
    key_rows = slot_len + MEM_KEYS
    place_blocks(weight, parts, GATHER_QKV, block, 16, slice(0, 3 * WIDTH))
    for part, masks in zip((near, far), layout.group_masks()):
        for k, mask in enumerate(masks):
            at = rank ^ mask
            grad_rows[aligned(at, ROWS), :] = part[k, :ROWS, :]
            more = high(part[k, ROWS:, :])
            cell = [[more[8 * a : 8 * a + 8, LANES * b : LANES * (b + 1)] for b in range(4)] for a in range(2)]
            log_row[:, aligned(at, LANES)] = cell[0][0] + cell[0][1] + cell[0][2]
            delta_row[:, aligned(at, LANES)] = cell[0][3] + cell[1][0] + cell[1][1]
            squares[at] = cell[1][2]
    grad_rows[slot_len:filled, :] = grad_mem[...]
    grad_rows[filled:, :] = jnp.zeros((key_rows - filled, WIDTH), BF)
    log_row[:, slot_len:] = lse_mem[...]
    delta_row[:, slot_len:] = delta_mem[...]

    own_keep = jnp.where(own_valid((OWN, 1), slot, group, rank, length, mem_rows), 0.0, -1e30)
    own_bias = jnp.concatenate([own_keep, own_keep], 0)
    chunk = min(slot_len, 512)
    spans = [(s, chunk) for s in range(0, slot_len, chunk)]
    spans[-1] = (spans[-1][0], chunk + MEM_KEYS)

    def own_rows(ref, lanes):
        return jnp.concatenate([ref[aligned(rank, ROWS), lanes], ref[slot_len:filled, lanes]], 0)

    for pair in range(HEADS // 2):
        at = pair * LANES
        q_lanes = slice(at, at + LANES)
        k_lanes = slice(WIDTH + at, WIDTH + at + LANES)
        v_lanes = slice(2 * WIDTH + at, 2 * WIDTH + at + LANES)
        own_q = both_heads(own_rows(qkv, q_lanes), 0.125)
        own_k = both_heads(own_rows(qkv, k_lanes), 0.125)
        own_v = both_heads(own_rows(qkv, v_lanes))
        own_g = both_heads(own_rows(grad_rows, q_lanes))
        log_column = head_column(lse_col[...], pair)
        delta_column = head_column(delta_col[...], pair)
        d_query = jnp.zeros((2 * OWN, LANES), F32)
        d_key = jnp.zeros((2 * OWN, LANES), F32)
        d_value = jnp.zeros((2 * OWN, LANES), F32)
        for start, size in spans:
            span = slice(start, start + size)
            keep = (
                lax.broadcasted_iota(jnp.int32, (1, size), 1) + start
            )
            half = (keep >> 6) & 1
            position = ((half ^ slot) * group + (keep >> 7)) * HEAD_DIM + (keep & 63)
            good = jnp.logical_or(
                jnp.logical_and(keep < slot_len, position < length),
                jnp.logical_and(keep >= slot_len, keep < slot_len + mem_rows),
            )
            bias = jnp.where(good, 0.0, -1e30)
            keys, values = qkv[span, k_lanes], qkv[span, v_lanes]
            weights = jnp.exp(dot(own_q, keys, NT) + bias - log_column)
            slopes = dot(own_g, values, NT)
            scores = low(weights * (slopes - delta_column))
            d_query += dot(scores, keys)

            queries, grads = qkv[span, q_lanes], grad_rows[span, q_lanes]

            def row_pair(ref):
                return jnp.concatenate(
                    [
                        jnp.broadcast_to(ref[2 * pair + k : 2 * pair + k + 1, span], (OWN, size))
                        for k in range(2)
                    ],
                    0,
                )

            weights = jnp.exp(dot(own_k, queries, NT) + own_bias - row_pair(log_row))
            slopes = dot(own_v, grads, NT)
            scores = low(weights * (slopes - row_pair(delta_row)))
            d_value += dot(low(weights), grads)
            d_key += dot(scores, queries)
        packed[:, q_lanes] = low(join_heads(d_query) * 0.125)
        packed[:, k_lanes] = low(join_heads(d_key) * 0.125)
        packed[:, v_lanes] = low(join_heads(d_value))

    share = 1.0 / group
    row = lax.broadcasted_iota(jnp.int32, (OWN, 1), 0)
    row_weight = low(jnp.where(row < ROWS, 1.0, share))
    rows = jnp.concatenate([tokens[slot], arrived[...], memory[slot]], 0)
    scaled = packed[...] * row_weight
    for at in range(0, 3 * WIDTH, WIDTH):
        cols = slice(at, at + WIDTH)
        grad_weight[:, cols] = low(dot(rows, scaled[:, cols], TN))
    emit_blocks(
        grad_weight, keep_out, send_out, REDUCE_QKV, block, 16, slice(0, 16), slice(0, 3 * WIDTH)
    )
    query_bias = jnp.sum(high(scaled[:, :WIDTH]), axis=0, keepdims=True)
    value_bias = jnp.sum(high(scaled[:, 2 * WIDTH :]), axis=0, keepdims=True)
    vec = jnp.concatenate([query_bias, value_bias, vector_grads[2:8, :]], 0)
    ups = up_grads[...]
    lane8 = lane_index((8, LANES))
    for p in range(BLOCKS):
        g = p // 8
        top = roll_lanes(vec[:, g * LANES : (g + 1) * LANES], -16 * (p % 8))
        top = jnp.where(lane8 < 16, top, 0.0)
        g = p // 2
        bottom = roll_lanes(ups[:, g * LANES : (g + 1) * LANES], -64 * (p % 2))
        both = jnp.concatenate([top, bottom], 0)
        extra[p * 16 : (p + 1) * 16, :] = split_lanes(both)
    emit_blocks(
        extra,
        keep_out,
        send_out,
        REDUCE_QKV,
        block,
        16,
        slice(0, 16),
        slice(3 * WIDTH, 3 * WIDTH + LANES),
    )

    grad_in = first_grad[...] + dot(packed[...], weight[...], NT)
    square = squares[0]
    for k in range(1, group):
        square += squares[k]
    square = square[:4] + square[4:]
    square = jnp.concatenate([square[k : k + 1] for k in range(4)], 1)
    first, second, _ = split_three(square)
    tail = low(jnp.concatenate([first, second, jnp.zeros((14, WIDTH), F32)], 0))
    own_out[:64, :] = low(grad_in[:64])
    own_out[64:96, :] = low(grad_in[ROWS:])
    own_out[96:, :] = tail
    give_out[:96, :] = low(grad_in[64:])
    give_out[96:, :] = tail


def split_lanes(v):
    first = high(low(v))
    second = pltpu.roll(v - first, 64, v.ndim - 1)
    lanes = lax.broadcasted_iota(jnp.int32, v.shape, v.ndim - 1)
    return low(jnp.where(lanes < 64, first, second))


def fold_kernel(width, keep, other, keep_out, send_out):
    half = keep.shape[0] // 2
    for start, out in ((0, keep_out), (half, send_out)):
        span = slice(start, start + half)
        total = high(keep[span, :, :width]) + high(other[span, :, :width])
        out[:, :, :width] = low(total)
        for k in range(half):
            extra = high(keep[start + k, :, width:]) + high(other[start + k, :, width:])
            out[k, :, width:] = split_lanes(extra + pltpu.roll(extra, 64, 1))


def fold_with_extra(keep, other):
    shape = (keep.shape[0] // 2,) + keep.shape[1:]
    return pl.pallas_call(
        functools.partial(fold_kernel, 3 * WIDTH),
        out_shape=[jax.ShapeDtypeStruct(shape, BF)] * 2,
        name="fold",
    )(keep, other)


def fold_plain(keep, other):
    half = keep.shape[0] // 2
    return tuple(
        low(high(keep[part]) + high(other[part])) for part in (slice(0, half), slice(half, None))
    )


def emit_kernel(layout, mem_rows, *refs):
    lengths, out_own, out_got, grad_own, grad_got = refs[:5]
    out_tokens, out_memory, grad_tokens, grad_memory, rms = refs[5:]
    slot = lax.axis_index("seq") // layout.group
    for own, got, tokens, memory in (
        (out_own, out_got, out_tokens, out_memory),
        (grad_own, grad_got, grad_tokens, grad_memory),
    ):
        for source, at in ((own, slot), (got, 1 - slot)):
            tokens[at] = source[:64, :]
            memory[at] = low(high(source[64:96, :])[:mem_rows])
    result = []
    for source, at in ((grad_own, slot), (grad_got, 1 - slot)):
        tail = high(source[96:112, :])
        square = tail[0:1] + tail[1:2]
        result.append(jnp.sqrt(square / lengths[at].astype(F32)))
    row = lax.broadcasted_iota(jnp.int32, (2, WIDTH), 0)
    rms[...] = jnp.where(row == slot, result[0], result[1])


def call(kernel, name, outs, scratch, args, smem=1, limit=48, flops=0):
    vmem = pl.BlockSpec(memory_space=pltpu.VMEM)
    in_specs = [pl.BlockSpec(memory_space=pltpu.SMEM)] * smem + [vmem] * (len(args) - smem)
    size = sum(a.size * a.dtype.itemsize for a in args)
    return pl.pallas_call(
        kernel,
        out_shape=[jax.ShapeDtypeStruct(shape, kind) for shape, kind in outs],
        in_specs=in_specs,
        out_specs=[vmem] * len(outs),
        scratch_shapes=[pltpu.VMEM(shape, kind) for shape, kind in scratch],
        compiler_params=pltpu.CompilerParams(vmem_limit_bytes=limit * MIB),
        cost_estimate=pl.CostEstimate(flops=flops, bytes_accessed=size, transcendentals=0),
        name=name,
    )(*args)


def local(
    layout,
    tokens,
    memory,
    lengths,
    w_qkv,
    b_query,
    b_value,
    w_out,
    b_out,
    gain_one,
    shift_one,
    w_up,
    b_up,
    w_down,
    b_down,
    gain_two,
    shift_two,
    cot_tokens,
    cot_memory,
):
    mem_rows = memory.shape[1]
    tok_rows = tokens.shape[1]
    slot_len = tok_rows * layout.seq
    key_rows = slot_len + MEM_KEYS
    partner = layout.seq_bits - 1
    slot = lax.axis_index("seq") // layout.group

    def pick(x, at):
        return lax.dynamic_index_in_dim(x, at, 0, False)

    arrived = layout.swap(pick(tokens, 1 - slot), partner)
    near, far = layout.gather_group(jnp.concatenate([pick(tokens, slot), arrived], 0)[None])

    vectors = jnp.stack(
        [b_query, b_value, b_out, gain_one, shift_one, b_down, gain_two, shift_two]
    )
    vectors = layout.join_low(vectors, 1)
    extra = jnp.concatenate(
        [
            jnp.pad(vectors, ((0, 0), (0, LANES - 16))),
            jnp.pad(layout.join_low(b_up, 0)[None], ((0, 7), (0, LANES - 64))),
        ],
        0,
    )
    first = jnp.concatenate([layout.join_low(w_qkv, 0), layout.join_low(w_out, 0), extra], 1)
    qkv_parts = layout.gather(first[None], GATHER_QKV)
    up_parts = layout.gather(layout.join_low(w_up, 0)[None], GATHER_UP)
    down_parts = layout.gather(layout.join_low(w_down, 0)[None], GATHER_DOWN)
    cot_arrived = layout.swap(pick(cot_tokens, 1 - slot), partner)
    pad_rows = ((0, 0), (0, MEM_PAD - mem_rows), (0, 0))
    memory_full = jnp.pad(memory, pad_rows)
    cot_memory_full = jnp.pad(cot_memory, pad_rows)

    qkv, attn, lse_col, vector_rows, up_bias = call(
        functools.partial(forward_kernel, layout, mem_rows, slot_len),
        "attention_forward",
        [
            ((key_rows, 3 * WIDTH), BF),
            ((OWN, WIDTH), F32),
            ((OWN, LANES), F32),
            ((8, WIDTH), F32),
            ((8, FF), F32),
        ],
        [((slot_len + MEM_PAD, WIDTH), BF), ((WIDTH, 3 * WIDTH), BF), ((WIDTH, LANES), BF)],
        (lengths, near, far, memory_full, *qkv_parts),
    )
    (
        pack,
        grad_mem,
        lse_mem,
        delta_mem,
        delta_col,
        first_grad,
        out_own,
        out_send,
        attn_low,
        branch_low,
        hidden_low,
        grad_linear,
        active,
        feed_low,
        vector_grads,
        up_grads,
    ) = call(
        functools.partial(feed_kernel, layout, mem_rows),
        "feed_forward",
        [
            ((1, ROWS + 16, WIDTH), BF),
            ((MEM_PAD, WIDTH), BF),
            ((8, LANES), F32),
            ((8, LANES), F32),
            ((OWN, LANES), F32),
            ((OWN, WIDTH), F32),
            ((64 + MEM_PAD, WIDTH), BF),
            ((64 + MEM_PAD, WIDTH), BF),
            ((OWN, WIDTH), BF),
            ((OWN, WIDTH), BF),
            ((OWN, WIDTH), BF),
            ((OWN, FF), BF),
            ((OWN, FF), BF),
            ((OWN, WIDTH), BF),
            ((8, WIDTH), F32),
            ((8, FF), F32),
        ],
        [((WIDTH, WIDTH), BF), ((WIDTH, FF), BF), ((FF, WIDTH), BF), ((OWN, FF), F32)],
        (
            lengths,
            tokens,
            arrived,
            memory_full,
            cot_tokens,
            cot_arrived,
            cot_memory_full,
            attn,
            lse_col,
            vector_rows,
            up_bias,
            *qkv_parts,
            *up_parts,
            *down_parts,
        ),
    )
    grads_near, grads_far = layout.gather_group(pack)
    out_got = layout.swap(out_send, partner)
    half = BLOCKS // 2
    up_keep, up_send, down_keep, down_send = call(
        functools.partial(weight_kernel, layout),
        "weight_gradients",
        [
            ((half, 16, FF), BF),
            ((half, 16, FF), BF),
            ((half, 80, WIDTH), BF),
            ((half, 80, WIDTH), BF),
        ],
        [((WIDTH, FF), BF), ((FF, WIDTH), BF), ((WIDTH, WIDTH), BF)],
        (attn_low, branch_low, hidden_low, grad_linear, active, feed_low),
        smem=0,
    )
    up_total = layout.reduce(up_keep, up_send, REDUCE_UP, fold_plain)
    down_total = layout.reduce(down_keep, down_send, REDUCE_DOWN, fold_plain)
    qkv_keep, qkv_send, grad_own, grad_send = call(
        functools.partial(backward_kernel, layout, mem_rows, slot_len),
        "attention_backward",
        [
            ((half, 16, 3 * WIDTH + LANES), BF),
            ((half, 16, 3 * WIDTH + LANES), BF),
            ((112, WIDTH), BF),
            ((112, WIDTH), BF),
        ],
        [
            ((WIDTH, 3 * WIDTH), BF),
            ((key_rows, WIDTH), BF),
            ((8, key_rows), F32),
            ((8, key_rows), F32),
            ((layout.group, 8, LANES), F32),
            ((OWN, 3 * WIDTH), BF),
            ((WIDTH, 3 * WIDTH), BF),
            ((WIDTH, LANES), BF),
        ],
        (
            lengths,
            tokens,
            arrived,
            memory_full,
            qkv,
            grads_near,
            grads_far,
            grad_mem,
            lse_mem,
            delta_mem,
            lse_col,
            delta_col,
            first_grad,
            vector_grads,
            up_grads,
            *qkv_parts,
        ),
    )
    qkv_total = layout.reduce(qkv_keep, qkv_send, REDUCE_QKV, fold_with_extra)
    grad_got = layout.swap(grad_send, partner)

    def add(pair):
        return high(pair[0][0]) + high(pair[1][0])

    up_sum = layout.reduce_low(add(up_total), 0)
    down_sum = add(down_total)
    out_sum = layout.reduce_low(down_sum[64:], 0)
    down_sum = layout.reduce_low(down_sum[:64], 0)
    qkv_sum = add(qkv_total)
    extra_sum = qkv_sum[:, 3 * WIDTH :]
    qkv_sum = layout.reduce_low(qkv_sum[:, : 3 * WIDTH], 0)
    vec = layout.reduce_low(extra_sum[:8, :16] + extra_sum[:8, 64:80], 1)
    up_vec = layout.reduce_low(extra_sum[8, :64] + extra_sum[8, 64:], 0)

    out_tokens, out_memory, grad_tokens, grad_memory, rms = call(
        functools.partial(emit_kernel, layout, mem_rows),
        "emit",
        [
            (tokens.shape, BF),
            (memory.shape, BF),
            (tokens.shape, BF),
            (memory.shape, BF),
            ((2, WIDTH), F32),
        ],
        [],
        (lengths, out_own, out_got, grad_own, grad_got),
    )
    return (
        out_tokens,
        out_memory,
        grad_tokens,
        grad_memory,
        qkv_sum,
        vec[0],
        vec[1],
        out_sum,
        vec[2],
        vec[3],
        vec[4],
        up_sum,
        up_vec,
        down_sum,
        vec[5],
        vec[6],
        vec[7],
        rms,
    )


def solution(mesh):
    rows = P("dp", "seq", None)
    slots = P("dp", None, None)
    matrix = P(("dp", "seq"), None)
    vector = P(("dp", "seq"))
    weights = (
        matrix,
        vector,
        vector,
        matrix,
        vector,
        vector,
        vector,
        matrix,
        vector,
        matrix,
        vector,
        vector,
        vector,
    )
    return jax.shard_map(
        functools.partial(local, Layout(mesh)),
        mesh=mesh,
        in_specs=(rows, slots, P("dp"), *weights, rows, slots),
        out_specs=(rows, slots, rows, slots, *weights, P("dp", None)),
        check_vma=False,
    )
```

time: 1170 us -> 157 us (0.13)
  waiting for transfers between devices: 722 us -> 63.3 us
  blocking collectives: 276 us -> 0 us
  matrix products: 66.6 us -> 0 us
  starting transfers between devices: 0.54 us -> 40.1 us
  local copies, waits for them, and re-layouts: 49.9 us -> 12.2 us
  Pallas kernels: 0 us -> 29 us
  other arithmetic: 32.7 us -> 11.1 us
  between operations: 14.2 us -> 1.1 us
    reduce_scatter x4 -> x0, waiting for transfers between devices: 465 us -> none  [local(): lax.psum_scatter(totals, ('dp', 'seq'), scatter_dimension=0, tiled=True)]
    all_gather x11 -> x0, blocking collectives: 180 us -> none  [the longest x6 77.3 us: joined(): lax.all_gather(a.astype(kind), axis)]
    while x10 -> x0, waiting for transfers between devices: 130 us -> none
    unnamed x2 -> x0, blocking collectives: 80.6 us -> none
    all_gather x3 -> x0, waiting for transfers between devices: 79.7 us -> none  [the longest x1 58.4 us: local(): lax.all_gather(shards[9], ('dp', 'seq'), axis=0, tiled=True)]
    dot_general x72 -> x0, matrix products: 66.6 us -> none  [the longest x2 8.18 us: one_slot(): jnp.einsum('rd,rf->df', hidden_low, linear_scaled, preferred_element_type...]
    ppermute x0 -> x41, waiting for transfers between devices: none -> 63.3 us  [swap(): return lax.ppermute(x, axis, [(i, i ^ mask) for i in range(size)])]
    psum x2 -> x0, waiting for transfers between devices: 42.5 us -> none  [one_slot(): lax.psum((memory_on_tokens[0].reshape(mem_rows, model_width), tokens_on_m...]
  transfers between devices with their start and end apart: 13 -> 41, of which waited for: 12 -> 16; matrix products, arithmetic and copies ran while one was open for 7% -> 10% of each run, Pallas kernels for 0% -> 13%
where the time goes in v1:
time: 157 us
  waiting for transfers between devices  63.3 us (40%)
  starting transfers between devices  40.1 us (26%)
  Pallas kernels  29 us (18%)
  local copies, waits for them, and re-layouts  12.2 us (8%)
  other arithmetic  11.1 us (7%)
    ppermute x41, waiting for transfers between devices, swap(): return lax.ppermute(x, axis, [(i, i ^ mask) for i in range(size)])  63.3 us
    ppermute x41, starting transfers between devices, swap(): return lax.ppermute(x, axis, [(i, i ^ mask) for i in range(size)])  40.1 us
    pallas_call x5, Pallas kernels, call(): pl.pallas_call(kernel, out_shape=[jax.ShapeDtypeStruct(shape, kind) for s...  20.7 us
    pallas_call x4, Pallas kernels, fold_with_extra(): pl.pallas_call(functools.partial(fold_kernel, 3 * WIDTH), out_shape=[jax....  8.31 us
    unnamed x51, local copies, waits for them, and re-layouts  8.02 us
    convert_element_type x8, other arithmetic, low(): return v.astype(BF)  6.04 us
  transfers between devices with their start and end apart: 41, of which 16 were waited for; matrix products, arithmetic and copies ran while one was open for 10% of the time, Pallas kernels for 13%

profile of v1, /device:TPU:0, one launch (start us, length us, event | category | flops | bytes accessed | tf_op | source)
XLA Modules:
  0.0 156.7 jit_solution(15021505795197994780)
XLA Ops:
  0.7 4.1 %collective-permute-start.10 = (bf16[1,16,2048]{2,1,0:T(8,128)(2,1)}, bf16[1,16,2048]{2,1,0:T(8,128)(2,1)S(1)}, u32[]{:S(2)}, u32[]{:S(2)}) collective-permute-start(bf16[1,16,2048]{2,1,0:T(8,128)(2,1)} %bitcast.51), channel_id=1, source_target_pairs={{0,4},{1,5},{2,6},{3,7},{4,0},{5,1},{6,2},{7,3},{8,12},{9,13},{10,... | collective-permute-start | bytes 196616 | tf_op jit(solution)/shard_map/ppermute | solution.py:75
  6.5 2.8 %collective-permute-start.4 = (bf16[1,16,2176]{2,1,0:T(8,128)(2,1)S(1)}, bf16[1,16,2176]{2,1,0:T(8,128)(2,1)S(1)}, u32[]{:S(2)}, u32[]{:S(2)}) collective-permute-start(bf16[1,16,2176]{2,1,0:T(8,128)(2,1)S(1)} %fusion.8), channel_id=1, source_target_pairs={{0,4},{1,5},{2,6},{3,7},{4,0},{5,1},{6,2},{7,3},{8,12},{9,13},{10,... | collective-permute-start | bytes 208904 | tf_op jit(solution)/shard_map/ppermute | solution.py:75
  10.4 3.1 %collective-permute-done.16 = bf16[1,64,512]{2,1,0:T(8,128)(2,1)S(1)} collective-permute-done((bf16[1,64,512]{2,1,0:T(8,128)(2,1)}, bf16[1,64,512]{2,1,0:T(8,128)(2,1)S(1)}, u32[]{:S(2)}, u32[]{:S(2)}) %collective-permute-start.16) | collective-permute-done | bytes 65568 | tf_op jit(solution)/shard_map/ppermute | solution.py:75
  14.4 1.7 %collective-permute-start.17 = (bf16[2,64,512]{2,1,0:T(8,128)(2,1)S(1)}, bf16[2,64,512]{2,1,0:T(8,128)(2,1)S(1)}, u32[]{:S(2)}, u32[]{:S(2)}) collective-permute-start(bf16[2,64,512]{2,1,0:T(8,128)(2,1)S(1)} %pad_maximum_fusion.9), channel_id=1, source_target_pairs={{0,2},{1,3},{2,0},{3,1},{4,6},{5,7},{6,4},{7,5},{8,10},{9,11},{10,... | collective-permute-start | bytes 393224 | tf_op jit(solution)/shard_map/ppermute | solution.py:75
  16.1 1.6 collective-permute-start.5
  18.5 1.6 %collective-permute-start.11 = (bf16[2,16,2048]{2,1,0:T(8,128)(2,1)S(1)}, bf16[2,16,2048]{2,1,0:T(8,128)(2,1)S(1)}, u32[]{:S(2)}, u32[]{:S(2)}) collective-permute-start(bf16[2,16,2048]{2,1,0:T(8,128)(2,1)S(1)} %pad_maximum_fusion.8), channel_id=1, source_target_pairs={{0,16},{8,24},{16,0},{24,8},{1,17},{9,25},{17,1},{25,9},{2,18},{10... | collective-permute-start | bytes 393224 | tf_op jit(solution)/shard_map/ppermute | solution.py:75
  20.1 1.8 %collective-permute-start.18 = (bf16[4,64,512]{2,1,0:T(8,128)(2,1)S(1)}, bf16[4,64,512]{2,1,0:T(8,128)(2,1)S(1)}, u32[]{:S(2)}, u32[]{:S(2)}) collective-permute-start(bf16[4,64,512]{2,1,0:T(8,128)(2,1)S(1)} %pad_maximum_fusion.6), channel_id=1, source_target_pairs={{0,8},{8,0},{16,24},{24,16},{1,9},{9,1},{17,25},{25,17},{2,10},{10... | collective-permute-start | bytes 786440 | tf_op jit(solution)/shard_map/ppermute | solution.py:75
  21.9 1.6 %collective-permute-start.6 = (bf16[4,16,2176]{2,1,0:T(8,128)(2,1)S(1)}, bf16[4,16,2176]{2,1,0:T(8,128)(2,1)S(1)}, u32[]{:S(2)}, u32[]{:S(2)}) collective-permute-start(bf16[4,16,2176]{2,1,0:T(8,128)(2,1)S(1)} %pad_maximum_fusion.3), channel_id=1, source_target_pairs={{0,16},{8,24},{16,0},{24,8},{1,17},{9,25},{17,1},{25,9},{2,18},{10... | collective-permute-start | bytes 835592 | tf_op jit(solution)/shard_map/ppermute | solution.py:75
  24.7 3.3 %collective-permute-done.18 = bf16[4,64,512]{2,1,0:T(8,128)(2,1)S(1)} collective-permute-done((bf16[4,64,512]{2,1,0:T(8,128)(2,1)S(1)}, bf16[4,64,512]{2,1,0:T(8,128)(2,1)S(1)}, u32[]{:S(2)}, u32[]{:S(2)}) %collective-permute-start.18) | collective-permute-done | bytes 262176 | tf_op jit(solution)/shard_map/ppermute | solution.py:75
  28.0 1.8 %collective-permute-start.19 = (bf16[8,64,512]{2,1,0:T(8,128)(2,1)S(1)}, bf16[8,64,512]{2,1,0:T(8,128)(2,1)S(1)}, u32[]{:S(2)}, u32[]{:S(2)}) collective-permute-start(bf16[8,64,512]{2,1,0:T(8,128)(2,1)S(1)} %pad_maximum_fusion.2.refs_19_), channel_id=1, source_target_pairs={{0,16},{8,24},{16,0},{24,8},{1,17},{9,25},{17,1},{25,9},{2,18},{10... | collective-permute-start | bytes 1572872 | tf_op jit(solution)/shard_map/ppermute | solution.py:75
  33.8 12.0 %collective-permute-done.2 = bf16[1,128,512]{2,1,0:T(8,128)(2,1)S(1)} collective-permute-done((bf16[1,128,512]{2,1,0:T(8,128)(2,1)S(1)}, bf16[1,128,512]{2,1,0:T(8,128)(2,1)S(1)}, u32[]{:S(2)}, u32[]{:S(2)}) %collective-permute-start.2) | collective-permute-done | bytes 131104 | tf_op jit(solution)/shard_map/ppermute | solution.py:75
  48.5 3.1 %collective-permute-start.1 = (bf16[64,512]{1,0:T(8,128)(2,1)S(1)}, bf16[64,512]{1,0:T(8,128)(2,1)S(1)}, u32[]{:S(2)}, u32[]{:S(2)}) collective-permute-start(bf16[64,512]{1,0:T(8,128)(2,1)S(1)} %dynamic-slice_bitcast_fusion.1), channel_id=1, source_target_pairs={{0,4},{1,5},{2,6},{3,7},{4,0},{5,1},{6,2},{7,3},{8,12},{9,13},{10,... | collective-permute-start | bytes 196616 | tf_op jit(solution)/shard_map/ppermute | solution.py:75
  51.7 3.8 %attention_forward.1 = (bf16[640,1536]{1,0:T(8,128)(2,1)S(1)}, f32[160,512]{1,0:T(8,128)S(1)}, f32[160,128]{1,0:T(8,128)S(1)}, f32[8,512]{1,0:T(8,128)S(1)}, f32[8,2048]{1,0:T(8,128)S(1)}) custom-call(s32[2]{0:T(128)S(1)} %copy-done.14, bf16[2,128,512]{2,1,0:T(8,128)(2,1)S(1)} %pad_maximum_fusion.4.refs_1_, ...), custom_call_target="tpu_custom_call" | custom-call | bytes 2818056 | tf_op jit(solution)/shard_map/attention_forward/pallas_call | solution.py:631
  57.6 6.5 %feed_forward.1 = (bf16[1,144,512]{2,1,0:T(8,128)(2,1)S(1)}, bf16[32,512]{1,0:T(8,128)(2,1)S(1)}, f32[8,128]{1,0:T(8,128)S(1)}, f32[8,128]{1,0:T(8,128)S(1)}, f3...) custom-call(s32[2]{0:T(128)S(1)} %copy-done.14, ...), custom_call_target="tpu_custom_call" | custom-call | bytes 7438344 | tf_op jit(solution)/shard_map/feed_forward/pallas_call | solution.py:631
  66.5 2.7 %weight_gradients.1 = (bf16[16,16,2048]{2,1,0:T(8,128)(2,1)S(1)}, bf16[16,16,2048]{2,1,0:T(8,128)(2,1)S(1)}, bf16[16,80,512]{2,1,0:T(8,128)(2,1)S(1)}, bf16[16,80,512]{2,1,0:T(8,128)(2,1)}) custom-call(bf16[160,512]{1,0:T(8,128)(2,1)S(1)} %get-tuple-element.91.refs_0_, bf16[160,512]{1,0:T(8,128)(2,1)S(1)} %get-tuple-element.92.refs_1_, ...), custom_call_target="tpu_custom_call" | custom-call | bytes 1966080 | tf_op jit(solution)/shard_map/weight_gradients/pallas_call | solution.py:631
  69.8 5.6 %collective-permute-done.23 = bf16[1,144,512]{2,1,0:T(8,128)(2,1)S(1)} collective-permute-done((bf16[1,144,512]{2,1,0:T(8,128)(2,1)S(1)}, bf16[1,144,512]{2,1,0:T(8,128)(2,1)S(1)}, u32[]{:S(2)}, u32[]{:S(2)}) %collective-permute-start.23) | collective-permute-done | bytes 147488 | tf_op jit(solution)/shard_map/ppermute | solution.py:75
  77.1 6.4 %attention_backward.1 = (bf16[16,16,1664]{2,1,0:T(8,128)(2,1)S(1)}, bf16[16,16,1664]{2,1,0:T(8,128)(2,1)S(1)}, bf16[112,512]{1,0:T(8,128)(2,1)S(1)}, bf16[112,512]{1,0:T(8,128)(2,1)S(1)}) custom-call(s32[2]{0:T(128)S(1)} %copy-done.14, bf16[2,64,512]{2,1,0:T(8,128)(2,1)S(1)} %copy-done.9, bf16[64,512]{1,0:T(8,128)(2,1)S(1)} %collective-permute-done.refs_2_, ...), custom_call_target="tpu_custom_call" | custom-call | bytes 5660680 | tf_op jit(solution)/shard_map/attention_backward/pallas_call | solution.py:631
  86.9 2.7 %fold.4 = (bf16[8,16,1664]{2,1,0:T(8,128)(2,1)}, bf16[8,16,1664]{2,1,0:T(8,128)(2,1)}) custom-call(bf16[16,16,1664]{2,1,0:T(8,128)(2,1)} %copy-done.10, bf16[16,16,1664]{2,1,0:T(8,128)(2,1)} %copy-done.15), custom_call_target="tpu_custom_call" | custom-call | tf_op jit(solution)/shard_map/fold/pallas_call | solution.py:593
  91.1 8.3 %collective-permute-done.37 = bf16[8,16,2048]{2,1,0:T(8,128)(2,1)} collective-permute-done((bf16[8,16,2048]{2,1,0:T(8,128)(2,1)}, bf16[8,16,2048]{2,1,0:T(8,128)(2,1)}, u32[]{:S(2)}, u32[]{:S(2)}) %collective-permute-start.37) | collective-permute-done | bytes 524320 | tf_op jit(solution)/shard_map/ppermute | solution.py:75
  99.4 1.9 %add_convert_fusion.7 = (bf16[4,16,2048]{2,1,0:T(8,128)(2,1)S(1)}, bf16[4,16,2048]{2,1,0:T(8,128)(2,1)}) fusion(bf16[8,16,2048]{2,1,0:T(8,128)(2,1)} %collective-permute-done.37, bf16[8,16,2048]{2,1,0:T(8,128)(2,1)S(1)} %get-tuple-element.122), kind=kLoop, calls=%fused_computation.10 | loop fusion | flops 1048576 | bytes 1572864 | tf_op jit(solution)/shard_map/convert_element_type | solution.py:41
  102.8 1.7 %add_convert_fusion.1 = (bf16[8,80,512]{2,1,0:T(8,128)(2,1)S(1)}, bf16[8,80,512]{2,1,0:T(8,128)(2,1)S(1)}) fusion(bf16[16,80,512]{2,1,0:T(8,128)(2,1)} %collective-permute-done.31, bf16[16,80,512]{2,1,0:T(8,128)(2,1)S(1)} %get-tuple-element.97), kind=kLoop, calls=%fused_computation.1 | loop fusion | flops 2621440 | bytes 3932160 | tf_op jit(solution)/shard_map/convert_element_type | solution.py:41
  104.6 2.1 %fold.5 = (bf16[4,16,1664]{2,1,0:T(8,128)(2,1)}, bf16[4,16,1664]{2,1,0:T(8,128)(2,1)}) custom-call(bf16[8,16,1664]{2,1,0:T(8,128)(2,1)} %get-tuple-element.83.keep, bf16[8,16,1664]{2,1,0:T(8,128)(2,1)} %collective-permute-done.27.other), custom_call_target="tpu_custom_call" | custom-call | tf_op jit(solution)/shard_map/fold/pallas_call | solution.py:593
  106.7 1.9 %collective-permute-start.28 = (bf16[4,16,1664]{2,1,0:T(8,128)(2,1)}, bf16[4,16,1664]{2,1,0:T(8,128)(2,1)S(1)}, u32[]{:S(2)}, u32[]{:S(2)}) collective-permute-start(bf16[4,16,1664]{2,1,0:T(8,128)(2,1)} %get-tuple-element.86), channel_id=1, source_target_pairs={{0,8},{8,0},{16,24},{24,16},{1,9},{9,1},{17,25},{25,17},{2,10},{10... | collective-permute-start | bytes 638984 | tf_op jit(solution)/shard_map/ppermute | solution.py:75
  111.9 2.2 %collective-permute-start.22 = (bf16[96,512]{1,0:T(8,128)(2,1)S(1)}, bf16[96,512]{1,0:T(8,128)(2,1)S(1)}, u32[]{:S(2)}, u32[]{:S(2)}) collective-permute-start(bf16[96,512]{1,0:T(8,128)(2,1)S(1)} %get-tuple-element.65), channel_id=1, source_target_pairs={{0,4},{1,5},{2,6},{3,7},{4,0},{5,1},{6,2},{7,3},{8,12},{9,13},{10,... | collective-permute-start | bytes 294920 | tf_op jit(solution)/shard_map/ppermute | solution.py:75
  114.0 8.1 %collective-permute-done.22.refs_2_ = bf16[96,512]{1,0:T(8,128)(2,1)S(1)} collective-permute-done((bf16[96,512]{1,0:T(8,128)(2,1)S(1)}, bf16[96,512]{1,0:T(8,128)(2,1)S(1)}, u32[]{:S(2)}, u32[]{:S(2)}) %collective-permute-start.22) | collective-permute-done | bytes 98336 | tf_op jit(solution)/shard_map/ppermute | solution.py:75
  124.7 1.8 %collective-permute-done.28.other = bf16[4,16,1664]{2,1,0:T(8,128)(2,1)S(1)} collective-permute-done((bf16[4,16,1664]{2,1,0:T(8,128)(2,1)}, bf16[4,16,1664]{2,1,0:T(8,128)(2,1)S(1)}, u32[]{:S(2)}, u32[]{:S(2)}) %collective-permute-start.28) | collective-permute-done | bytes 213024 | tf_op jit(solution)/shard_map/ppermute | solution.py:75
  127.1 1.9 %fold.6 = (bf16[2,16,1664]{2,1,0:T(8,128)(2,1)}, bf16[2,16,1664]{2,1,0:T(8,128)(2,1)}) custom-call(bf16[4,16,1664]{2,1,0:T(8,128)(2,1)} %get-tuple-element.85.keep, bf16[4,16,1664]{2,1,0:T(8,128)(2,1)} %copy-done.19), custom_call_target="tpu_custom_call" | custom-call | tf_op jit(solution)/shard_map/fold/pallas_call | solution.py:593
  131.5 4.3 %collective-permute-done.29.other = bf16[2,16,1664]{2,1,0:T(8,128)(2,1)S(1)} collective-permute-done((bf16[2,16,1664]{2,1,0:T(8,128)(2,1)}, bf16[2,16,1664]{2,1,0:T(8,128)(2,1)S(1)}, u32[]{:S(2)}, u32[]{:S(2)}) %collective-permute-start.29) | collective-permute-done | bytes 106528 | tf_op jit(solution)/shard_map/ppermute | solution.py:75
  136.5 1.7 %fold.7 = (bf16[1,16,1664]{2,1,0:T(8,128)(2,1)}, bf16[1,16,1664]{2,1,0:T(8,128)(2,1)}) custom-call(bf16[2,16,1664]{2,1,0:T(8,128)(2,1)} %get-tuple-element.87.keep, bf16[2,16,1664]{2,1,0:T(8,128)(2,1)} %copy-done.20), custom_call_target="tpu_custom_call" | custom-call | tf_op jit(solution)/shard_map/fold/pallas_call | solution.py:593
  138.9 4.6 %collective-permute-done.30 = bf16[1,16,1664]{2,1,0:T(8,128)(2,1)S(1)} collective-permute-done((bf16[1,16,1664]{2,1,0:T(8,128)(2,1)}, bf16[1,16,1664]{2,1,0:T(8,128)(2,1)S(1)}, u32[]{:S(2)}, u32[]{:S(2)}) %collective-permute-start.30) | collective-permute-done | bytes 53280 | tf_op jit(solution)/shard_map/ppermute | solution.py:75
  145.6 4.2 %collective-permute-done.34 = bf16[2,80,512]{2,1,0:T(8,128)(2,1)S(1)} collective-permute-done((bf16[2,80,512]{2,1,0:T(8,128)(2,1)S(1)}, bf16[2,80,512]{2,1,0:T(8,128)(2,1)S(1)}, u32[]{:S(2)}, u32[]{:S(2)}) %collective-permute-start.34) | collective-permute-done | bytes 163872 | tf_op jit(solution)/shard_map/ppermute | solution.py:75
  151.2 4.2 %collective-permute-done.35 = bf16[1,80,512]{2,1,0:T(8,128)(2,1)S(1)} collective-permute-done((bf16[1,80,512]{2,1,0:T(8,128)(2,1)S(1)}, bf16[1,80,512]{2,1,0:T(8,128)(2,1)S(1)}, u32[]{:S(2)}, u32[]{:S(2)}) %collective-permute-start.35) | collective-permute-done | bytes 81952 | tf_op jit(solution)/shard_map/ppermute | solution.py:75
  (145 shorter events, 40.7 us)
Async XLA Ops:
  0.7 16.9 %collective-permute-start.10 = (bf16[1,16,2048]{2,1,0:T(8,128)(2,1)}, bf16[1,16,2048]{2,1,0:T(8,128)(2,1)S(1)}, u32[]{:S(2)}, u32[]{:S(2)}) collective-permute-start(bf16[1,16,2048]{2,1,0:T(8,128)(2,1)} %bitcast.51), channel_id=1, source_target_pairs={{0,4},{1,5},{2,6},{3,7},{4,0},{5,1},{6,2},{7,3},{8,12},{9,13},{10,... | collective-permute-start | bytes 196616 | tf_op jit(solution)/shard_map/ppermute | solution.py:75
  4.8 8.7 %collective-permute-start.16 = (bf16[1,64,512]{2,1,0:T(8,128)(2,1)}, bf16[1,64,512]{2,1,0:T(8,128)(2,1)S(1)}, u32[]{:S(2)}, u32[]{:S(2)}) collective-permute-start(bf16[1,64,512]{2,1,0:T(8,128)(2,1)} %bitcast.47), channel_id=1, source_target_pairs={{0,4},{1,5},{2,6},{3,7},{4,0},{5,1},{6,2},{7,3},{8,12},{9,13},{10,... | collective-permute-start | bytes 196616 | tf_op jit(solution)/shard_map/ppermute | solution.py:75
  6.5 9.5 %collective-permute-start.4 = (bf16[1,16,2176]{2,1,0:T(8,128)(2,1)S(1)}, bf16[1,16,2176]{2,1,0:T(8,128)(2,1)S(1)}, u32[]{:S(2)}, u32[]{:S(2)}) collective-permute-start(bf16[1,16,2176]{2,1,0:T(8,128)(2,1)S(1)} %fusion.8), channel_id=1, source_target_pairs={{0,4},{1,5},{2,6},{3,7},{4,0},{5,1},{6,2},{7,3},{8,12},{9,13},{10,... | collective-permute-start | bytes 208904 | tf_op jit(solution)/shard_map/ppermute | solution.py:75
  10.2 22.0 %collective-permute-start = (bf16[64,512]{1,0:T(8,128)(2,1)S(1)}, bf16[64,512]{1,0:T(8,128)(2,1)S(1)}, u32[]{:S(2)}, u32[]{:S(2)}) collective-permute-start(bf16[64,512]{1,0:T(8,128)(2,1)S(1)} %get-tuple-element.133), channel_id=1, source_target_pairs={{0,4},{1,5},{2,6},{3,7},{4,0},{5,1},{6,2},{7,3},{8,12},{9,13},{10,... | collective-permute-start | bytes 196616 | tf_op jit(solution)/shard_map/ppermute | solution.py:75
  16.1 5.8 %collective-permute-start.5 = (bf16[2,16,2176]{2,1,0:T(8,128)(2,1)S(1)}, bf16[2,16,2176]{2,1,0:T(8,128)(2,1)S(1)}, u32[]{:S(2)}, u32[]{:S(2)}) collective-permute-start(bf16[2,16,2176]{2,1,0:T(8,128)(2,1)S(1)} %pad_maximum_fusion.7), channel_id=1, source_target_pairs={{0,8},{8,0},{16,24},{24,16},{1,9},{9,1},{17,25},{25,17},{2,10},{10... | collective-permute-start | bytes 417800 | tf_op jit(solution)/shard_map/ppermute | solution.py:75
  20.1 7.8 %collective-permute-start.18 = (bf16[4,64,512]{2,1,0:T(8,128)(2,1)S(1)}, bf16[4,64,512]{2,1,0:T(8,128)(2,1)S(1)}, u32[]{:S(2)}, u32[]{:S(2)}) collective-permute-start(bf16[4,64,512]{2,1,0:T(8,128)(2,1)S(1)} %pad_maximum_fusion.6), channel_id=1, source_target_pairs={{0,8},{8,0},{16,24},{24,16},{1,9},{9,1},{17,25},{25,17},{2,10},{10... | collective-permute-start | bytes 786440 | tf_op jit(solution)/shard_map/ppermute | solution.py:75
  21.9 8.3 %collective-permute-start.6 = (bf16[4,16,2176]{2,1,0:T(8,128)(2,1)S(1)}, bf16[4,16,2176]{2,1,0:T(8,128)(2,1)S(1)}, u32[]{:S(2)}, u32[]{:S(2)}) collective-permute-start(bf16[4,16,2176]{2,1,0:T(8,128)(2,1)S(1)} %pad_maximum_fusion.3), channel_id=1, source_target_pairs={{0,16},{8,24},{16,0},{24,8},{1,17},{9,25},{17,1},{25,9},{2,18},{10... | collective-permute-start | bytes 835592 | tf_op jit(solution)/shard_map/ppermute | solution.py:75
  23.5 7.7 %collective-permute-start.12 = (bf16[4,16,2048]{2,1,0:T(8,128)(2,1)S(1)}, bf16[4,16,2048]{2,1,0:T(8,128)(2,1)S(1)}, u32[]{:S(2)}, u32[]{:S(2)}) collective-permute-start(bf16[4,16,2048]{2,1,0:T(8,128)(2,1)S(1)} %pad_maximum_fusion.5), channel_id=1, source_target_pairs={{0,2},{1,3},{2,0},{3,1},{4,6},{5,7},{6,4},{7,5},{8,10},{9,11},{10,... | collective-permute-start | bytes 786440 | tf_op jit(solution)/shard_map/ppermute | solution.py:75
  28.0 19.5 %collective-permute-start.19 = (bf16[8,64,512]{2,1,0:T(8,128)(2,1)S(1)}, bf16[8,64,512]{2,1,0:T(8,128)(2,1)S(1)}, u32[]{:S(2)}, u32[]{:S(2)}) collective-permute-start(bf16[8,64,512]{2,1,0:T(8,128)(2,1)S(1)} %pad_maximum_fusion.2.refs_19_), channel_id=1, source_target_pairs={{0,16},{8,24},{16,0},{24,8},{1,17},{9,25},{17,1},{25,9},{2,18},{10... | collective-permute-start | bytes 1572872 | tf_op jit(solution)/shard_map/ppermute | solution.py:75
  30.3 15.6 %collective-permute-start.7 = (bf16[8,16,2176]{2,1,0:T(8,128)(2,1)S(1)}, bf16[8,16,2176]{2,1,0:T(8,128)(2,1)S(1)}, u32[]{:S(2)}, u32[]{:S(2)}) collective-permute-start(bf16[8,16,2176]{2,1,0:T(8,128)(2,1)S(1)} %pad_maximum_fusion.refs_4_.refs_11_.refs_15_), channel_id=1, source_target_pairs={{0,2},{1,3},{2,0},{3,1},{4,6},{5,7},{6,4},{7,5},{8,10},{9,11},{10,... | collective-permute-start | bytes 1671176 | tf_op jit(solution)/shard_map/ppermute | solution.py:75
  31.3 16.6 %collective-permute-start.13 = (bf16[8,16,2048]{2,1,0:T(8,128)(2,1)S(1)}, bf16[8,16,2048]{2,1,0:T(8,128)(2,1)S(1)}, u32[]{:S(2)}, u32[]{:S(2)}) collective-permute-start(bf16[8,16,2048]{2,1,0:T(8,128)(2,1)S(1)} %pad_maximum_fusion.1.refs_15_), channel_id=1, source_target_pairs={{0,8},{8,0},{16,24},{24,16},{1,9},{9,1},{17,25},{25,17},{2,10},{10... | collective-permute-start | bytes 1572872 | tf_op jit(solution)/shard_map/ppermute | solution.py:75
  32.2 15.9 %collective-permute-start.8 = (bf16[8,16,2176]{2,1,0:T(8,128)(2,1)S(1)}, bf16[8,16,2176]{2,1,0:T(8,128)(2,1)S(1)}, u32[]{:S(2)}, u32[]{:S(2)}) collective-permute-start(bf16[8,16,2176]{2,1,0:T(8,128)(2,1)S(1)} %pad_maximum_fusion.refs_4_.refs_11_.refs_15_), channel_id=1, source_target_pairs={{0,1},{1,0},{2,3},{3,2},{4,5},{5,4},{6,7},{7,6},{8,9},{9,8},{10,11... | collective-permute-start | bytes 1671176 | tf_op jit(solution)/shard_map/ppermute | solution.py:75
  32.2 13.6 %collective-permute-start.2 = (bf16[1,128,512]{2,1,0:T(8,128)(2,1)S(1)}, bf16[1,128,512]{2,1,0:T(8,128)(2,1)S(1)}, u32[]{:S(2)}, u32[]{:S(2)}) collective-permute-start(bf16[1,128,512]{2,1,0:T(8,128)(2,1)S(1)} %maximum_bitcast_fusion), channel_id=1, source_target_pairs={{0,2},{1,3},{2,0},{3,1},{4,6},{5,7},{6,4},{7,5},{8,10},{9,11},{10,... | collective-permute-start | bytes 393224 | tf_op jit(solution)/shard_map/ppermute | solution.py:75
  47.4 9.3 %collective-permute-start.20 = (bf16[8,64,512]{2,1,0:T(8,128)(2,1)S(1)}, bf16[8,64,512]{2,1,0:T(8,128)(2,1)S(1)}, u32[]{:S(2)}, u32[]{:S(2)}) collective-permute-start(bf16[8,64,512]{2,1,0:T(8,128)(2,1)S(1)} %pad_maximum_fusion.2.refs_19_), channel_id=1, source_target_pairs={{0,1},{1,0},{2,3},{3,2},{4,5},{5,4},{6,7},{7,6},{8,9},{9,8},{10,11... | collective-permute-start | bytes 1572872 | tf_op jit(solution)/shard_map/ppermute | solution.py:75
  47.6 9.2 %collective-permute-start.14 = (bf16[8,16,2048]{2,1,0:T(8,128)(2,1)S(1)}, bf16[8,16,2048]{2,1,0:T(8,128)(2,1)S(1)}, u32[]{:S(2)}, u32[]{:S(2)}) collective-permute-start(bf16[8,16,2048]{2,1,0:T(8,128)(2,1)S(1)} %pad_maximum_fusion.1.refs_15_), channel_id=1, source_target_pairs={{0,1},{1,0},{2,3},{3,2},{4,5},{5,4},{6,7},{7,6},{8,9},{9,8},{10,11... | collective-permute-start | bytes 1572872 | tf_op jit(solution)/shard_map/ppermute | solution.py:75
  48.0 8.8 %collective-permute-start.21 = (bf16[8,64,512]{2,1,0:T(8,128)(2,1)S(1)}, bf16[8,64,512]{2,1,0:T(8,128)(2,1)S(1)}, u32[]{:S(2)}, u32[]{:S(2)}) collective-permute-start(bf16[8,64,512]{2,1,0:T(8,128)(2,1)S(1)} %collective-permute-done.19.refs_20_), channel_id=1, source_target_pairs={{0,1},{1,0},{2,3},{3,2},{4,5},{5,4},{6,7},{7,6},{8,9},{9,8},{10,11... | collective-permute-start | bytes 1572872 | tf_op jit(solution)/shard_map/ppermute | solution.py:75
  48.1 8.7 %collective-permute-start.15 = (bf16[8,16,2048]{2,1,0:T(8,128)(2,1)S(1)}, bf16[8,16,2048]{2,1,0:T(8,128)(2,1)S(1)}, u32[]{:S(2)}, u32[]{:S(2)}) collective-permute-start(bf16[8,16,2048]{2,1,0:T(8,128)(2,1)S(1)} %collective-permute-done.13.refs_16_), channel_id=1, source_target_pairs={{0,1},{1,0},{2,3},{3,2},{4,5},{5,4},{6,7},{7,6},{8,9},{9,8},{10,11... | collective-permute-start | bytes 1572872 | tf_op jit(solution)/shard_map/ppermute | solution.py:75
  48.5 8.3 %collective-permute-start.1 = (bf16[64,512]{1,0:T(8,128)(2,1)S(1)}, bf16[64,512]{1,0:T(8,128)(2,1)S(1)}, u32[]{:S(2)}, u32[]{:S(2)}) collective-permute-start(bf16[64,512]{1,0:T(8,128)(2,1)S(1)} %dynamic-slice_bitcast_fusion.1), channel_id=1, source_target_pairs={{0,4},{1,5},{2,6},{3,7},{4,0},{5,1},{6,2},{7,3},{8,12},{9,13},{10,... | collective-permute-start | bytes 196616 | tf_op jit(solution)/shard_map/ppermute | solution.py:75
  69.2 14.5 %collective-permute-start.36 = (bf16[16,16,2048]{2,1,0:T(8,128)(2,1)S(1)}, bf16[16,16,2048]{2,1,0:T(8,128)(2,1)S(1)}, u32[]{:S(2)}, u32[]{:S(2)}) collective-permute-start(bf16[16,16,2048]{2,1,0:T(8,128)(2,1)S(1)} %get-tuple-element.100), channel_id=1, source_target_pairs={{0,1},{1,0},{2,3},{3,2},{4,5},{5,4},{6,7},{7,6},{8,9},{9,8},{10,11... | collective-permute-start | bytes 3145736 | tf_op jit(solution)/shard_map/ppermute | solution.py:75
  69.2 6.3 %collective-permute-start.23 = (bf16[1,144,512]{2,1,0:T(8,128)(2,1)S(1)}, bf16[1,144,512]{2,1,0:T(8,128)(2,1)S(1)}, u32[]{:S(2)}, u32[]{:S(2)}) collective-permute-start(bf16[1,144,512]{2,1,0:T(8,128)(2,1)S(1)} %get-tuple-element.67), channel_id=1, source_target_pairs={{0,2},{1,3},{2,0},{3,1},{4,6},{5,7},{6,4},{7,5},{8,10},{9,11},{10,... | collective-permute-start | bytes 442376 | tf_op jit(solution)/shard_map/ppermute | solution.py:75
  75.5 27.3 %collective-permute-start.31 = (bf16[16,80,512]{2,1,0:T(8,128)(2,1)}, bf16[16,80,512]{2,1,0:T(8,128)(2,1)}, u32[]{:S(2)}, u32[]{:S(2)}) collective-permute-start(bf16[16,80,512]{2,1,0:T(8,128)(2,1)} %get-tuple-element.98), channel_id=1, source_target_pairs={{0,1},{1,0},{2,3},{3,2},{4,5},{5,4},{6,7},{7,6},{8,9},{9,8},{10,11... | collective-permute-start | bytes 3932168 | tf_op jit(solution)/shard_map/ppermute | solution.py:75
  84.9 14.5 %collective-permute-start.37 = (bf16[8,16,2048]{2,1,0:T(8,128)(2,1)}, bf16[8,16,2048]{2,1,0:T(8,128)(2,1)}, u32[]{:S(2)}, u32[]{:S(2)}) collective-permute-start(bf16[8,16,2048]{2,1,0:T(8,128)(2,1)} %get-tuple-element.123), channel_id=1, source_target_pairs={{0,2},{1,3},{2,0},{3,1},{4,6},{5,7},{6,4},{7,5},{8,10},{9,11},{10,... | collective-permute-start | bytes 1572872 | tf_op jit(solution)/shard_map/ppermute | solution.py:75
  89.5 15.1 %collective-permute-start.27 = (bf16[8,16,1664]{2,1,0:T(8,128)(2,1)}, bf16[8,16,1664]{2,1,0:T(8,128)(2,1)}, u32[]{:S(2)}, u32[]{:S(2)}) collective-permute-start(bf16[8,16,1664]{2,1,0:T(8,128)(2,1)} %get-tuple-element.84), channel_id=1, source_target_pairs={{0,16},{8,24},{16,0},{24,8},{1,17},{9,25},{17,1},{25,9},{2,18},{10... | collective-permute-start | bytes 1277960 | tf_op jit(solution)/shard_map/ppermute | solution.py:75
  101.3 8.1 %collective-permute-start.38 = (bf16[4,16,2048]{2,1,0:T(8,128)(2,1)}, bf16[4,16,2048]{2,1,0:T(8,128)(2,1)}, u32[]{:S(2)}, u32[]{:S(2)}) collective-permute-start(bf16[4,16,2048]{2,1,0:T(8,128)(2,1)} %get-tuple-element.127), channel_id=1, source_target_pairs={{0,16},{8,24},{16,0},{24,8},{1,17},{9,25},{17,1},{25,9},{2,18},{10... | collective-permute-start | bytes 786440 | tf_op jit(solution)/shard_map/ppermute | solution.py:75
  104.5 26.5 %collective-permute-start.32 = (bf16[8,80,512]{2,1,0:T(8,128)(2,1)S(1)}, bf16[8,80,512]{2,1,0:T(8,128)(2,1)S(1)}, u32[]{:S(2)}, u32[]{:S(2)}) collective-permute-start(bf16[8,80,512]{2,1,0:T(8,128)(2,1)S(1)} %get-tuple-element.121), channel_id=1, source_target_pairs={{0,8},{8,0},{16,24},{24,16},{1,9},{9,1},{17,25},{25,17},{2,10},{10... | collective-permute-start | bytes 1966088 | tf_op jit(solution)/shard_map/ppermute | solution.py:75
  106.7 19.7 %collective-permute-start.28 = (bf16[4,16,1664]{2,1,0:T(8,128)(2,1)}, bf16[4,16,1664]{2,1,0:T(8,128)(2,1)S(1)}, u32[]{:S(2)}, u32[]{:S(2)}) collective-permute-start(bf16[4,16,1664]{2,1,0:T(8,128)(2,1)} %get-tuple-element.86), channel_id=1, source_target_pairs={{0,8},{8,0},{16,24},{24,16},{1,9},{9,1},{17,25},{25,17},{2,10},{10... | collective-permute-start | bytes 638984 | tf_op jit(solution)/shard_map/ppermute | solution.py:75
  110.4 19.2 %collective-permute-start.39 = (bf16[2,16,2048]{2,1,0:T(8,128)(2,1)S(1)}, bf16[2,16,2048]{2,1,0:T(8,128)(2,1)S(1)}, u32[]{:S(2)}, u32[]{:S(2)}) collective-permute-start(bf16[2,16,2048]{2,1,0:T(8,128)(2,1)S(1)} %get-tuple-element.131), channel_id=1, source_target_pairs={{0,8},{8,0},{16,24},{24,16},{1,9},{9,1},{17,25},{25,17},{2,10},{10... | collective-permute-start | bytes 393224 | tf_op jit(solution)/shard_map/ppermute | solution.py:75
  111.1 11.0 %collective-permute-start.25 = (bf16[112,512]{1,0:T(8,128)(2,1)S(1)}, bf16[112,512]{1,0:T(8,128)(2,1)S(1)}, u32[]{:S(2)}, u32[]{:S(2)}) collective-permute-start(bf16[112,512]{1,0:T(8,128)(2,1)S(1)} %get-tuple-element.76), channel_id=1, source_target_pairs={{0,4},{1,5},{2,6},{3,7},{4,0},{5,1},{6,2},{7,3},{8,12},{9,13},{10,... | collective-permute-start | bytes 344072 | tf_op jit(solution)/shard_map/ppermute | solution.py:75
  111.9 10.2 %collective-permute-start.22 = (bf16[96,512]{1,0:T(8,128)(2,1)S(1)}, bf16[96,512]{1,0:T(8,128)(2,1)S(1)}, u32[]{:S(2)}, u32[]{:S(2)}) collective-permute-start(bf16[96,512]{1,0:T(8,128)(2,1)S(1)} %get-tuple-element.65), channel_id=1, source_target_pairs={{0,4},{1,5},{2,6},{3,7},{4,0},{5,1},{6,2},{7,3},{8,12},{9,13},{10,... | collective-permute-start | bytes 294920 | tf_op jit(solution)/shard_map/ppermute | solution.py:75
  129.0 6.8 %collective-permute-start.29 = (bf16[2,16,1664]{2,1,0:T(8,128)(2,1)}, bf16[2,16,1664]{2,1,0:T(8,128)(2,1)S(1)}, u32[]{:S(2)}, u32[]{:S(2)}) collective-permute-start(bf16[2,16,1664]{2,1,0:T(8,128)(2,1)} %get-tuple-element.88), channel_id=1, source_target_pairs={{0,2},{1,3},{2,0},{3,1},{4,6},{5,7},{6,4},{7,5},{8,10},{9,11},{10,... | collective-permute-start | bytes 319496 | tf_op jit(solution)/shard_map/ppermute | solution.py:75
  129.6 8.6 %collective-permute-start.40 = (bf16[1,16,2048]{2,1,0:T(8,128)(2,1)S(1)}, bf16[1,16,2048]{2,1,0:T(8,128)(2,1)S(1)}, u32[]{:S(2)}, u32[]{:S(2)}) collective-permute-start(bf16[1,16,2048]{2,1,0:T(8,128)(2,1)S(1)} %add_convert_fusion.14), channel_id=1, source_target_pairs={{0,4},{1,5},{2,6},{3,7},{4,0},{5,1},{6,2},{7,3},{8,12},{9,13},{10,... | collective-permute-start | bytes 196616 | tf_op jit(solution)/shard_map/ppermute | solution.py:75
  131.2 13.2 %collective-permute-start.33 = (bf16[4,80,512]{2,1,0:T(8,128)(2,1)S(1)}, bf16[4,80,512]{2,1,0:T(8,128)(2,1)S(1)}, u32[]{:S(2)}, u32[]{:S(2)}) collective-permute-start(bf16[4,80,512]{2,1,0:T(8,128)(2,1)S(1)} %get-tuple-element.125), channel_id=1, source_target_pairs={{0,2},{1,3},{2,0},{3,1},{4,6},{5,7},{6,4},{7,5},{8,10},{9,11},{10,... | collective-permute-start | bytes 983048 | tf_op jit(solution)/shard_map/ppermute | solution.py:75
  (32 other events, 281.3 us)

commit v2 on v1

--- a/solution.py
+++ b/solution.py
@@ -25,12 +25,17 @@
 NT = (((1,), (1,)), ((), ()))
 TN = (((0,), (0,)), ((), ()))
 
-GATHER_QKV = (2, 3, 4, 1, 0)
-GATHER_UP = (2, 4, 1, 3, 0)
-GATHER_DOWN = (2, 1, 3, 4, 0)
+GATHER_QKV = (2, 1, 3, 4, 0)
+GATHER_UP = (2, 3, 4, 1, 0)
+GATHER_DOWN = (2, 4, 1, 3, 0)
 REDUCE_UP = (0, 1, 4, 3, 2)
 REDUCE_DOWN = (0, 3, 1, 4, 2)
 REDUCE_QKV = (0, 4, 3, 1, 2)
+PAIRS = BLOCKS // 2
+PAIR_UP = (2, 3, 0, 1)
+PAIR_DOWN = (3, 2, 0, 1)
+PAIR_QKV = (2, 3, 1, 0)
+GIVEN = FF + 2 * WIDTH + WIDTH // 2 + FF // 2 + WIDTH // 2
 
 
 def dot(a, b, dims=NN):
@@ -77,6 +82,9 @@
     def block_swap(self, x, bit):
         return self.swap(x, bit + self.low_bits)
 
+    def pair_swap(self, x, bit):
+        return self.swap(x, bit + 1)
+
     def device(self):
         return lax.axis_index("dp") * self.seq + lax.axis_index("seq")
 
@@ -107,11 +115,12 @@
         last = self.block_swap(held, order[3])
         return held, last, self.block_swap(held, order[4]), self.block_swap(last, order[4])
 
-    def reduce(self, keep, send, order, fold):
-        other = self.block_swap(send, order[0])
+    def reduce(self, keep, send, order, fold, swap=None):
+        swap = swap or self.block_swap
+        other = swap(send, order[0])
         for bit in order[1:]:
             keep, send = fold(keep, other)
-            other = self.block_swap(send, bit)
+            other = swap(send, bit)
         return keep, other
 
     def gather_group(self, x):
@@ -141,9 +150,10 @@
 
 
 def reduce_masks(order):
+    bits = len(order)
     return [
-        sum(((place >> (4 - k)) & 1) << bit for k, bit in enumerate(order))
-        for place in range(BLOCKS)
+        sum(((place >> (bits - 1 - k)) & 1) << bit for k, bit in enumerate(order))
+        for place in range(1 << bits)
     ]
 
 
@@ -154,9 +164,11 @@
 
 
 def emit_blocks(source, keep, send, order, block, unit, at, lanes):
-    for place, mask in enumerate(reduce_masks(order)):
-        target = keep if place < BLOCKS // 2 else send
-        target[place % (BLOCKS // 2), at, lanes] = source[aligned(block ^ mask, unit), :]
+    masks = reduce_masks(order)
+    half = len(masks) // 2
+    for place, mask in enumerate(masks):
+        target = keep if place < half else send
+        target[place % half, at, lanes] = source[aligned(block ^ mask, unit), :]
 
 
 def roll_lanes(v, shift):
@@ -624,7 +636,7 @@
     rms[...] = jnp.where(row == slot, result[0], result[1])
 
 
-def call(kernel, name, outs, scratch, args, smem=1, limit=48, flops=0):
+def call(kernel, name, outs, scratch, args, smem=1, limit=32, flops=0):
     vmem = pl.BlockSpec(memory_space=pltpu.VMEM)
     in_specs = [pl.BlockSpec(memory_space=pltpu.SMEM)] * smem + [vmem] * (len(args) - smem)
     size = sum(a.size * a.dtype.itemsize for a in args)
@@ -640,7 +652,7 @@
     )(*args)
 
 
-def local(
+def local_wide(
     layout,
     tokens,
     memory,
@@ -870,6 +882,688 @@
     )
 
 
+def prepare_kernel(*refs):
+    w_qkv, w_out = refs[:2]
+    vectors, b_up = refs[2:10], refs[10]
+    first, up_cell, sems = refs[11:14]
+    cells = refs[14:]
+    moves = [
+        (w_qkv, first.at[:, : 3 * WIDTH]),
+        (w_out, first.at[:, 3 * WIDTH : 4 * WIDTH]),
+        (b_up, up_cell),
+    ]
+    moves += [(v, cells[k]) for k, v in enumerate(vectors)]
+    copies = [
+        pltpu.make_async_copy(source, target, sems.at[k])
+        for k, (source, target) in enumerate(moves)
+    ]
+    for copy in copies:
+        copy.start()
+    for copy in copies:
+        copy.wait()
+    blank = jnp.zeros((1, LANES - 16), F32)
+    rows = [jnp.concatenate([high(v[...]).reshape(1, 16), blank], 1) for v in cells]
+    rows.append(jnp.concatenate([high(up_cell[...]).reshape(1, 64), blank[:, :64]], 1))
+    rows.append(jnp.zeros((7, LANES), F32))
+    first[:, 4 * WIDTH :] = low(jnp.concatenate(rows, 0))
+
+
+def gather_vectors(extra):
+    pieces, ups = [], []
+    for g in range(4):
+        total = jnp.zeros((8, LANES), F32)
+        for p in range(8):
+            at = (8 * g + p) * 16
+            total += roll_lanes(high(extra[at : at + 16, :])[:8], 16 * p)
+        pieces.append(total)
+    for g in range(16):
+        total = jnp.zeros((8, LANES), F32)
+        for p in range(2):
+            at = (2 * g + p) * 16
+            total += roll_lanes(high(extra[at : at + 16, :])[8:], 64 * p)
+        ups.append(total)
+    return jnp.concatenate(pieces, 1), jnp.concatenate(ups, 1)
+
+
+def quad_forward_kernel(layout, mem_rows, slot_len, *refs):
+    lengths, near, far, memory, w0, w1, w2, w3 = refs[:8]
+    attn, qkv_own, rows, w_own, vectors, up_bias = refs[8:14]
+    qkv, weight, extra = refs[14:]
+    group = layout.group
+    place = lax.axis_index("seq")
+    slot, rank = place // group, place % group
+    block = layout.block()
+    length = lengths[slot]
+    parts = (w0, w1, w2, w3)
+    place_blocks(weight, parts, GATHER_QKV, block, 16, slice(0, 3 * WIDTH))
+    place_blocks(extra, parts, GATHER_QKV, block, 16, slice(4 * WIDTH, 4 * WIDTH + LANES))
+    for part, masks in zip((near, far), layout.group_masks()):
+        for k, mask in enumerate(masks):
+            rows[aligned(rank ^ mask, ROWS), :] = part[k]
+    rows[slot_len : slot_len + MEM_PAD, :] = memory[...]
+    vector_rows, up_rows = gather_vectors(extra)
+    vectors[...] = vector_rows
+    up_bias[...] = up_rows
+
+    key_rows = slot_len + MEM_KEYS
+    filled = slot_len + MEM_PAD
+    qkv[filled:key_rows, :] = jnp.zeros((key_rows - filled, 3 * WIDTH), BF)
+    for part, shift in enumerate((vector_rows[0:1], None, vector_rows[1:2])):
+        lanes = slice(part * WIDTH, (part + 1) * WIDTH)
+        value = dot(rows[...], weight[:, lanes])
+        qkv[:filled, lanes] = low(value if shift is None else value + shift)
+    for part in range(3):
+        own = pl.ds(pl.multiple_of(part * WIDTH + rank * LANES, LANES), LANES)
+        qkv_own[:, part * LANES : (part + 1) * LANES] = qkv[:, own]
+        w_own[:, part * LANES : (part + 1) * LANES] = weight[:, own]
+
+    keep = key_valid((1, key_rows), 1, slot, group, length, slot_len, mem_rows)
+    bias = jnp.where(keep, 0.0, -1e30)
+    for pair in range(HEADS // 2):
+        at = pair * LANES
+        own = jnp.concatenate(
+            [qkv[aligned(rank, ROWS), at : at + LANES], qkv[slot_len:filled, at : at + LANES]], 0
+        )
+        keys = qkv[:, WIDTH + at : WIDTH + at + LANES]
+        values = qkv[:, 2 * WIDTH + at : 2 * WIDTH + at + LANES]
+        scores = dot(both_heads(own, 0.125), keys, NT) + bias
+        highest = jnp.max(scores, axis=1, keepdims=True)
+        expos = jnp.exp(scores - highest)
+        total = jnp.sum(expos, axis=1, keepdims=True)
+        attn[:, at : at + LANES] = join_heads(dot(low(expos), values) / total)
+
+
+def quad_feed_kernel(layout, mem_rows, *refs):
+    lengths, tokens, arrived, memory, cots, cot_arrived, cot_memory = refs[:7]
+    attn, vectors, up_bias = refs[7:10]
+    outs, ups, downs = refs[10:14], refs[14:18], refs[18:22]
+    pack, grad_mem, first_grad, out_own, out_send = refs[22:27]
+    own, give, vector_grads, up_grads, w_heads = refs[27:32]
+    w_out, w_up, w_down, slope, grad_linear = refs[32:]
+    group = layout.group
+    place = lax.axis_index("seq")
+    slot, rank = place // group, place % group
+    core = place % 2
+    block = layout.block()
+    length = lengths[slot]
+    place_blocks(w_up, ups, GATHER_UP, block, 16, slice(0, FF))
+    place_blocks(w_out, outs, GATHER_QKV, block, 16, slice(3 * WIDTH, 4 * WIDTH))
+    place_blocks(w_down, downs, GATHER_DOWN, block, 64, slice(0, WIDTH))
+    w_heads[...] = w_out[aligned(rank, LANES), :]
+
+    vec = vectors[...]
+    out_bias, gain_one, shift_one, down_bias, gain_two, shift_two = [
+        vec[k : k + 1] for k in range(2, 8)
+    ]
+    rows = jnp.concatenate([high(tokens[slot]), high(arrived[...]), high(memory[...])], 0)
+    cot = jnp.concatenate([high(cots[slot]), high(cot_arrived[...]), high(cot_memory[...])], 0)
+    valid = jnp.where(own_valid((OWN, 1), slot, group, rank, length, mem_rows), 1.0, 0.0)
+    row = lax.broadcasted_iota(jnp.int32, (OWN, 1), 0)
+    weight = jnp.where(row < ROWS, 1.0, 1.0 / group)
+    weight_low = low(weight)
+
+    def total(v):
+        return jnp.sum(v * weight, axis=0, keepdims=True)
+
+    def hand_out(value, start):
+        half = value.shape[1] // 2
+        first, second = value[:, :half], value[:, half:]
+        mine = core == 0
+        own[:, start : start + half] = jnp.where(mine, first, second)
+        give[:, start : start + half] = jnp.where(mine, second, first)
+
+    heads_out = low(attn[...])
+    branch = dot(heads_out, w_out[...]) + out_bias
+    normed_one, inverse_one = normalize(rows + branch)
+    hidden_one = normed_one * gain_one + shift_one
+    hidden_low = low(hidden_one)
+    for target in (own, give):
+        target[:, FF : FF + WIDTH] = hidden_low
+        target[:, FF + WIDTH : FF + 2 * WIDTH] = heads_out
+    feed = jnp.zeros((OWN, WIDTH), F32) + down_bias
+    for at in range(0, FF, WIDTH):
+        cols = slice(at, at + WIDTH)
+        t = dot(hidden_low, w_up[:, cols]) + up_bias[0:1, cols]
+        square = t * t
+        bent = jnp.tanh(0.7978845608 * (t + 0.044715 * (square * t)))
+        half = 0.5 * (1.0 + bent)
+        slope[:, cols] = half + (0.5 * 0.7978845608) * t * (1.0 - bent * bent) * (
+            1.0 + (3 * 0.044715) * square
+        )
+        act = low(t * half)
+        own[:, cols] = act
+        give[:, cols] = act
+        feed += dot(act, w_down[cols, :])
+    normed_two, inverse_two = normalize(hidden_one + feed)
+    output = (normed_two * gain_two + shift_two) * valid
+    out_own[:HEAD_DIM, :] = low(output[:HEAD_DIM])
+    out_own[HEAD_DIM:, :] = low(output[ROWS:])
+    out_send[...] = low(output[HEAD_DIM:])
+    token_valid = jnp.where(row < ROWS, valid, 0.0)
+    squares = jnp.sum(feed * feed * token_valid, axis=0, keepdims=True)
+
+    g = cot * valid
+    grads = [None] * 8
+    grads[6] = total(g * normed_two)
+    grads[7] = total(g)
+    second = norm_back(g * gain_two, normed_two, inverse_two)
+    grad_feed = low(second)
+    hand_out(grad_feed * weight_low, FF + 2 * WIDTH)
+    grads[5] = total(high(grad_feed))
+    grad_hidden = second
+    for at in range(0, FF, WIDTH):
+        cols = slice(at, at + WIDTH)
+        linear = low(dot(grad_feed, w_down[cols, :], NT) * slope[:, cols])
+        grad_linear[:, cols] = linear * weight_low
+        up_grads[:, cols] = jnp.broadcast_to(total(high(linear)), (8, WIDTH))
+        grad_hidden += dot(linear, w_up[:, cols], NT)
+    at = FF + 2 * WIDTH + WIDTH // 2
+    own[:, at : at + FF // 2] = grad_linear[:, aligned(core, FF // 2)]
+    give[:, at : at + FF // 2] = grad_linear[:, aligned(1 - core, FF // 2)]
+    grads[3] = total(grad_hidden * normed_one)
+    grads[4] = total(grad_hidden)
+    first = norm_back(grad_hidden * gain_one, normed_one, inverse_one)
+    first_grad[...] = first
+    grad_branch = low(first)
+    hand_out(grad_branch * weight_low, FF + 2 * WIDTH + WIDTH // 2 + FF // 2)
+    grads[2] = total(high(grad_branch))
+    grads[0] = grads[1] = jnp.zeros((1, WIDTH), F32)
+    vector_grads[...] = jnp.concatenate(grads, 0)
+    pack[0, :ROWS, :] = grad_branch[:ROWS]
+    pack[0, ROWS:, :] = low(
+        jnp.concatenate([*split_three(squares), jnp.zeros((13, WIDTH), F32)], 0)
+    )
+    grad_mem[...] = grad_branch[ROWS:]
+
+
+def quad_weight_kernel(layout, *refs):
+    own, got, up_keep, up_send, down_keep, down_send, up, down, out = refs
+
+    def both(start, size):
+        cols = slice(start, start + size)
+        return jnp.concatenate([own[:, cols], got[:, cols]], 0)
+
+    pair = layout.block() >> 1
+    half = WIDTH // 2
+    at = FF + 2 * WIDTH
+    grad_feed = both(at, half)
+    linear = at + half
+    grad_branch = both(linear + FF // 2, half)
+    for start in range(0, FF, WIDTH):
+        down[start : start + WIDTH, :] = low(dot(both(start, WIDTH), grad_feed, TN))
+    value = low(dot(both(FF + WIDTH, WIDTH), grad_branch, TN))
+    for p in range(BLOCKS):
+        out[p % 2, p // 2 * 16 : p // 2 * 16 + 16, :] = value[16 * p : 16 * p + 16]
+    every = slice(0, half)
+    emit_blocks(down, down_keep, down_send, PAIR_DOWN, pair, 128, slice(0, 128), every)
+    for k, (keep, send, order) in enumerate(
+        ((up_keep, up_send, PAIR_UP), (down_keep, down_send, PAIR_DOWN))
+    ):
+        emit_blocks(out.at[k], keep, send, order, pair, 16, slice(128, 144), every)
+    hidden = both(FF, WIDTH)
+    for start in range(0, FF // 2, WIDTH):
+        up[:, start : start + WIDTH] = low(dot(hidden, both(linear + start, WIDTH), TN))
+    for k in range(4):
+        emit_blocks(
+            up.at[:, half * k : half * (k + 1)],
+            up_keep,
+            up_send,
+            PAIR_UP,
+            pair,
+            32,
+            slice(32 * k, 32 * k + 32),
+            every,
+        )
+
+
+def quad_backward_kernel(layout, mem_rows, slot_len, *refs):
+    lengths, qkv, rows, w_own, w_heads, near, far, grad_mem, vector_grads, up_grads = refs[:10]
+    keep_out, send_out, in_keep, in_send, tail = refs[10:15]
+    grad_rows, squares, packed, grad_weight, grad_in, vec, extra = refs[15:]
+    group = layout.group
+    place = lax.axis_index("seq")
+    slot, rank = place // group, place % group
+    pair = layout.block() >> 1
+    length = lengths[slot]
+    filled = slot_len + MEM_PAD
+    key_rows = slot_len + MEM_KEYS
+    for part, masks in zip((near, far), layout.group_masks()):
+        for k, mask in enumerate(masks):
+            at = rank ^ mask
+            grad_rows[aligned(at, ROWS), :] = part[k, :ROWS, :]
+            squares[at] = high(part[k, ROWS:, :])
+    grad_rows[slot_len:filled, :] = grad_mem[...]
+
+    keep = key_valid((1, key_rows), 1, slot, group, length, slot_len, mem_rows)
+    bias = jnp.where(keep, 0.0, -1e30)
+    grad_attn = low(dot(grad_rows[...], w_heads[...], NT))
+    queries = qkv[:filled, :LANES]
+    keys = qkv[:, LANES : 2 * LANES]
+    values = qkv[:, 2 * LANES :]
+    d_query = jnp.zeros((filled, LANES), F32)
+    d_key = jnp.zeros((key_rows, LANES), F32)
+    d_value = jnp.zeros((key_rows, LANES), F32)
+    for mask in half_masks():
+        query = queries * (mask * 0.125)
+        grads = grad_attn * mask
+        scores = dot(query, keys, NT) + bias
+        expos = jnp.exp(scores - jnp.max(scores, axis=1, keepdims=True))
+        weights = expos * (1.0 / jnp.sum(expos, axis=1, keepdims=True))
+        weights_low = low(weights)
+        heads_out = dot(weights_low, values)
+        delta = jnp.sum(high(grads) * heads_out, axis=1, keepdims=True)
+        slopes = low(weights * (dot(grads, values, NT) - delta))
+        d_query += dot(slopes, keys) * (high(mask) * 0.125)
+        d_key += dot(slopes, query, TN)
+        d_value += dot(weights_low, grads, TN)
+    packed[:, :LANES] = low(d_query)
+    packed[:, LANES : 2 * LANES] = low(d_key[:filled])
+    packed[:, 2 * LANES :] = low(d_value[:filled])
+
+    grad_weight[...] = low(dot(rows[...], packed[...], TN))
+    for part in range(3):
+        emit_blocks(
+            grad_weight.at[:, part * LANES : (part + 1) * LANES],
+            keep_out,
+            send_out,
+            PAIR_QKV,
+            pair,
+            32,
+            slice(32 * part, 32 * part + 32),
+            slice(0, LANES),
+        )
+    grad_in[...] = low(dot(packed[...], w_own[...], NT))
+    for k, (target, mask) in enumerate(((in_keep, 0), (in_keep, 1), (in_send, 2), (in_send, 3))):
+        start = (k % 2) * ROWS
+        target[start : start + ROWS, :] = grad_in[aligned(rank ^ mask, ROWS), :]
+    for target in (in_keep, in_send):
+        target[2 * ROWS :, :] = grad_in[slot_len:filled, :]
+
+    vec[...] = vector_grads[...]
+    own = aligned(rank, LANES)
+    vec[0:1, own] = jnp.sum(high(packed[:, :LANES]), axis=0, keepdims=True)
+    vec[1:2, own] = jnp.sum(high(packed[:, 2 * LANES :]), axis=0, keepdims=True)
+    lanes = lane_index((8, LANES))
+    sublane = lax.broadcasted_iota(jnp.int32, (8, LANES), 0)
+    for p in range(0, BLOCKS, 2):
+        both = []
+        for q in (p, p + 1):
+            g = q // 8
+            cell = roll_lanes(vec[:, g * LANES : (g + 1) * LANES], -16 * (q % 8))
+            g = q // 2
+            ups = up_grads[:, g * LANES : (g + 1) * LANES]
+            up = jnp.zeros((8, LANES), F32)
+            for k in range(4):
+                up = jnp.where(sublane == k, roll_lanes(ups, 16 - 64 * (q % 2) - 16 * k), up)
+            both.append(jnp.where(lanes < 16, cell, jnp.where(lanes < 32, up, 0.0)))
+        extra[p * 8 : p * 8 + 16, :] = low(jnp.concatenate(both, 0))
+    emit_blocks(extra, keep_out, send_out, PAIR_QKV, pair, 16, slice(96, 112), slice(0, LANES))
+
+    square = squares[0]
+    for k in range(1, group):
+        square += squares[k]
+    square = square[0:1] + square[1:2] + square[2:3]
+    tail[...] = low(jnp.concatenate([*split_three(square), jnp.zeros((13, WIDTH), F32)], 0))
+
+
+def feed_rows(core):
+    at = [pl.ds(pl.multiple_of(32 * k + 16 * core, 16), 16) for k in range(4)]
+    at.append(pl.ds(pl.multiple_of(144 + 64 * core, 16), 64))
+    at.append(pl.ds(pl.multiple_of(128 + 144 * core, 16), 16))
+    return at
+
+
+def turn_feed_kernel(keep, other, send):
+    start = 0
+    for at in feed_rows(1 - lax.axis_index("seq") % 2):
+        send[start : start + at.size, :] = low(high(keep[0, at, :]) + high(other[0, at, :]))
+        start += at.size
+
+
+def emit_feed_kernel(keep, other, got, w_up, w_down, w_out):
+    core = lax.axis_index("seq") % 2
+    half = WIDTH // 2
+    own, theirs = aligned(core, half), aligned(1 - core, half)
+    start = 0
+    for k, at in enumerate(feed_rows(core)):
+        total = high(keep[0, at, :]) + high(other[0, at, :])
+        arrived = high(got[start : start + at.size, :])
+        start += at.size
+        if k < 4:
+            w_up[:, pl.ds(pl.multiple_of(core * 1024 + half * k, half), half)] = total
+            w_up[:, pl.ds(pl.multiple_of((1 - core) * 1024 + half * k, half), half)] = arrived
+        else:
+            target = w_down if k == 4 else w_out
+            target[:, own] = total
+            target[:, theirs] = arrived
+
+
+def turn_qkv_kernel(keep, other, send):
+    away = 1 - lax.axis_index("seq") % 2
+    for k, source in enumerate((keep, other)):
+        for part in range(3):
+            at = pl.ds(pl.multiple_of(32 * part + 16 * away, 16), 16)
+            start = 48 * k + 16 * part
+            send[start : start + 16, :] = source[0, at, :]
+    send[96:112, :] = low(high(keep[0, 96:112, :]) + high(other[0, 96:112, :]))
+
+
+def emit_qkv_kernel(keep, other, got, w_qkv, *vectors):
+    place = lax.axis_index("seq")
+    core, rank = place % 2, place % 4
+    for part in range(3):
+        at = pl.ds(pl.multiple_of(32 * part + 16 * core, 16), 16)
+        pieces = (
+            (rank, keep[0, at, :]),
+            (rank ^ 2, other[0, at, :]),
+            (rank ^ 1, got[16 * part : 16 * part + 16, :]),
+            (rank ^ 3, got[48 + 16 * part : 64 + 16 * part, :]),
+        )
+        for whose, piece in pieces:
+            lanes = pl.ds(pl.multiple_of(part * WIDTH + whose * LANES, LANES), LANES)
+            w_qkv[:, lanes] = high(piece)
+    total = high(keep[0, 96:112, :]) + high(other[0, 96:112, :]) + high(got[96:112, :])
+    total = jnp.where(core == 0, total[:8], total[8:])
+    for k in range(8):
+        vectors[k][...] = total[k, :16]
+    lanes = lane_index((1, LANES))
+    ups = jnp.zeros((1, LANES), F32)
+    for k in range(4):
+        rolled = roll_lanes(total[k : k + 1], 16 * k - 16)
+        ups = jnp.where(jnp.logical_and(lanes >= 16 * k, lanes < 16 * k + 16), rolled, ups)
+    vectors[8][...] = ups[0, :64]
+
+
+def emit_tokens_kernel(layout, mem_rows, *refs):
+    lengths, out_own, grad_own, grad_got, tail = refs[:5]
+    out_tokens, out_memory, grad_tokens, grad_memory, rms = refs[5:]
+    slot = lax.axis_index("seq") // layout.group
+    pieces = (
+        (out_own, 0, 64, slot, out_tokens, out_memory),
+        (grad_got, 112, 176, 1 - slot, out_tokens, out_memory),
+        (grad_own, 0, 128, slot, grad_tokens, grad_memory),
+        (grad_got, 0, 64, 1 - slot, grad_tokens, grad_memory),
+    )
+    for source, start, mem, at, tokens, memory in pieces:
+        tokens[at] = source[start : start + 64, :]
+        memory[at] = low(high(source[mem : mem + 32, :])[:mem_rows])
+    result = []
+    for cell, at in ((tail[...], slot), (grad_got[96:112, :], 1 - slot)):
+        cell = high(cell)
+        square = cell[0:1] + cell[1:2] + cell[2:3]
+        result.append(jnp.sqrt(square / lengths[at].astype(F32)))
+    row = lax.broadcasted_iota(jnp.int32, (2, WIDTH), 0)
+    rms[...] = jnp.where(row == slot, result[0], result[1])
+
+
+def local_quad(
+    layout,
+    tokens,
+    memory,
+    lengths,
+    w_qkv,
+    b_query,
+    b_value,
+    w_out,
+    b_out,
+    gain_one,
+    shift_one,
+    w_up,
+    b_up,
+    w_down,
+    b_down,
+    gain_two,
+    shift_two,
+    cot_tokens,
+    cot_memory,
+):
+    mem_rows = memory.shape[1]
+    slot_len = tokens.shape[1] * layout.seq
+    key_rows = slot_len + MEM_KEYS
+    filled = slot_len + MEM_PAD
+    partner = layout.seq_bits - 1
+    slot = lax.axis_index("seq") // layout.group
+
+    def pick(x, at):
+        return lax.dynamic_index_in_dim(x, at, 0, False)
+
+    small = (b_query, b_value, b_out, gain_one, shift_one, b_down, gain_two, shift_two)
+    first = pl.pallas_call(
+        prepare_kernel,
+        out_shape=jax.ShapeDtypeStruct((16, 4 * WIDTH + LANES), BF),
+        in_specs=[pl.BlockSpec(memory_space=pl.ANY)] * 11,
+        out_specs=pl.BlockSpec(memory_space=pltpu.VMEM),
+        scratch_shapes=[pltpu.VMEM((64,), BF), pltpu.SemaphoreType.DMA((11,))]
+        + [pltpu.VMEM((16,), BF)] * 8,
+        name="prepare",
+    )(w_qkv, w_out, *small, b_up)
+
+    def after(x, *others):
+        return lax.optimization_barrier((x, *others))[0]
+
+    def gather(held, order, *ready):
+        held = jnp.concatenate([held, layout.block_swap(held, order[1])], 0)
+        held = jnp.concatenate([held, layout.block_swap(held, order[2])], 0)
+        held = after(held, *ready)
+        last = layout.block_swap(held, order[3])
+        return held, last, layout.block_swap(held, 0), layout.block_swap(last, 0)
+
+    def begin(x, order):
+        x = x[None]
+        return jnp.concatenate([x, layout.block_swap(x, order[0])], 0)
+
+    second = begin(w_up, GATHER_UP)
+    third = begin(w_down, GATHER_DOWN)
+    first = begin(first, GATHER_QKV)
+    arrived = layout.swap(pick(after(tokens, first), 1 - slot), partner)
+    near = jnp.concatenate([pick(tokens, slot), arrived], 0)[None]
+    near = jnp.concatenate([near, layout.swap(near, 1)], 0)
+    cot_arrived = layout.swap(pick(after(cot_tokens, third), 1 - slot), partner)
+    pad_rows = ((0, MEM_PAD - mem_rows), (0, 0))
+    own_memory = jnp.pad(pick(after(memory, third), slot), pad_rows)
+    own_cot_memory = jnp.pad(pick(after(cot_memory, third), slot), pad_rows)
+    far = layout.swap(near, 0)
+    up_parts = gather(second, GATHER_UP, near, own_memory, own_cot_memory)
+    down_parts = gather(third, GATHER_DOWN)
+    qkv_parts = gather(first, GATHER_QKV)
+
+    attn, qkv_own, rows, w_own, vector_rows, up_bias = call(
+        functools.partial(quad_forward_kernel, layout, mem_rows, slot_len),
+        "attention_forward",
+        [
+            ((OWN, WIDTH), F32),
+            ((key_rows, 3 * LANES), BF),
+            ((filled, WIDTH), BF),
+            ((WIDTH, 3 * LANES), BF),
+            ((8, WIDTH), F32),
+            ((8, FF), F32),
+        ],
+        [((key_rows, 3 * WIDTH), BF), ((WIDTH, 3 * WIDTH), BF), ((WIDTH, LANES), BF)],
+        (lengths, near, far, own_memory, *qkv_parts),
+        flops=4 * 10**9,
+    )
+    (
+        pack,
+        grad_mem,
+        first_grad,
+        out_own,
+        out_send,
+        own,
+        give,
+        vector_grads,
+        up_grads,
+        w_heads,
+    ) = call(
+        functools.partial(quad_feed_kernel, layout, mem_rows),
+        "feed_forward",
+        [
+            ((1, ROWS + 16, WIDTH), BF),
+            ((MEM_PAD, WIDTH), BF),
+            ((OWN, WIDTH), F32),
+            ((64 + MEM_PAD, WIDTH), BF),
+            ((64 + MEM_PAD, WIDTH), BF),
+            ((OWN, GIVEN), BF),
+            ((OWN, GIVEN), BF),
+            ((8, WIDTH), F32),
+            ((8, FF), F32),
+            ((LANES, WIDTH), BF),
+        ],
+        [
+            ((WIDTH, WIDTH), BF),
+            ((WIDTH, FF), BF),
+            ((FF, WIDTH), BF),
+            ((OWN, FF), F32),
+            ((OWN, FF), BF),
+        ],
+        (
+            lengths,
+            tokens,
+            arrived,
+            own_memory,
+            cot_tokens,
+            cot_arrived,
+            own_cot_memory,
+            attn,
+            vector_rows,
+            up_bias,
+            *qkv_parts,
+            *up_parts,
+            *down_parts,
+        ),
+        flops=6 * 10**9,
+    )
+    taken = layout.swap(give, 0)
+    grads_next = layout.swap(pack, 1)
+    half = PAIRS // 2
+    up_keep, up_send, down_keep, down_send = call(
+        functools.partial(quad_weight_kernel, layout),
+        "weight_gradients",
+        [
+            ((half, 144, WIDTH // 2), BF),
+            ((half, 144, WIDTH // 2), BF),
+            ((half, 144, WIDTH // 2), BF),
+            ((half, 144, WIDTH // 2), BF),
+        ],
+        [((WIDTH, FF // 2), BF), ((FF, WIDTH // 2), BF), ((2, WIDTH // 2, WIDTH // 2), BF)],
+        (own, taken),
+        smem=0,
+        flops=3 * 10**9,
+    )
+    grads_next, _ = lax.optimization_barrier((grads_next, up_send))
+    grads_near = jnp.concatenate([pack, grads_next], 0)
+    grads_far = layout.swap(grads_near, 0)
+    qkv_keep, qkv_send, in_keep, in_send, tail = call(
+        functools.partial(quad_backward_kernel, layout, mem_rows, slot_len),
+        "attention_backward",
+        [
+            ((half, 112, LANES), BF),
+            ((half, 112, LANES), BF),
+            ((2 * ROWS + MEM_PAD, WIDTH), BF),
+            ((2 * ROWS + MEM_PAD, WIDTH), BF),
+            ((16, WIDTH), BF),
+        ],
+        [
+            ((filled, WIDTH), BF),
+            ((layout.group, 16, WIDTH), F32),
+            ((filled, 3 * LANES), BF),
+            ((WIDTH, 3 * LANES), BF),
+            ((filled, WIDTH), BF),
+            ((8, WIDTH), F32),
+            ((8 * BLOCKS, LANES), BF),
+        ],
+        (
+            lengths,
+            qkv_own,
+            rows,
+            w_own,
+            w_heads,
+            grads_near,
+            grads_far,
+            grad_mem,
+            vector_grads,
+            up_grads,
+        ),
+        flops=6 * 10**9,
+    )
+    swap = layout.pair_swap
+    up_other, down_other = swap(up_send, PAIR_UP[0]), swap(down_send, PAIR_DOWN[0])
+    up_keep, up_send = fold_plain(up_keep, up_other)
+    down_keep, down_send = fold_plain(down_keep, down_other)
+    qkv_send = after(qkv_send, up_send)
+    up_ready, down_ready = up_send, down_send
+    up_other, down_other = swap(up_send, PAIR_UP[1]), swap(down_send, PAIR_DOWN[1])
+    up_keep, up_send = fold_plain(up_keep, up_other)
+    down_keep, down_send = fold_plain(down_keep, down_other)
+    feed_keep = jnp.concatenate([up_keep, down_keep], 1)
+    feed_send = jnp.concatenate([up_send, down_send], 1)
+    feed_other = swap(feed_send, PAIR_UP[2])
+    feed_keep, feed_send = fold_plain(feed_keep, feed_other)
+    in_sum = high(in_keep) + high(after(layout.swap(in_send, 1), up_ready, down_ready))
+    in_send = low(in_sum[ROWS:])
+    in_got = layout.swap(in_send, 0)
+    grad_own = low(
+        jnp.concatenate([in_sum[:ROWS], high(in_send[ROWS:])], 0) + high(in_got) + first_grad
+    )
+    grad_got = layout.swap(jnp.concatenate([grad_own[64:], tail, out_send], 0), partner)
+
+    feed_total = feed_keep, swap(after(feed_send, grad_got), PAIR_UP[3])
+    qkv_total = layout.reduce(qkv_keep, qkv_send, PAIR_QKV, fold_plain, swap)
+
+    (feed_send,) = call(
+        turn_feed_kernel, "turn_feed", [((144, WIDTH // 2), BF)], [], feed_total, smem=0
+    )
+    out_tokens, out_memory, grad_tokens, grad_memory, rms = call(
+        functools.partial(emit_tokens_kernel, layout, mem_rows),
+        "emit_tokens",
+        [
+            (tokens.shape, BF),
+            (memory.shape, BF),
+            (tokens.shape, BF),
+            (memory.shape, BF),
+            ((2, WIDTH), F32),
+        ],
+        [],
+        (lengths, out_own, grad_own, grad_got, tail),
+    )
+    (qkv_send,) = call(turn_qkv_kernel, "turn_qkv", [((112, LANES), BF)], [], qkv_total, smem=0)
+    qkv_sum, *vec = call(
+        emit_qkv_kernel,
+        "emit_qkv",
+        [(w_qkv.shape, F32)] + [((16,), F32)] * 8 + [((64,), F32)],
+        [],
+        (*qkv_total, layout.swap(qkv_send, 0)),
+        smem=0,
+    )
+    up_sum, down_sum, out_sum = call(
+        emit_feed_kernel,
+        "emit_feed",
+        [(w_up.shape, F32), (w_down.shape, F32), (w_out.shape, F32)],
+        [],
+        (*feed_total, after(layout.swap(feed_send, 0), rms, qkv_sum)),
+        smem=0,
+    )
+    return (
+        out_tokens,
+        out_memory,
+        grad_tokens,
+        grad_memory,
+        qkv_sum,
+        vec[0],
+        vec[1],
+        out_sum,
+        vec[2],
+        vec[3],
+        vec[4],
+        up_sum,
+        vec[8],
+        down_sum,
+        vec[5],
+        vec[6],
+        vec[7],
+        rms,
+    )
+
+
 def solution(mesh):
     rows = P("dp", "seq", None)
     slots = P("dp", None, None)
@@ -890,8 +1584,10 @@
         vector,
         vector,
     )
+    layout = Layout(mesh)
+    quad = layout.group == 4 and layout.devices == BLOCKS
     return jax.shard_map(
-        functools.partial(local, Layout(mesh)),
+        functools.partial(local_quad if quad else local_wide, layout),
         mesh=mesh,
         in_specs=(rows, slots, P("dp"), *weights, rows, slots),
         out_specs=(rows, slots, rows, slots, *weights, P("dp", None)),

time: 157 us -> 127 us (0.81)
  Pallas kernels: 29 us -> 19.5 us
  local copies, waits for them, and re-layouts: 12.2 us -> 4.68 us
  other arithmetic: 11.1 us -> 3.75 us
  waiting for transfers between devices: 63.3 us -> 57.6 us
    pallas_call x4 -> x1, Pallas kernels: 8.31 us -> 1.55 us  [local_quad(): pl.pallas_call(prepare_kernel, out_shape=jax.ShapeDtypeStruct((16, 4 * WI...]
    unnamed x51 -> x15, local copies, waits for them, and re-layouts: 8.02 us -> 1.34 us
    ppermute x41 -> x40, waiting for transfers between devices: 63.3 us -> 57.6 us  [swap(): return lax.ppermute(x, axis, [(i, i ^ mask) for i in range(size)])]
    convert_element_type x8 -> x9, other arithmetic: 6.04 us -> 0.69 us  [low(): return v.astype(BF)]
    pallas_call x5 -> x9, Pallas kernels: 20.7 us -> 17.9 us  [call(): pl.pallas_call(kernel, out_shape=[jax.ShapeDtypeStruct(shape, kind) for s...]
    add x5 -> x1, other arithmetic: 2.19 us -> 0.1 us  [local_quad(): high(in_keep) + high(after(layout.swap(in_send, 1), up_ready, down_ready))]
    slice x3, local copies, waits for them, and re-layouts: 1.93 us -> 0.04 us  [the longest x1 0.02 us: local_quad(): in_sum[:ROWS]]
    optimization_barrier x0 -> x2, local copies, waits for them, and re-layouts: none -> 1.57 us  [after(): return lax.optimization_barrier((x, *others))[0]]
  transfers between devices with their start and end apart: 41 -> 40, of which waited for: 16 -> 19; matrix products, arithmetic and copies ran while one was open for 10% -> 7% of each run, Pallas kernels for 13% -> 11%
where the time goes in v2:
time: 127 us
  waiting for transfers between devices  57.6 us (45%)
  starting transfers between devices  40 us (31%)
  Pallas kernels  19.5 us (15%)
  local copies, waits for them, and re-layouts  4.68 us (4%)
  other arithmetic  3.75 us (3%)
    ppermute x40, waiting for transfers between devices, swap(): return lax.ppermute(x, axis, [(i, i ^ mask) for i in range(size)])  57.6 us
    ppermute x40, starting transfers between devices, swap(): return lax.ppermute(x, axis, [(i, i ^ mask) for i in range(size)])  40 us
    pallas_call x9, Pallas kernels, call(): pl.pallas_call(kernel, out_shape=[jax.ShapeDtypeStruct(shape, kind) for s...  17.9 us
    concatenate x3, other arithmetic, begin(): return jnp.concatenate([x, layout.block_swap(x, order[0])], 0)  2.61 us
  transfers between devices with their start and end apart: 40, of which 19 were waited for; matrix products, arithmetic and copies ran while one was open for 7% of the time, Pallas kernels for 11%

profile of v2, /device:TPU:0, one launch (start us, length us, event | category | flops | bytes accessed | tf_op | source)
XLA Modules:
  0.0 126.6 jit_solution(2893681279923709675)
XLA Ops:
  0.7 4.1 %collective-permute-start.11 = (bf16[1,16,2048]{2,1,0:T(8,128)(2,1)}, bf16[1,16,2048]{2,1,0:T(8,128)(2,1)S(1)}, u32[]{:S(2)}, u32[]{:S(2)}) collective-permute-start(bf16[1,16,2048]{2,1,0:T(8,128)(2,1)} %bitcast.19), channel_id=1, source_target_pairs={{0,4},{1,5},{2,6},{3,7},{4,0},{5,1},{6,2},{7,3},{8,12},{9,13},{10,... | collective-permute-start | bytes 196616 | tf_op jit(solution)/shard_map/ppermute | solution.py:80
  4.9 1.6 %prepare.1 = bf16[16,2176]{1,0:T(8,128)(2,1)} custom-call(bf16[16,1536]{1,0:T(8,128)(2,1)} %refs_0_.5, bf16[16,512]{1,0:T(8,128)(2,1)} %refs_1_.2, bf16[16]{0:T(256)(128)(2,1)} %refs_2_.1, bf16[16]{0:T(256)(128)(2,1)} %refs_3_.1, bf16[16]{0:T(256)(128)(2,1)} %refs_4_.2, bf16[16]{0:T(256)(128)(2,1)} %refs_5_.1, bf16[16]{0:T(256)(128)(2,1)} %refs_6_.1, ...), custom_call_target="tpu_custom_call" | custom-call | tf_op jit(solution)/shard_map/prepare/pallas_call | solution.py:1331
  6.4 2.9 %collective-permute-start = (bf16[1,16,2176]{2,1,0:T(8,128)(2,1)}, bf16[1,16,2176]{2,1,0:T(8,128)(2,1)S(1)}, u32[]{:S(2)}, u32[]{:S(2)}) collective-permute-start(bf16[1,16,2176]{2,1,0:T(8,128)(2,1)} %bitcast.15), channel_id=1, source_target_pairs={{0,4},{1,5},{2,6},{3,7},{4,0},{5,1},{6,2},{7,3},{8,12},{9,13},{10,... | collective-permute-start | bytes 208904 | tf_op jit(solution)/shard_map/ppermute | solution.py:80
  10.2 3.3 %collective-permute-done.2 = bf16[1,64,512]{2,1,0:T(8,128)(2,1)S(1)} collective-permute-done((bf16[1,64,512]{2,1,0:T(8,128)(2,1)}, bf16[1,64,512]{2,1,0:T(8,128)(2,1)S(1)}, u32[]{:S(2)}, u32[]{:S(2)}) %collective-permute-start.2) | collective-permute-done | bytes 65568 | tf_op jit(solution)/shard_map/ppermute | solution.py:80
  14.4 1.5 %collective-permute-start.17 = (bf16[2,64,512]{2,1,0:T(8,128)(2,1)S(1)}, bf16[2,64,512]{2,1,0:T(8,128)(2,1)S(1)}, u32[]{:S(2)}, u32[]{:S(2)}) collective-permute-start(bf16[2,64,512]{2,1,0:T(8,128)(2,1)S(1)} %pad_maximum_fusion.11), channel_id=1, source_target_pairs={{0,16},{8,24},{16,0},{24,8},{1,17},{9,25},{17,1},{25,9},{2,18},{10... | collective-permute-start | bytes 393224 | tf_op jit(solution)/shard_map/ppermute | solution.py:80
  20.3 3.3 %collective-permute-start.1 = (bf16[64,512]{1,0:T(8,128)(2,1)S(1)}, bf16[64,512]{1,0:T(8,128)(2,1)S(1)}, u32[]{:S(2)}, u32[]{:S(2)}) collective-permute-start(bf16[64,512]{1,0:T(8,128)(2,1)S(1)} %dynamic-slice_bitcast_fusion.2), channel_id=1, source_target_pairs={{0,4},{1,5},{2,6},{3,7},{4,0},{5,1},{6,2},{7,3},{8,12},{9,13},{10,... | collective-permute-start | bytes 196616 | tf_op jit(solution)/shard_map/ppermute | solution.py:80
  23.7 1.6 %collective-permute-start.12 = (bf16[2,16,2048]{2,1,0:T(8,128)(2,1)S(1)}, bf16[2,16,2048]{2,1,0:T(8,128)(2,1)S(1)}, u32[]{:S(2)}, u32[]{:S(2)}) collective-permute-start(bf16[2,16,2048]{2,1,0:T(8,128)(2,1)S(1)} %pad_maximum_fusion.12), channel_id=1, source_target_pairs={{0,8},{8,0},{16,24},{24,16},{1,9},{9,1},{17,25},{25,17},{2,10},{10... | collective-permute-start | bytes 393224 | tf_op jit(solution)/shard_map/ppermute | solution.py:80
  26.4 1.4 %collective-permute-start.4 = (bf16[1,128,512]{2,1,0:T(8,128)(2,1)S(1)}, bf16[1,128,512]{2,1,0:T(8,128)(2,1)S(1)}, u32[]{:S(2)}, u32[]{:S(2)}) collective-permute-start(bf16[1,128,512]{2,1,0:T(8,128)(2,1)S(1)} %maximum_bitcast_fusion), channel_id=1, source_target_pairs={{0,2},{1,3},{2,0},{3,1},{4,6},{5,7},{6,4},{7,5},{8,10},{9,11},{10,... | collective-permute-start | bytes 393224 | tf_op jit(solution)/shard_map/ppermute | solution.py:80
  27.8 1.6 %collective-permute-start.7 = (bf16[4,16,2176]{2,1,0:T(8,128)(2,1)S(1)}, bf16[4,16,2176]{2,1,0:T(8,128)(2,1)S(1)}, u32[]{:S(2)}, u32[]{:S(2)}) collective-permute-start(bf16[4,16,2176]{2,1,0:T(8,128)(2,1)S(1)} %pad_maximum_fusion.4), channel_id=1, source_target_pairs={{0,8},{8,0},{16,24},{24,16},{1,9},{9,1},{17,25},{25,17},{2,10},{10... | collective-permute-start | bytes 835592 | tf_op jit(solution)/shard_map/ppermute | solution.py:80
  30.8 4.2 %collective-permute-done.7 = bf16[4,16,2176]{2,1,0:T(8,128)(2,1)S(1)} collective-permute-done((bf16[4,16,2176]{2,1,0:T(8,128)(2,1)S(1)}, bf16[4,16,2176]{2,1,0:T(8,128)(2,1)S(1)}, u32[]{:S(2)}, u32[]{:S(2)}) %collective-permute-start.7) | collective-permute-done | bytes 278560 | tf_op jit(solution)/shard_map/ppermute | solution.py:80
  37.1 1.2 collective-permute-start.19
  39.2 8.7 %collective-permute-done.8.refs_5_.refs_11_ = bf16[8,16,2176]{2,1,0:T(8,128)(2,1)S(1)} collective-permute-done((bf16[8,16,2176]{2,1,0:T(8,128)(2,1)S(1)}, bf16[8,16,2176]{2,1,0:T(8,128)(2,1)S(1)}, u32[]{:S(2)}, u32[]{:S(2)}) %collective-permute-start.8) | collective-permute-done | bytes 557088 | tf_op jit(solution)/shard_map/ppermute | solution.py:80
  48.4 1.8 %collective-permute-done.5.refs_2_ = bf16[2,128,512]{2,1,0:T(8,128)(2,1)S(1)} collective-permute-done((bf16[2,128,512]{2,1,0:T(8,128)(2,1)S(1)}, bf16[2,128,512]{2,1,0:T(8,128)(2,1)S(1)}, u32[]{:S(2)}, u32[]{:S(2)}) %collective-permute-start.5) | collective-permute-done | bytes 262176 | tf_op jit(solution)/shard_map/ppermute | solution.py:80
  52.0 2.7 %collective-permute-start.3 = (bf16[64,512]{1,0:T(8,128)(2,1)S(1)}, bf16[64,512]{1,0:T(8,128)(2,1)S(1)}, u32[]{:S(2)}, u32[]{:S(2)}) collective-permute-start(bf16[64,512]{1,0:T(8,128)(2,1)S(1)} %dynamic-slice_bitcast_fusion.1), channel_id=1, source_target_pairs={{0,4},{1,5},{2,6},{3,7},{4,0},{5,1},{6,2},{7,3},{8,12},{9,13},{10,... | collective-permute-start | bytes 196616 | tf_op jit(solution)/shard_map/ppermute | solution.py:80
  54.7 3.8 %attention_forward.1 = (f32[160,512]{1,0:T(8,128)S(1)}, bf16[640,384]{1,0:T(8,128)(2,1)S(1)}, bf16[544,512]{1,0:T(8,128)(2,1)S(1)}, bf16[512,384]{1,0:T(8,128)(2...) custom-call(s32[2]{0:T(128)S(1)} %copy-done.2, bf16[2,128,512]{2,1,0:T(8,128)(2,1)S(1)} %pad_maximum_fusion.5.refs_1_, ...), custom_call_target="tpu_custom_call" | custom-call | flops 4000000000 | bytes 2785288 | tf_op jit(solution)/shard_map/attention_forward/pallas_call | solution.py:643
  58.8 4.9 %feed_forward.1 = (bf16[1,144,512]{2,1,0:T(8,128)(2,1)S(1)}, bf16[32,512]{1,0:T(8,128)(2,1)S(1)}, f32[160,512]{1,0:T(8,128)S(1)}, bf16[96,512]{1,0:T(8,128)(2,1)...) custom-call(s32[2]{0:T(128)S(1)} %copy-done.2, ...), custom_call_target="tpu_custom_call" | custom-call | flops 6000000000 | bytes 7290888 | tf_op jit(solution)/shard_map/feed_forward/pallas_call | solution.py:643
  64.8 2.2 %collective-permute-done.23.refs_1_ = bf16[160,4608]{1,0:T(8,128)(2,1)S(1)} collective-permute-done((bf16[160,4608]{1,0:T(8,128)(2,1)S(1)}, bf16[160,4608]{1,0:T(8,128)(2,1)S(1)}, u32[]{:S(2)}, u32[]{:S(2)}) %collective-permute-start.23) | collective-permute-done | bytes 1474592 | tf_op jit(solution)/shard_map/ppermute | solution.py:80
  67.0 1.5 %weight_gradients.1 = (bf16[8,144,256]{2,1,0:T(8,128)(2,1)S(1)}, bf16[8,144,256]{2,1,0:T(8,128)(2,1)S(1)}, bf16[8,144,256]{2,1,0:T(8,128)(2,1)S(1)}, bf16[8,144,256]{2,1,0:T(8,128)(2,1)S(1)}) custom-call(bf16[160,4608]{1,0:T(8,128)(2,1)S(1)} %get-tuple-element.85.refs_0_, bf16[160,4608]{1,0:T(8,128)(2,1)S(1)} %collective-permute-done.23.refs_1_), custom_call_target="tpu_custom_call" | custom-call | flops 3000000000 | bytes 2949120 | tf_op jit(solution)/shard_map/weight_gradients/pallas_call | solution.py:643
  68.6 1.5 %collective-permute-done.22 = bf16[1,144,512]{2,1,0:T(8,128)(2,1)S(1)} collective-permute-done((bf16[1,144,512]{2,1,0:T(8,128)(2,1)S(1)}, bf16[1,144,512]{2,1,0:T(8,128)(2,1)S(1)}, u32[]{:S(2)}, u32[]{:S(2)}) %collective-permute-start.22) | collective-permute-done | bytes 147488 | tf_op jit(solution)/shard_map/ppermute | solution.py:80
  72.1 5.0 %attention_backward.1 = (bf16[8,112,128]{2,1,0:T(8,128)(2,1)S(1)}, bf16[8,112,128]{2,1,0:T(8,128)(2,1)S(1)}, bf16[288,512]{1,0:T(8,128)(2,1)S(1)}, bf16[288,512]{1,0:T(8,128)(2,1)S(1)}, bf16[16,512]{1,0:T(8,128)(2,1)S(1)}) custom-call(s32[2]{0:T(128)S(1)} %copy-done.2, bf16[640,384]{1,0:T(8,128)(2,1)S(1)} %get-tuple-element.80.refs_1_, ...), custom_call_target="tpu_custom_call" | custom-call | flops 6000000000 | bytes 2277384 | tf_op jit(solution)/shard_map/attention_backward/pallas_call | solution.py:643
  78.3 7.6 %collective-permute-done.27 = bf16[8,144,256]{2,1,0:T(8,128)(2,1)S(1)} collective-permute-done((bf16[8,144,256]{2,1,0:T(8,128)(2,1)S(1)}, bf16[8,144,256]{2,1,0:T(8,128)(2,1)S(1)}, u32[]{:S(2)}, u32[]{:S(2)}) %collective-permute-start.27) | collective-permute-done | bytes 589856 | tf_op jit(solution)/shard_map/ppermute | solution.py:80
  86.0 1.5 %collective-permute-start.36 = (bf16[4,144,256]{2,1,0:T(8,128)(2,1)S(1)}, bf16[4,144,256]{2,1,0:T(8,128)(2,1)S(1)}, u32[]{:S(2)}, u32[]{:S(2)}) collective-permute-start(bf16[4,144,256]{2,1,0:T(8,128)(2,1)S(1)} %get-tuple-element.161), channel_id=1, source_target_pairs={{0,8},{8,0},{16,24},{24,16},{1,9},{9,1},{17,25},{25,17},{2,10},{10... | collective-permute-start | bytes 884744 | tf_op jit(solution)/shard_map/ppermute | solution.py:80
  88.2 1.1 collective-permute-start.30
  89.6 1.3 %collective-permute-done.28 = bf16[160,512]{1,0:T(8,128)(2,1)S(1)} collective-permute-done((bf16[160,512]{1,0:T(8,128)(2,1)S(1)}, bf16[160,512]{1,0:T(8,128)(2,1)S(1)}, u32[]{:S(2)}, u32[]{:S(2)}) %collective-permute-start.28) | collective-permute-done | bytes 163872 | tf_op jit(solution)/shard_map/ppermute | solution.py:80
  91.0 4.9 %collective-permute-done.36 = bf16[4,144,256]{2,1,0:T(8,128)(2,1)S(1)} collective-permute-done((bf16[4,144,256]{2,1,0:T(8,128)(2,1)S(1)}, bf16[4,144,256]{2,1,0:T(8,128)(2,1)S(1)}, u32[]{:S(2)}, u32[]{:S(2)}) %collective-permute-start.36) | collective-permute-done | bytes 294944 | tf_op jit(solution)/shard_map/ppermute | solution.py:80
  97.3 2.8 %collective-permute-start.29 = (bf16[208,512]{1,0:T(8,128)(2,1)S(1)}, bf16[208,512]{1,0:T(8,128)(2,1)S(1)}, u32[]{:S(2)}, u32[]{:S(2)}) collective-permute-start(bf16[208,512]{1,0:T(8,128)(2,1)S(1)} %pad_maximum_fusion.8), channel_id=1, source_target_pairs={{0,4},{1,5},{2,6},{3,7},{4,0},{5,1},{6,2},{7,3},{8,12},{9,13},{10,... | collective-permute-start | bytes 638984 | tf_op jit(solution)/shard_map/ppermute | solution.py:80
  100.8 7.3 %collective-permute-done.37 = bf16[2,288,256]{2,1,0:T(8,128)(2,1)S(1)} collective-permute-done((bf16[2,288,256]{2,1,0:T(8,128)(2,1)S(1)}, bf16[2,288,256]{2,1,0:T(8,128)(2,1)S(1)}, u32[]{:S(2)}, u32[]{:S(2)}) %collective-permute-start.37) | collective-permute-done | bytes 294944 | tf_op jit(solution)/shard_map/ppermute | solution.py:80
  108.2 1.9 %collective-permute-start.38 = (bf16[1,288,256]{2,1,0:T(8,128)(2,1)S(1)}, bf16[1,288,256]{2,1,0:T(8,128)(2,1)S(1)}, u32[]{:S(2)}, u32[]{:S(2)}) collective-permute-start(bf16[1,288,256]{2,1,0:T(8,128)(2,1)S(1)} %get-tuple-element.111), channel_id=1, source_target_pairs={{0,4},{1,5},{2,6},{3,7},{4,0},{5,1},{6,2},{7,3},{8,12},{9,13},{10,... | collective-permute-start | bytes 442376 | tf_op jit(solution)/shard_map/ppermute | solution.py:80
  110.1 1.1 collective-permute-start.32
  111.3 6.7 %collective-permute-done.38.other = bf16[1,288,256]{2,1,0:T(8,128)(2,1)S(1)} collective-permute-done((bf16[1,288,256]{2,1,0:T(8,128)(2,1)S(1)}, bf16[1,288,256]{2,1,0:T(8,128)(2,1)S(1)}, u32[]{:S(2)}, u32[]{:S(2)}) %collective-permute-start.38) | collective-permute-done | bytes 147488 | tf_op jit(solution)/shard_map/ppermute | solution.py:80
  118.8 3.8 %collective-permute-done.33.other = bf16[1,112,128]{2,1,0:T(8,128)(2,1)S(1)} collective-permute-done((bf16[1,112,128]{2,1,0:T(8,128)(2,1)S(1)}, bf16[1,112,128]{2,1,0:T(8,128)(2,1)S(1)}, u32[]{:S(2)}, u32[]{:S(2)}) %collective-permute-start.33) | collective-permute-done | bytes 28704 | tf_op jit(solution)/shard_map/ppermute | solution.py:80
  122.6 1.3 %emit_tokens.1 = (bf16[2,64,512]{2,1,0:T(8,128)(2,1)}, bf16[2,20,512]{2,1,0:T(8,128)(2,1)S(1)}, bf16[2,64,512]{2,1,0:T(8,128)(2,1)}, bf16[2,20,512]{2,1,0:T(8,128)(2,1)S(1)}, f32[2,512]{1,0:T(2,128)}) custom-call(s32[2]{0:T(128)S(1)} %copy-done.2, bf16[96,512]{1,0:T(8,128)(2,1)S(1)} %get-tuple-element.79.refs_1_, bf16[160,512]{1,0:T(8,128)(2,1)S(1)} %fusion.1.refs_2_, ...), custom_call_target="tpu_custom_call" | custom-call | bytes 491528 | tf_op jit(solution)/shard_map/emit_tokens/pallas_call | solution.py:643
  (109 shorter events, 25.5 us)
Async XLA Ops:
  0.7 15.2 %collective-permute-start.11 = (bf16[1,16,2048]{2,1,0:T(8,128)(2,1)}, bf16[1,16,2048]{2,1,0:T(8,128)(2,1)S(1)}, u32[]{:S(2)}, u32[]{:S(2)}) collective-permute-start(bf16[1,16,2048]{2,1,0:T(8,128)(2,1)} %bitcast.19), channel_id=1, source_target_pairs={{0,4},{1,5},{2,6},{3,7},{4,0},{5,1},{6,2},{7,3},{8,12},{9,13},{10,... | collective-permute-start | bytes 196616 | tf_op jit(solution)/shard_map/ppermute | solution.py:80
  4.8 8.7 %collective-permute-start.2 = (bf16[1,64,512]{2,1,0:T(8,128)(2,1)}, bf16[1,64,512]{2,1,0:T(8,128)(2,1)S(1)}, u32[]{:S(2)}, u32[]{:S(2)}) collective-permute-start(bf16[1,64,512]{2,1,0:T(8,128)(2,1)} %bitcast.23), channel_id=1, source_target_pairs={{0,4},{1,5},{2,6},{3,7},{4,0},{5,1},{6,2},{7,3},{8,12},{9,13},{10,... | collective-permute-start | bytes 196616 | tf_op jit(solution)/shard_map/ppermute | solution.py:80
  6.4 11.9 %collective-permute-start = (bf16[1,16,2176]{2,1,0:T(8,128)(2,1)}, bf16[1,16,2176]{2,1,0:T(8,128)(2,1)S(1)}, u32[]{:S(2)}, u32[]{:S(2)}) collective-permute-start(bf16[1,16,2176]{2,1,0:T(8,128)(2,1)} %bitcast.15), channel_id=1, source_target_pairs={{0,4},{1,5},{2,6},{3,7},{4,0},{5,1},{6,2},{7,3},{8,12},{9,13},{10,... | collective-permute-start | bytes 208904 | tf_op jit(solution)/shard_map/ppermute | solution.py:80
  14.4 15.7 %collective-permute-start.17 = (bf16[2,64,512]{2,1,0:T(8,128)(2,1)S(1)}, bf16[2,64,512]{2,1,0:T(8,128)(2,1)S(1)}, u32[]{:S(2)}, u32[]{:S(2)}) collective-permute-start(bf16[2,64,512]{2,1,0:T(8,128)(2,1)S(1)} %pad_maximum_fusion.11), channel_id=1, source_target_pairs={{0,16},{8,24},{16,0},{24,8},{1,17},{9,25},{17,1},{25,9},{2,18},{10... | collective-permute-start | bytes 393224 | tf_op jit(solution)/shard_map/ppermute | solution.py:80
  19.2 8.6 %collective-permute-start.6 = (bf16[2,16,2176]{2,1,0:T(8,128)(2,1)S(1)}, bf16[2,16,2176]{2,1,0:T(8,128)(2,1)S(1)}, u32[]{:S(2)}, u32[]{:S(2)}) collective-permute-start(bf16[2,16,2176]{2,1,0:T(8,128)(2,1)S(1)} %pad_maximum_fusion.10), channel_id=1, source_target_pairs={{0,2},{1,3},{2,0},{3,1},{4,6},{5,7},{6,4},{7,5},{8,10},{9,11},{10,... | collective-permute-start | bytes 417800 | tf_op jit(solution)/shard_map/ppermute | solution.py:80
  20.3 6.0 %collective-permute-start.1 = (bf16[64,512]{1,0:T(8,128)(2,1)S(1)}, bf16[64,512]{1,0:T(8,128)(2,1)S(1)}, u32[]{:S(2)}, u32[]{:S(2)}) collective-permute-start(bf16[64,512]{1,0:T(8,128)(2,1)S(1)} %dynamic-slice_bitcast_fusion.2), channel_id=1, source_target_pairs={{0,4},{1,5},{2,6},{3,7},{4,0},{5,1},{6,2},{7,3},{8,12},{9,13},{10,... | collective-permute-start | bytes 196616 | tf_op jit(solution)/shard_map/ppermute | solution.py:80
  26.4 9.3 %collective-permute-start.4 = (bf16[1,128,512]{2,1,0:T(8,128)(2,1)S(1)}, bf16[1,128,512]{2,1,0:T(8,128)(2,1)S(1)}, u32[]{:S(2)}, u32[]{:S(2)}) collective-permute-start(bf16[1,128,512]{2,1,0:T(8,128)(2,1)S(1)} %maximum_bitcast_fusion), channel_id=1, source_target_pairs={{0,2},{1,3},{2,0},{3,1},{4,6},{5,7},{6,4},{7,5},{8,10},{9,11},{10,... | collective-permute-start | bytes 393224 | tf_op jit(solution)/shard_map/ppermute | solution.py:80
  27.8 7.1 %collective-permute-start.7 = (bf16[4,16,2176]{2,1,0:T(8,128)(2,1)S(1)}, bf16[4,16,2176]{2,1,0:T(8,128)(2,1)S(1)}, u32[]{:S(2)}, u32[]{:S(2)}) collective-permute-start(bf16[4,16,2176]{2,1,0:T(8,128)(2,1)S(1)} %pad_maximum_fusion.4), channel_id=1, source_target_pairs={{0,8},{8,0},{16,24},{24,16},{1,9},{9,1},{17,25},{25,17},{2,10},{10... | collective-permute-start | bytes 835592 | tf_op jit(solution)/shard_map/ppermute | solution.py:80
  29.4 7.1 %collective-permute-start.13 = (bf16[4,16,2048]{2,1,0:T(8,128)(2,1)S(1)}, bf16[4,16,2048]{2,1,0:T(8,128)(2,1)S(1)}, u32[]{:S(2)}, u32[]{:S(2)}) collective-permute-start(bf16[4,16,2048]{2,1,0:T(8,128)(2,1)S(1)} %pad_maximum_fusion.6), channel_id=1, source_target_pairs={{0,16},{8,24},{16,0},{24,8},{1,17},{9,25},{17,1},{25,9},{2,18},{10... | collective-permute-start | bytes 786440 | tf_op jit(solution)/shard_map/ppermute | solution.py:80
  30.0 7.0 %collective-permute-start.18 = (bf16[4,64,512]{2,1,0:T(8,128)(2,1)S(1)}, bf16[4,64,512]{2,1,0:T(8,128)(2,1)S(1)}, u32[]{:S(2)}, u32[]{:S(2)}) collective-permute-start(bf16[4,64,512]{2,1,0:T(8,128)(2,1)S(1)} %pad_maximum_fusion.7), channel_id=1, source_target_pairs={{0,2},{1,3},{2,0},{3,1},{4,6},{5,7},{6,4},{7,5},{8,10},{9,11},{10,... | collective-permute-start | bytes 786440 | tf_op jit(solution)/shard_map/ppermute | solution.py:80
  35.1 12.8 %collective-permute-start.8 = (bf16[8,16,2176]{2,1,0:T(8,128)(2,1)S(1)}, bf16[8,16,2176]{2,1,0:T(8,128)(2,1)S(1)}, u32[]{:S(2)}, u32[]{:S(2)}) collective-permute-start(bf16[8,16,2176]{2,1,0:T(8,128)(2,1)S(1)} %pad_maximum_fusion.refs_4_.refs_10_), channel_id=1, source_target_pairs={{0,16},{8,24},{16,0},{24,8},{1,17},{9,25},{17,1},{25,9},{2,18},{10... | collective-permute-start | bytes 1671176 | tf_op jit(solution)/shard_map/ppermute | solution.py:80
  36.5 15.0 %collective-permute-start.9 = (bf16[8,16,2176]{2,1,0:T(8,128)(2,1)S(1)}, bf16[8,16,2176]{2,1,0:T(8,128)(2,1)S(1)}, u32[]{:S(2)}, u32[]{:S(2)}) collective-permute-start(bf16[8,16,2176]{2,1,0:T(8,128)(2,1)S(1)} %pad_maximum_fusion.refs_4_.refs_10_), channel_id=1, source_target_pairs={{0,1},{1,0},{2,3},{3,2},{4,5},{5,4},{6,7},{7,6},{8,9},{9,8},{10,11... | collective-permute-start | bytes 1671176 | tf_op jit(solution)/shard_map/ppermute | solution.py:80
  37.1 14.0 %collective-permute-start.19 = (bf16[8,64,512]{2,1,0:T(8,128)(2,1)S(1)}, bf16[8,64,512]{2,1,0:T(8,128)(2,1)S(1)}, u32[]{:S(2)}, u32[]{:S(2)}) collective-permute-start(bf16[8,64,512]{2,1,0:T(8,128)(2,1)S(1)} %pad_maximum_fusion.2.refs_18_), channel_id=1, source_target_pairs={{0,8},{8,0},{16,24},{24,16},{1,9},{9,1},{17,25},{25,17},{2,10},{10... | collective-permute-start | bytes 1572872 | tf_op jit(solution)/shard_map/ppermute | solution.py:80
  38.3 13.2 %collective-permute-start.14 = (bf16[8,16,2048]{2,1,0:T(8,128)(2,1)S(1)}, bf16[8,16,2048]{2,1,0:T(8,128)(2,1)S(1)}, u32[]{:S(2)}, u32[]{:S(2)}) collective-permute-start(bf16[8,16,2048]{2,1,0:T(8,128)(2,1)S(1)} %pad_maximum_fusion.1.refs_14_), channel_id=1, source_target_pairs={{0,2},{1,3},{2,0},{3,1},{4,6},{5,7},{6,4},{7,5},{8,10},{9,11},{10,... | collective-permute-start | bytes 1572872 | tf_op jit(solution)/shard_map/ppermute | solution.py:80
  50.2 8.6 %collective-permute-start.20 = (bf16[8,64,512]{2,1,0:T(8,128)(2,1)S(1)}, bf16[8,64,512]{2,1,0:T(8,128)(2,1)S(1)}, u32[]{:S(2)}, u32[]{:S(2)}) collective-permute-start(bf16[8,64,512]{2,1,0:T(8,128)(2,1)S(1)} %pad_maximum_fusion.2.refs_18_), channel_id=1, source_target_pairs={{0,1},{1,0},{2,3},{3,2},{4,5},{5,4},{6,7},{7,6},{8,9},{9,8},{10,11... | collective-permute-start | bytes 1572872 | tf_op jit(solution)/shard_map/ppermute | solution.py:80
  51.1 7.7 %collective-permute-start.15 = (bf16[8,16,2048]{2,1,0:T(8,128)(2,1)S(1)}, bf16[8,16,2048]{2,1,0:T(8,128)(2,1)S(1)}, u32[]{:S(2)}, u32[]{:S(2)}) collective-permute-start(bf16[8,16,2048]{2,1,0:T(8,128)(2,1)S(1)} %pad_maximum_fusion.1.refs_14_), channel_id=1, source_target_pairs={{0,1},{1,0},{2,3},{3,2},{4,5},{5,4},{6,7},{7,6},{8,9},{9,8},{10,11... | collective-permute-start | bytes 1572872 | tf_op jit(solution)/shard_map/ppermute | solution.py:80
  51.5 7.3 %collective-permute-start.21 = (bf16[8,64,512]{2,1,0:T(8,128)(2,1)S(1)}, bf16[8,64,512]{2,1,0:T(8,128)(2,1)S(1)}, u32[]{:S(2)}, u32[]{:S(2)}) collective-permute-start(bf16[8,64,512]{2,1,0:T(8,128)(2,1)S(1)} %collective-permute-done.19.refs_19_), channel_id=1, source_target_pairs={{0,1},{1,0},{2,3},{3,2},{4,5},{5,4},{6,7},{7,6},{8,9},{9,8},{10,11... | collective-permute-start | bytes 1572872 | tf_op jit(solution)/shard_map/ppermute | solution.py:80
  51.6 7.2 %collective-permute-start.16 = (bf16[8,16,2048]{2,1,0:T(8,128)(2,1)S(1)}, bf16[8,16,2048]{2,1,0:T(8,128)(2,1)S(1)}, u32[]{:S(2)}, u32[]{:S(2)}) collective-permute-start(bf16[8,16,2048]{2,1,0:T(8,128)(2,1)S(1)} %collective-permute-done.14.refs_15_), channel_id=1, source_target_pairs={{0,1},{1,0},{2,3},{3,2},{4,5},{5,4},{6,7},{7,6},{8,9},{9,8},{10,11... | collective-permute-start | bytes 1572872 | tf_op jit(solution)/shard_map/ppermute | solution.py:80
  52.0 6.7 %collective-permute-start.3 = (bf16[64,512]{1,0:T(8,128)(2,1)S(1)}, bf16[64,512]{1,0:T(8,128)(2,1)S(1)}, u32[]{:S(2)}, u32[]{:S(2)}) collective-permute-start(bf16[64,512]{1,0:T(8,128)(2,1)S(1)} %dynamic-slice_bitcast_fusion.1), channel_id=1, source_target_pairs={{0,4},{1,5},{2,6},{3,7},{4,0},{5,1},{6,2},{7,3},{8,12},{9,13},{10,... | collective-permute-start | bytes 196616 | tf_op jit(solution)/shard_map/ppermute | solution.py:80
  63.8 6.3 %collective-permute-start.22 = (bf16[1,144,512]{2,1,0:T(8,128)(2,1)S(1)}, bf16[1,144,512]{2,1,0:T(8,128)(2,1)S(1)}, u32[]{:S(2)}, u32[]{:S(2)}) collective-permute-start(bf16[1,144,512]{2,1,0:T(8,128)(2,1)S(1)} %get-tuple-element.84), channel_id=1, source_target_pairs={{0,2},{1,3},{2,0},{3,1},{4,6},{5,7},{6,4},{7,5},{8,10},{9,11},{10,... | collective-permute-start | bytes 442376 | tf_op jit(solution)/shard_map/ppermute | solution.py:80
  70.1 15.7 %collective-permute-start.27 = (bf16[8,144,256]{2,1,0:T(8,128)(2,1)S(1)}, bf16[8,144,256]{2,1,0:T(8,128)(2,1)S(1)}, u32[]{:S(2)}, u32[]{:S(2)}) collective-permute-start(bf16[8,144,256]{2,1,0:T(8,128)(2,1)S(1)} %get-tuple-element.96), channel_id=1, source_target_pairs={{0,16},{8,24},{16,0},{24,8},{1,17},{9,25},{17,1},{25,9},{2,18},{10... | collective-permute-start | bytes 1769480 | tf_op jit(solution)/shard_map/ppermute | solution.py:80
  71.2 16.2 %collective-permute-start.26 = (bf16[8,144,256]{2,1,0:T(8,128)(2,1)S(1)}, bf16[8,144,256]{2,1,0:T(8,128)(2,1)S(1)}, u32[]{:S(2)}, u32[]{:S(2)}) collective-permute-start(bf16[8,144,256]{2,1,0:T(8,128)(2,1)S(1)} %get-tuple-element.87), channel_id=1, source_target_pairs={{0,8},{8,0},{16,24},{24,16},{1,9},{9,1},{17,25},{25,17},{2,10},{10... | collective-permute-start | bytes 1769480 | tf_op jit(solution)/shard_map/ppermute | solution.py:80
  77.2 12.2 %collective-permute-start.25 = (bf16[288,512]{1,0:T(8,128)(2,1)S(1)}, bf16[288,512]{1,0:T(8,128)(2,1)S(1)}, u32[]{:S(2)}, u32[]{:S(2)}) collective-permute-start(bf16[288,512]{1,0:T(8,128)(2,1)S(1)} %get-tuple-element.93), channel_id=1, source_target_pairs={{0,2},{1,3},{2,0},{3,1},{4,6},{5,7},{6,4},{7,5},{8,10},{9,11},{10,... | collective-permute-start | bytes 884744 | tf_op jit(solution)/shard_map/ppermute | solution.py:80
  86.0 10.0 %collective-permute-start.36 = (bf16[4,144,256]{2,1,0:T(8,128)(2,1)S(1)}, bf16[4,144,256]{2,1,0:T(8,128)(2,1)S(1)}, u32[]{:S(2)}, u32[]{:S(2)}) collective-permute-start(bf16[4,144,256]{2,1,0:T(8,128)(2,1)S(1)} %get-tuple-element.161), channel_id=1, source_target_pairs={{0,8},{8,0},{16,24},{24,16},{1,9},{9,1},{17,25},{25,17},{2,10},{10... | collective-permute-start | bytes 884744 | tf_op jit(solution)/shard_map/ppermute | solution.py:80
  87.6 8.5 %collective-permute-start.35 = (bf16[4,144,256]{2,1,0:T(8,128)(2,1)S(1)}, bf16[4,144,256]{2,1,0:T(8,128)(2,1)S(1)}, u32[]{:S(2)}, u32[]{:S(2)}) collective-permute-start(bf16[4,144,256]{2,1,0:T(8,128)(2,1)S(1)} %get-tuple-element.163), channel_id=1, source_target_pairs={{0,16},{8,24},{16,0},{24,8},{1,17},{9,25},{17,1},{25,9},{2,18},{10... | collective-permute-start | bytes 884744 | tf_op jit(solution)/shard_map/ppermute | solution.py:80
  88.2 11.9 %collective-permute-start.30 = (bf16[8,112,128]{2,1,0:T(8,128)(2,1)S(1)}, bf16[8,112,128]{2,1,0:T(8,128)(2,1)S(1)}, u32[]{:S(2)}, u32[]{:S(2)}) collective-permute-start(bf16[8,112,128]{2,1,0:T(8,128)(2,1)S(1)} %get-tuple-element.107), channel_id=1, source_target_pairs={{0,8},{8,0},{16,24},{24,16},{1,9},{9,1},{17,25},{25,17},{2,10},{10... | collective-permute-start | bytes 688136 | tf_op jit(solution)/shard_map/ppermute | solution.py:80
  96.2 11.9 %collective-permute-start.37 = (bf16[2,288,256]{2,1,0:T(8,128)(2,1)S(1)}, bf16[2,288,256]{2,1,0:T(8,128)(2,1)S(1)}, u32[]{:S(2)}, u32[]{:S(2)}) collective-permute-start(bf16[2,288,256]{2,1,0:T(8,128)(2,1)S(1)} %pad_maximum_fusion.3), channel_id=1, source_target_pairs={{0,2},{1,3},{2,0},{3,1},{4,6},{5,7},{6,4},{7,5},{8,10},{9,11},{10,... | collective-permute-start | bytes 884744 | tf_op jit(solution)/shard_map/ppermute | solution.py:80
  97.3 10.9 %collective-permute-start.29 = (bf16[208,512]{1,0:T(8,128)(2,1)S(1)}, bf16[208,512]{1,0:T(8,128)(2,1)S(1)}, u32[]{:S(2)}, u32[]{:S(2)}) collective-permute-start(bf16[208,512]{1,0:T(8,128)(2,1)S(1)} %pad_maximum_fusion.8), channel_id=1, source_target_pairs={{0,4},{1,5},{2,6},{3,7},{4,0},{5,1},{6,2},{7,3},{8,12},{9,13},{10,... | collective-permute-start | bytes 638984 | tf_op jit(solution)/shard_map/ppermute | solution.py:80
  100.2 9.9 %collective-permute-start.31 = (bf16[4,112,128]{2,1,0:T(8,128)(2,1)S(1)}, bf16[4,112,128]{2,1,0:T(8,128)(2,1)S(1)}, u32[]{:S(2)}, u32[]{:S(2)}) collective-permute-start(bf16[4,112,128]{2,1,0:T(8,128)(2,1)S(1)} %get-tuple-element.173), channel_id=1, source_target_pairs={{0,16},{8,24},{16,0},{24,8},{1,17},{9,25},{17,1},{25,9},{2,18},{10... | collective-permute-start | bytes 344072 | tf_op jit(solution)/shard_map/ppermute | solution.py:80
  108.2 9.8 %collective-permute-start.38 = (bf16[1,288,256]{2,1,0:T(8,128)(2,1)S(1)}, bf16[1,288,256]{2,1,0:T(8,128)(2,1)S(1)}, u32[]{:S(2)}, u32[]{:S(2)}) collective-permute-start(bf16[1,288,256]{2,1,0:T(8,128)(2,1)S(1)} %get-tuple-element.111), channel_id=1, source_target_pairs={{0,4},{1,5},{2,6},{3,7},{4,0},{5,1},{6,2},{7,3},{8,12},{9,13},{10,... | collective-permute-start | bytes 442376 | tf_op jit(solution)/shard_map/ppermute | solution.py:80
  110.1 8.4 %collective-permute-start.32 = (bf16[2,112,128]{2,1,0:T(8,128)(2,1)S(1)}, bf16[2,112,128]{2,1,0:T(8,128)(2,1)S(1)}, u32[]{:S(2)}, u32[]{:S(2)}) collective-permute-start(bf16[2,112,128]{2,1,0:T(8,128)(2,1)S(1)} %get-tuple-element.175), channel_id=1, source_target_pairs={{0,4},{1,5},{2,6},{3,7},{4,0},{5,1},{6,2},{7,3},{8,12},{9,13},{10,... | collective-permute-start | bytes 172040 | tf_op jit(solution)/shard_map/ppermute | solution.py:80
  118.0 7.9 %collective-permute-start.39 = (bf16[144,256]{1,0:T(8,128)(2,1)S(1)}, bf16[144,256]{1,0:T(8,128)(2,1)S(1)}, u32[]{:S(2)}, u32[]{:S(2)}) collective-permute-start(bf16[144,256]{1,0:T(8,128)(2,1)S(1)} %turn_feed.1), channel_id=1, source_target_pairs={{0,1},{1,0},{2,3},{3,2},{4,5},{5,4},{6,7},{7,6},{8,9},{9,8},{10,11... | collective-permute-start | bytes 221192 | tf_op jit(solution)/shard_map/ppermute | solution.py:80
  (14 other events, 144.4 us)

commit v3 on v2

--- a/solution.py
+++ b/solution.py
@@ -25,17 +25,16 @@
 NT = (((1,), (1,)), ((), ()))
 TN = (((0,), (0,)), ((), ()))
 
-GATHER_QKV = (2, 1, 3, 4, 0)
-GATHER_UP = (2, 3, 4, 1, 0)
-GATHER_DOWN = (2, 4, 1, 3, 0)
+GATHER_QKV = (2, 1, 4, 3, 0)
+GATHER_UP = (2, 3, 1, 4, 0)
+GATHER_DOWN = (2, 4, 3, 1, 0)
 REDUCE_UP = (0, 1, 4, 3, 2)
 REDUCE_DOWN = (0, 3, 1, 4, 2)
 REDUCE_QKV = (0, 4, 3, 1, 2)
 PAIRS = BLOCKS // 2
-PAIR_UP = (2, 3, 0, 1)
-PAIR_DOWN = (3, 2, 0, 1)
-PAIR_QKV = (2, 3, 1, 0)
-GIVEN = FF + 2 * WIDTH + WIDTH // 2 + FF // 2 + WIDTH // 2
+PAIR_MAIN = ((2, 3, 0, 1), (3, 2, 0, 1))
+PAIR_REST = ((0, 3, 2, 1), (0, 2, 3, 1))
+PAIR_QKV = ((3, 2, 1), (2, 3, 1))
 
 
 def dot(a, b, dims=NN):
@@ -85,6 +84,10 @@
     def pair_swap(self, x, bit):
         return self.swap(x, bit + 1)
 
+    def pair_swap_by_core(self, x, bits):
+        pairs = [(i, i ^ (2 << bits[i % 2])) for i in range(self.devices)]
+        return lax.ppermute(x, ("dp", "seq"), pairs)
+
     def device(self):
         return lax.axis_index("dp") * self.seq + lax.axis_index("seq")
 
@@ -169,6 +172,15 @@
     for place, mask in enumerate(masks):
         target = keep if place < half else send
         target[place % half, at, lanes] = source[aligned(block ^ mask, unit), :]
+
+
+def emit_pairs(source, keep, send, orders, pair, core, unit, at):
+    masks = [reduce_masks(order) for order in orders]
+    count = len(masks[0]) // 2
+    for spot, (first, second) in enumerate(zip(*masks)):
+        target = keep if spot < count else send
+        whose = pair ^ jnp.where(core == 0, first, second)
+        target[spot % count, at, :] = source[aligned(whose, unit), :]
 
 
 def roll_lanes(v, shift):
@@ -244,7 +256,7 @@
     length = lengths[slot]
     parts = (w0, w1, w2, w3)
     place_blocks(weight, parts, GATHER_QKV, block, 16, slice(0, 3 * WIDTH))
-    place_blocks(extra, parts, GATHER_QKV, block, 16, slice(4 * WIDTH, 4 * WIDTH + LANES))
+    place_blocks(extra, parts, GATHER_QKV, block, 16, slice(4 * WIDTH, FIRST))
     for part, masks in zip((near, far), layout.group_masks()):
         for k, mask in enumerate(masks):
             rows[aligned(rank ^ mask, ROWS), :] = part[k]
@@ -882,16 +894,25 @@
     )
 
 
-def prepare_kernel(*refs):
-    w_qkv, w_out = refs[:2]
-    vectors, b_up = refs[2:10], refs[10]
-    first, up_cell, sems = refs[11:14]
-    cells = refs[14:]
-    moves = [
-        (w_qkv, first.at[:, : 3 * WIDTH]),
-        (w_out, first.at[:, 3 * WIDTH : 4 * WIDTH]),
-        (b_up, up_cell),
-    ]
+FIRST = 4 * WIDTH + LANES
+
+
+def prepare_kernel(layout, *refs):
+    tokens, w_qkv, w_out = refs[:3]
+    vectors, b_up = refs[3:11], refs[11]
+    own, give = refs[12:14]
+    up_cell, sems = refs[14:16]
+    cells = refs[16:]
+    slot = lax.axis_index("seq") // layout.group
+    moves = [(b_up, up_cell)]
+    for target in (own, give):
+        moves.append((w_qkv, target.at[:, : 3 * WIDTH]))
+        moves.append((w_out, target.at[:, 3 * WIDTH : 4 * WIDTH]))
+    for k in range(4):
+        rows = slice(16 * k, 16 * k + 16)
+        lanes = slice(FIRST + k * WIDTH, FIRST + (k + 1) * WIDTH)
+        moves.append((tokens.at[slot, rows], own.at[:, lanes]))
+        moves.append((tokens.at[1 - slot, rows], give.at[:, lanes]))
     moves += [(v, cells[k]) for k, v in enumerate(vectors)]
     copies = [
         pltpu.make_async_copy(source, target, sems.at[k])
@@ -905,7 +926,13 @@
     rows = [jnp.concatenate([high(v[...]).reshape(1, 16), blank], 1) for v in cells]
     rows.append(jnp.concatenate([high(up_cell[...]).reshape(1, 64), blank[:, :64]], 1))
     rows.append(jnp.zeros((7, LANES), F32))
-    first[:, 4 * WIDTH :] = low(jnp.concatenate(rows, 0))
+    extra = low(jnp.concatenate(rows, 0))
+    own[:, 4 * WIDTH : FIRST] = extra
+    give[:, 4 * WIDTH : FIRST] = extra
+
+
+def stacked_rows(value):
+    return jnp.concatenate([value[:, k * WIDTH : (k + 1) * WIDTH] for k in range(4)], 0)
 
 
 def gather_vectors(extra):
@@ -936,10 +963,12 @@
     length = lengths[slot]
     parts = (w0, w1, w2, w3)
     place_blocks(weight, parts, GATHER_QKV, block, 16, slice(0, 3 * WIDTH))
-    place_blocks(extra, parts, GATHER_QKV, block, 16, slice(4 * WIDTH, 4 * WIDTH + LANES))
-    for part, masks in zip((near, far), layout.group_masks()):
+    place_blocks(extra, parts, GATHER_QKV, block, 16, slice(4 * WIDTH, FIRST))
+    for part, start, masks in zip((near, far), (FIRST, 0), layout.group_masks()):
         for k, mask in enumerate(masks):
-            rows[aligned(rank ^ mask, ROWS), :] = part[k]
+            for part_half in range(2):
+                at = aligned((rank ^ mask) * 2 + part_half, 64)
+                rows[at, :] = stacked_rows(part[2 * k + part_half, :, start:])
     rows[slot_len : slot_len + MEM_PAD, :] = memory[...]
     vector_rows, up_rows = gather_vectors(extra)
     vectors[...] = vector_rows
@@ -952,10 +981,11 @@
         lanes = slice(part * WIDTH, (part + 1) * WIDTH)
         value = dot(rows[...], weight[:, lanes])
         qkv[:filled, lanes] = low(value if shift is None else value + shift)
+    half = WIDTH // 2
     for part in range(3):
-        own = pl.ds(pl.multiple_of(part * WIDTH + rank * LANES, LANES), LANES)
-        qkv_own[:, part * LANES : (part + 1) * LANES] = qkv[:, own]
-        w_own[:, part * LANES : (part + 1) * LANES] = weight[:, own]
+        own = aligned(2 * part + place % 2, half)
+        qkv_own[:, part * half : (part + 1) * half] = qkv[:, own]
+        w_own[:, part * half : (part + 1) * half] = weight[:, own]
 
     keep = key_valid((1, key_rows), 1, slot, group, length, slot_len, mem_rows)
     bias = jnp.where(keep, 0.0, -1e30)
@@ -973,48 +1003,59 @@
         attn[:, at : at + LANES] = join_heads(dot(low(expos), values) / total)
 
 
+PACK = 32
+
+ACT_LANES = FF + 2 * WIDTH + WIDTH // 2
+LINEAR_LANES = FF // 2 + WIDTH // 2
+
+
+def hand_out(core, own, give, value, start):
+    half = value.shape[1] // 2
+    first, second = value[:, :half], value[:, half:]
+    mine = core == 0
+    own[:, start : start + half] = jnp.where(mine, first, second)
+    give[:, start : start + half] = jnp.where(mine, second, first)
+
+
+def row_weights(group):
+    row = lax.broadcasted_iota(jnp.int32, (OWN, 1), 0)
+    return jnp.where(row < ROWS, 1.0, 1.0 / group)
+
+
 def quad_feed_kernel(layout, mem_rows, *refs):
     lengths, tokens, arrived, memory, cots, cot_arrived, cot_memory = refs[:7]
     attn, vectors, up_bias = refs[7:10]
     outs, ups, downs = refs[10:14], refs[14:18], refs[18:22]
-    pack, grad_mem, first_grad, out_own, out_send = refs[22:27]
-    own, give, vector_grads, up_grads, w_heads = refs[27:32]
-    w_out, w_up, w_down, slope, grad_linear = refs[32:]
+    out_own, out_send, own, give, sums, squares_out, w_heads = refs[22:29]
+    w_out, w_up, w_down, slope, second_out, normed_out, inverse_out = refs[29:]
     group = layout.group
     place = lax.axis_index("seq")
     slot, rank = place // group, place % group
-    core = place % 2
     block = layout.block()
     length = lengths[slot]
+    place_blocks(w_out, outs, GATHER_QKV, block, 16, slice(3 * WIDTH, 4 * WIDTH))
     place_blocks(w_up, ups, GATHER_UP, block, 16, slice(0, FF))
-    place_blocks(w_out, outs, GATHER_QKV, block, 16, slice(3 * WIDTH, 4 * WIDTH))
     place_blocks(w_down, downs, GATHER_DOWN, block, 64, slice(0, WIDTH))
-    w_heads[...] = w_out[aligned(rank, LANES), :]
+    w_heads[...] = w_out[aligned(place % 2, WIDTH // 2), :]
 
     vec = vectors[...]
     out_bias, gain_one, shift_one, down_bias, gain_two, shift_two = [
         vec[k : k + 1] for k in range(2, 8)
     ]
-    rows = jnp.concatenate([high(tokens[slot]), high(arrived[...]), high(memory[...])], 0)
+    got = high(stacked_rows(arrived[...]))
+    rows = jnp.concatenate([high(tokens[slot]), got, high(memory[...])], 0)
     cot = jnp.concatenate([high(cots[slot]), high(cot_arrived[...]), high(cot_memory[...])], 0)
     valid = jnp.where(own_valid((OWN, 1), slot, group, rank, length, mem_rows), 1.0, 0.0)
-    row = lax.broadcasted_iota(jnp.int32, (OWN, 1), 0)
-    weight = jnp.where(row < ROWS, 1.0, 1.0 / group)
-    weight_low = low(weight)
+    weight = row_weights(group)
 
     def total(v):
         return jnp.sum(v * weight, axis=0, keepdims=True)
-
-    def hand_out(value, start):
-        half = value.shape[1] // 2
-        first, second = value[:, :half], value[:, half:]
-        mine = core == 0
-        own[:, start : start + half] = jnp.where(mine, first, second)
-        give[:, start : start + half] = jnp.where(mine, second, first)
 
     heads_out = low(attn[...])
     branch = dot(heads_out, w_out[...]) + out_bias
     normed_one, inverse_one = normalize(rows + branch)
+    normed_out[...] = normed_one
+    inverse_out[...] = jnp.broadcast_to(inverse_one, (OWN, LANES))
     hidden_one = normed_one * gain_one + shift_one
     hidden_low = low(hidden_one)
     for target in (own, give):
@@ -1039,231 +1080,244 @@
     out_own[:HEAD_DIM, :] = low(output[:HEAD_DIM])
     out_own[HEAD_DIM:, :] = low(output[ROWS:])
     out_send[...] = low(output[HEAD_DIM:])
+    row = lax.broadcasted_iota(jnp.int32, (OWN, 1), 0)
     token_valid = jnp.where(row < ROWS, valid, 0.0)
     squares = jnp.sum(feed * feed * token_valid, axis=0, keepdims=True)
-
+    squares_out[...] = low(
+        jnp.concatenate([*split_three(squares), jnp.zeros((13, WIDTH), F32)], 0)
+    )
     g = cot * valid
-    grads = [None] * 8
-    grads[6] = total(g * normed_two)
-    grads[7] = total(g)
     second = norm_back(g * gain_two, normed_two, inverse_two)
+    second_out[...] = second
     grad_feed = low(second)
-    hand_out(grad_feed * weight_low, FF + 2 * WIDTH)
-    grads[5] = total(high(grad_feed))
+    hand_out(place % 2, own, give, grad_feed * low(weight), FF + 2 * WIDTH)
+    blank = jnp.zeros((5, WIDTH), F32)
+    sums[...] = jnp.concatenate(
+        [blank, total(high(grad_feed)), total(g * normed_two), total(g)], 0
+    )
+
+
+def quad_slope_kernel(layout, *refs):
+    vectors, sums, squares, w_out, w_up, w_down, slope, second_in, normed_in, inverse_in = refs[:10]
+    pack, grad_mem, first_grad, own, give, grad_linear = refs[10:]
+    place = lax.axis_index("seq")
+    core = place % 2
+    weight = row_weights(layout.group)
+    weight_low = low(weight)
+
+    def total(v):
+        return jnp.sum(v * weight, axis=0, keepdims=True)
+
+    ups = []
+    second = second_in[...]
+    grad_feed = low(second)
     grad_hidden = second
     for at in range(0, FF, WIDTH):
         cols = slice(at, at + WIDTH)
         linear = low(dot(grad_feed, w_down[cols, :], NT) * slope[:, cols])
         grad_linear[:, cols] = linear * weight_low
-        up_grads[:, cols] = jnp.broadcast_to(total(high(linear)), (8, WIDTH))
+        ups.append(total(high(linear)))
         grad_hidden += dot(linear, w_up[:, cols], NT)
-    at = FF + 2 * WIDTH + WIDTH // 2
-    own[:, at : at + FF // 2] = grad_linear[:, aligned(core, FF // 2)]
-    give[:, at : at + FF // 2] = grad_linear[:, aligned(1 - core, FF // 2)]
-    grads[3] = total(grad_hidden * normed_one)
-    grads[4] = total(grad_hidden)
-    first = norm_back(grad_hidden * gain_one, normed_one, inverse_one)
+    own[:, : FF // 2] = grad_linear[:, aligned(core, FF // 2)]
+    give[:, : FF // 2] = grad_linear[:, aligned(1 - core, FF // 2)]
+    normed_one = normed_in[...]
+    gains = [total(grad_hidden * normed_one), total(grad_hidden)]
+    first = norm_back(grad_hidden * vectors[3:4, :], normed_one, inverse_in[:, :1])
     first_grad[...] = first
     grad_branch = low(first)
-    hand_out(grad_branch * weight_low, FF + 2 * WIDTH + WIDTH // 2 + FF // 2)
-    grads[2] = total(high(grad_branch))
-    grads[0] = grads[1] = jnp.zeros((1, WIDTH), F32)
-    vector_grads[...] = jnp.concatenate(grads, 0)
+    hand_out(core, own, give, grad_branch * weight_low, FF // 2)
+    sizes = jnp.concatenate([total(high(grad_branch)), *gains, sums[5:8, :], *ups], 0)
+    first, second, _ = split_three(sizes)
+    blank = jnp.zeros((PACK - 23, WIDTH), F32)
     pack[0, :ROWS, :] = grad_branch[:ROWS]
     pack[0, ROWS:, :] = low(
-        jnp.concatenate([*split_three(squares), jnp.zeros((13, WIDTH), F32)], 0)
+        jnp.concatenate([high(squares[...])[:3], first, second, blank], 0)
     )
     grad_mem[...] = grad_branch[ROWS:]
 
 
+MAIN_ROWS = 176
+REST_ROWS = 112
+FEED_ROWS = MAIN_ROWS + REST_ROWS
+
+
 def quad_weight_kernel(layout, *refs):
-    own, got, up_keep, up_send, down_keep, down_send, up, down, out = refs
-
-    def both(start, size):
-        cols = slice(start, start + size)
-        return jnp.concatenate([own[:, cols], got[:, cols]], 0)
-
+    acts, got_acts, linear, got_linear = refs[:4]
+    main, rest = refs[4:6], refs[6:8]
+    up, down, out = refs[8:]
+    core = lax.axis_index("seq") % 2
     pair = layout.block() >> 1
     half = WIDTH // 2
-    at = FF + 2 * WIDTH
-    grad_feed = both(at, half)
-    linear = at + half
-    grad_branch = both(linear + FF // 2, half)
+
+    def both(first, second, start, size):
+        cols = slice(start, start + size)
+        return jnp.concatenate([first[:, cols], second[:, cols]], 0)
+
+    def emit(source, target, unit, start):
+        orders = PAIR_MAIN if target is main else PAIR_REST
+        at = slice(start, start + unit)
+        emit_pairs(source, *target, orders, pair, core, unit, at)
+
+    grad_feed = both(acts, got_acts, FF + 2 * WIDTH, half)
     for start in range(0, FF, WIDTH):
-        down[start : start + WIDTH, :] = low(dot(both(start, WIDTH), grad_feed, TN))
-    value = low(dot(both(FF + WIDTH, WIDTH), grad_branch, TN))
+        act = both(acts, got_acts, start, WIDTH)
+        down[start : start + WIDTH, :] = low(dot(act, grad_feed, TN))
+    emit(down, main, 128, 0)
+    hidden = both(acts, got_acts, FF, WIDTH)
+    for start in range(0, FF // 2, WIDTH):
+        up[:, start : start + WIDTH] = low(dot(hidden, both(linear, got_linear, start, WIDTH), TN))
+    heads_out = both(acts, got_acts, FF + WIDTH, WIDTH)
+    value = low(dot(heads_out, both(linear, got_linear, FF // 2, half), TN))
     for p in range(BLOCKS):
         out[p % 2, p // 2 * 16 : p // 2 * 16 + 16, :] = value[16 * p : 16 * p + 16]
-    every = slice(0, half)
-    emit_blocks(down, down_keep, down_send, PAIR_DOWN, pair, 128, slice(0, 128), every)
-    for k, (keep, send, order) in enumerate(
-        ((up_keep, up_send, PAIR_UP), (down_keep, down_send, PAIR_DOWN))
-    ):
-        emit_blocks(out.at[k], keep, send, order, pair, 16, slice(128, 144), every)
-    hidden = both(FF, WIDTH)
-    for start in range(0, FF // 2, WIDTH):
-        up[:, start : start + WIDTH] = low(dot(hidden, both(linear + start, WIDTH), TN))
     for k in range(4):
-        emit_blocks(
-            up.at[:, half * k : half * (k + 1)],
-            up_keep,
-            up_send,
-            PAIR_UP,
-            pair,
-            32,
-            slice(32 * k, 32 * k + 32),
-            every,
-        )
+        target, start = (main, 128) if k == 0 else (rest, 32 * k - 32)
+        emit(up.at[:, half * k : half * (k + 1)], target, 32, start)
+    emit(out.at[0], main, 16, 160)
+    emit(out.at[1], rest, 16, 96)
 
 
 def quad_backward_kernel(layout, mem_rows, slot_len, *refs):
-    lengths, qkv, rows, w_own, w_heads, near, far, grad_mem, vector_grads, up_grads = refs[:10]
-    keep_out, send_out, in_keep, in_send, tail = refs[10:15]
-    grad_rows, squares, packed, grad_weight, grad_in, vec, extra = refs[15:]
+    lengths, qkv, rows, w_own, w_heads, near, far, grad_mem = refs[:8]
+    keep_out, send_out, in_keep, in_send, tail = refs[8:13]
+    grad_rows, sums, packed, grad_weight, extra = refs[13:]
     group = layout.group
     place = lax.axis_index("seq")
     slot, rank = place // group, place % group
+    core = place % 2
     pair = layout.block() >> 1
     length = lengths[slot]
     filled = slot_len + MEM_PAD
     key_rows = slot_len + MEM_KEYS
+    half = WIDTH // 2
     for part, masks in zip((near, far), layout.group_masks()):
         for k, mask in enumerate(masks):
             at = rank ^ mask
             grad_rows[aligned(at, ROWS), :] = part[k, :ROWS, :]
-            squares[at] = high(part[k, ROWS:, :])
+            sums[at] = high(part[k, ROWS:, :])
     grad_rows[slot_len:filled, :] = grad_mem[...]
 
     keep = key_valid((1, key_rows), 1, slot, group, length, slot_len, mem_rows)
     bias = jnp.where(keep, 0.0, -1e30)
     grad_attn = low(dot(grad_rows[...], w_heads[...], NT))
-    queries = qkv[:filled, :LANES]
-    keys = qkv[:, LANES : 2 * LANES]
-    values = qkv[:, 2 * LANES :]
-    d_query = jnp.zeros((filled, LANES), F32)
-    d_key = jnp.zeros((key_rows, LANES), F32)
-    d_value = jnp.zeros((key_rows, LANES), F32)
-    for mask in half_masks():
-        query = queries * (mask * 0.125)
-        grads = grad_attn * mask
-        scores = dot(query, keys, NT) + bias
-        expos = jnp.exp(scores - jnp.max(scores, axis=1, keepdims=True))
-        weights = expos * (1.0 / jnp.sum(expos, axis=1, keepdims=True))
-        weights_low = low(weights)
-        heads_out = dot(weights_low, values)
-        delta = jnp.sum(high(grads) * heads_out, axis=1, keepdims=True)
-        slopes = low(weights * (dot(grads, values, NT) - delta))
-        d_query += dot(slopes, keys) * (high(mask) * 0.125)
-        d_key += dot(slopes, query, TN)
-        d_value += dot(weights_low, grads, TN)
-    packed[:, :LANES] = low(d_query)
-    packed[:, LANES : 2 * LANES] = low(d_key[:filled])
-    packed[:, 2 * LANES :] = low(d_value[:filled])
-
-    grad_weight[...] = low(dot(rows[...], packed[...], TN))
+    for k in range(2):
+        at = [slice(part * half + k * LANES, part * half + (k + 1) * LANES) for part in range(3)]
+        queries, keys, values = qkv[:filled, at[0]], qkv[:, at[1]], qkv[:, at[2]]
+        d_query = jnp.zeros((filled, LANES), F32)
+        d_key = jnp.zeros((key_rows, LANES), F32)
+        d_value = jnp.zeros((key_rows, LANES), F32)
+        for mask in half_masks():
+            query = queries * (mask * 0.125)
+            grads = grad_attn[:, k * LANES : (k + 1) * LANES] * mask
+            scores = dot(query, keys, NT) + bias
+            expos = jnp.exp(scores - jnp.max(scores, axis=1, keepdims=True))
+            weights = expos * (1.0 / jnp.sum(expos, axis=1, keepdims=True))
+            weights_low = low(weights)
+            slopes = dot(grads, values, NT)
+            delta = jnp.sum(high(weights_low) * slopes, axis=1, keepdims=True)
+            slopes = low(weights * (slopes - delta))
+            d_query += dot(slopes, keys) * (high(mask) * 0.125)
+            d_key += dot(slopes, query, TN)
+            d_value += dot(weights_low, grads, TN)
+        packed[:, at[0]] = low(d_query)
+        packed[:, at[1]] = low(d_key[:filled])
+        packed[:, at[2]] = low(d_value[:filled])
+
+    def emit(source, unit, at):
+        emit_pairs(source, keep_out, send_out, PAIR_QKV, pair, core, unit, at)
+
     for part in range(3):
-        emit_blocks(
-            grad_weight.at[:, part * LANES : (part + 1) * LANES],
-            keep_out,
-            send_out,
-            PAIR_QKV,
-            pair,
-            32,
-            slice(32 * part, 32 * part + 32),
-            slice(0, LANES),
-        )
-    grad_in[...] = low(dot(packed[...], w_own[...], NT))
-    for k, (target, mask) in enumerate(((in_keep, 0), (in_keep, 1), (in_send, 2), (in_send, 3))):
-        start = (k % 2) * ROWS
-        target[start : start + ROWS, :] = grad_in[aligned(rank ^ mask, ROWS), :]
-    for target in (in_keep, in_send):
-        target[2 * ROWS :, :] = grad_in[slot_len:filled, :]
-
-    vec[...] = vector_grads[...]
-    own = aligned(rank, LANES)
-    vec[0:1, own] = jnp.sum(high(packed[:, :LANES]), axis=0, keepdims=True)
-    vec[1:2, own] = jnp.sum(high(packed[:, 2 * LANES :]), axis=0, keepdims=True)
+        lanes = slice(part * half, (part + 1) * half)
+        grad_weight[...] = low(dot(rows[...], packed[:, lanes], TN))
+        emit(grad_weight, 32, slice(32 * part, 32 * part + 32))
+    for target, at in ((in_keep, rank), (in_send, rank ^ 1)):
+        target[:ROWS, :] = low(dot(packed[aligned(at, ROWS), :], w_own[...], NT))
+    grad_in = low(dot(packed[slot_len:filled, :], w_own[...], NT))
+    in_keep[ROWS:, :] = grad_in
+    in_send[ROWS:, :] = grad_in
+
+    total = sums[0]
+    for k in range(1, group):
+        total += sums[k]
+    square = total[0:1] + total[1:2] + total[2:3]
+    tail[...] = low(jnp.concatenate([*split_three(square), jnp.zeros((13, WIDTH), F32)], 0))
+    sizes = total[3:13] + total[13:23]
+    first_core = core == 0
+    blank = jnp.zeros((1, half), F32)
+    biases = []
+    for part in (0, 2):
+        value = packed[:, part * half : (part + 1) * half]
+        value = jnp.sum(high(value), axis=0, keepdims=True)
+        first, second = jnp.where(first_core, value, 0.0), jnp.where(first_core, 0.0, value)
+        biases.append(jnp.concatenate([first, second], 1))
+    vec = jnp.concatenate([*biases, sizes[:6]], 0)
+    ups = jnp.concatenate([sizes[6:10], jnp.zeros((4, WIDTH), F32)], 0)
     lanes = lane_index((8, LANES))
     sublane = lax.broadcasted_iota(jnp.int32, (8, LANES), 0)
     for p in range(0, BLOCKS, 2):
         both = []
         for q in (p, p + 1):
+            mine = core == q % 2
             g = q // 8
-            cell = roll_lanes(vec[:, g * LANES : (g + 1) * LANES], -16 * (q % 8))
-            g = q // 2
-            ups = up_grads[:, g * LANES : (g + 1) * LANES]
+            columns = slice(g * LANES, (g + 1) * LANES)
+            cell = roll_lanes(vec[:, columns], -16 * (q % 8))
+            cell = jnp.where(sublane < 2, cell, jnp.where(mine, cell, 0.0))
+            g = q % 8 // 2
+            row = ups[q // 8 : q // 8 + 1, g * LANES : (g + 1) * LANES]
+            row = jnp.broadcast_to(jnp.where(mine, row, 0.0), (8, LANES))
             up = jnp.zeros((8, LANES), F32)
             for k in range(4):
-                up = jnp.where(sublane == k, roll_lanes(ups, 16 - 64 * (q % 2) - 16 * k), up)
+                up = jnp.where(sublane == k, roll_lanes(row, 16 - 64 * (q % 2) - 16 * k), up)
             both.append(jnp.where(lanes < 16, cell, jnp.where(lanes < 32, up, 0.0)))
-        extra[p * 8 : p * 8 + 16, :] = low(jnp.concatenate(both, 0))
-    emit_blocks(extra, keep_out, send_out, PAIR_QKV, pair, 16, slice(96, 112), slice(0, LANES))
-
-    square = squares[0]
-    for k in range(1, group):
-        square += squares[k]
-    square = square[0:1] + square[1:2] + square[2:3]
-    tail[...] = low(jnp.concatenate([*split_three(square), jnp.zeros((13, WIDTH), F32)], 0))
+        wide = jnp.concatenate(both, 1)
+        extra[p * 8 : p * 8 + 16, :] = low(jnp.concatenate([wide, jnp.zeros_like(wide)], 0))
+    emit(extra, 16, slice(96, 112))
 
 
 def feed_rows(core):
-    at = [pl.ds(pl.multiple_of(32 * k + 16 * core, 16), 16) for k in range(4)]
-    at.append(pl.ds(pl.multiple_of(144 + 64 * core, 16), 64))
-    at.append(pl.ds(pl.multiple_of(128 + 144 * core, 16), 16))
+    starts = [128, *(MAIN_ROWS + 32 * k for k in range(3))]
+    at = [pl.ds(pl.multiple_of(start + 16 * core, 16), 16) for start in starts]
+    at.append(pl.ds(pl.multiple_of(64 * core, 64), 64))
+    at.append(pl.ds(pl.multiple_of(160 + 112 * core, 16), 16))
     return at
 
 
-def turn_feed_kernel(keep, other, send):
+def qkv_rows(core):
+    return [pl.ds(pl.multiple_of(FEED_ROWS + 32 * k + 16 * core, 16), 16) for k in range(3)]
+
+
+EXTRA_ROWS = pl.ds(FEED_ROWS + 96, 16)
+
+
+def turn_kernel(keep, other, send):
     start = 0
-    for at in feed_rows(1 - lax.axis_index("seq") % 2):
+    core = 1 - lax.axis_index("seq") % 2
+    for at in [*feed_rows(core), *qkv_rows(core), EXTRA_ROWS]:
         send[start : start + at.size, :] = low(high(keep[0, at, :]) + high(other[0, at, :]))
         start += at.size
 
 
-def emit_feed_kernel(keep, other, got, w_up, w_down, w_out):
+def emit_kernel_quad(keep, other, got, w_up, w_down, w_out, w_qkv, *vectors):
     core = lax.axis_index("seq") % 2
     half = WIDTH // 2
-    own, theirs = aligned(core, half), aligned(1 - core, half)
     start = 0
-    for k, at in enumerate(feed_rows(core)):
+    places = [*feed_rows(core), *qkv_rows(core), EXTRA_ROWS]
+    for k, at in enumerate(places):
         total = high(keep[0, at, :]) + high(other[0, at, :])
         arrived = high(got[start : start + at.size, :])
         start += at.size
         if k < 4:
-            w_up[:, pl.ds(pl.multiple_of(core * 1024 + half * k, half), half)] = total
-            w_up[:, pl.ds(pl.multiple_of((1 - core) * 1024 + half * k, half), half)] = arrived
+            target, own, theirs = w_up, 4 * core + k, 4 - 4 * core + k
+        elif k < 6:
+            target, own, theirs = (w_down, w_out)[k - 4], core, 1 - core
+        elif k < 9:
+            target, own, theirs = w_qkv, 2 * k - 12 + core, 2 * k - 11 - core
         else:
-            target = w_down if k == 4 else w_out
-            target[:, own] = total
-            target[:, theirs] = arrived
-
-
-def turn_qkv_kernel(keep, other, send):
-    away = 1 - lax.axis_index("seq") % 2
-    for k, source in enumerate((keep, other)):
-        for part in range(3):
-            at = pl.ds(pl.multiple_of(32 * part + 16 * away, 16), 16)
-            start = 48 * k + 16 * part
-            send[start : start + 16, :] = source[0, at, :]
-    send[96:112, :] = low(high(keep[0, 96:112, :]) + high(other[0, 96:112, :]))
-
-
-def emit_qkv_kernel(keep, other, got, w_qkv, *vectors):
-    place = lax.axis_index("seq")
-    core, rank = place % 2, place % 4
-    for part in range(3):
-        at = pl.ds(pl.multiple_of(32 * part + 16 * core, 16), 16)
-        pieces = (
-            (rank, keep[0, at, :]),
-            (rank ^ 2, other[0, at, :]),
-            (rank ^ 1, got[16 * part : 16 * part + 16, :]),
-            (rank ^ 3, got[48 + 16 * part : 64 + 16 * part, :]),
-        )
-        for whose, piece in pieces:
-            lanes = pl.ds(pl.multiple_of(part * WIDTH + whose * LANES, LANES), LANES)
-            w_qkv[:, lanes] = high(piece)
-    total = high(keep[0, 96:112, :]) + high(other[0, 96:112, :]) + high(got[96:112, :])
-    total = jnp.where(core == 0, total[:8], total[8:])
+            total += arrived
+            continue
+        target[:, aligned(own, half)] = total
+        target[:, aligned(theirs, half)] = arrived
+    total = jnp.where(core == 0, total[:8, :LANES], total[:8, LANES:])
     for k in range(8):
         vectors[k][...] = total[k, :16]
     lanes = lane_index((1, LANES))
@@ -1274,7 +1328,7 @@
     vectors[8][...] = ups[0, :64]
 
 
-def emit_tokens_kernel(layout, mem_rows, *refs):
+def emit_tokens_kernel(layout, *refs):
     lengths, out_own, grad_own, grad_got, tail = refs[:5]
     out_tokens, out_memory, grad_tokens, grad_memory, rms = refs[5:]
     slot = lax.axis_index("seq") // layout.group
@@ -1284,9 +1338,15 @@
         (grad_own, 0, 128, slot, grad_tokens, grad_memory),
         (grad_got, 0, 64, 1 - slot, grad_tokens, grad_memory),
     )
-    for source, start, mem, at, tokens, memory in pieces:
+    cells = [[None, None], [None, None]]
+    for k, (source, start, mem, at, tokens, _) in enumerate(pieces):
         tokens[at] = source[start : start + 64, :]
-        memory[at] = low(high(source[mem : mem + 32, :])[:mem_rows])
+        cells[k // 2][k % 2] = high(source[mem : mem + 32, :])
+    for (own, got), memory in zip(cells, (out_memory, grad_memory)):
+        first = jnp.where(slot == 0, own, got)
+        second = jnp.where(slot == 0, got, own)
+        rows = memory.shape[0]
+        memory[...] = low(jnp.stack([first[:rows], second[:rows]], 1))
     result = []
     for cell, at in ((tail[...], slot), (grad_got[96:112, :], 1 - slot)):
         cell = high(cell)
@@ -1328,53 +1388,51 @@
         return lax.dynamic_index_in_dim(x, at, 0, False)
 
     small = (b_query, b_value, b_out, gain_one, shift_one, b_down, gain_two, shift_two)
-    first = pl.pallas_call(
-        prepare_kernel,
-        out_shape=jax.ShapeDtypeStruct((16, 4 * WIDTH + LANES), BF),
-        in_specs=[pl.BlockSpec(memory_space=pl.ANY)] * 11,
-        out_specs=pl.BlockSpec(memory_space=pltpu.VMEM),
-        scratch_shapes=[pltpu.VMEM((64,), BF), pltpu.SemaphoreType.DMA((11,))]
+    own, give = pl.pallas_call(
+        functools.partial(prepare_kernel, layout),
+        out_shape=[jax.ShapeDtypeStruct((16, FIRST + FF), BF)] * 2,
+        in_specs=[pl.BlockSpec(memory_space=pl.ANY)] * 12,
+        out_specs=[pl.BlockSpec(memory_space=pltpu.VMEM)] * 2,
+        scratch_shapes=[pltpu.VMEM((64,), BF), pltpu.SemaphoreType.DMA((21,))]
         + [pltpu.VMEM((16,), BF)] * 8,
         name="prepare",
-    )(w_qkv, w_out, *small, b_up)
+    )(tokens, w_qkv, w_out, *small, b_up)
 
     def after(x, *others):
         return lax.optimization_barrier((x, *others))[0]
 
-    def gather(held, order, *ready):
-        held = jnp.concatenate([held, layout.block_swap(held, order[1])], 0)
-        held = jnp.concatenate([held, layout.block_swap(held, order[2])], 0)
-        held = after(held, *ready)
-        last = layout.block_swap(held, order[3])
+    def doubled(held, bit):
+        return jnp.concatenate([held, layout.block_swap(held, bit)], 0)
+
+    def finish(held, order, *ready):
+        last = after(layout.block_swap(held, order[3]), *ready)
         return held, last, layout.block_swap(held, 0), layout.block_swap(last, 0)
 
-    def begin(x, order):
-        x = x[None]
-        return jnp.concatenate([x, layout.block_swap(x, order[0])], 0)
-
-    second = begin(w_up, GATHER_UP)
-    third = begin(w_down, GATHER_DOWN)
-    first = begin(first, GATHER_QKV)
-    arrived = layout.swap(pick(after(tokens, first), 1 - slot), partner)
-    near = jnp.concatenate([pick(tokens, slot), arrived], 0)[None]
-    near = jnp.concatenate([near, layout.swap(near, 1)], 0)
-    cot_arrived = layout.swap(pick(after(cot_tokens, third), 1 - slot), partner)
+    second = doubled(w_up[None], GATHER_UP[0])
+    third = doubled(w_down[None], GATHER_DOWN[0])
+    got = layout.swap(give, partner)[None]
+    arrived = got[0, :, FIRST:]
+    near = doubled(jnp.concatenate([own[None], got], 0), GATHER_QKV[1])
+    far = layout.swap(near[:, :, FIRST:], 0)
+    first = doubled(near[:, :, :FIRST], GATHER_QKV[2])
+    second = doubled(doubled(second, GATHER_UP[1]), GATHER_UP[2])
+    third = doubled(doubled(third, GATHER_DOWN[1]), GATHER_DOWN[2])
+    cot_arrived = layout.swap(pick(after(cot_tokens, first), 1 - slot), partner)
     pad_rows = ((0, MEM_PAD - mem_rows), (0, 0))
-    own_memory = jnp.pad(pick(after(memory, third), slot), pad_rows)
-    own_cot_memory = jnp.pad(pick(after(cot_memory, third), slot), pad_rows)
-    far = layout.swap(near, 0)
-    up_parts = gather(second, GATHER_UP, near, own_memory, own_cot_memory)
-    down_parts = gather(third, GATHER_DOWN)
-    qkv_parts = gather(first, GATHER_QKV)
+    own_memory = jnp.pad(pick(memory, slot), pad_rows)
+    own_cot_memory = jnp.pad(pick(cot_memory, slot), pad_rows)
+    qkv_parts = finish(first, GATHER_QKV, cot_arrived)
+    up_parts = finish(second, GATHER_UP)
+    down_parts = finish(third, GATHER_DOWN)
 
     attn, qkv_own, rows, w_own, vector_rows, up_bias = call(
         functools.partial(quad_forward_kernel, layout, mem_rows, slot_len),
         "attention_forward",
         [
             ((OWN, WIDTH), F32),
-            ((key_rows, 3 * LANES), BF),
+            ((key_rows, 3 * WIDTH // 2), BF),
             ((filled, WIDTH), BF),
-            ((WIDTH, 3 * LANES), BF),
+            ((WIDTH, 3 * WIDTH // 2), BF),
             ((8, WIDTH), F32),
             ((8, FF), F32),
         ],
@@ -1383,38 +1441,40 @@
         flops=4 * 10**9,
     )
     (
-        pack,
-        grad_mem,
-        first_grad,
         out_own,
         out_send,
-        own,
-        give,
-        vector_grads,
-        up_grads,
+        acts,
+        acts_give,
+        sums,
+        squares,
         w_heads,
+        w_out_all,
+        w_up_all,
+        w_down_all,
+        slope,
+        second_grad,
+        normed_one,
+        inverse_one,
     ) = call(
         functools.partial(quad_feed_kernel, layout, mem_rows),
         "feed_forward",
         [
-            ((1, ROWS + 16, WIDTH), BF),
-            ((MEM_PAD, WIDTH), BF),
-            ((OWN, WIDTH), F32),
             ((64 + MEM_PAD, WIDTH), BF),
             ((64 + MEM_PAD, WIDTH), BF),
-            ((OWN, GIVEN), BF),
-            ((OWN, GIVEN), BF),
+            ((OWN, ACT_LANES), BF),
+            ((OWN, ACT_LANES), BF),
             ((8, WIDTH), F32),
-            ((8, FF), F32),
-            ((LANES, WIDTH), BF),
-        ],
-        [
+            ((16, WIDTH), BF),
+            ((WIDTH // 2, WIDTH), BF),
             ((WIDTH, WIDTH), BF),
             ((WIDTH, FF), BF),
             ((FF, WIDTH), BF),
             ((OWN, FF), F32),
-            ((OWN, FF), BF),
+            ((OWN, WIDTH), F32),
+            ((OWN, WIDTH), F32),
+            ((OWN, LANES), F32),
         ],
+        [],
         (
             lengths,
             tokens,
@@ -1430,116 +1490,129 @@
             *up_parts,
             *down_parts,
         ),
-        flops=6 * 10**9,
-    )
-    taken = layout.swap(give, 0)
+        flops=3 * 10**9,
+    )
+    acts_got = layout.swap(acts_give, 0)
+    pack, grad_mem, first_grad, linear, linear_give = call(
+        functools.partial(quad_slope_kernel, layout),
+        "feed_backward",
+        [
+            ((1, ROWS + PACK, WIDTH), BF),
+            ((MEM_PAD, WIDTH), BF),
+            ((OWN, WIDTH), F32),
+            ((OWN, LINEAR_LANES), BF),
+            ((OWN, LINEAR_LANES), BF),
+        ],
+        [((OWN, FF), BF)],
+        (
+            vector_rows,
+            sums,
+            squares,
+            w_out_all,
+            w_up_all,
+            w_down_all,
+            slope,
+            second_grad,
+            normed_one,
+            inverse_one,
+        ),
+        smem=0,
+        flops=3 * 10**9,
+    )
+    linear_got = layout.swap(linear_give, 0)
     grads_next = layout.swap(pack, 1)
     half = PAIRS // 2
-    up_keep, up_send, down_keep, down_send = call(
+    main_keep, main_send, rest_keep, rest_send = call(
         functools.partial(quad_weight_kernel, layout),
         "weight_gradients",
-        [
-            ((half, 144, WIDTH // 2), BF),
-            ((half, 144, WIDTH // 2), BF),
-            ((half, 144, WIDTH // 2), BF),
-            ((half, 144, WIDTH // 2), BF),
-        ],
+        [((half, MAIN_ROWS, WIDTH // 2), BF)] * 2 + [((half, REST_ROWS, WIDTH // 2), BF)] * 2,
         [((WIDTH, FF // 2), BF), ((FF, WIDTH // 2), BF), ((2, WIDTH // 2, WIDTH // 2), BF)],
-        (own, taken),
+        (acts, after(acts_got, pack), linear, linear_got),
         smem=0,
-        flops=3 * 10**9,
-    )
-    grads_next, _ = lax.optimization_barrier((grads_next, up_send))
+        flops=10**9,
+    )
+    grads_next = after(grads_next, main_send)
     grads_near = jnp.concatenate([pack, grads_next], 0)
     grads_far = layout.swap(grads_near, 0)
     qkv_keep, qkv_send, in_keep, in_send, tail = call(
         functools.partial(quad_backward_kernel, layout, mem_rows, slot_len),
         "attention_backward",
         [
-            ((half, 112, LANES), BF),
-            ((half, 112, LANES), BF),
-            ((2 * ROWS + MEM_PAD, WIDTH), BF),
-            ((2 * ROWS + MEM_PAD, WIDTH), BF),
+            ((half // 2, 112, WIDTH // 2), BF),
+            ((half // 2, 112, WIDTH // 2), BF),
+            ((OWN, WIDTH), BF),
+            ((OWN, WIDTH), BF),
             ((16, WIDTH), BF),
         ],
         [
             ((filled, WIDTH), BF),
-            ((layout.group, 16, WIDTH), F32),
-            ((filled, 3 * LANES), BF),
-            ((WIDTH, 3 * LANES), BF),
-            ((filled, WIDTH), BF),
-            ((8, WIDTH), F32),
-            ((8 * BLOCKS, LANES), BF),
+            ((layout.group, PACK, WIDTH), F32),
+            ((filled, 3 * WIDTH // 2), BF),
+            ((WIDTH, WIDTH // 2), BF),
+            ((8 * BLOCKS, WIDTH // 2), BF),
         ],
-        (
-            lengths,
-            qkv_own,
-            rows,
-            w_own,
-            w_heads,
-            grads_near,
-            grads_far,
-            grad_mem,
-            vector_grads,
-            up_grads,
-        ),
-        flops=6 * 10**9,
-    )
-    swap = layout.pair_swap
-    up_other, down_other = swap(up_send, PAIR_UP[0]), swap(down_send, PAIR_DOWN[0])
-    up_keep, up_send = fold_plain(up_keep, up_other)
-    down_keep, down_send = fold_plain(down_keep, down_other)
-    qkv_send = after(qkv_send, up_send)
-    up_ready, down_ready = up_send, down_send
-    up_other, down_other = swap(up_send, PAIR_UP[1]), swap(down_send, PAIR_DOWN[1])
-    up_keep, up_send = fold_plain(up_keep, up_other)
-    down_keep, down_send = fold_plain(down_keep, down_other)
-    feed_keep = jnp.concatenate([up_keep, down_keep], 1)
-    feed_send = jnp.concatenate([up_send, down_send], 1)
-    feed_other = swap(feed_send, PAIR_UP[2])
-    feed_keep, feed_send = fold_plain(feed_keep, feed_other)
-    in_sum = high(in_keep) + high(after(layout.swap(in_send, 1), up_ready, down_ready))
-    in_send = low(in_sum[ROWS:])
+        (lengths, qkv_own, rows, w_own, w_heads, grads_near, grads_far, grad_mem),
+        flops=0,
+    )
+    swap = layout.pair_swap_by_core
+
+    def bits(orders, step):
+        return tuple(order[step] for order in orders)
+
+    main_other = swap(main_send, bits(PAIR_MAIN, 0))
+    rest_other = swap(rest_send, bits(PAIR_REST, 0))
+    main_keep, main_send = fold_plain(main_keep, main_other)
+    rest_keep, rest_send = fold_plain(rest_keep, rest_other)
+    qkv_send = after(qkv_send, main_send, rest_send)
+    both_send = jnp.concatenate([main_send, rest_send, qkv_send], 1)
+    both_other = swap(both_send, bits(PAIR_QKV, 0))
+    main_keep, main_send = fold_plain(main_keep, both_other[:, :MAIN_ROWS])
+    both_keep = jnp.concatenate([rest_keep, qkv_keep], 1)
+    both_keep, both_send = fold_plain(both_keep, both_other[:, MAIN_ROWS:])
+    second_ready = both_send
+    main_other = swap(main_send, bits(PAIR_MAIN, 2))
+    both_other = swap(both_send, bits(PAIR_QKV, 1))
+    main_keep, main_send = fold_plain(main_keep, main_other)
+    both_keep, both_send = fold_plain(both_keep, both_other)
+    all_keep = jnp.concatenate([main_keep, both_keep], 1)
+    all_send = jnp.concatenate([main_send, both_send], 1)
+
     in_got = layout.swap(in_send, 0)
-    grad_own = low(
-        jnp.concatenate([in_sum[:ROWS], high(in_send[ROWS:])], 0) + high(in_got) + first_grad
-    )
+    grad_own = low(high(in_keep) + high(in_got) + first_grad)
     grad_got = layout.swap(jnp.concatenate([grad_own[64:], tail, out_send], 0), partner)
-
-    feed_total = feed_keep, swap(after(feed_send, grad_got), PAIR_UP[3])
-    qkv_total = layout.reduce(qkv_keep, qkv_send, PAIR_QKV, fold_plain, swap)
-
-    (feed_send,) = call(
-        turn_feed_kernel, "turn_feed", [((144, WIDTH // 2), BF)], [], feed_total, smem=0
-    )
+    grad_got = after(grad_got, all_send)
+
     out_tokens, out_memory, grad_tokens, grad_memory, rms = call(
-        functools.partial(emit_tokens_kernel, layout, mem_rows),
+        functools.partial(emit_tokens_kernel, layout),
         "emit_tokens",
         [
             (tokens.shape, BF),
-            (memory.shape, BF),
+            ((mem_rows, 2, WIDTH), BF),
             (tokens.shape, BF),
-            (memory.shape, BF),
+            ((mem_rows, 2, WIDTH), BF),
             ((2, WIDTH), F32),
         ],
         [],
         (lengths, out_own, grad_own, grad_got, tail),
     )
-    (qkv_send,) = call(turn_qkv_kernel, "turn_qkv", [((112, LANES), BF)], [], qkv_total, smem=0)
-    qkv_sum, *vec = call(
-        emit_qkv_kernel,
-        "emit_qkv",
-        [(w_qkv.shape, F32)] + [((16,), F32)] * 8 + [((64,), F32)],
+    all_other = swap(all_send, bits(PAIR_MAIN, 3))
+    order = (1, 0, 2)
+    all_other, out_memory, grad_memory, rms = lax.optimization_barrier(
+        (all_other, out_memory, grad_memory, rms)
+    )
+    out_memory, grad_memory = jnp.transpose(out_memory, order), jnp.transpose(grad_memory, order)
+    (turned,) = call(
+        turn_kernel, "turn", [((208, WIDTH // 2), BF)], [], (all_keep, all_other), smem=0
+    )
+    turned = layout.swap(turned, 0)
+    up_sum, down_sum, out_sum, qkv_sum, *vec = call(
+        emit_kernel_quad,
+        "emit_weights",
+        [(w_up.shape, F32), (w_down.shape, F32), (w_out.shape, F32), (w_qkv.shape, F32)]
+        + [((16,), F32)] * 8
+        + [((64,), F32)],
         [],
-        (*qkv_total, layout.swap(qkv_send, 0)),
-        smem=0,
-    )
-    up_sum, down_sum, out_sum = call(
-        emit_feed_kernel,
-        "emit_feed",
-        [(w_up.shape, F32), (w_down.shape, F32), (w_out.shape, F32)],
-        [],
-        (*feed_total, after(layout.swap(feed_send, 0), rms, qkv_sum)),
+        (all_keep, all_other, turned),
         smem=0,
     )
     return (

time: 127 us -> 113 us (0.89)
  waiting for transfers between devices: 57.6 us -> 46 us
  starting transfers between devices: 40 us -> 34.9 us
  Pallas kernels: 19.5 us -> 23.9 us
  local copies, waits for them, and re-layouts: 4.68 us -> 1.8 us
    ppermute x40 -> x27, waiting for transfers between devices: 57.6 us -> 26.4 us  [swap(): return lax.ppermute(x, axis, [(i, i ^ mask) for i in range(size)])]
    ppermute x0 -> x6, waiting for transfers between devices: none -> 19.6 us  [pair_swap_by_core(): return lax.ppermute(x, ('dp', 'seq'), pairs)]
    ppermute x40 -> x27, starting transfers between devices: 40 us -> 24.5 us  [swap(): return lax.ppermute(x, axis, [(i, i ^ mask) for i in range(size)])]
    ppermute x0 -> x6, starting transfers between devices: none -> 10.4 us  [pair_swap_by_core(): return lax.ppermute(x, ('dp', 'seq'), pairs)]
    pallas_call x9 -> x8, Pallas kernels: 17.9 us -> 22.1 us  [call(): pl.pallas_call(kernel, out_shape=[jax.ShapeDtypeStruct(shape, kind) for s...]
    squeeze x4 -> x1, local copies, waits for them, and re-layouts: 1.7 us -> 0.01 us  [pick(): return lax.dynamic_index_in_dim(x, at, 0, False)]
    optimization_barrier x2 -> x0, local copies, waits for them, and re-layouts: 1.57 us -> none  [after(): return lax.optimization_barrier((x, *others))[0]]
    concatenate x11 -> x12, other arithmetic: 2.93 us -> 3.93 us  [the longest x8 2.84 us: doubled(): return jnp.concatenate([held, layout.block_swap(held, bit)], 0)]
  transfers between devices with their start and end apart: 40 -> 33, of which waited for: 19 -> 15; matrix products, arithmetic and copies ran while one was open for 7% -> 5% of each run, Pallas kernels for 11% -> 17%
where the time goes in v3:
time: 113 us
  waiting for transfers between devices  46 us (41%)
  starting transfers between devices  34.9 us (31%)
  Pallas kernels  23.9 us (21%)
  other arithmetic  4.65 us (4%)
  local copies, waits for them, and re-layouts  1.8 us (2%)
  between operations  1.22 us (1%)
    ppermute x27, waiting for transfers between devices, swap(): return lax.ppermute(x, axis, [(i, i ^ mask) for i in range(size)])  26.4 us
    ppermute x27, starting transfers between devices, swap(): return lax.ppermute(x, axis, [(i, i ^ mask) for i in range(size)])  24.5 us
    pallas_call x8, Pallas kernels, call(): pl.pallas_call(kernel, out_shape=[jax.ShapeDtypeStruct(shape, kind) for s...  22.1 us
    ppermute x6, waiting for transfers between devices, pair_swap_by_core(): return lax.ppermute(x, ('dp', 'seq'), pairs)  19.6 us
    ppermute x6, starting transfers between devices, pair_swap_by_core(): return lax.ppermute(x, ('dp', 'seq'), pairs)  10.4 us
    concatenate x8, other arithmetic, doubled(): return jnp.concatenate([held, layout.block_swap(held, bit)], 0)  2.84 us
  transfers between devices with their start and end apart: 33, of which 15 were waited for; matrix products, arithmetic and copies ran while one was open for 5% of the time, Pallas kernels for 17%

profile of v3, /device:TPU:0, one launch (start us, length us, event | category | flops | bytes accessed | tf_op | source)
XLA Modules:
  0.0 112.5 jit_solution(4994823433173977051)
XLA Ops:
  0.7 4.1 %collective-permute-start.14 = (bf16[1,64,512]{2,1,0:T(8,128)(2,1)}, bf16[1,64,512]{2,1,0:T(8,128)(2,1)S(1)}, u32[]{:S(2)}, u32[]{:S(2)}) collective-permute-start(bf16[1,64,512]{2,1,0:T(8,128)(2,1)} %bitcast.19), channel_id=1, source_target_pairs={{0,4},{1,5},{2,6},{3,7},{4,0},{5,1},{6,2},{7,3},{8,12},{9,13},{10,... | collective-permute-start | bytes 196616 | tf_op jit(solution)/shard_map/ppermute | solution.py:79
  4.8 1.8 %prepare.1 = (bf16[16,4224]{1,0:T(8,128)(2,1)}, bf16[16,4224]{1,0:T(8,128)(2,1)}) custom-call(bf16[2,64,512]{2,1,0:T(8,128)(2,1)} %refs_1_.3, bf16[16,1536]{1,0:T(8,128)(2,1)} %refs_1_.2, bf16[16,512]{1,0:T(8,128)(2,1)} %refs_2_.1, bf16[16]{0:T(256)(128)(2,1)} %refs_3_.1, bf16[16]{0:T(256)(128)(2,1)} %refs_4_.2, bf16[16]{0:T(256)(128)(2,1)} %refs_5_.1, ...), custom_call_target="tpu_custom_call" | custom-call | tf_op jit(solution)/shard_map/prepare/pallas_call | solution.py:1391
  6.7 2.9 %collective-permute-start.8 = (bf16[1,16,2048]{2,1,0:T(8,128)(2,1)}, bf16[1,16,2048]{2,1,0:T(8,128)(2,1)S(1)}, u32[]{:S(2)}, u32[]{:S(2)}) collective-permute-start(bf16[1,16,2048]{2,1,0:T(8,128)(2,1)} %bitcast.23), channel_id=1, source_target_pairs={{0,4},{1,5},{2,6},{3,7},{4,0},{5,1},{6,2},{7,3},{8,12},{9,13},{10,... | collective-permute-start | bytes 196616 | tf_op jit(solution)/shard_map/ppermute | solution.py:79
  10.5 1.6 %collective-permute-start.15 = (bf16[2,64,512]{2,1,0:T(8,128)(2,1)S(1)}, bf16[2,64,512]{2,1,0:T(8,128)(2,1)S(1)}, u32[]{:S(2)}, u32[]{:S(2)}) collective-permute-start(bf16[2,64,512]{2,1,0:T(8,128)(2,1)S(1)} %pad_maximum_fusion.13), channel_id=1, source_target_pairs={{0,16},{8,24},{16,0},{24,8},{1,17},{9,25},{17,1},{25,9},{2,18},{10... | collective-permute-start | bytes 393224 | tf_op jit(solution)/shard_map/ppermute | solution.py:79
  12.0 5.8 %collective-permute-done = bf16[16,4224]{1,0:T(8,128)(2,1)S(1)} collective-permute-done((bf16[16,4224]{1,0:T(8,128)(2,1)}, bf16[16,4224]{1,0:T(8,128)(2,1)S(1)}, u32[]{:S(2)}, u32[]{:S(2)}) %collective-permute-start) | collective-permute-done | bytes 135200 | tf_op jit(solution)/shard_map/ppermute | solution.py:79
  19.8 1.6 %collective-permute-start.9 = (bf16[2,16,2048]{2,1,0:T(8,128)(2,1)S(1)}, bf16[2,16,2048]{2,1,0:T(8,128)(2,1)S(1)}, u32[]{:S(2)}, u32[]{:S(2)}) collective-permute-start(bf16[2,16,2048]{2,1,0:T(8,128)(2,1)S(1)} %pad_maximum_fusion.12), channel_id=1, source_target_pairs={{0,8},{8,0},{16,24},{24,16},{1,9},{9,1},{17,25},{25,17},{2,10},{10... | collective-permute-start | bytes 393224 | tf_op jit(solution)/shard_map/ppermute | solution.py:79
  22.8 2.7 %collective-permute-done.1 = bf16[2,16,4224]{2,1,0:T(8,128)(2,1)S(1)} collective-permute-done((bf16[2,16,4224]{2,1,0:T(8,128)(2,1)S(1)}, bf16[2,16,4224]{2,1,0:T(8,128)(2,1)S(1)}, u32[]{:S(2)}, u32[]{:S(2)}) %collective-permute-start.1) | collective-permute-done | bytes 270368 | tf_op jit(solution)/shard_map/ppermute | solution.py:79
  25.6 1.6 %collective-permute-start.2 = (bf16[4,16,2176]{2,1,0:T(8,128)(2,1)S(1)}, bf16[4,16,2176]{2,1,0:T(8,128)(2,1)S(1)}, u32[]{:S(2)}, u32[]{:S(2)}) collective-permute-start(bf16[4,16,2176]{2,1,0:T(8,128)(2,1)S(1)} %slice.119), channel_id=1, source_target_pairs={{0,16},{8,24},{16,0},{24,8},{1,17},{9,25},{17,1},{25,9},{2,18},{10... | collective-permute-start | bytes 835592 | tf_op jit(solution)/shard_map/ppermute | solution.py:79
  28.3 1.8 %collective-permute-done.16 = bf16[4,64,512]{2,1,0:T(8,128)(2,1)S(1)} collective-permute-done((bf16[4,64,512]{2,1,0:T(8,128)(2,1)S(1)}, bf16[4,64,512]{2,1,0:T(8,128)(2,1)S(1)}, u32[]{:S(2)}, u32[]{:S(2)}) %collective-permute-start.16) | collective-permute-done | bytes 262176 | tf_op jit(solution)/shard_map/ppermute | solution.py:79
  30.3 1.5 %collective-permute-start.17 = (bf16[8,64,512]{2,1,0:T(8,128)(2,1)S(1)}, bf16[8,64,512]{2,1,0:T(8,128)(2,1)}, u32[]{:S(2)}, u32[]{:S(2)}) collective-permute-start(bf16[8,64,512]{2,1,0:T(8,128)(2,1)S(1)} %pad_maximum_fusion.4.refs_18_), channel_id=1, source_target_pairs={{0,2},{1,3},{2,0},{3,1},{4,6},{5,7},{6,4},{7,5},{8,10},{9,11},{10,... | collective-permute-start | bytes 1572872 | tf_op jit(solution)/shard_map/ppermute | solution.py:79
  32.4 1.6 %collective-permute-start.5 = (bf16[8,16,2176]{2,1,0:T(8,128)(2,1)S(1)}, bf16[8,16,2176]{2,1,0:T(8,128)(2,1)S(1)}, u32[]{:S(2)}, u32[]{:S(2)}) collective-permute-start(bf16[8,16,2176]{2,1,0:T(8,128)(2,1)S(1)} %pad_maximum_fusion.1.refs_4_.refs_10_), channel_id=1, source_target_pairs={{0,8},{8,0},{16,24},{24,16},{1,9},{9,1},{17,25},{25,17},{2,10},{10... | collective-permute-start | bytes 1671176 | tf_op jit(solution)/shard_map/ppermute | solution.py:79
  34.0 2.2 %collective-permute-done.10 = bf16[4,16,2048]{2,1,0:T(8,128)(2,1)S(1)} collective-permute-done((bf16[4,16,2048]{2,1,0:T(8,128)(2,1)S(1)}, bf16[4,16,2048]{2,1,0:T(8,128)(2,1)S(1)}, u32[]{:S(2)}, u32[]{:S(2)}) %collective-permute-start.10) | collective-permute-done | bytes 262176 | tf_op jit(solution)/shard_map/ppermute | solution.py:79
  36.4 1.5 %collective-permute-start.3 = (bf16[64,512]{1,0:T(8,128)(2,1)S(1)}, bf16[64,512]{1,0:T(8,128)(2,1)S(1)}, u32[]{:S(2)}, u32[]{:S(2)}) collective-permute-start(bf16[64,512]{1,0:T(8,128)(2,1)S(1)} %dynamic-slice_bitcast_fusion), channel_id=1, source_target_pairs={{0,4},{1,5},{2,6},{3,7},{4,0},{5,1},{6,2},{7,3},{8,12},{9,13},{10,... | collective-permute-start | bytes 196616 | tf_op jit(solution)/shard_map/ppermute | solution.py:79
  38.6 6.2 %collective-permute-done.3.refs_5_ = bf16[64,512]{1,0:T(8,128)(2,1)S(1)} collective-permute-done((bf16[64,512]{1,0:T(8,128)(2,1)S(1)}, bf16[64,512]{1,0:T(8,128)(2,1)S(1)}, u32[]{:S(2)}, u32[]{:S(2)}) %collective-permute-start.3) | collective-permute-done | bytes 65568 | tf_op jit(solution)/shard_map/ppermute | solution.py:79
  44.9 2.6 %collective-permute-done.5.refs_5_.refs_11_ = bf16[8,16,2176]{2,1,0:T(8,128)(2,1)S(1)} collective-permute-done((bf16[8,16,2176]{2,1,0:T(8,128)(2,1)S(1)}, bf16[8,16,2176]{2,1,0:T(8,128)(2,1)S(1)}, u32[]{:S(2)}, u32[]{:S(2)}) %collective-permute-start.5) | collective-permute-done | bytes 557088 | tf_op jit(solution)/shard_map/ppermute | solution.py:79
  49.7 4.4 %attention_forward.1 = (f32[160,512]{1,0:T(8,128)S(1)}, bf16[640,768]{1,0:T(8,128)(2,1)S(1)}, bf16[544,512]{1,0:T(8,128)(2,1)S(1)}, bf16[512,768]{1,0:T(8,128)(2...) custom-call(s32[2]{0:T(128)S(1)} %copy-done.2, bf16[4,16,4224]{2,1,0:T(8,128)(2,1)S(1)} %pad_maximum_fusion.2.refs_1_, ...), custom_call_target="tpu_custom_call" | custom-call | flops 4000000000 | bytes 3063816 | tf_op jit(solution)/shard_map/attention_forward/pallas_call | solution.py:655
  54.1 4.0 %feed_forward.1 = (bf16[96,512]{1,0:T(8,128)(2,1)S(1)}, bf16[96,512]{1,0:T(8,128)(2,1)S(1)}, bf16[160,3328]{1,0:T(8,128)(2,1)S(1)}, bf16[160,3328]{1,0:T(8,128)(...) custom-call(s32[2]{0:T(128)S(1)} %copy-done.2, ...), custom_call_target="tpu_custom_call" | custom-call | flops 3000000000 | bytes 7290888 | tf_op jit(solution)/shard_map/feed_forward/pallas_call | solution.py:655
  58.5 1.9 %feed_backward.1 = (bf16[1,160,512]{2,1,0:T(8,128)(2,1)S(1)}, bf16[32,512]{1,0:T(8,128)(2,1)S(1)}, f32[160,512]{1,0:T(8,128)S(1)}, bf16[160,1280]{1,0:T(8,128)(2,1)S(1)}, bf16[160,1280]{1,0:T(8,128)(2,1)S(1)}) custom-call(f32[8,512]{1,0:T(8,128)S(1)} %get-tuple-element.87.refs_8_.refs_0_, f32[8,512]{1,0:T(8,128)S(1)} %get-tuple-element.94.refs_1_, ...), custom_call_target="tpu_custom_call" | custom-call | flops 3000000000 | bytes 6815744 | tf_op jit(solution)/shard_map/feed_backward/pallas_call | solution.py:655
  60.6 2.0 %collective-permute-start.20 = (bf16[1,160,512]{2,1,0:T(8,128)(2,1)S(1)}, bf16[1,160,512]{2,1,0:T(8,128)(2,1)S(1)}, u32[]{:S(2)}, u32[]{:S(2)}) collective-permute-start(bf16[1,160,512]{2,1,0:T(8,128)(2,1)S(1)} %get-tuple-element.103), channel_id=1, source_target_pairs={{0,2},{1,3},{2,0},{3,1},{4,6},{5,7},{6,4},{7,5},{8,10},{9,11},{10,... | collective-permute-start | bytes 491528 | tf_op jit(solution)/shard_map/ppermute | solution.py:79
  62.6 1.5 %weight_gradients.1 = (bf16[8,176,256]{2,1,0:T(8,128)(2,1)S(1)}, bf16[8,176,256]{2,1,0:T(8,128)(2,1)S(1)}, bf16[8,112,256]{2,1,0:T(8,128)(2,1)S(1)}, bf16[8,112,256]{2,1,0:T(8,128)(2,1)S(1)}) custom-call(bf16[160,3328]{1,0:T(8,128)(2,1)S(1)} %get-tuple-element.104.refs_0_, bf16[160,3328]{1,0:T(8,128)(2,1)S(1)} %collective-permute-done.21.refs_1_, ...), custom_call_target="tpu_custom_call" | custom-call | flops 1000000000 | bytes 2949120 | tf_op jit(solution)/shard_map/weight_gradients/pallas_call | solution.py:655
  64.2 1.4 %collective-permute-start.27 = (bf16[8,112,256]{2,1,0:T(8,128)(2,1)S(1)}, bf16[8,112,256]{2,1,0:T(8,128)(2,1)S(1)}, u32[]{:S(2)}, u32[]{:S(2)}) collective-permute-start(bf16[8,112,256]{2,1,0:T(8,128)(2,1)S(1)} %get-tuple-element.119), channel_id=1, source_target_pairs={{0,2},{1,3},{2,0},{3,1},{4,6},{5,7},{6,4},{7,5},{8,10},{9,11},{10,... | collective-permute-start | bytes 1376264 | tf_op jit(solution)/shard_map/ppermute | solution.py:89
  65.6 1.5 %collective-permute-start.26 = (bf16[8,176,256]{2,1,0:T(8,128)(2,1)S(1)}, bf16[8,176,256]{2,1,0:T(8,128)(2,1)S(1)}, u32[]{:S(2)}, u32[]{:S(2)}) collective-permute-start(bf16[8,176,256]{2,1,0:T(8,128)(2,1)S(1)} %get-tuple-element.109), channel_id=1, source_target_pairs={{0,8},{1,17},{2,10},{3,19},{4,12},{5,21},{6,14},{7,23},{8,0},{9,25... | collective-permute-start | bytes 2162696 | tf_op jit(solution)/shard_map/ppermute | solution.py:89
  67.4 1.6 %collective-permute-done.23.refs_6_ = bf16[2,160,512]{2,1,0:T(8,128)(2,1)S(1)} collective-permute-done((bf16[2,160,512]{2,1,0:T(8,128)(2,1)S(1)}, bf16[2,160,512]{2,1,0:T(8,128)(2,1)S(1)}, u32[]{:S(2)}, u32[]{:S(2)}) %collective-permute-start.23) | collective-permute-done | bytes 327712 | tf_op jit(solution)/shard_map/ppermute | solution.py:79
  69.0 8.2 %attention_backward.1 = (bf16[4,112,256]{2,1,0:T(8,128)(2,1)S(1)}, bf16[4,112,256]{2,1,0:T(8,128)(2,1)S(1)}, bf16[160,512]{1,0:T(8,128)(2,1)S(1)}, bf16[160,512]{1,0:T(8,128)(2,1)S(1)}, bf16[16,512]{1,0:T(8,128)(2,1)S(1)}) custom-call(s32[2]{0:T(128)S(1)} %copy-done.2, bf16[640,768]{1,0:T(8,128)(2,1)S(1)} %get-tuple-element.90.refs_1_, ...), custom_call_target="tpu_custom_call" | custom-call | bytes 3276808 | tf_op jit(solution)/shard_map/attention_backward/pallas_call | solution.py:655
  77.6 1.8 %collective-permute-start.28 = (bf16[4,400,256]{2,1,0:T(8,128)(2,1)S(1)}, bf16[4,400,256]{2,1,0:T(8,128)(2,1)S(1)}, u32[]{:S(2)}, u32[]{:S(2)}) collective-permute-start(bf16[4,400,256]{2,1,0:T(8,128)(2,1)S(1)} %pad_maximum_fusion), channel_id=1, source_target_pairs={{0,16},{1,9},{2,18},{3,11},{4,20},{5,13},{6,22},{7,15},{8,24},{9,1... | collective-permute-start | bytes 2457608 | tf_op jit(solution)/shard_map/ppermute | solution.py:89
  81.0 2.3 %collective-permute-start.25 = (bf16[208,512]{1,0:T(8,128)(2,1)S(1)}, bf16[208,512]{1,0:T(8,128)(2,1)S(1)}, u32[]{:S(2)}, u32[]{:S(2)}) collective-permute-start(bf16[208,512]{1,0:T(8,128)(2,1)S(1)} %pad_maximum_fusion.9), channel_id=1, source_target_pairs={{0,4},{1,5},{2,6},{3,7},{4,0},{5,1},{6,2},{7,3},{8,12},{9,13},{10,... | collective-permute-start | bytes 638984 | tf_op jit(solution)/shard_map/ppermute | solution.py:79
  83.2 6.8 %collective-permute-done.28 = bf16[4,400,256]{2,1,0:T(8,128)(2,1)S(1)} collective-permute-done((bf16[4,400,256]{2,1,0:T(8,128)(2,1)S(1)}, bf16[4,400,256]{2,1,0:T(8,128)(2,1)S(1)}, u32[]{:S(2)}, u32[]{:S(2)}) %collective-permute-start.28) | collective-permute-done | bytes 819232 | tf_op jit(solution)/shard_map/ppermute | solution.py:89
  90.1 1.8 %collective-permute-start.29 = (bf16[2,176,256]{2,1,0:T(8,128)(2,1)S(1)}, bf16[2,176,256]{2,1,0:T(8,128)(2,1)S(1)}, u32[]{:S(2)}, u32[]{:S(2)}) collective-permute-start(bf16[2,176,256]{2,1,0:T(8,128)(2,1)S(1)} %get-tuple-element.151), channel_id=1, source_target_pairs={{0,2},{1,3},{2,0},{3,1},{4,6},{5,7},{6,4},{7,5},{8,10},{9,11},{10,... | collective-permute-start | bytes 540680 | tf_op jit(solution)/shard_map/ppermute | solution.py:89
  92.0 1.5 %collective-permute-start.30 = (bf16[2,224,256]{2,1,0:T(8,128)(2,1)S(1)}, bf16[2,224,256]{2,1,0:T(8,128)(2,1)S(1)}, u32[]{:S(2)}, u32[]{:S(2)}) collective-permute-start(bf16[2,224,256]{2,1,0:T(8,128)(2,1)S(1)} %get-tuple-element.149), channel_id=1, source_target_pairs={{0,8},{1,17},{2,10},{3,19},{4,12},{5,21},{6,14},{7,23},{8,0},{9,25... | collective-permute-start | bytes 688136 | tf_op jit(solution)/shard_map/ppermute | solution.py:89
  93.6 4.1 %collective-permute-done.29 = bf16[2,176,256]{2,1,0:T(8,128)(2,1)S(1)} collective-permute-done((bf16[2,176,256]{2,1,0:T(8,128)(2,1)S(1)}, bf16[2,176,256]{2,1,0:T(8,128)(2,1)S(1)}, u32[]{:S(2)}, u32[]{:S(2)}) %collective-permute-start.29) | collective-permute-done | bytes 180256 | tf_op jit(solution)/shard_map/ppermute | solution.py:89
  98.2 2.3 %collective-permute-start.31 = (bf16[1,400,256]{2,1,0:T(8,128)(2,1)S(1)}, bf16[1,400,256]{2,1,0:T(8,128)(2,1)S(1)}, u32[]{:S(2)}, u32[]{:S(2)}) collective-permute-start(bf16[1,400,256]{2,1,0:T(8,128)(2,1)S(1)} %pad_maximum_fusion.10), channel_id=1, source_target_pairs={{0,4},{1,5},{2,6},{3,7},{4,0},{5,1},{6,2},{7,3},{8,12},{9,13},{10,... | collective-permute-start | bytes 614408 | tf_op jit(solution)/shard_map/ppermute | solution.py:89
  101.9 8.3 %collective-permute-done.31.other = bf16[1,400,256]{2,1,0:T(8,128)(2,1)S(1)} collective-permute-done((bf16[1,400,256]{2,1,0:T(8,128)(2,1)S(1)}, bf16[1,400,256]{2,1,0:T(8,128)(2,1)S(1)}, u32[]{:S(2)}, u32[]{:S(2)}) %collective-permute-start.31) | collective-permute-done | bytes 204832 | tf_op jit(solution)/shard_map/ppermute | solution.py:89
  (93 shorter events, 16.4 us)
Async XLA Ops:
  0.7 8.9 %collective-permute-start.14 = (bf16[1,64,512]{2,1,0:T(8,128)(2,1)}, bf16[1,64,512]{2,1,0:T(8,128)(2,1)S(1)}, u32[]{:S(2)}, u32[]{:S(2)}) collective-permute-start(bf16[1,64,512]{2,1,0:T(8,128)(2,1)} %bitcast.19), channel_id=1, source_target_pairs={{0,4},{1,5},{2,6},{3,7},{4,0},{5,1},{6,2},{7,3},{8,12},{9,13},{10,... | collective-permute-start | bytes 196616 | tf_op jit(solution)/shard_map/ppermute | solution.py:79
  6.6 11.2 %collective-permute-start = (bf16[16,4224]{1,0:T(8,128)(2,1)}, bf16[16,4224]{1,0:T(8,128)(2,1)S(1)}, u32[]{:S(2)}, u32[]{:S(2)}) collective-permute-start(bf16[16,4224]{1,0:T(8,128)(2,1)} %get-tuple-element.82), channel_id=1, source_target_pairs={{0,4},{1,5},{2,6},{3,7},{4,0},{5,1},{6,2},{7,3},{8,12},{9,13},{10,... | collective-permute-start | bytes 405512 | tf_op jit(solution)/shard_map/ppermute | solution.py:79
  6.7 12.2 %collective-permute-start.8 = (bf16[1,16,2048]{2,1,0:T(8,128)(2,1)}, bf16[1,16,2048]{2,1,0:T(8,128)(2,1)S(1)}, u32[]{:S(2)}, u32[]{:S(2)}) collective-permute-start(bf16[1,16,2048]{2,1,0:T(8,128)(2,1)} %bitcast.23), channel_id=1, source_target_pairs={{0,4},{1,5},{2,6},{3,7},{4,0},{5,1},{6,2},{7,3},{8,12},{9,13},{10,... | collective-permute-start | bytes 196616 | tf_op jit(solution)/shard_map/ppermute | solution.py:79
  10.5 10.9 %collective-permute-start.15 = (bf16[2,64,512]{2,1,0:T(8,128)(2,1)S(1)}, bf16[2,64,512]{2,1,0:T(8,128)(2,1)S(1)}, u32[]{:S(2)}, u32[]{:S(2)}) collective-permute-start(bf16[2,64,512]{2,1,0:T(8,128)(2,1)S(1)} %pad_maximum_fusion.13), channel_id=1, source_target_pairs={{0,16},{8,24},{16,0},{24,8},{1,17},{9,25},{17,1},{25,9},{2,18},{10... | collective-permute-start | bytes 393224 | tf_op jit(solution)/shard_map/ppermute | solution.py:79
  18.8 6.7 %collective-permute-start.1 = (bf16[2,16,4224]{2,1,0:T(8,128)(2,1)S(1)}, bf16[2,16,4224]{2,1,0:T(8,128)(2,1)S(1)}, u32[]{:S(2)}, u32[]{:S(2)}) collective-permute-start(bf16[2,16,4224]{2,1,0:T(8,128)(2,1)S(1)} %pad_maximum_fusion.5), channel_id=1, source_target_pairs={{0,2},{1,3},{2,0},{3,1},{4,6},{5,7},{6,4},{7,5},{8,10},{9,11},{10,... | collective-permute-start | bytes 811016 | tf_op jit(solution)/shard_map/ppermute | solution.py:79
  19.8 7.4 %collective-permute-start.9 = (bf16[2,16,2048]{2,1,0:T(8,128)(2,1)S(1)}, bf16[2,16,2048]{2,1,0:T(8,128)(2,1)S(1)}, u32[]{:S(2)}, u32[]{:S(2)}) collective-permute-start(bf16[2,16,2048]{2,1,0:T(8,128)(2,1)S(1)} %pad_maximum_fusion.12), channel_id=1, source_target_pairs={{0,8},{8,0},{16,24},{24,16},{1,9},{9,1},{17,25},{25,17},{2,10},{10... | collective-permute-start | bytes 393224 | tf_op jit(solution)/shard_map/ppermute | solution.py:79
  22.2 7.9 %collective-permute-start.16 = (bf16[4,64,512]{2,1,0:T(8,128)(2,1)S(1)}, bf16[4,64,512]{2,1,0:T(8,128)(2,1)S(1)}, u32[]{:S(2)}, u32[]{:S(2)}) collective-permute-start(bf16[4,64,512]{2,1,0:T(8,128)(2,1)S(1)} %pad_maximum_fusion.7), channel_id=1, source_target_pairs={{0,8},{8,0},{16,24},{24,16},{1,9},{9,1},{17,25},{25,17},{2,10},{10... | collective-permute-start | bytes 786440 | tf_op jit(solution)/shard_map/ppermute | solution.py:79
  25.6 6.6 %collective-permute-start.2 = (bf16[4,16,2176]{2,1,0:T(8,128)(2,1)S(1)}, bf16[4,16,2176]{2,1,0:T(8,128)(2,1)S(1)}, u32[]{:S(2)}, u32[]{:S(2)}) collective-permute-start(bf16[4,16,2176]{2,1,0:T(8,128)(2,1)S(1)} %slice.119), channel_id=1, source_target_pairs={{0,16},{8,24},{16,0},{24,8},{1,17},{9,25},{17,1},{25,9},{2,18},{10... | collective-permute-start | bytes 835592 | tf_op jit(solution)/shard_map/ppermute | solution.py:79
  27.3 8.9 %collective-permute-start.10 = (bf16[4,16,2048]{2,1,0:T(8,128)(2,1)S(1)}, bf16[4,16,2048]{2,1,0:T(8,128)(2,1)S(1)}, u32[]{:S(2)}, u32[]{:S(2)}) collective-permute-start(bf16[4,16,2048]{2,1,0:T(8,128)(2,1)S(1)} %pad_maximum_fusion.6), channel_id=1, source_target_pairs={{0,2},{1,3},{2,0},{3,1},{4,6},{5,7},{6,4},{7,5},{8,10},{9,11},{10,... | collective-permute-start | bytes 786440 | tf_op jit(solution)/shard_map/ppermute | solution.py:79
  30.3 17.4 %collective-permute-start.17 = (bf16[8,64,512]{2,1,0:T(8,128)(2,1)S(1)}, bf16[8,64,512]{2,1,0:T(8,128)(2,1)}, u32[]{:S(2)}, u32[]{:S(2)}) collective-permute-start(bf16[8,64,512]{2,1,0:T(8,128)(2,1)S(1)} %pad_maximum_fusion.4.refs_18_), channel_id=1, source_target_pairs={{0,2},{1,3},{2,0},{3,1},{4,6},{5,7},{6,4},{7,5},{8,10},{9,11},{10,... | collective-permute-start | bytes 1572872 | tf_op jit(solution)/shard_map/ppermute | solution.py:79
  32.3 16.4 %collective-permute-start.6 = (bf16[8,16,2176]{2,1,0:T(8,128)(2,1)S(1)}, bf16[8,16,2176]{2,1,0:T(8,128)(2,1)S(1)}, u32[]{:S(2)}, u32[]{:S(2)}) collective-permute-start(bf16[8,16,2176]{2,1,0:T(8,128)(2,1)S(1)} %pad_maximum_fusion.1.refs_4_.refs_10_), channel_id=1, source_target_pairs={{0,1},{1,0},{2,3},{3,2},{4,5},{5,4},{6,7},{7,6},{8,9},{9,8},{10,11... | collective-permute-start | bytes 1671176 | tf_op jit(solution)/shard_map/ppermute | solution.py:79
  32.4 15.0 %collective-permute-start.5 = (bf16[8,16,2176]{2,1,0:T(8,128)(2,1)S(1)}, bf16[8,16,2176]{2,1,0:T(8,128)(2,1)S(1)}, u32[]{:S(2)}, u32[]{:S(2)}) collective-permute-start(bf16[8,16,2176]{2,1,0:T(8,128)(2,1)S(1)} %pad_maximum_fusion.1.refs_4_.refs_10_), channel_id=1, source_target_pairs={{0,8},{8,0},{16,24},{24,16},{1,9},{9,1},{17,25},{25,17},{2,10},{10... | collective-permute-start | bytes 1671176 | tf_op jit(solution)/shard_map/ppermute | solution.py:79
  36.2 12.0 %collective-permute-start.11 = (bf16[8,16,2048]{2,1,0:T(8,128)(2,1)S(1)}, bf16[8,16,2048]{2,1,0:T(8,128)(2,1)}, u32[]{:S(2)}, u32[]{:S(2)}) collective-permute-start(bf16[8,16,2048]{2,1,0:T(8,128)(2,1)S(1)} %pad_maximum_fusion.3.refs_14_), channel_id=1, source_target_pairs={{0,16},{8,24},{16,0},{24,8},{1,17},{9,25},{17,1},{25,9},{2,18},{10... | collective-permute-start | bytes 1572872 | tf_op jit(solution)/shard_map/ppermute | solution.py:79
  36.4 8.5 %collective-permute-start.3 = (bf16[64,512]{1,0:T(8,128)(2,1)S(1)}, bf16[64,512]{1,0:T(8,128)(2,1)S(1)}, u32[]{:S(2)}, u32[]{:S(2)}) collective-permute-start(bf16[64,512]{1,0:T(8,128)(2,1)S(1)} %dynamic-slice_bitcast_fusion), channel_id=1, source_target_pairs={{0,4},{1,5},{2,6},{3,7},{4,0},{5,1},{6,2},{7,3},{8,12},{9,13},{10,... | collective-permute-start | bytes 196616 | tf_op jit(solution)/shard_map/ppermute | solution.py:79
  44.8 3.4 %collective-permute-start.4 = (bf16[4,16,2048]{2,1,0:T(8,128)(2,1)}, bf16[4,16,2048]{2,1,0:T(8,128)(2,1)}, u32[]{:S(2)}, u32[]{:S(2)}) collective-permute-start(bf16[4,16,2048]{2,1,0:T(8,128)(2,1)} %slice.120), channel_id=1, source_target_pairs={{0,1},{1,0},{2,3},{3,2},{4,5},{5,4},{6,7},{7,6},{8,9},{9,8},{10,11... | collective-permute-start | bytes 786440 | tf_op jit(solution)/shard_map/ppermute | solution.py:79
  47.4 2.2 %collective-permute-start.7 = (bf16[8,16,2176]{2,1,0:T(8,128)(2,1)S(1)}, bf16[8,16,2176]{2,1,0:T(8,128)(2,1)S(1)}, u32[]{:S(2)}, u32[]{:S(2)}) collective-permute-start(bf16[8,16,2176]{2,1,0:T(8,128)(2,1)S(1)} %collective-permute-done.5.refs_5_.refs_11_), channel_id=1, source_target_pairs={{0,1},{1,0},{2,3},{3,2},{4,5},{5,4},{6,7},{7,6},{8,9},{9,8},{10,11... | collective-permute-start | bytes 1671176 | tf_op jit(solution)/shard_map/ppermute | solution.py:79
  47.6 6.4 %collective-permute-start.18 = (bf16[8,64,512]{2,1,0:T(8,128)(2,1)S(1)}, bf16[8,64,512]{2,1,0:T(8,128)(2,1)S(1)}, u32[]{:S(2)}, u32[]{:S(2)}) collective-permute-start(bf16[8,64,512]{2,1,0:T(8,128)(2,1)S(1)} %pad_maximum_fusion.4.refs_18_), channel_id=1, source_target_pairs={{0,1},{1,0},{2,3},{3,2},{4,5},{5,4},{6,7},{7,6},{8,9},{9,8},{10,11... | collective-permute-start | bytes 1572872 | tf_op jit(solution)/shard_map/ppermute | solution.py:79
  48.2 5.8 %collective-permute-start.12 = (bf16[8,16,2048]{2,1,0:T(8,128)(2,1)S(1)}, bf16[8,16,2048]{2,1,0:T(8,128)(2,1)S(1)}, u32[]{:S(2)}, u32[]{:S(2)}) collective-permute-start(bf16[8,16,2048]{2,1,0:T(8,128)(2,1)S(1)} %pad_maximum_fusion.3.refs_14_), channel_id=1, source_target_pairs={{0,1},{1,0},{2,3},{3,2},{4,5},{5,4},{6,7},{7,6},{8,9},{9,8},{10,11... | collective-permute-start | bytes 1572872 | tf_op jit(solution)/shard_map/ppermute | solution.py:79
  48.3 5.8 %collective-permute-start.19 = (bf16[8,64,512]{2,1,0:T(8,128)(2,1)}, bf16[8,64,512]{2,1,0:T(8,128)(2,1)S(1)}, u32[]{:S(2)}, u32[]{:S(2)}) collective-permute-start(bf16[8,64,512]{2,1,0:T(8,128)(2,1)} %collective-permute-done.17.refs_19_), channel_id=1, source_target_pairs={{0,1},{1,0},{2,3},{3,2},{4,5},{5,4},{6,7},{7,6},{8,9},{9,8},{10,11... | collective-permute-start | bytes 1572872 | tf_op jit(solution)/shard_map/ppermute | solution.py:79
  48.7 5.3 %collective-permute-start.13 = (bf16[8,16,2048]{2,1,0:T(8,128)(2,1)}, bf16[8,16,2048]{2,1,0:T(8,128)(2,1)S(1)}, u32[]{:S(2)}, u32[]{:S(2)}) collective-permute-start(bf16[8,16,2048]{2,1,0:T(8,128)(2,1)} %collective-permute-done.11.refs_15_), channel_id=1, source_target_pairs={{0,1},{1,0},{2,3},{3,2},{4,5},{5,4},{6,7},{7,6},{8,9},{9,8},{10,11... | collective-permute-start | bytes 1572872 | tf_op jit(solution)/shard_map/ppermute | solution.py:79
  58.1 4.6 %collective-permute-start.21 = (bf16[160,3328]{1,0:T(8,128)(2,1)S(1)}, bf16[160,3328]{1,0:T(8,128)(2,1)S(1)}, u32[]{:S(2)}, u32[]{:S(2)}) collective-permute-start(bf16[160,3328]{1,0:T(8,128)(2,1)S(1)} %get-tuple-element.105), channel_id=1, source_target_pairs={{0,1},{1,0},{2,3},{3,2},{4,5},{5,4},{6,7},{7,6},{8,9},{9,8},{10,11... | collective-permute-start | bytes 3194888 | tf_op jit(solution)/shard_map/ppermute | solution.py:79
  60.4 2.2 %collective-permute-start.22 = (bf16[160,1280]{1,0:T(8,128)(2,1)S(1)}, bf16[160,1280]{1,0:T(8,128)(2,1)S(1)}, u32[]{:S(2)}, u32[]{:S(2)}) collective-permute-start(bf16[160,1280]{1,0:T(8,128)(2,1)S(1)} %get-tuple-element.108), channel_id=1, source_target_pairs={{0,1},{1,0},{2,3},{3,2},{4,5},{5,4},{6,7},{7,6},{8,9},{9,8},{10,11... | collective-permute-start | bytes 1228808 | tf_op jit(solution)/shard_map/ppermute | solution.py:79
  60.6 6.7 %collective-permute-start.20 = (bf16[1,160,512]{2,1,0:T(8,128)(2,1)S(1)}, bf16[1,160,512]{2,1,0:T(8,128)(2,1)S(1)}, u32[]{:S(2)}, u32[]{:S(2)}) collective-permute-start(bf16[1,160,512]{2,1,0:T(8,128)(2,1)S(1)} %get-tuple-element.103), channel_id=1, source_target_pairs={{0,2},{1,3},{2,0},{3,1},{4,6},{5,7},{6,4},{7,5},{8,10},{9,11},{10,... | collective-permute-start | bytes 491528 | tf_op jit(solution)/shard_map/ppermute | solution.py:79
  64.2 13.0 %collective-permute-start.27 = (bf16[8,112,256]{2,1,0:T(8,128)(2,1)S(1)}, bf16[8,112,256]{2,1,0:T(8,128)(2,1)S(1)}, u32[]{:S(2)}, u32[]{:S(2)}) collective-permute-start(bf16[8,112,256]{2,1,0:T(8,128)(2,1)S(1)} %get-tuple-element.119), channel_id=1, source_target_pairs={{0,2},{1,3},{2,0},{3,1},{4,6},{5,7},{6,4},{7,5},{8,10},{9,11},{10,... | collective-permute-start | bytes 1376264 | tf_op jit(solution)/shard_map/ppermute | solution.py:89
  65.6 11.7 %collective-permute-start.26 = (bf16[8,176,256]{2,1,0:T(8,128)(2,1)S(1)}, bf16[8,176,256]{2,1,0:T(8,128)(2,1)S(1)}, u32[]{:S(2)}, u32[]{:S(2)}) collective-permute-start(bf16[8,176,256]{2,1,0:T(8,128)(2,1)S(1)} %get-tuple-element.109), channel_id=1, source_target_pairs={{0,8},{1,17},{2,10},{3,19},{4,12},{5,21},{6,14},{7,23},{8,0},{9,25... | collective-permute-start | bytes 2162696 | tf_op jit(solution)/shard_map/ppermute | solution.py:89
  67.3 1.7 %collective-permute-start.23 = (bf16[2,160,512]{2,1,0:T(8,128)(2,1)S(1)}, bf16[2,160,512]{2,1,0:T(8,128)(2,1)S(1)}, u32[]{:S(2)}, u32[]{:S(2)}) collective-permute-start(bf16[2,160,512]{2,1,0:T(8,128)(2,1)S(1)} %constant_dynamic-update-slice_fusion.refs_5_), channel_id=1, source_target_pairs={{0,1},{1,0},{2,3},{3,2},{4,5},{5,4},{6,7},{7,6},{8,9},{9,8},{10,11... | collective-permute-start | bytes 983048 | tf_op jit(solution)/shard_map/ppermute | solution.py:79
  77.6 12.4 %collective-permute-start.28 = (bf16[4,400,256]{2,1,0:T(8,128)(2,1)S(1)}, bf16[4,400,256]{2,1,0:T(8,128)(2,1)S(1)}, u32[]{:S(2)}, u32[]{:S(2)}) collective-permute-start(bf16[4,400,256]{2,1,0:T(8,128)(2,1)S(1)} %pad_maximum_fusion), channel_id=1, source_target_pairs={{0,16},{1,9},{2,18},{3,11},{4,20},{5,13},{6,22},{7,15},{8,24},{9,1... | collective-permute-start | bytes 2457608 | tf_op jit(solution)/shard_map/ppermute | solution.py:89
  79.5 1.4 %collective-permute-start.24 = (bf16[160,512]{1,0:T(8,128)(2,1)S(1)}, bf16[160,512]{1,0:T(8,128)(2,1)S(1)}, u32[]{:S(2)}, u32[]{:S(2)}) collective-permute-start(bf16[160,512]{1,0:T(8,128)(2,1)S(1)} %get-tuple-element.113), channel_id=1, source_target_pairs={{0,1},{1,0},{2,3},{3,2},{4,5},{5,4},{6,7},{7,6},{8,9},{9,8},{10,11... | collective-permute-start | bytes 491528 | tf_op jit(solution)/shard_map/ppermute | solution.py:79
  81.0 19.5 %collective-permute-start.25 = (bf16[208,512]{1,0:T(8,128)(2,1)S(1)}, bf16[208,512]{1,0:T(8,128)(2,1)S(1)}, u32[]{:S(2)}, u32[]{:S(2)}) collective-permute-start(bf16[208,512]{1,0:T(8,128)(2,1)S(1)} %pad_maximum_fusion.9), channel_id=1, source_target_pairs={{0,4},{1,5},{2,6},{3,7},{4,0},{5,1},{6,2},{7,3},{8,12},{9,13},{10,... | collective-permute-start | bytes 638984 | tf_op jit(solution)/shard_map/ppermute | solution.py:79
  90.1 7.5 %collective-permute-start.29 = (bf16[2,176,256]{2,1,0:T(8,128)(2,1)S(1)}, bf16[2,176,256]{2,1,0:T(8,128)(2,1)S(1)}, u32[]{:S(2)}, u32[]{:S(2)}) collective-permute-start(bf16[2,176,256]{2,1,0:T(8,128)(2,1)S(1)} %get-tuple-element.151), channel_id=1, source_target_pairs={{0,2},{1,3},{2,0},{3,1},{4,6},{5,7},{6,4},{7,5},{8,10},{9,11},{10,... | collective-permute-start | bytes 540680 | tf_op jit(solution)/shard_map/ppermute | solution.py:89
  92.0 6.1 %collective-permute-start.30 = (bf16[2,224,256]{2,1,0:T(8,128)(2,1)S(1)}, bf16[2,224,256]{2,1,0:T(8,128)(2,1)S(1)}, u32[]{:S(2)}, u32[]{:S(2)}) collective-permute-start(bf16[2,224,256]{2,1,0:T(8,128)(2,1)S(1)} %get-tuple-element.149), channel_id=1, source_target_pairs={{0,8},{1,17},{2,10},{3,19},{4,12},{5,21},{6,14},{7,23},{8,0},{9,25... | collective-permute-start | bytes 688136 | tf_op jit(solution)/shard_map/ppermute | solution.py:89
  98.2 12.0 %collective-permute-start.31 = (bf16[1,400,256]{2,1,0:T(8,128)(2,1)S(1)}, bf16[1,400,256]{2,1,0:T(8,128)(2,1)S(1)}, u32[]{:S(2)}, u32[]{:S(2)}) collective-permute-start(bf16[1,400,256]{2,1,0:T(8,128)(2,1)S(1)} %pad_maximum_fusion.10), channel_id=1, source_target_pairs={{0,4},{1,5},{2,6},{3,7},{4,0},{5,1},{6,2},{7,3},{8,12},{9,13},{10,... | collective-permute-start | bytes 614408 | tf_op jit(solution)/shard_map/ppermute | solution.py:89
  (10 other events, 128.4 us)

commit v4 on v3

--- a/solution.py
+++ b/solution.py
@@ -964,11 +964,11 @@
     parts = (w0, w1, w2, w3)
     place_blocks(weight, parts, GATHER_QKV, block, 16, slice(0, 3 * WIDTH))
     place_blocks(extra, parts, GATHER_QKV, block, 16, slice(4 * WIDTH, FIRST))
-    for part, start, masks in zip((near, far), (FIRST, 0), layout.group_masks()):
+    for part, masks in zip((near, far), layout.group_masks()):
         for k, mask in enumerate(masks):
             for part_half in range(2):
                 at = aligned((rank ^ mask) * 2 + part_half, 64)
-                rows[at, :] = stacked_rows(part[2 * k + part_half, :, start:])
+                rows[at, :] = stacked_rows(part[2 * k + part_half])
     rows[slot_len : slot_len + MEM_PAD, :] = memory[...]
     vector_rows, up_rows = gather_vectors(extra)
     vectors[...] = vector_rows
@@ -1003,6 +1003,7 @@
         attn[:, at : at + LANES] = join_heads(dot(low(expos), values) / total)
 
 
+STRIP = 32
 PACK = 32
 
 ACT_LANES = FF + 2 * WIDTH + WIDTH // 2
@@ -1027,7 +1028,8 @@
     attn, vectors, up_bias = refs[7:10]
     outs, ups, downs = refs[10:14], refs[14:18], refs[18:22]
     out_own, out_send, own, give, sums, squares_out, w_heads = refs[22:29]
-    w_out, w_up, w_down, slope, second_out, normed_out, inverse_out = refs[29:]
+    w_out, w_up, w_down, slope, second_out, normed_out, inverse_out = refs[29:36]
+    inputs, cot, feed, linear = refs[36:]
     group = layout.group
     place = lax.axis_index("seq")
     slot, rank = place // group, place % group
@@ -1042,98 +1044,137 @@
     out_bias, gain_one, shift_one, down_bias, gain_two, shift_two = [
         vec[k : k + 1] for k in range(2, 8)
     ]
-    got = high(stacked_rows(arrived[...]))
-    rows = jnp.concatenate([high(tokens[slot]), got, high(memory[...])], 0)
-    cot = jnp.concatenate([high(cots[slot]), high(cot_arrived[...]), high(cot_memory[...])], 0)
-    valid = jnp.where(own_valid((OWN, 1), slot, group, rank, length, mem_rows), 1.0, 0.0)
-    weight = row_weights(group)
-
-    def total(v):
-        return jnp.sum(v * weight, axis=0, keepdims=True)
+    inputs[:64, :] = high(tokens[slot])
+    inputs[64:ROWS, :] = high(stacked_rows(arrived[...]))
+    inputs[ROWS:, :] = high(memory[...])
+    cot[:64, :] = high(cots[slot])
+    cot[64:ROWS, :] = high(cot_arrived[...])
+    cot[ROWS:, :] = high(cot_memory[...])
+    valid_all = jnp.where(own_valid((OWN, 1), slot, group, rank, length, mem_rows), 1.0, 0.0)
+    weight_all = row_weights(group)
+    strips = [slice(start, start + STRIP) for start in range(0, OWN, STRIP)]
 
     heads_out = low(attn[...])
-    branch = dot(heads_out, w_out[...]) + out_bias
-    normed_one, inverse_one = normalize(rows + branch)
-    normed_out[...] = normed_one
-    inverse_out[...] = jnp.broadcast_to(inverse_one, (OWN, LANES))
-    hidden_one = normed_one * gain_one + shift_one
-    hidden_low = low(hidden_one)
     for target in (own, give):
-        target[:, FF : FF + WIDTH] = hidden_low
         target[:, FF + WIDTH : FF + 2 * WIDTH] = heads_out
-    feed = jnp.zeros((OWN, WIDTH), F32) + down_bias
+    feed[...] = dot(heads_out, w_out[...])
+    for strip in strips:
+        normed, inverse = normalize(inputs[strip, :] + (feed[strip, :] + out_bias))
+        normed_out[strip, :] = normed
+        inverse_out[strip, :] = jnp.broadcast_to(inverse, (STRIP, LANES))
+        hidden = normed * gain_one + shift_one
+        inputs[strip, :] = hidden
+        hidden_low = low(hidden)
+        own[strip, FF : FF + WIDTH] = hidden_low
+        give[strip, FF : FF + WIDTH] = hidden_low
     for at in range(0, FF, WIDTH):
         cols = slice(at, at + WIDTH)
-        t = dot(hidden_low, w_up[:, cols]) + up_bias[0:1, cols]
-        square = t * t
-        bent = jnp.tanh(0.7978845608 * (t + 0.044715 * (square * t)))
-        half = 0.5 * (1.0 + bent)
-        slope[:, cols] = half + (0.5 * 0.7978845608) * t * (1.0 - bent * bent) * (
-            1.0 + (3 * 0.044715) * square
-        )
-        act = low(t * half)
-        own[:, cols] = act
-        give[:, cols] = act
-        feed += dot(act, w_down[cols, :])
-    normed_two, inverse_two = normalize(hidden_one + feed)
-    output = (normed_two * gain_two + shift_two) * valid
-    out_own[:HEAD_DIM, :] = low(output[:HEAD_DIM])
-    out_own[HEAD_DIM:, :] = low(output[ROWS:])
-    out_send[...] = low(output[HEAD_DIM:])
-    row = lax.broadcasted_iota(jnp.int32, (OWN, 1), 0)
-    token_valid = jnp.where(row < ROWS, valid, 0.0)
-    squares = jnp.sum(feed * feed * token_valid, axis=0, keepdims=True)
+        linear[:, cols] = dot(own[:, FF : FF + WIDTH], w_up[:, cols])
+    for at in range(0, FF, WIDTH):
+        cols = slice(at, at + WIDTH)
+        for strip in strips:
+            t = linear[strip, cols] + up_bias[0:1, cols]
+            square = t * t
+            bent = jnp.tanh(0.7978845608 * (t + 0.044715 * (square * t)))
+            half = 0.5 * (1.0 + bent)
+            slope[strip, cols] = half + (0.5 * 0.7978845608) * t * (1.0 - bent * bent) * (
+                1.0 + (3 * 0.044715) * square
+            )
+            act = low(t * half)
+            own[strip, cols] = act
+            give[strip, cols] = act
+        product = dot(own[:, cols], w_down[cols, :])
+        feed[...] = product if at == 0 else feed[...] + product
+    squares = jnp.zeros((1, WIDTH), F32)
+    parts = [jnp.zeros((1, WIDTH), F32)] * 3
+    for strip in strips:
+        valid, weight = valid_all[strip], weight_all[strip]
+        branch = feed[strip, :] + down_bias
+        normed, inverse = normalize(inputs[strip, :] + branch)
+        output = low((normed * gain_two + shift_two) * valid)
+        if strip.start < HEAD_DIM:
+            out_own[strip, :] = output
+        else:
+            out_send[strip.start - HEAD_DIM : strip.stop - HEAD_DIM, :] = output
+        if strip.start < ROWS:
+            squares += jnp.sum(branch * branch * valid, axis=0, keepdims=True)
+        else:
+            out_own[HEAD_DIM:, :] = output
+        g = cot[strip, :] * valid
+        second = norm_back(g * gain_two, normed, inverse)
+        second_out[strip, :] = second
+        grad_feed = low(second)
+        terms = high(grad_feed), g * normed, g
+        parts = [
+            part + jnp.sum(term * weight, axis=0, keepdims=True)
+            for part, term in zip(parts, terms)
+        ]
+        scaled = grad_feed * low(weight)
+        half = WIDTH // 2
+        first_core = place % 2 == 0
+        own[strip, FF + 2 * WIDTH :] = jnp.where(first_core, scaled[:, :half], scaled[:, half:])
+        give[strip, FF + 2 * WIDTH :] = jnp.where(first_core, scaled[:, half:], scaled[:, :half])
     squares_out[...] = low(
         jnp.concatenate([*split_three(squares), jnp.zeros((13, WIDTH), F32)], 0)
     )
-    g = cot * valid
-    second = norm_back(g * gain_two, normed_two, inverse_two)
-    second_out[...] = second
-    grad_feed = low(second)
-    hand_out(place % 2, own, give, grad_feed * low(weight), FF + 2 * WIDTH)
-    blank = jnp.zeros((5, WIDTH), F32)
-    sums[...] = jnp.concatenate(
-        [blank, total(high(grad_feed)), total(g * normed_two), total(g)], 0
-    )
+    sums[...] = jnp.concatenate([jnp.zeros((5, WIDTH), F32), *parts], 0)
 
 
 def quad_slope_kernel(layout, *refs):
     vectors, sums, squares, w_out, w_up, w_down, slope, second_in, normed_in, inverse_in = refs[:10]
-    pack, grad_mem, first_grad, own, give, grad_linear = refs[10:]
+    pack, grad_mem, first_grad, own, give = refs[10:15]
+    grad_linear, product, grad_hidden, halves = refs[15:]
     place = lax.axis_index("seq")
     core = place % 2
     weight = row_weights(layout.group)
     weight_low = low(weight)
 
-    def total(v):
-        return jnp.sum(v * weight, axis=0, keepdims=True)
-
-    ups = []
-    second = second_in[...]
-    grad_feed = low(second)
-    grad_hidden = second
+    strips = [slice(start, start + STRIP) for start in range(0, OWN, STRIP)]
+    grad_feed = low(second_in[...])
     for at in range(0, FF, WIDTH):
         cols = slice(at, at + WIDTH)
-        linear = low(dot(grad_feed, w_down[cols, :], NT) * slope[:, cols])
-        grad_linear[:, cols] = linear * weight_low
-        ups.append(total(high(linear)))
-        grad_hidden += dot(linear, w_up[:, cols], NT)
-    own[:, : FF // 2] = grad_linear[:, aligned(core, FF // 2)]
-    give[:, : FF // 2] = grad_linear[:, aligned(1 - core, FF // 2)]
-    normed_one = normed_in[...]
-    gains = [total(grad_hidden * normed_one), total(grad_hidden)]
-    first = norm_back(grad_hidden * vectors[3:4, :], normed_one, inverse_in[:, :1])
-    first_grad[...] = first
-    grad_branch = low(first)
-    hand_out(core, own, give, grad_branch * weight_low, FF // 2)
-    sizes = jnp.concatenate([total(high(grad_branch)), *gains, sums[5:8, :], *ups], 0)
+        product[:, cols] = dot(grad_feed, w_down[cols, :], NT)
+    ups = []
+    for at in range(0, FF, WIDTH):
+        cols = slice(at, at + WIDTH)
+        part = jnp.zeros((1, WIDTH), F32)
+        for strip in strips:
+            linear = low(product[strip, cols] * slope[strip, cols])
+            grad_linear[strip, cols] = linear
+            part += jnp.sum(high(linear) * weight[strip], axis=0, keepdims=True)
+            halves[at // (FF // 2), strip, at % (FF // 2) : at % (FF // 2) + WIDTH] = (
+                linear * weight_low[strip]
+            )
+        ups.append(part)
+    grad_hidden[...] = dot(grad_linear[...], w_up[...], NT)
+    own[:, : FF // 2] = halves[core]
+    give[:, : FF // 2] = halves[1 - core]
+    parts = [jnp.zeros((1, WIDTH), F32)] * 3
+    for strip in strips:
+        hidden = second_in[strip, :] + grad_hidden[strip, :]
+        normed = normed_in[strip, :]
+        first = norm_back(hidden * vectors[3:4, :], normed, inverse_in[strip, :1])
+        first_grad[strip, :] = first
+        grad_branch = low(first)
+        terms = high(grad_branch), hidden * normed, hidden
+        parts = [
+            part + jnp.sum(term * weight[strip], axis=0, keepdims=True)
+            for part, term in zip(parts, terms)
+        ]
+        scaled = grad_branch * weight_low[strip]
+        half = WIDTH // 2
+        own[strip, FF // 2 :] = jnp.where(core == 0, scaled[:, :half], scaled[:, half:])
+        give[strip, FF // 2 :] = jnp.where(core == 0, scaled[:, half:], scaled[:, :half])
+        if strip.start < ROWS:
+            pack[0, strip, :] = grad_branch
+        else:
+            grad_mem[...] = grad_branch
+    sizes = jnp.concatenate([*parts, sums[5:8, :], *ups], 0)
     first, second, _ = split_three(sizes)
     blank = jnp.zeros((PACK - 23, WIDTH), F32)
-    pack[0, :ROWS, :] = grad_branch[:ROWS]
     pack[0, ROWS:, :] = low(
         jnp.concatenate([high(squares[...])[:3], first, second, blank], 0)
     )
-    grad_mem[...] = grad_branch[ROWS:]
 
 
 MAIN_ROWS = 176
@@ -1412,9 +1453,11 @@
     third = doubled(w_down[None], GATHER_DOWN[0])
     got = layout.swap(give, partner)[None]
     arrived = got[0, :, FIRST:]
-    near = doubled(jnp.concatenate([own[None], got], 0), GATHER_QKV[1])
-    far = layout.swap(near[:, :, FIRST:], 0)
-    first = doubled(near[:, :, :FIRST], GATHER_QKV[2])
+    held = jnp.concatenate([own[None], got], 0)
+    first = doubled(held[:, :, :FIRST], GATHER_QKV[1])
+    near = doubled(after(held[:, :, FIRST:], first), GATHER_QKV[1])
+    far = layout.swap(near, 0)
+    first = doubled(first, GATHER_QKV[2])
     second = doubled(doubled(second, GATHER_UP[1]), GATHER_UP[2])
     third = doubled(doubled(third, GATHER_DOWN[1]), GATHER_DOWN[2])
     cot_arrived = layout.swap(pick(after(cot_tokens, first), 1 - slot), partner)
@@ -1474,7 +1517,12 @@
             ((OWN, WIDTH), F32),
             ((OWN, LANES), F32),
         ],
-        [],
+        [
+            ((OWN, WIDTH), F32),
+            ((OWN, WIDTH), F32),
+            ((OWN, WIDTH), F32),
+            ((OWN, FF), F32),
+        ],
         (
             lengths,
             tokens,
@@ -1503,7 +1551,12 @@
             ((OWN, LINEAR_LANES), BF),
             ((OWN, LINEAR_LANES), BF),
         ],
-        [((OWN, FF), BF)],
+        [
+            ((OWN, FF), BF),
+            ((OWN, FF), F32),
+            ((OWN, WIDTH), F32),
+            ((2, OWN, FF // 2), BF),
+        ],
         (
             vector_rows,
             sums,

time: 113 us -> 109 us (0.965)
  waiting for transfers between devices: 46 us -> 39.2 us
  starting transfers between devices: 34.9 us -> 38.9 us
    ppermute x27 -> x28, waiting for transfers between devices: 26.4 us -> 18.4 us  [swap(): return lax.ppermute(x, axis, [(i, i ^ mask) for i in range(size)])]
    ppermute x27 -> x28, starting transfers between devices: 24.5 us -> 30.5 us  [swap(): return lax.ppermute(x, axis, [(i, i ^ mask) for i in range(size)])]
    ppermute x6, starting transfers between devices: 10.4 us -> 8.46 us  [pair_swap_by_core(): return lax.ppermute(x, ('dp', 'seq'), pairs)]
    ppermute x6, waiting for transfers between devices: 19.6 us -> 20.9 us  [pair_swap_by_core(): return lax.ppermute(x, ('dp', 'seq'), pairs)]
  transfers between devices with their start and end apart: 33 -> 34, of which waited for: 15 -> 14; matrix products, arithmetic and copies ran while one was open for 5% -> 6% of each run, Pallas kernels for 17% -> 17%
where the time goes in v4:
time: 109 us
  waiting for transfers between devices  39.2 us (36%)
  starting transfers between devices  38.9 us (36%)
  Pallas kernels  23.1 us (21%)
  other arithmetic  5.42 us (5%)
  between operations  1.19 us (1%)
    ppermute x28, starting transfers between devices, swap(): return lax.ppermute(x, axis, [(i, i ^ mask) for i in range(size)])  30.5 us
    pallas_call x8, Pallas kernels, call(): pl.pallas_call(kernel, out_shape=[jax.ShapeDtypeStruct(shape, kind) for s...  21.3 us
    ppermute x6, waiting for transfers between devices, pair_swap_by_core(): return lax.ppermute(x, ('dp', 'seq'), pairs)  20.9 us
    ppermute x28, waiting for transfers between devices, swap(): return lax.ppermute(x, axis, [(i, i ^ mask) for i in range(size)])  18.4 us
    ppermute x6, starting transfers between devices, pair_swap_by_core(): return lax.ppermute(x, ('dp', 'seq'), pairs)  8.46 us
    concatenate x8, other arithmetic, doubled(): return jnp.concatenate([held, layout.block_swap(held, bit)], 0)  2.81 us
  transfers between devices with their start and end apart: 34, of which 14 were waited for; matrix products, arithmetic and copies ran while one was open for 6% of the time, Pallas kernels for 17%

profile of v4, /device:TPU:0, one launch (start us, length us, event | category | flops | bytes accessed | tf_op | source)
XLA Modules:
  0.0 108.9 jit_solution(1050771210513606222)
XLA Ops:
  0.7 4.1 %collective-permute-start.9 = (bf16[1,16,2048]{2,1,0:T(8,128)(2,1)}, bf16[1,16,2048]{2,1,0:T(8,128)(2,1)S(1)}, u32[]{:S(2)}, u32[]{:S(2)}) collective-permute-start(bf16[1,16,2048]{2,1,0:T(8,128)(2,1)} %bitcast.23), channel_id=1, source_target_pairs={{0,4},{1,5},{2,6},{3,7},{4,0},{5,1},{6,2},{7,3},{8,12},{9,13},{10,... | collective-permute-start | bytes 196616 | tf_op jit(solution)/shard_map/ppermute | solution.py:79
  4.9 1.8 %prepare.1 = (bf16[16,4224]{1,0:T(8,128)(2,1)}, bf16[16,4224]{1,0:T(8,128)(2,1)}) custom-call(bf16[2,64,512]{2,1,0:T(8,128)(2,1)} %refs_1_.3, bf16[16,1536]{1,0:T(8,128)(2,1)} %refs_1_.2, bf16[16,512]{1,0:T(8,128)(2,1)} %refs_2_.1, bf16[16]{0:T(256)(128)(2,1)} %refs_3_.1, bf16[16]{0:T(256)(128)(2,1)} %refs_4_.2, bf16[16]{0:T(256)(128)(2,1)} %refs_5_.1, ...), custom_call_target="tpu_custom_call" | custom-call | tf_op jit(solution)/shard_map/prepare/pallas_call | solution.py:1432
  6.7 2.9 %collective-permute-start = (bf16[16,4224]{1,0:T(8,128)(2,1)}, bf16[16,4224]{1,0:T(8,128)(2,1)S(1)}, u32[]{:S(2)}, u32[]{:S(2)}) collective-permute-start(bf16[16,4224]{1,0:T(8,128)(2,1)} %get-tuple-element.83), channel_id=1, source_target_pairs={{0,4},{1,5},{2,6},{3,7},{4,0},{5,1},{6,2},{7,3},{8,12},{9,13},{10,... | collective-permute-start | bytes 405512 | tf_op jit(solution)/shard_map/ppermute | solution.py:79
  10.4 1.6 %collective-permute-start.10 = (bf16[2,16,2048]{2,1,0:T(8,128)(2,1)S(1)}, bf16[2,16,2048]{2,1,0:T(8,128)(2,1)S(1)}, u32[]{:S(2)}, u32[]{:S(2)}) collective-permute-start(bf16[2,16,2048]{2,1,0:T(8,128)(2,1)S(1)} %pad_maximum_fusion.12), channel_id=1, source_target_pairs={{0,8},{8,0},{16,24},{24,16},{1,9},{9,1},{17,25},{25,17},{2,10},{10... | collective-permute-start | bytes 393224 | tf_op jit(solution)/shard_map/ppermute | solution.py:79
  12.0 2.9 %collective-permute-done.15 = bf16[1,64,512]{2,1,0:T(8,128)(2,1)S(1)} collective-permute-done((bf16[1,64,512]{2,1,0:T(8,128)(2,1)}, bf16[1,64,512]{2,1,0:T(8,128)(2,1)S(1)}, u32[]{:S(2)}, u32[]{:S(2)}) %collective-permute-start.15) | collective-permute-done | bytes 65568 | tf_op jit(solution)/shard_map/ppermute | solution.py:79
  15.8 1.5 %collective-permute-start.16 = (bf16[2,64,512]{2,1,0:T(8,128)(2,1)S(1)}, bf16[2,64,512]{2,1,0:T(8,128)(2,1)S(1)}, u32[]{:S(2)}, u32[]{:S(2)}) collective-permute-start(bf16[2,64,512]{2,1,0:T(8,128)(2,1)S(1)} %pad_maximum_fusion.13), channel_id=1, source_target_pairs={{0,16},{8,24},{16,0},{24,8},{1,17},{9,25},{17,1},{25,9},{2,18},{10... | collective-permute-start | bytes 393224 | tf_op jit(solution)/shard_map/ppermute | solution.py:79
  20.7 1.5 %collective-permute-start.11 = (bf16[4,16,2048]{2,1,0:T(8,128)(2,1)S(1)}, bf16[4,16,2048]{2,1,0:T(8,128)(2,1)S(1)}, u32[]{:S(2)}, u32[]{:S(2)}) collective-permute-start(bf16[4,16,2048]{2,1,0:T(8,128)(2,1)S(1)} %pad_maximum_fusion.5), channel_id=1, source_target_pairs={{0,2},{1,3},{2,0},{3,1},{4,6},{5,7},{6,4},{7,5},{8,10},{9,11},{10,... | collective-permute-start | bytes 786440 | tf_op jit(solution)/shard_map/ppermute | solution.py:79
  22.2 1.7 %collective-permute-start.17 = (bf16[4,64,512]{2,1,0:T(8,128)(2,1)S(1)}, bf16[4,64,512]{2,1,0:T(8,128)(2,1)S(1)}, u32[]{:S(2)}, u32[]{:S(2)}) collective-permute-start(bf16[4,64,512]{2,1,0:T(8,128)(2,1)S(1)} %pad_maximum_fusion.6), channel_id=1, source_target_pairs={{0,8},{8,0},{16,24},{24,16},{1,9},{9,1},{17,25},{25,17},{2,10},{10... | collective-permute-start | bytes 786440 | tf_op jit(solution)/shard_map/ppermute | solution.py:79
  23.9 2.3 %collective-permute-start.2 = (bf16[4,16,2176]{2,1,0:T(8,128)(2,1)S(1)}, bf16[4,16,2176]{2,1,0:T(8,128)(2,1)S(1)}, u32[]{:S(2)}, u32[]{:S(2)}) collective-permute-start(bf16[4,16,2176]{2,1,0:T(8,128)(2,1)S(1)} %pad_maximum_fusion.4), channel_id=1, source_target_pairs={{0,16},{8,24},{16,0},{24,8},{1,17},{9,25},{17,1},{25,9},{2,18},{10... | collective-permute-start | bytes 835592 | tf_op jit(solution)/shard_map/ppermute | solution.py:79
  26.3 3.3 %collective-permute-done.17 = bf16[4,64,512]{2,1,0:T(8,128)(2,1)S(1)} collective-permute-done((bf16[4,64,512]{2,1,0:T(8,128)(2,1)S(1)}, bf16[4,64,512]{2,1,0:T(8,128)(2,1)S(1)}, u32[]{:S(2)}, u32[]{:S(2)}) %collective-permute-start.17) | collective-permute-done | bytes 262176 | tf_op jit(solution)/shard_map/ppermute | solution.py:79
  31.6 1.5 %collective-permute-start.6 = (bf16[8,16,2176]{2,1,0:T(8,128)(2,1)S(1)}, bf16[8,16,2176]{2,1,0:T(8,128)(2,1)S(1)}, u32[]{:S(2)}, u32[]{:S(2)}) collective-permute-start(bf16[8,16,2176]{2,1,0:T(8,128)(2,1)S(1)} %pad_maximum_fusion.1.refs_4_.refs_10_), channel_id=1, source_target_pairs={{0,8},{8,0},{16,24},{24,16},{1,9},{9,1},{17,25},{25,17},{2,10},{10... | collective-permute-start | bytes 1671176 | tf_op jit(solution)/shard_map/ppermute | solution.py:79
  33.1 1.6 %collective-permute-start.12 = (bf16[8,16,2048]{2,1,0:T(8,128)(2,1)S(1)}, bf16[8,16,2048]{2,1,0:T(8,128)(2,1)}, u32[]{:S(2)}, u32[]{:S(2)}) collective-permute-start(bf16[8,16,2048]{2,1,0:T(8,128)(2,1)S(1)} %pad_maximum_fusion.2.refs_14_), channel_id=1, source_target_pairs={{0,16},{8,24},{16,0},{24,8},{1,17},{9,25},{17,1},{25,9},{2,18},{10... | collective-permute-start | bytes 1572872 | tf_op jit(solution)/shard_map/ppermute | solution.py:79
  34.8 2.8 %collective-permute-start.3 = (bf16[64,512]{1,0:T(8,128)(2,1)S(1)}, bf16[64,512]{1,0:T(8,128)(2,1)S(1)}, u32[]{:S(2)}, u32[]{:S(2)}) collective-permute-start(bf16[64,512]{1,0:T(8,128)(2,1)S(1)} %dynamic-slice_bitcast_fusion), channel_id=1, source_target_pairs={{0,4},{1,5},{2,6},{3,7},{4,0},{5,1},{6,2},{7,3},{8,12},{9,13},{10,... | collective-permute-start | bytes 196616 | tf_op jit(solution)/shard_map/ppermute | solution.py:79
  37.6 5.5 %collective-permute-done.3.refs_5_ = bf16[64,512]{1,0:T(8,128)(2,1)S(1)} collective-permute-done((bf16[64,512]{1,0:T(8,128)(2,1)S(1)}, bf16[64,512]{1,0:T(8,128)(2,1)S(1)}, u32[]{:S(2)}, u32[]{:S(2)}) %collective-permute-start.3) | collective-permute-done | bytes 65568 | tf_op jit(solution)/shard_map/ppermute | solution.py:79
  46.5 3.9 %attention_forward.1 = (f32[160,512]{1,0:T(8,128)S(1)}, bf16[640,768]{1,0:T(8,128)(2,1)S(1)}, bf16[544,512]{1,0:T(8,128)(2,1)S(1)}, bf16[512,768]{1,0:T(8,128)(2...) custom-call(s32[2]{0:T(128)S(1)} %copy-done.2, bf16[4,16,2048]{2,1,0:T(8,128)(2,1)S(1)} %constant_dynamic-update-slice_fusion.refs_1_, ...), custom_call_target="tpu_custom_call" | custom-call | flops 4000000000 | bytes 2785288 | tf_op jit(solution)/shard_map/attention_forward/pallas_call | solution.py:655
  50.4 3.7 %feed_forward.1 = (bf16[96,512]{1,0:T(8,128)(2,1)S(1)}, bf16[96,512]{1,0:T(8,128)(2,1)S(1)}, bf16[160,3328]{1,0:T(8,128)(2,1)S(1)}, bf16[160,3328]{1,0:T(8,128)(...) custom-call(s32[2]{0:T(128)S(1)} %copy-done.2, ...), custom_call_target="tpu_custom_call" | custom-call | flops 3000000000 | bytes 7290888 | tf_op jit(solution)/shard_map/feed_forward/pallas_call | solution.py:655
  54.3 1.8 %feed_backward.1 = (bf16[1,160,512]{2,1,0:T(8,128)(2,1)S(1)}, bf16[32,512]{1,0:T(8,128)(2,1)S(1)}, f32[160,512]{1,0:T(8,128)S(1)}, bf16[160,1280]{1,0:T(8,128)(2,1)S(1)}, bf16[160,1280]{1,0:T(8,128)(2,1)S(1)}) custom-call(f32[8,512]{1,0:T(8,128)S(1)} %get-tuple-element.89.refs_8_.refs_0_, f32[8,512]{1,0:T(8,128)S(1)} %get-tuple-element.96.refs_1_, ...), custom_call_target="tpu_custom_call" | custom-call | flops 3000000000 | bytes 6815744 | tf_op jit(solution)/shard_map/feed_backward/pallas_call | solution.py:655
  56.6 3.9 %collective-permute-start.21 = (bf16[1,160,512]{2,1,0:T(8,128)(2,1)S(1)}, bf16[1,160,512]{2,1,0:T(8,128)(2,1)S(1)}, u32[]{:S(2)}, u32[]{:S(2)}) collective-permute-start(bf16[1,160,512]{2,1,0:T(8,128)(2,1)S(1)} %get-tuple-element.105), channel_id=1, source_target_pairs={{0,2},{1,3},{2,0},{3,1},{4,6},{5,7},{6,4},{7,5},{8,10},{9,11},{10,... | collective-permute-start | bytes 491528 | tf_op jit(solution)/shard_map/ppermute | solution.py:79
  60.5 1.5 %weight_gradients.1 = (bf16[8,176,256]{2,1,0:T(8,128)(2,1)S(1)}, bf16[8,176,256]{2,1,0:T(8,128)(2,1)S(1)}, bf16[8,112,256]{2,1,0:T(8,128)(2,1)S(1)}, bf16[8,112,256]{2,1,0:T(8,128)(2,1)S(1)}) custom-call(bf16[160,3328]{1,0:T(8,128)(2,1)S(1)} %get-tuple-element.106.refs_0_, bf16[160,3328]{1,0:T(8,128)(2,1)S(1)} %collective-permute-done.22.refs_1_, ...), custom_call_target="tpu_custom_call" | custom-call | flops 1000000000 | bytes 2949120 | tf_op jit(solution)/shard_map/weight_gradients/pallas_call | solution.py:655
  62.0 1.4 %collective-permute-start.28 = (bf16[8,112,256]{2,1,0:T(8,128)(2,1)S(1)}, bf16[8,112,256]{2,1,0:T(8,128)(2,1)S(1)}, u32[]{:S(2)}, u32[]{:S(2)}) collective-permute-start(bf16[8,112,256]{2,1,0:T(8,128)(2,1)S(1)} %get-tuple-element.121), channel_id=1, source_target_pairs={{0,2},{1,3},{2,0},{3,1},{4,6},{5,7},{6,4},{7,5},{8,10},{9,11},{10,... | collective-permute-start | bytes 1376264 | tf_op jit(solution)/shard_map/ppermute | solution.py:89
  63.5 1.5 %collective-permute-start.27 = (bf16[8,176,256]{2,1,0:T(8,128)(2,1)S(1)}, bf16[8,176,256]{2,1,0:T(8,128)(2,1)S(1)}, u32[]{:S(2)}, u32[]{:S(2)}) collective-permute-start(bf16[8,176,256]{2,1,0:T(8,128)(2,1)S(1)} %get-tuple-element.111), channel_id=1, source_target_pairs={{0,8},{1,17},{2,10},{3,19},{4,12},{5,21},{6,14},{7,23},{8,0},{9,25... | collective-permute-start | bytes 2162696 | tf_op jit(solution)/shard_map/ppermute | solution.py:89
  65.2 1.6 %collective-permute-done.24.refs_6_ = bf16[2,160,512]{2,1,0:T(8,128)(2,1)S(1)} collective-permute-done((bf16[2,160,512]{2,1,0:T(8,128)(2,1)S(1)}, bf16[2,160,512]{2,1,0:T(8,128)(2,1)S(1)}, u32[]{:S(2)}, u32[]{:S(2)}) %collective-permute-start.24) | collective-permute-done | bytes 327712 | tf_op jit(solution)/shard_map/ppermute | solution.py:79
  66.8 8.1 %attention_backward.1 = (bf16[4,112,256]{2,1,0:T(8,128)(2,1)S(1)}, bf16[4,112,256]{2,1,0:T(8,128)(2,1)S(1)}, bf16[160,512]{1,0:T(8,128)(2,1)S(1)}, bf16[160,512]{1,0:T(8,128)(2,1)S(1)}, bf16[16,512]{1,0:T(8,128)(2,1)S(1)}) custom-call(s32[2]{0:T(128)S(1)} %copy-done.2, bf16[640,768]{1,0:T(8,128)(2,1)S(1)} %get-tuple-element.92.refs_1_, ...), custom_call_target="tpu_custom_call" | custom-call | bytes 3276808 | tf_op jit(solution)/shard_map/attention_backward/pallas_call | solution.py:655
  75.4 1.6 %collective-permute-start.29 = (bf16[4,400,256]{2,1,0:T(8,128)(2,1)S(1)}, bf16[4,400,256]{2,1,0:T(8,128)(2,1)S(1)}, u32[]{:S(2)}, u32[]{:S(2)}) collective-permute-start(bf16[4,400,256]{2,1,0:T(8,128)(2,1)S(1)} %pad_maximum_fusion), channel_id=1, source_target_pairs={{0,16},{1,9},{2,18},{3,11},{4,20},{5,13},{6,22},{7,15},{8,24},{9,1... | collective-permute-start | bytes 2457608 | tf_op jit(solution)/shard_map/ppermute | solution.py:89
  77.0 1.4 %collective-permute-done.25 = bf16[160,512]{1,0:T(8,128)(2,1)S(1)} collective-permute-done((bf16[160,512]{1,0:T(8,128)(2,1)S(1)}, bf16[160,512]{1,0:T(8,128)(2,1)S(1)}, u32[]{:S(2)}, u32[]{:S(2)}) %collective-permute-start.25) | collective-permute-done | bytes 163872 | tf_op jit(solution)/shard_map/ppermute | solution.py:79
  78.5 1.6 %collective-permute-start.26 = (bf16[208,512]{1,0:T(8,128)(2,1)S(1)}, bf16[208,512]{1,0:T(8,128)(2,1)S(1)}, u32[]{:S(2)}, u32[]{:S(2)}) collective-permute-start(bf16[208,512]{1,0:T(8,128)(2,1)S(1)} %pad_maximum_fusion.8), channel_id=1, source_target_pairs={{0,4},{1,5},{2,6},{3,7},{4,0},{5,1},{6,2},{7,3},{8,12},{9,13},{10,... | collective-permute-start | bytes 638984 | tf_op jit(solution)/shard_map/ppermute | solution.py:79
  80.0 7.8 %collective-permute-done.29 = bf16[4,400,256]{2,1,0:T(8,128)(2,1)S(1)} collective-permute-done((bf16[4,400,256]{2,1,0:T(8,128)(2,1)S(1)}, bf16[4,400,256]{2,1,0:T(8,128)(2,1)S(1)}, u32[]{:S(2)}, u32[]{:S(2)}) %collective-permute-start.29) | collective-permute-done | bytes 819232 | tf_op jit(solution)/shard_map/ppermute | solution.py:89
  87.9 1.8 %collective-permute-start.30 = (bf16[2,176,256]{2,1,0:T(8,128)(2,1)S(1)}, bf16[2,176,256]{2,1,0:T(8,128)(2,1)S(1)}, u32[]{:S(2)}, u32[]{:S(2)}) collective-permute-start(bf16[2,176,256]{2,1,0:T(8,128)(2,1)S(1)} %get-tuple-element.153), channel_id=1, source_target_pairs={{0,2},{1,3},{2,0},{3,1},{4,6},{5,7},{6,4},{7,5},{8,10},{9,11},{10,... | collective-permute-start | bytes 540680 | tf_op jit(solution)/shard_map/ppermute | solution.py:89
  89.8 1.6 %collective-permute-start.31 = (bf16[2,224,256]{2,1,0:T(8,128)(2,1)S(1)}, bf16[2,224,256]{2,1,0:T(8,128)(2,1)S(1)}, u32[]{:S(2)}, u32[]{:S(2)}) collective-permute-start(bf16[2,224,256]{2,1,0:T(8,128)(2,1)S(1)} %get-tuple-element.151), channel_id=1, source_target_pairs={{0,8},{1,17},{2,10},{3,19},{4,12},{5,21},{6,14},{7,23},{8,0},{9,25... | collective-permute-start | bytes 688136 | tf_op jit(solution)/shard_map/ppermute | solution.py:89
  91.4 3.8 %collective-permute-done.30 = bf16[2,176,256]{2,1,0:T(8,128)(2,1)S(1)} collective-permute-done((bf16[2,176,256]{2,1,0:T(8,128)(2,1)S(1)}, bf16[2,176,256]{2,1,0:T(8,128)(2,1)S(1)}, u32[]{:S(2)}, u32[]{:S(2)}) %collective-permute-start.30) | collective-permute-done | bytes 180256 | tf_op jit(solution)/shard_map/ppermute | solution.py:89
  96.6 1.4 %emit_tokens.1 = (bf16[2,64,512]{2,1,0:T(8,128)(2,1)}, bf16[20,2,512]{2,1,0:T(2,128)(2,1)}, bf16[2,64,512]{2,1,0:T(8,128)(2,1)}, bf16[20,2,512]{2,1,0:T(2,128)(2,1)}, f32[2,512]{1,0:T(2,128)}) custom-call(s32[2]{0:T(128)S(1)} %copy-done.2, bf16[96,512]{1,0:T(8,128)(2,1)S(1)} %get-tuple-element.91.refs_1_, bf16[160,512]{1,0:T(8,128)(2,1)S(1)} %add_convert_fusion.8.refs_2_, ...), custom_call_target="tpu_custom_call" | custom-call | bytes 491528 | tf_op jit(solution)/shard_map/emit_tokens/pallas_call | solution.py:655
  97.9 8.6 %collective-permute-done.32.other = bf16[1,400,256]{2,1,0:T(8,128)(2,1)S(1)} collective-permute-done((bf16[1,400,256]{2,1,0:T(8,128)(2,1)S(1)}, bf16[1,400,256]{2,1,0:T(8,128)(2,1)S(1)}, u32[]{:S(2)}, u32[]{:S(2)}) %collective-permute-start.32) | collective-permute-done | bytes 204832 | tf_op jit(solution)/shard_map/ppermute | solution.py:89
  (94 shorter events, 15.8 us)
Async XLA Ops:
  0.7 8.9 %collective-permute-start.9 = (bf16[1,16,2048]{2,1,0:T(8,128)(2,1)}, bf16[1,16,2048]{2,1,0:T(8,128)(2,1)S(1)}, u32[]{:S(2)}, u32[]{:S(2)}) collective-permute-start(bf16[1,16,2048]{2,1,0:T(8,128)(2,1)} %bitcast.23), channel_id=1, source_target_pairs={{0,4},{1,5},{2,6},{3,7},{4,0},{5,1},{6,2},{7,3},{8,12},{9,13},{10,... | collective-permute-start | bytes 196616 | tf_op jit(solution)/shard_map/ppermute | solution.py:79
  4.8 10.1 %collective-permute-start.15 = (bf16[1,64,512]{2,1,0:T(8,128)(2,1)}, bf16[1,64,512]{2,1,0:T(8,128)(2,1)S(1)}, u32[]{:S(2)}, u32[]{:S(2)}) collective-permute-start(bf16[1,64,512]{2,1,0:T(8,128)(2,1)} %bitcast.19), channel_id=1, source_target_pairs={{0,4},{1,5},{2,6},{3,7},{4,0},{5,1},{6,2},{7,3},{8,12},{9,13},{10,... | collective-permute-start | bytes 196616 | tf_op jit(solution)/shard_map/ppermute | solution.py:79
  6.7 10.6 %collective-permute-start = (bf16[16,4224]{1,0:T(8,128)(2,1)}, bf16[16,4224]{1,0:T(8,128)(2,1)S(1)}, u32[]{:S(2)}, u32[]{:S(2)}) collective-permute-start(bf16[16,4224]{1,0:T(8,128)(2,1)} %get-tuple-element.83), channel_id=1, source_target_pairs={{0,4},{1,5},{2,6},{3,7},{4,0},{5,1},{6,2},{7,3},{8,12},{9,13},{10,... | collective-permute-start | bytes 405512 | tf_op jit(solution)/shard_map/ppermute | solution.py:79
  10.4 9.3 %collective-permute-start.10 = (bf16[2,16,2048]{2,1,0:T(8,128)(2,1)S(1)}, bf16[2,16,2048]{2,1,0:T(8,128)(2,1)S(1)}, u32[]{:S(2)}, u32[]{:S(2)}) collective-permute-start(bf16[2,16,2048]{2,1,0:T(8,128)(2,1)S(1)} %pad_maximum_fusion.12), channel_id=1, source_target_pairs={{0,8},{8,0},{16,24},{24,16},{1,9},{9,1},{17,25},{25,17},{2,10},{10... | collective-permute-start | bytes 393224 | tf_op jit(solution)/shard_map/ppermute | solution.py:79
  15.8 6.4 %collective-permute-start.16 = (bf16[2,64,512]{2,1,0:T(8,128)(2,1)S(1)}, bf16[2,64,512]{2,1,0:T(8,128)(2,1)S(1)}, u32[]{:S(2)}, u32[]{:S(2)}) collective-permute-start(bf16[2,64,512]{2,1,0:T(8,128)(2,1)S(1)} %pad_maximum_fusion.13), channel_id=1, source_target_pairs={{0,16},{8,24},{16,0},{24,8},{1,17},{9,25},{17,1},{25,9},{2,18},{10... | collective-permute-start | bytes 393224 | tf_op jit(solution)/shard_map/ppermute | solution.py:79
  18.2 5.7 %collective-permute-start.1 = (bf16[2,16,2176]{2,1,0:T(8,128)(2,1)S(1)}, bf16[2,16,2176]{2,1,0:T(8,128)(2,1)S(1)}, u32[]{:S(2)}, u32[]{:S(2)}) collective-permute-start(bf16[2,16,2176]{2,1,0:T(8,128)(2,1)S(1)} %fusion.1), channel_id=1, source_target_pairs={{0,2},{1,3},{2,0},{3,1},{4,6},{5,7},{6,4},{7,5},{8,10},{9,11},{10,... | collective-permute-start | bytes 417800 | tf_op jit(solution)/shard_map/ppermute | solution.py:79
  20.7 12.4 %collective-permute-start.11 = (bf16[4,16,2048]{2,1,0:T(8,128)(2,1)S(1)}, bf16[4,16,2048]{2,1,0:T(8,128)(2,1)S(1)}, u32[]{:S(2)}, u32[]{:S(2)}) collective-permute-start(bf16[4,16,2048]{2,1,0:T(8,128)(2,1)S(1)} %pad_maximum_fusion.5), channel_id=1, source_target_pairs={{0,2},{1,3},{2,0},{3,1},{4,6},{5,7},{6,4},{7,5},{8,10},{9,11},{10,... | collective-permute-start | bytes 786440 | tf_op jit(solution)/shard_map/ppermute | solution.py:79
  22.2 7.4 %collective-permute-start.17 = (bf16[4,64,512]{2,1,0:T(8,128)(2,1)S(1)}, bf16[4,64,512]{2,1,0:T(8,128)(2,1)S(1)}, u32[]{:S(2)}, u32[]{:S(2)}) collective-permute-start(bf16[4,64,512]{2,1,0:T(8,128)(2,1)S(1)} %pad_maximum_fusion.6), channel_id=1, source_target_pairs={{0,8},{8,0},{16,24},{24,16},{1,9},{9,1},{17,25},{25,17},{2,10},{10... | collective-permute-start | bytes 786440 | tf_op jit(solution)/shard_map/ppermute | solution.py:79
  23.9 7.6 %collective-permute-start.2 = (bf16[4,16,2176]{2,1,0:T(8,128)(2,1)S(1)}, bf16[4,16,2176]{2,1,0:T(8,128)(2,1)S(1)}, u32[]{:S(2)}, u32[]{:S(2)}) collective-permute-start(bf16[4,16,2176]{2,1,0:T(8,128)(2,1)S(1)} %pad_maximum_fusion.4), channel_id=1, source_target_pairs={{0,16},{8,24},{16,0},{24,8},{1,17},{9,25},{17,1},{25,9},{2,18},{10... | collective-permute-start | bytes 835592 | tf_op jit(solution)/shard_map/ppermute | solution.py:79
  26.2 8.5 %collective-permute-start.4 = (bf16[2,16,2048]{2,1,0:T(8,128)(2,1)S(1)}, bf16[2,16,2048]{2,1,0:T(8,128)(2,1)S(1)}, u32[]{:S(2)}, u32[]{:S(2)}) collective-permute-start(bf16[2,16,2048]{2,1,0:T(8,128)(2,1)S(1)} %pad_maximum_fusion.11), channel_id=1, source_target_pairs={{0,2},{1,3},{2,0},{3,1},{4,6},{5,7},{6,4},{7,5},{8,10},{9,11},{10,... | collective-permute-start | bytes 393224 | tf_op jit(solution)/shard_map/ppermute | solution.py:79
  29.7 14.9 %collective-permute-start.18 = (bf16[8,64,512]{2,1,0:T(8,128)(2,1)S(1)}, bf16[8,64,512]{2,1,0:T(8,128)(2,1)}, u32[]{:S(2)}, u32[]{:S(2)}) collective-permute-start(bf16[8,64,512]{2,1,0:T(8,128)(2,1)S(1)} %pad_maximum_fusion.3.refs_18_), channel_id=1, source_target_pairs={{0,2},{1,3},{2,0},{3,1},{4,6},{5,7},{6,4},{7,5},{8,10},{9,11},{10,... | collective-permute-start | bytes 1572872 | tf_op jit(solution)/shard_map/ppermute | solution.py:79
  31.6 12.4 %collective-permute-start.6 = (bf16[8,16,2176]{2,1,0:T(8,128)(2,1)S(1)}, bf16[8,16,2176]{2,1,0:T(8,128)(2,1)S(1)}, u32[]{:S(2)}, u32[]{:S(2)}) collective-permute-start(bf16[8,16,2176]{2,1,0:T(8,128)(2,1)S(1)} %pad_maximum_fusion.1.refs_4_.refs_10_), channel_id=1, source_target_pairs={{0,8},{8,0},{16,24},{24,16},{1,9},{9,1},{17,25},{25,17},{2,10},{10... | collective-permute-start | bytes 1671176 | tf_op jit(solution)/shard_map/ppermute | solution.py:79
  33.1 11.6 %collective-permute-start.12 = (bf16[8,16,2048]{2,1,0:T(8,128)(2,1)S(1)}, bf16[8,16,2048]{2,1,0:T(8,128)(2,1)}, u32[]{:S(2)}, u32[]{:S(2)}) collective-permute-start(bf16[8,16,2048]{2,1,0:T(8,128)(2,1)S(1)} %pad_maximum_fusion.2.refs_14_), channel_id=1, source_target_pairs={{0,16},{8,24},{16,0},{24,8},{1,17},{9,25},{17,1},{25,9},{2,18},{10... | collective-permute-start | bytes 1572872 | tf_op jit(solution)/shard_map/ppermute | solution.py:79
  34.7 10.6 %collective-permute-start.7 = (bf16[8,16,2176]{2,1,0:T(8,128)(2,1)S(1)}, bf16[8,16,2176]{2,1,0:T(8,128)(2,1)S(1)}, u32[]{:S(2)}, u32[]{:S(2)}) collective-permute-start(bf16[8,16,2176]{2,1,0:T(8,128)(2,1)S(1)} %pad_maximum_fusion.1.refs_4_.refs_10_), channel_id=1, source_target_pairs={{0,1},{1,0},{2,3},{3,2},{4,5},{5,4},{6,7},{7,6},{8,9},{9,8},{10,11... | collective-permute-start | bytes 1671176 | tf_op jit(solution)/shard_map/ppermute | solution.py:79
  34.8 8.3 %collective-permute-start.3 = (bf16[64,512]{1,0:T(8,128)(2,1)S(1)}, bf16[64,512]{1,0:T(8,128)(2,1)S(1)}, u32[]{:S(2)}, u32[]{:S(2)}) collective-permute-start(bf16[64,512]{1,0:T(8,128)(2,1)S(1)} %dynamic-slice_bitcast_fusion), channel_id=1, source_target_pairs={{0,4},{1,5},{2,6},{3,7},{4,0},{5,1},{6,2},{7,3},{8,12},{9,13},{10,... | collective-permute-start | bytes 196616 | tf_op jit(solution)/shard_map/ppermute | solution.py:79
  43.1 2.0 %collective-permute-start.5 = (bf16[4,16,2048]{2,1,0:T(8,128)(2,1)S(1)}, bf16[4,16,2048]{2,1,0:T(8,128)(2,1)S(1)}, u32[]{:S(2)}, u32[]{:S(2)}) collective-permute-start(bf16[4,16,2048]{2,1,0:T(8,128)(2,1)S(1)} %constant_dynamic-update-slice_fusion.refs_1_), channel_id=1, source_target_pairs={{0,1},{1,0},{2,3},{3,2},{4,5},{5,4},{6,7},{7,6},{8,9},{9,8},{10,11... | collective-permute-start | bytes 786440 | tf_op jit(solution)/shard_map/ppermute | solution.py:79
  44.0 2.4 %collective-permute-start.8 = (bf16[8,16,2176]{2,1,0:T(8,128)(2,1)S(1)}, bf16[8,16,2176]{2,1,0:T(8,128)(2,1)S(1)}, u32[]{:S(2)}, u32[]{:S(2)}) collective-permute-start(bf16[8,16,2176]{2,1,0:T(8,128)(2,1)S(1)} %collective-permute-done.6.refs_5_.refs_11_), channel_id=1, source_target_pairs={{0,1},{1,0},{2,3},{3,2},{4,5},{5,4},{6,7},{7,6},{8,9},{9,8},{10,11... | collective-permute-start | bytes 1671176 | tf_op jit(solution)/shard_map/ppermute | solution.py:79
  44.6 5.8 %collective-permute-start.19 = (bf16[8,64,512]{2,1,0:T(8,128)(2,1)S(1)}, bf16[8,64,512]{2,1,0:T(8,128)(2,1)S(1)}, u32[]{:S(2)}, u32[]{:S(2)}) collective-permute-start(bf16[8,64,512]{2,1,0:T(8,128)(2,1)S(1)} %pad_maximum_fusion.3.refs_18_), channel_id=1, source_target_pairs={{0,1},{1,0},{2,3},{3,2},{4,5},{5,4},{6,7},{7,6},{8,9},{9,8},{10,11... | collective-permute-start | bytes 1572872 | tf_op jit(solution)/shard_map/ppermute | solution.py:79
  44.8 5.6 %collective-permute-start.13 = (bf16[8,16,2048]{2,1,0:T(8,128)(2,1)S(1)}, bf16[8,16,2048]{2,1,0:T(8,128)(2,1)S(1)}, u32[]{:S(2)}, u32[]{:S(2)}) collective-permute-start(bf16[8,16,2048]{2,1,0:T(8,128)(2,1)S(1)} %pad_maximum_fusion.2.refs_14_), channel_id=1, source_target_pairs={{0,1},{1,0},{2,3},{3,2},{4,5},{5,4},{6,7},{7,6},{8,9},{9,8},{10,11... | collective-permute-start | bytes 1572872 | tf_op jit(solution)/shard_map/ppermute | solution.py:79
  45.1 5.3 %collective-permute-start.20 = (bf16[8,64,512]{2,1,0:T(8,128)(2,1)}, bf16[8,64,512]{2,1,0:T(8,128)(2,1)S(1)}, u32[]{:S(2)}, u32[]{:S(2)}) collective-permute-start(bf16[8,64,512]{2,1,0:T(8,128)(2,1)} %collective-permute-done.18.refs_19_), channel_id=1, source_target_pairs={{0,1},{1,0},{2,3},{3,2},{4,5},{5,4},{6,7},{7,6},{8,9},{9,8},{10,11... | collective-permute-start | bytes 1572872 | tf_op jit(solution)/shard_map/ppermute | solution.py:79
  45.3 5.1 %collective-permute-start.14 = (bf16[8,16,2048]{2,1,0:T(8,128)(2,1)}, bf16[8,16,2048]{2,1,0:T(8,128)(2,1)S(1)}, u32[]{:S(2)}, u32[]{:S(2)}) collective-permute-start(bf16[8,16,2048]{2,1,0:T(8,128)(2,1)} %collective-permute-done.12.refs_15_), channel_id=1, source_target_pairs={{0,1},{1,0},{2,3},{3,2},{4,5},{5,4},{6,7},{7,6},{8,9},{9,8},{10,11... | collective-permute-start | bytes 1572872 | tf_op jit(solution)/shard_map/ppermute | solution.py:79
  54.1 6.4 %collective-permute-start.22 = (bf16[160,3328]{1,0:T(8,128)(2,1)S(1)}, bf16[160,3328]{1,0:T(8,128)(2,1)S(1)}, u32[]{:S(2)}, u32[]{:S(2)}) collective-permute-start(bf16[160,3328]{1,0:T(8,128)(2,1)S(1)} %get-tuple-element.107), channel_id=1, source_target_pairs={{0,1},{1,0},{2,3},{3,2},{4,5},{5,4},{6,7},{7,6},{8,9},{9,8},{10,11... | collective-permute-start | bytes 3194888 | tf_op jit(solution)/shard_map/ppermute | solution.py:79
  56.2 4.3 %collective-permute-start.23 = (bf16[160,1280]{1,0:T(8,128)(2,1)S(1)}, bf16[160,1280]{1,0:T(8,128)(2,1)S(1)}, u32[]{:S(2)}, u32[]{:S(2)}) collective-permute-start(bf16[160,1280]{1,0:T(8,128)(2,1)S(1)} %get-tuple-element.110), channel_id=1, source_target_pairs={{0,1},{1,0},{2,3},{3,2},{4,5},{5,4},{6,7},{7,6},{8,9},{9,8},{10,11... | collective-permute-start | bytes 1228808 | tf_op jit(solution)/shard_map/ppermute | solution.py:79
  56.6 8.5 %collective-permute-start.21 = (bf16[1,160,512]{2,1,0:T(8,128)(2,1)S(1)}, bf16[1,160,512]{2,1,0:T(8,128)(2,1)S(1)}, u32[]{:S(2)}, u32[]{:S(2)}) collective-permute-start(bf16[1,160,512]{2,1,0:T(8,128)(2,1)S(1)} %get-tuple-element.105), channel_id=1, source_target_pairs={{0,2},{1,3},{2,0},{3,1},{4,6},{5,7},{6,4},{7,5},{8,10},{9,11},{10,... | collective-permute-start | bytes 491528 | tf_op jit(solution)/shard_map/ppermute | solution.py:79
  62.0 13.0 %collective-permute-start.28 = (bf16[8,112,256]{2,1,0:T(8,128)(2,1)S(1)}, bf16[8,112,256]{2,1,0:T(8,128)(2,1)S(1)}, u32[]{:S(2)}, u32[]{:S(2)}) collective-permute-start(bf16[8,112,256]{2,1,0:T(8,128)(2,1)S(1)} %get-tuple-element.121), channel_id=1, source_target_pairs={{0,2},{1,3},{2,0},{3,1},{4,6},{5,7},{6,4},{7,5},{8,10},{9,11},{10,... | collective-permute-start | bytes 1376264 | tf_op jit(solution)/shard_map/ppermute | solution.py:89
  63.5 11.7 %collective-permute-start.27 = (bf16[8,176,256]{2,1,0:T(8,128)(2,1)S(1)}, bf16[8,176,256]{2,1,0:T(8,128)(2,1)S(1)}, u32[]{:S(2)}, u32[]{:S(2)}) collective-permute-start(bf16[8,176,256]{2,1,0:T(8,128)(2,1)S(1)} %get-tuple-element.111), channel_id=1, source_target_pairs={{0,8},{1,17},{2,10},{3,19},{4,12},{5,21},{6,14},{7,23},{8,0},{9,25... | collective-permute-start | bytes 2162696 | tf_op jit(solution)/shard_map/ppermute | solution.py:89
  65.1 1.7 %collective-permute-start.24 = (bf16[2,160,512]{2,1,0:T(8,128)(2,1)S(1)}, bf16[2,160,512]{2,1,0:T(8,128)(2,1)S(1)}, u32[]{:S(2)}, u32[]{:S(2)}) collective-permute-start(bf16[2,160,512]{2,1,0:T(8,128)(2,1)S(1)} %constant_dynamic-update-slice_fusion.2.refs_5_), channel_id=1, source_target_pairs={{0,1},{1,0},{2,3},{3,2},{4,5},{5,4},{6,7},{7,6},{8,9},{9,8},{10,11... | collective-permute-start | bytes 983048 | tf_op jit(solution)/shard_map/ppermute | solution.py:79
  75.4 12.4 %collective-permute-start.29 = (bf16[4,400,256]{2,1,0:T(8,128)(2,1)S(1)}, bf16[4,400,256]{2,1,0:T(8,128)(2,1)S(1)}, u32[]{:S(2)}, u32[]{:S(2)}) collective-permute-start(bf16[4,400,256]{2,1,0:T(8,128)(2,1)S(1)} %pad_maximum_fusion), channel_id=1, source_target_pairs={{0,16},{1,9},{2,18},{3,11},{4,20},{5,13},{6,22},{7,15},{8,24},{9,1... | collective-permute-start | bytes 2457608 | tf_op jit(solution)/shard_map/ppermute | solution.py:89
  78.5 18.1 %collective-permute-start.26 = (bf16[208,512]{1,0:T(8,128)(2,1)S(1)}, bf16[208,512]{1,0:T(8,128)(2,1)S(1)}, u32[]{:S(2)}, u32[]{:S(2)}) collective-permute-start(bf16[208,512]{1,0:T(8,128)(2,1)S(1)} %pad_maximum_fusion.8), channel_id=1, source_target_pairs={{0,4},{1,5},{2,6},{3,7},{4,0},{5,1},{6,2},{7,3},{8,12},{9,13},{10,... | collective-permute-start | bytes 638984 | tf_op jit(solution)/shard_map/ppermute | solution.py:79
  87.9 7.3 %collective-permute-start.30 = (bf16[2,176,256]{2,1,0:T(8,128)(2,1)S(1)}, bf16[2,176,256]{2,1,0:T(8,128)(2,1)S(1)}, u32[]{:S(2)}, u32[]{:S(2)}) collective-permute-start(bf16[2,176,256]{2,1,0:T(8,128)(2,1)S(1)} %get-tuple-element.153), channel_id=1, source_target_pairs={{0,2},{1,3},{2,0},{3,1},{4,6},{5,7},{6,4},{7,5},{8,10},{9,11},{10,... | collective-permute-start | bytes 540680 | tf_op jit(solution)/shard_map/ppermute | solution.py:89
  89.8 6.1 %collective-permute-start.31 = (bf16[2,224,256]{2,1,0:T(8,128)(2,1)S(1)}, bf16[2,224,256]{2,1,0:T(8,128)(2,1)S(1)}, u32[]{:S(2)}, u32[]{:S(2)}) collective-permute-start(bf16[2,224,256]{2,1,0:T(8,128)(2,1)S(1)} %get-tuple-element.151), channel_id=1, source_target_pairs={{0,8},{1,17},{2,10},{3,19},{4,12},{5,21},{6,14},{7,23},{8,0},{9,25... | collective-permute-start | bytes 688136 | tf_op jit(solution)/shard_map/ppermute | solution.py:89
  96.0 10.6 %collective-permute-start.32 = (bf16[1,400,256]{2,1,0:T(8,128)(2,1)S(1)}, bf16[1,400,256]{2,1,0:T(8,128)(2,1)S(1)}, u32[]{:S(2)}, u32[]{:S(2)}) collective-permute-start(bf16[1,400,256]{2,1,0:T(8,128)(2,1)S(1)} %pad_maximum_fusion.9), channel_id=1, source_target_pairs={{0,4},{1,5},{2,6},{3,7},{4,0},{5,1},{6,2},{7,3},{8,12},{9,13},{10,... | collective-permute-start | bytes 614408 | tf_op jit(solution)/shard_map/ppermute | solution.py:89
  (10 other events, 110.4 us)

commit v5 on v4

--- a/solution.py
+++ b/solution.py
@@ -1004,7 +1004,7 @@
 
 
 STRIP = 32
-PACK = 32
+PACK = 16
 
 ACT_LANES = FF + 2 * WIDTH + WIDTH // 2
 LINEAR_LANES = FF // 2 + WIDTH // 2
@@ -1170,10 +1170,9 @@
         else:
             grad_mem[...] = grad_branch
     sizes = jnp.concatenate([*parts, sums[5:8, :], *ups], 0)
-    first, second, _ = split_three(sizes)
-    blank = jnp.zeros((PACK - 23, WIDTH), F32)
+    blank = jnp.zeros((PACK - 13, WIDTH), F32)
     pack[0, ROWS:, :] = low(
-        jnp.concatenate([high(squares[...])[:3], first, second, blank], 0)
+        jnp.concatenate([high(squares[...])[:3], sizes, blank], 0)
     )
 
 
@@ -1282,7 +1281,7 @@
         total += sums[k]
     square = total[0:1] + total[1:2] + total[2:3]
     tail[...] = low(jnp.concatenate([*split_three(square), jnp.zeros((13, WIDTH), F32)], 0))
-    sizes = total[3:13] + total[13:23]
+    sizes = total[3:13]
     first_core = core == 0
     blank = jnp.zeros((1, half), F32)
     biases = []

time: 109 us -> 109 us (level)
  transfers between devices with their start and end apart: 34 -> 34, of which waited for: 14 -> 13; matrix products, arithmetic and copies ran while one was open for 6% -> 6% of each run, Pallas kernels for 17% -> 17%
where the time goes in v5:
time: 109 us
  waiting for transfers between devices  39.8 us (37%)
  starting transfers between devices  38.1 us (35%)
  Pallas kernels  23.1 us (21%)
  other arithmetic  5.42 us (5%)
  between operations  1.2 us (1%)
    ppermute x28, starting transfers between devices, swap(): return lax.ppermute(x, axis, [(i, i ^ mask) for i in range(size)])  29.9 us
    ppermute x6, waiting for transfers between devices, pair_swap_by_core(): return lax.ppermute(x, ('dp', 'seq'), pairs)  21.7 us
    pallas_call x8, Pallas kernels, call(): pl.pallas_call(kernel, out_shape=[jax.ShapeDtypeStruct(shape, kind) for s...  21.2 us
    ppermute x28, waiting for transfers between devices, swap(): return lax.ppermute(x, axis, [(i, i ^ mask) for i in range(size)])  18.2 us
    ppermute x6, starting transfers between devices, pair_swap_by_core(): return lax.ppermute(x, ('dp', 'seq'), pairs)  8.16 us
    concatenate x8, other arithmetic, doubled(): return jnp.concatenate([held, layout.block_swap(held, bit)], 0)  2.81 us
  transfers between devices with their start and end apart: 34, of which 13 were waited for; matrix products, arithmetic and copies ran while one was open for 6% of the time, Pallas kernels for 17%

profile of v5, /device:TPU:0, one launch (start us, length us, event | category | flops | bytes accessed | tf_op | source)
XLA Modules:
  0.0 108.7 jit_solution(13892090350153304777)
XLA Ops:
  0.7 4.1 %collective-permute-start.9 = (bf16[1,16,2048]{2,1,0:T(8,128)(2,1)}, bf16[1,16,2048]{2,1,0:T(8,128)(2,1)S(1)}, u32[]{:S(2)}, u32[]{:S(2)}) collective-permute-start(bf16[1,16,2048]{2,1,0:T(8,128)(2,1)} %bitcast.23), channel_id=1, source_target_pairs={{0,4},{1,5},{2,6},{3,7},{4,0},{5,1},{6,2},{7,3},{8,12},{9,13},{10,... | collective-permute-start | bytes 196616 | tf_op jit(solution)/shard_map/ppermute | solution.py:79
  4.9 1.8 %prepare.1 = (bf16[16,4224]{1,0:T(8,128)(2,1)}, bf16[16,4224]{1,0:T(8,128)(2,1)}) custom-call(bf16[2,64,512]{2,1,0:T(8,128)(2,1)} %refs_1_.3, bf16[16,1536]{1,0:T(8,128)(2,1)} %refs_1_.2, bf16[16,512]{1,0:T(8,128)(2,1)} %refs_2_.1, bf16[16]{0:T(256)(128)(2,1)} %refs_3_.1, bf16[16]{0:T(256)(128)(2,1)} %refs_4_.2, bf16[16]{0:T(256)(128)(2,1)} %refs_5_.1, ...), custom_call_target="tpu_custom_call" | custom-call | tf_op jit(solution)/shard_map/prepare/pallas_call | solution.py:1431
  6.7 2.9 %collective-permute-start = (bf16[16,4224]{1,0:T(8,128)(2,1)}, bf16[16,4224]{1,0:T(8,128)(2,1)S(1)}, u32[]{:S(2)}, u32[]{:S(2)}) collective-permute-start(bf16[16,4224]{1,0:T(8,128)(2,1)} %get-tuple-element.83), channel_id=1, source_target_pairs={{0,4},{1,5},{2,6},{3,7},{4,0},{5,1},{6,2},{7,3},{8,12},{9,13},{10,... | collective-permute-start | bytes 405512 | tf_op jit(solution)/shard_map/ppermute | solution.py:79
  10.4 1.6 %collective-permute-start.10 = (bf16[2,16,2048]{2,1,0:T(8,128)(2,1)S(1)}, bf16[2,16,2048]{2,1,0:T(8,128)(2,1)S(1)}, u32[]{:S(2)}, u32[]{:S(2)}) collective-permute-start(bf16[2,16,2048]{2,1,0:T(8,128)(2,1)S(1)} %pad_maximum_fusion.12), channel_id=1, source_target_pairs={{0,8},{8,0},{16,24},{24,16},{1,9},{9,1},{17,25},{25,17},{2,10},{10... | collective-permute-start | bytes 393224 | tf_op jit(solution)/shard_map/ppermute | solution.py:79
  12.0 2.9 %collective-permute-done.15 = bf16[1,64,512]{2,1,0:T(8,128)(2,1)S(1)} collective-permute-done((bf16[1,64,512]{2,1,0:T(8,128)(2,1)}, bf16[1,64,512]{2,1,0:T(8,128)(2,1)S(1)}, u32[]{:S(2)}, u32[]{:S(2)}) %collective-permute-start.15) | collective-permute-done | bytes 65568 | tf_op jit(solution)/shard_map/ppermute | solution.py:79
  15.8 1.5 %collective-permute-start.16 = (bf16[2,64,512]{2,1,0:T(8,128)(2,1)S(1)}, bf16[2,64,512]{2,1,0:T(8,128)(2,1)S(1)}, u32[]{:S(2)}, u32[]{:S(2)}) collective-permute-start(bf16[2,64,512]{2,1,0:T(8,128)(2,1)S(1)} %pad_maximum_fusion.13), channel_id=1, source_target_pairs={{0,16},{8,24},{16,0},{24,8},{1,17},{9,25},{17,1},{25,9},{2,18},{10... | collective-permute-start | bytes 393224 | tf_op jit(solution)/shard_map/ppermute | solution.py:79
  20.7 1.5 %collective-permute-start.11 = (bf16[4,16,2048]{2,1,0:T(8,128)(2,1)S(1)}, bf16[4,16,2048]{2,1,0:T(8,128)(2,1)S(1)}, u32[]{:S(2)}, u32[]{:S(2)}) collective-permute-start(bf16[4,16,2048]{2,1,0:T(8,128)(2,1)S(1)} %pad_maximum_fusion.5), channel_id=1, source_target_pairs={{0,2},{1,3},{2,0},{3,1},{4,6},{5,7},{6,4},{7,5},{8,10},{9,11},{10,... | collective-permute-start | bytes 786440 | tf_op jit(solution)/shard_map/ppermute | solution.py:79
  22.2 1.7 %collective-permute-start.17 = (bf16[4,64,512]{2,1,0:T(8,128)(2,1)S(1)}, bf16[4,64,512]{2,1,0:T(8,128)(2,1)S(1)}, u32[]{:S(2)}, u32[]{:S(2)}) collective-permute-start(bf16[4,64,512]{2,1,0:T(8,128)(2,1)S(1)} %pad_maximum_fusion.6), channel_id=1, source_target_pairs={{0,8},{8,0},{16,24},{24,16},{1,9},{9,1},{17,25},{25,17},{2,10},{10... | collective-permute-start | bytes 786440 | tf_op jit(solution)/shard_map/ppermute | solution.py:79
  23.9 2.3 %collective-permute-start.2 = (bf16[4,16,2176]{2,1,0:T(8,128)(2,1)S(1)}, bf16[4,16,2176]{2,1,0:T(8,128)(2,1)S(1)}, u32[]{:S(2)}, u32[]{:S(2)}) collective-permute-start(bf16[4,16,2176]{2,1,0:T(8,128)(2,1)S(1)} %pad_maximum_fusion.4), channel_id=1, source_target_pairs={{0,16},{8,24},{16,0},{24,8},{1,17},{9,25},{17,1},{25,9},{2,18},{10... | collective-permute-start | bytes 835592 | tf_op jit(solution)/shard_map/ppermute | solution.py:79
  26.3 3.3 %collective-permute-done.17 = bf16[4,64,512]{2,1,0:T(8,128)(2,1)S(1)} collective-permute-done((bf16[4,64,512]{2,1,0:T(8,128)(2,1)S(1)}, bf16[4,64,512]{2,1,0:T(8,128)(2,1)S(1)}, u32[]{:S(2)}, u32[]{:S(2)}) %collective-permute-start.17) | collective-permute-done | bytes 262176 | tf_op jit(solution)/shard_map/ppermute | solution.py:79
  31.6 1.5 %collective-permute-start.6 = (bf16[8,16,2176]{2,1,0:T(8,128)(2,1)S(1)}, bf16[8,16,2176]{2,1,0:T(8,128)(2,1)S(1)}, u32[]{:S(2)}, u32[]{:S(2)}) collective-permute-start(bf16[8,16,2176]{2,1,0:T(8,128)(2,1)S(1)} %pad_maximum_fusion.1.refs_4_.refs_10_), channel_id=1, source_target_pairs={{0,8},{8,0},{16,24},{24,16},{1,9},{9,1},{17,25},{25,17},{2,10},{10... | collective-permute-start | bytes 1671176 | tf_op jit(solution)/shard_map/ppermute | solution.py:79
  33.1 1.6 %collective-permute-start.12 = (bf16[8,16,2048]{2,1,0:T(8,128)(2,1)S(1)}, bf16[8,16,2048]{2,1,0:T(8,128)(2,1)}, u32[]{:S(2)}, u32[]{:S(2)}) collective-permute-start(bf16[8,16,2048]{2,1,0:T(8,128)(2,1)S(1)} %pad_maximum_fusion.2.refs_14_), channel_id=1, source_target_pairs={{0,16},{8,24},{16,0},{24,8},{1,17},{9,25},{17,1},{25,9},{2,18},{10... | collective-permute-start | bytes 1572872 | tf_op jit(solution)/shard_map/ppermute | solution.py:79
  34.8 2.8 %collective-permute-start.3 = (bf16[64,512]{1,0:T(8,128)(2,1)S(1)}, bf16[64,512]{1,0:T(8,128)(2,1)S(1)}, u32[]{:S(2)}, u32[]{:S(2)}) collective-permute-start(bf16[64,512]{1,0:T(8,128)(2,1)S(1)} %dynamic-slice_bitcast_fusion), channel_id=1, source_target_pairs={{0,4},{1,5},{2,6},{3,7},{4,0},{5,1},{6,2},{7,3},{8,12},{9,13},{10,... | collective-permute-start | bytes 196616 | tf_op jit(solution)/shard_map/ppermute | solution.py:79
  37.6 5.5 %collective-permute-done.3.refs_5_ = bf16[64,512]{1,0:T(8,128)(2,1)S(1)} collective-permute-done((bf16[64,512]{1,0:T(8,128)(2,1)S(1)}, bf16[64,512]{1,0:T(8,128)(2,1)S(1)}, u32[]{:S(2)}, u32[]{:S(2)}) %collective-permute-start.3) | collective-permute-done | bytes 65568 | tf_op jit(solution)/shard_map/ppermute | solution.py:79
  46.5 3.9 %attention_forward.1 = (f32[160,512]{1,0:T(8,128)S(1)}, bf16[640,768]{1,0:T(8,128)(2,1)S(1)}, bf16[544,512]{1,0:T(8,128)(2,1)S(1)}, bf16[512,768]{1,0:T(8,128)(2...) custom-call(s32[2]{0:T(128)S(1)} %copy-done.2, bf16[4,16,2048]{2,1,0:T(8,128)(2,1)S(1)} %constant_dynamic-update-slice_fusion.refs_1_, ...), custom_call_target="tpu_custom_call" | custom-call | flops 4000000000 | bytes 2785288 | tf_op jit(solution)/shard_map/attention_forward/pallas_call | solution.py:655
  50.4 3.7 %feed_forward.1 = (bf16[96,512]{1,0:T(8,128)(2,1)S(1)}, bf16[96,512]{1,0:T(8,128)(2,1)S(1)}, bf16[160,3328]{1,0:T(8,128)(2,1)S(1)}, bf16[160,3328]{1,0:T(8,128)(...) custom-call(s32[2]{0:T(128)S(1)} %copy-done.2, ...), custom_call_target="tpu_custom_call" | custom-call | flops 3000000000 | bytes 7290888 | tf_op jit(solution)/shard_map/feed_forward/pallas_call | solution.py:655
  54.3 1.8 %feed_backward.1 = (bf16[1,144,512]{2,1,0:T(8,128)(2,1)S(1)}, bf16[32,512]{1,0:T(8,128)(2,1)S(1)}, f32[160,512]{1,0:T(8,128)S(1)}, bf16[160,1280]{1,0:T(8,128)(2,1)S(1)}, bf16[160,1280]{1,0:T(8,128)(2,1)S(1)}) custom-call(f32[8,512]{1,0:T(8,128)S(1)} %get-tuple-element.89.refs_8_.refs_0_, f32[8,512]{1,0:T(8,128)S(1)} %get-tuple-element.96.refs_1_, ...), custom_call_target="tpu_custom_call" | custom-call | flops 3000000000 | bytes 6815744 | tf_op jit(solution)/shard_map/feed_backward/pallas_call | solution.py:655
  56.6 3.9 %collective-permute-start.21 = (bf16[1,144,512]{2,1,0:T(8,128)(2,1)S(1)}, bf16[1,144,512]{2,1,0:T(8,128)(2,1)S(1)}, u32[]{:S(2)}, u32[]{:S(2)}) collective-permute-start(bf16[1,144,512]{2,1,0:T(8,128)(2,1)S(1)} %get-tuple-element.105), channel_id=1, source_target_pairs={{0,2},{1,3},{2,0},{3,1},{4,6},{5,7},{6,4},{7,5},{8,10},{9,11},{10,... | collective-permute-start | bytes 442376 | tf_op jit(solution)/shard_map/ppermute | solution.py:79
  60.5 1.5 %weight_gradients.1 = (bf16[8,176,256]{2,1,0:T(8,128)(2,1)S(1)}, bf16[8,176,256]{2,1,0:T(8,128)(2,1)S(1)}, bf16[8,112,256]{2,1,0:T(8,128)(2,1)S(1)}, bf16[8,112,256]{2,1,0:T(8,128)(2,1)S(1)}) custom-call(bf16[160,3328]{1,0:T(8,128)(2,1)S(1)} %get-tuple-element.106.refs_0_, bf16[160,3328]{1,0:T(8,128)(2,1)S(1)} %collective-permute-done.22.refs_1_, ...), custom_call_target="tpu_custom_call" | custom-call | flops 1000000000 | bytes 2949120 | tf_op jit(solution)/shard_map/weight_gradients/pallas_call | solution.py:655
  62.0 1.4 %collective-permute-start.28 = (bf16[8,112,256]{2,1,0:T(8,128)(2,1)S(1)}, bf16[8,112,256]{2,1,0:T(8,128)(2,1)S(1)}, u32[]{:S(2)}, u32[]{:S(2)}) collective-permute-start(bf16[8,112,256]{2,1,0:T(8,128)(2,1)S(1)} %get-tuple-element.121), channel_id=1, source_target_pairs={{0,2},{1,3},{2,0},{3,1},{4,6},{5,7},{6,4},{7,5},{8,10},{9,11},{10,... | collective-permute-start | bytes 1376264 | tf_op jit(solution)/shard_map/ppermute | solution.py:89
  63.4 1.5 %collective-permute-start.27 = (bf16[8,176,256]{2,1,0:T(8,128)(2,1)S(1)}, bf16[8,176,256]{2,1,0:T(8,128)(2,1)S(1)}, u32[]{:S(2)}, u32[]{:S(2)}) collective-permute-start(bf16[8,176,256]{2,1,0:T(8,128)(2,1)S(1)} %get-tuple-element.111), channel_id=1, source_target_pairs={{0,8},{1,17},{2,10},{3,19},{4,12},{5,21},{6,14},{7,23},{8,0},{9,25... | collective-permute-start | bytes 2162696 | tf_op jit(solution)/shard_map/ppermute | solution.py:89
  65.1 1.6 %collective-permute-done.24.refs_6_ = bf16[2,144,512]{2,1,0:T(8,128)(2,1)S(1)} collective-permute-done((bf16[2,144,512]{2,1,0:T(8,128)(2,1)S(1)}, bf16[2,144,512]{2,1,0:T(8,128)(2,1)S(1)}, u32[]{:S(2)}, u32[]{:S(2)}) %collective-permute-start.24) | collective-permute-done | bytes 294944 | tf_op jit(solution)/shard_map/ppermute | solution.py:79
  66.6 8.1 %attention_backward.1 = (bf16[4,112,256]{2,1,0:T(8,128)(2,1)S(1)}, bf16[4,112,256]{2,1,0:T(8,128)(2,1)S(1)}, bf16[160,512]{1,0:T(8,128)(2,1)S(1)}, bf16[160,512]{1,0:T(8,128)(2,1)S(1)}, bf16[16,512]{1,0:T(8,128)(2,1)S(1)}) custom-call(s32[2]{0:T(128)S(1)} %copy-done.2, bf16[640,768]{1,0:T(8,128)(2,1)S(1)} %get-tuple-element.92.refs_1_, ...), custom_call_target="tpu_custom_call" | custom-call | bytes 3211272 | tf_op jit(solution)/shard_map/attention_backward/pallas_call | solution.py:655
  75.2 1.6 %collective-permute-start.29 = (bf16[4,400,256]{2,1,0:T(8,128)(2,1)S(1)}, bf16[4,400,256]{2,1,0:T(8,128)(2,1)S(1)}, u32[]{:S(2)}, u32[]{:S(2)}) collective-permute-start(bf16[4,400,256]{2,1,0:T(8,128)(2,1)S(1)} %pad_maximum_fusion), channel_id=1, source_target_pairs={{0,16},{1,9},{2,18},{3,11},{4,20},{5,13},{6,22},{7,15},{8,24},{9,1... | collective-permute-start | bytes 2457608 | tf_op jit(solution)/shard_map/ppermute | solution.py:89
  76.8 1.4 %collective-permute-done.25 = bf16[160,512]{1,0:T(8,128)(2,1)S(1)} collective-permute-done((bf16[160,512]{1,0:T(8,128)(2,1)S(1)}, bf16[160,512]{1,0:T(8,128)(2,1)S(1)}, u32[]{:S(2)}, u32[]{:S(2)}) %collective-permute-start.25) | collective-permute-done | bytes 163872 | tf_op jit(solution)/shard_map/ppermute | solution.py:79
  79.3 8.3 %collective-permute-done.29 = bf16[4,400,256]{2,1,0:T(8,128)(2,1)S(1)} collective-permute-done((bf16[4,400,256]{2,1,0:T(8,128)(2,1)S(1)}, bf16[4,400,256]{2,1,0:T(8,128)(2,1)S(1)}, u32[]{:S(2)}, u32[]{:S(2)}) %collective-permute-start.29) | collective-permute-done | bytes 819232 | tf_op jit(solution)/shard_map/ppermute | solution.py:89
  87.7 1.5 %collective-permute-start.30 = (bf16[2,176,256]{2,1,0:T(8,128)(2,1)S(1)}, bf16[2,176,256]{2,1,0:T(8,128)(2,1)S(1)}, u32[]{:S(2)}, u32[]{:S(2)}) collective-permute-start(bf16[2,176,256]{2,1,0:T(8,128)(2,1)S(1)} %get-tuple-element.153), channel_id=1, source_target_pairs={{0,2},{1,3},{2,0},{3,1},{4,6},{5,7},{6,4},{7,5},{8,10},{9,11},{10,... | collective-permute-start | bytes 540680 | tf_op jit(solution)/shard_map/ppermute | solution.py:89
  89.3 1.6 %collective-permute-start.31 = (bf16[2,224,256]{2,1,0:T(8,128)(2,1)S(1)}, bf16[2,224,256]{2,1,0:T(8,128)(2,1)S(1)}, u32[]{:S(2)}, u32[]{:S(2)}) collective-permute-start(bf16[2,224,256]{2,1,0:T(8,128)(2,1)S(1)} %get-tuple-element.151), channel_id=1, source_target_pairs={{0,8},{1,17},{2,10},{3,19},{4,12},{5,21},{6,14},{7,23},{8,0},{9,25... | collective-permute-start | bytes 688136 | tf_op jit(solution)/shard_map/ppermute | solution.py:89
  90.9 4.1 %collective-permute-done.30 = bf16[2,176,256]{2,1,0:T(8,128)(2,1)S(1)} collective-permute-done((bf16[2,176,256]{2,1,0:T(8,128)(2,1)S(1)}, bf16[2,176,256]{2,1,0:T(8,128)(2,1)S(1)}, u32[]{:S(2)}, u32[]{:S(2)}) %collective-permute-start.30) | collective-permute-done | bytes 180256 | tf_op jit(solution)/shard_map/ppermute | solution.py:89
  96.1 1.4 %emit_tokens.1 = (bf16[2,64,512]{2,1,0:T(8,128)(2,1)}, bf16[20,2,512]{2,1,0:T(2,128)(2,1)}, bf16[2,64,512]{2,1,0:T(8,128)(2,1)}, bf16[20,2,512]{2,1,0:T(2,128)(2,1)}, f32[2,512]{1,0:T(2,128)}) custom-call(s32[2]{0:T(128)S(1)} %copy-done.2, bf16[96,512]{1,0:T(8,128)(2,1)S(1)} %get-tuple-element.91.refs_1_, bf16[160,512]{1,0:T(8,128)(2,1)S(1)} %add_convert_fusion.8.refs_2_, ...), custom_call_target="tpu_custom_call" | custom-call | bytes 491528 | tf_op jit(solution)/shard_map/emit_tokens/pallas_call | solution.py:655
  97.5 8.9 %collective-permute-done.32.other = bf16[1,400,256]{2,1,0:T(8,128)(2,1)S(1)} collective-permute-done((bf16[1,400,256]{2,1,0:T(8,128)(2,1)S(1)}, bf16[1,400,256]{2,1,0:T(8,128)(2,1)S(1)}, u32[]{:S(2)}, u32[]{:S(2)}) %collective-permute-start.32) | collective-permute-done | bytes 204832 | tf_op jit(solution)/shard_map/ppermute | solution.py:89
  106.5 1.3 %collective-permute-done.33.got = bf16[208,256]{1,0:T(8,128)(2,1)S(1)} collective-permute-done((bf16[208,256]{1,0:T(8,128)(2,1)S(1)}, bf16[208,256]{1,0:T(8,128)(2,1)S(1)}, u32[]{:S(2)}, u32[]{:S(2)}) %collective-permute-start.33) | collective-permute-done | bytes 106528 | tf_op jit(solution)/shard_map/ppermute | solution.py:79
  (94 shorter events, 15.1 us)
Async XLA Ops:
  0.7 8.9 %collective-permute-start.9 = (bf16[1,16,2048]{2,1,0:T(8,128)(2,1)}, bf16[1,16,2048]{2,1,0:T(8,128)(2,1)S(1)}, u32[]{:S(2)}, u32[]{:S(2)}) collective-permute-start(bf16[1,16,2048]{2,1,0:T(8,128)(2,1)} %bitcast.23), channel_id=1, source_target_pairs={{0,4},{1,5},{2,6},{3,7},{4,0},{5,1},{6,2},{7,3},{8,12},{9,13},{10,... | collective-permute-start | bytes 196616 | tf_op jit(solution)/shard_map/ppermute | solution.py:79
  4.8 10.1 %collective-permute-start.15 = (bf16[1,64,512]{2,1,0:T(8,128)(2,1)}, bf16[1,64,512]{2,1,0:T(8,128)(2,1)S(1)}, u32[]{:S(2)}, u32[]{:S(2)}) collective-permute-start(bf16[1,64,512]{2,1,0:T(8,128)(2,1)} %bitcast.19), channel_id=1, source_target_pairs={{0,4},{1,5},{2,6},{3,7},{4,0},{5,1},{6,2},{7,3},{8,12},{9,13},{10,... | collective-permute-start | bytes 196616 | tf_op jit(solution)/shard_map/ppermute | solution.py:79
  6.7 10.6 %collective-permute-start = (bf16[16,4224]{1,0:T(8,128)(2,1)}, bf16[16,4224]{1,0:T(8,128)(2,1)S(1)}, u32[]{:S(2)}, u32[]{:S(2)}) collective-permute-start(bf16[16,4224]{1,0:T(8,128)(2,1)} %get-tuple-element.83), channel_id=1, source_target_pairs={{0,4},{1,5},{2,6},{3,7},{4,0},{5,1},{6,2},{7,3},{8,12},{9,13},{10,... | collective-permute-start | bytes 405512 | tf_op jit(solution)/shard_map/ppermute | solution.py:79
  10.4 9.3 %collective-permute-start.10 = (bf16[2,16,2048]{2,1,0:T(8,128)(2,1)S(1)}, bf16[2,16,2048]{2,1,0:T(8,128)(2,1)S(1)}, u32[]{:S(2)}, u32[]{:S(2)}) collective-permute-start(bf16[2,16,2048]{2,1,0:T(8,128)(2,1)S(1)} %pad_maximum_fusion.12), channel_id=1, source_target_pairs={{0,8},{8,0},{16,24},{24,16},{1,9},{9,1},{17,25},{25,17},{2,10},{10... | collective-permute-start | bytes 393224 | tf_op jit(solution)/shard_map/ppermute | solution.py:79
  15.8 6.4 %collective-permute-start.16 = (bf16[2,64,512]{2,1,0:T(8,128)(2,1)S(1)}, bf16[2,64,512]{2,1,0:T(8,128)(2,1)S(1)}, u32[]{:S(2)}, u32[]{:S(2)}) collective-permute-start(bf16[2,64,512]{2,1,0:T(8,128)(2,1)S(1)} %pad_maximum_fusion.13), channel_id=1, source_target_pairs={{0,16},{8,24},{16,0},{24,8},{1,17},{9,25},{17,1},{25,9},{2,18},{10... | collective-permute-start | bytes 393224 | tf_op jit(solution)/shard_map/ppermute | solution.py:79
  18.2 5.7 %collective-permute-start.1 = (bf16[2,16,2176]{2,1,0:T(8,128)(2,1)S(1)}, bf16[2,16,2176]{2,1,0:T(8,128)(2,1)S(1)}, u32[]{:S(2)}, u32[]{:S(2)}) collective-permute-start(bf16[2,16,2176]{2,1,0:T(8,128)(2,1)S(1)} %fusion.1), channel_id=1, source_target_pairs={{0,2},{1,3},{2,0},{3,1},{4,6},{5,7},{6,4},{7,5},{8,10},{9,11},{10,... | collective-permute-start | bytes 417800 | tf_op jit(solution)/shard_map/ppermute | solution.py:79
  20.7 12.4 %collective-permute-start.11 = (bf16[4,16,2048]{2,1,0:T(8,128)(2,1)S(1)}, bf16[4,16,2048]{2,1,0:T(8,128)(2,1)S(1)}, u32[]{:S(2)}, u32[]{:S(2)}) collective-permute-start(bf16[4,16,2048]{2,1,0:T(8,128)(2,1)S(1)} %pad_maximum_fusion.5), channel_id=1, source_target_pairs={{0,2},{1,3},{2,0},{3,1},{4,6},{5,7},{6,4},{7,5},{8,10},{9,11},{10,... | collective-permute-start | bytes 786440 | tf_op jit(solution)/shard_map/ppermute | solution.py:79
  22.2 7.4 %collective-permute-start.17 = (bf16[4,64,512]{2,1,0:T(8,128)(2,1)S(1)}, bf16[4,64,512]{2,1,0:T(8,128)(2,1)S(1)}, u32[]{:S(2)}, u32[]{:S(2)}) collective-permute-start(bf16[4,64,512]{2,1,0:T(8,128)(2,1)S(1)} %pad_maximum_fusion.6), channel_id=1, source_target_pairs={{0,8},{8,0},{16,24},{24,16},{1,9},{9,1},{17,25},{25,17},{2,10},{10... | collective-permute-start | bytes 786440 | tf_op jit(solution)/shard_map/ppermute | solution.py:79
  23.9 7.6 %collective-permute-start.2 = (bf16[4,16,2176]{2,1,0:T(8,128)(2,1)S(1)}, bf16[4,16,2176]{2,1,0:T(8,128)(2,1)S(1)}, u32[]{:S(2)}, u32[]{:S(2)}) collective-permute-start(bf16[4,16,2176]{2,1,0:T(8,128)(2,1)S(1)} %pad_maximum_fusion.4), channel_id=1, source_target_pairs={{0,16},{8,24},{16,0},{24,8},{1,17},{9,25},{17,1},{25,9},{2,18},{10... | collective-permute-start | bytes 835592 | tf_op jit(solution)/shard_map/ppermute | solution.py:79
  26.2 8.5 %collective-permute-start.4 = (bf16[2,16,2048]{2,1,0:T(8,128)(2,1)S(1)}, bf16[2,16,2048]{2,1,0:T(8,128)(2,1)S(1)}, u32[]{:S(2)}, u32[]{:S(2)}) collective-permute-start(bf16[2,16,2048]{2,1,0:T(8,128)(2,1)S(1)} %pad_maximum_fusion.11), channel_id=1, source_target_pairs={{0,2},{1,3},{2,0},{3,1},{4,6},{5,7},{6,4},{7,5},{8,10},{9,11},{10,... | collective-permute-start | bytes 393224 | tf_op jit(solution)/shard_map/ppermute | solution.py:79
  29.7 14.9 %collective-permute-start.18 = (bf16[8,64,512]{2,1,0:T(8,128)(2,1)S(1)}, bf16[8,64,512]{2,1,0:T(8,128)(2,1)}, u32[]{:S(2)}, u32[]{:S(2)}) collective-permute-start(bf16[8,64,512]{2,1,0:T(8,128)(2,1)S(1)} %pad_maximum_fusion.3.refs_18_), channel_id=1, source_target_pairs={{0,2},{1,3},{2,0},{3,1},{4,6},{5,7},{6,4},{7,5},{8,10},{9,11},{10,... | collective-permute-start | bytes 1572872 | tf_op jit(solution)/shard_map/ppermute | solution.py:79
  31.6 12.4 %collective-permute-start.6 = (bf16[8,16,2176]{2,1,0:T(8,128)(2,1)S(1)}, bf16[8,16,2176]{2,1,0:T(8,128)(2,1)S(1)}, u32[]{:S(2)}, u32[]{:S(2)}) collective-permute-start(bf16[8,16,2176]{2,1,0:T(8,128)(2,1)S(1)} %pad_maximum_fusion.1.refs_4_.refs_10_), channel_id=1, source_target_pairs={{0,8},{8,0},{16,24},{24,16},{1,9},{9,1},{17,25},{25,17},{2,10},{10... | collective-permute-start | bytes 1671176 | tf_op jit(solution)/shard_map/ppermute | solution.py:79
  33.1 11.6 %collective-permute-start.12 = (bf16[8,16,2048]{2,1,0:T(8,128)(2,1)S(1)}, bf16[8,16,2048]{2,1,0:T(8,128)(2,1)}, u32[]{:S(2)}, u32[]{:S(2)}) collective-permute-start(bf16[8,16,2048]{2,1,0:T(8,128)(2,1)S(1)} %pad_maximum_fusion.2.refs_14_), channel_id=1, source_target_pairs={{0,16},{8,24},{16,0},{24,8},{1,17},{9,25},{17,1},{25,9},{2,18},{10... | collective-permute-start | bytes 1572872 | tf_op jit(solution)/shard_map/ppermute | solution.py:79
  34.7 10.6 %collective-permute-start.7 = (bf16[8,16,2176]{2,1,0:T(8,128)(2,1)S(1)}, bf16[8,16,2176]{2,1,0:T(8,128)(2,1)S(1)}, u32[]{:S(2)}, u32[]{:S(2)}) collective-permute-start(bf16[8,16,2176]{2,1,0:T(8,128)(2,1)S(1)} %pad_maximum_fusion.1.refs_4_.refs_10_), channel_id=1, source_target_pairs={{0,1},{1,0},{2,3},{3,2},{4,5},{5,4},{6,7},{7,6},{8,9},{9,8},{10,11... | collective-permute-start | bytes 1671176 | tf_op jit(solution)/shard_map/ppermute | solution.py:79
  34.8 8.3 %collective-permute-start.3 = (bf16[64,512]{1,0:T(8,128)(2,1)S(1)}, bf16[64,512]{1,0:T(8,128)(2,1)S(1)}, u32[]{:S(2)}, u32[]{:S(2)}) collective-permute-start(bf16[64,512]{1,0:T(8,128)(2,1)S(1)} %dynamic-slice_bitcast_fusion), channel_id=1, source_target_pairs={{0,4},{1,5},{2,6},{3,7},{4,0},{5,1},{6,2},{7,3},{8,12},{9,13},{10,... | collective-permute-start | bytes 196616 | tf_op jit(solution)/shard_map/ppermute | solution.py:79
  43.1 2.0 %collective-permute-start.5 = (bf16[4,16,2048]{2,1,0:T(8,128)(2,1)S(1)}, bf16[4,16,2048]{2,1,0:T(8,128)(2,1)S(1)}, u32[]{:S(2)}, u32[]{:S(2)}) collective-permute-start(bf16[4,16,2048]{2,1,0:T(8,128)(2,1)S(1)} %constant_dynamic-update-slice_fusion.refs_1_), channel_id=1, source_target_pairs={{0,1},{1,0},{2,3},{3,2},{4,5},{5,4},{6,7},{7,6},{8,9},{9,8},{10,11... | collective-permute-start | bytes 786440 | tf_op jit(solution)/shard_map/ppermute | solution.py:79
  44.0 2.4 %collective-permute-start.8 = (bf16[8,16,2176]{2,1,0:T(8,128)(2,1)S(1)}, bf16[8,16,2176]{2,1,0:T(8,128)(2,1)S(1)}, u32[]{:S(2)}, u32[]{:S(2)}) collective-permute-start(bf16[8,16,2176]{2,1,0:T(8,128)(2,1)S(1)} %collective-permute-done.6.refs_5_.refs_11_), channel_id=1, source_target_pairs={{0,1},{1,0},{2,3},{3,2},{4,5},{5,4},{6,7},{7,6},{8,9},{9,8},{10,11... | collective-permute-start | bytes 1671176 | tf_op jit(solution)/shard_map/ppermute | solution.py:79
  44.6 5.8 %collective-permute-start.19 = (bf16[8,64,512]{2,1,0:T(8,128)(2,1)S(1)}, bf16[8,64,512]{2,1,0:T(8,128)(2,1)S(1)}, u32[]{:S(2)}, u32[]{:S(2)}) collective-permute-start(bf16[8,64,512]{2,1,0:T(8,128)(2,1)S(1)} %pad_maximum_fusion.3.refs_18_), channel_id=1, source_target_pairs={{0,1},{1,0},{2,3},{3,2},{4,5},{5,4},{6,7},{7,6},{8,9},{9,8},{10,11... | collective-permute-start | bytes 1572872 | tf_op jit(solution)/shard_map/ppermute | solution.py:79
  44.8 5.6 %collective-permute-start.13 = (bf16[8,16,2048]{2,1,0:T(8,128)(2,1)S(1)}, bf16[8,16,2048]{2,1,0:T(8,128)(2,1)S(1)}, u32[]{:S(2)}, u32[]{:S(2)}) collective-permute-start(bf16[8,16,2048]{2,1,0:T(8,128)(2,1)S(1)} %pad_maximum_fusion.2.refs_14_), channel_id=1, source_target_pairs={{0,1},{1,0},{2,3},{3,2},{4,5},{5,4},{6,7},{7,6},{8,9},{9,8},{10,11... | collective-permute-start | bytes 1572872 | tf_op jit(solution)/shard_map/ppermute | solution.py:79
  45.1 5.3 %collective-permute-start.20 = (bf16[8,64,512]{2,1,0:T(8,128)(2,1)}, bf16[8,64,512]{2,1,0:T(8,128)(2,1)S(1)}, u32[]{:S(2)}, u32[]{:S(2)}) collective-permute-start(bf16[8,64,512]{2,1,0:T(8,128)(2,1)} %collective-permute-done.18.refs_19_), channel_id=1, source_target_pairs={{0,1},{1,0},{2,3},{3,2},{4,5},{5,4},{6,7},{7,6},{8,9},{9,8},{10,11... | collective-permute-start | bytes 1572872 | tf_op jit(solution)/shard_map/ppermute | solution.py:79
  45.3 5.1 %collective-permute-start.14 = (bf16[8,16,2048]{2,1,0:T(8,128)(2,1)}, bf16[8,16,2048]{2,1,0:T(8,128)(2,1)S(1)}, u32[]{:S(2)}, u32[]{:S(2)}) collective-permute-start(bf16[8,16,2048]{2,1,0:T(8,128)(2,1)} %collective-permute-done.12.refs_15_), channel_id=1, source_target_pairs={{0,1},{1,0},{2,3},{3,2},{4,5},{5,4},{6,7},{7,6},{8,9},{9,8},{10,11... | collective-permute-start | bytes 1572872 | tf_op jit(solution)/shard_map/ppermute | solution.py:79
  54.1 6.4 %collective-permute-start.22 = (bf16[160,3328]{1,0:T(8,128)(2,1)S(1)}, bf16[160,3328]{1,0:T(8,128)(2,1)S(1)}, u32[]{:S(2)}, u32[]{:S(2)}) collective-permute-start(bf16[160,3328]{1,0:T(8,128)(2,1)S(1)} %get-tuple-element.107), channel_id=1, source_target_pairs={{0,1},{1,0},{2,3},{3,2},{4,5},{5,4},{6,7},{7,6},{8,9},{9,8},{10,11... | collective-permute-start | bytes 3194888 | tf_op jit(solution)/shard_map/ppermute | solution.py:79
  56.2 4.3 %collective-permute-start.23 = (bf16[160,1280]{1,0:T(8,128)(2,1)S(1)}, bf16[160,1280]{1,0:T(8,128)(2,1)S(1)}, u32[]{:S(2)}, u32[]{:S(2)}) collective-permute-start(bf16[160,1280]{1,0:T(8,128)(2,1)S(1)} %get-tuple-element.110), channel_id=1, source_target_pairs={{0,1},{1,0},{2,3},{3,2},{4,5},{5,4},{6,7},{7,6},{8,9},{9,8},{10,11... | collective-permute-start | bytes 1228808 | tf_op jit(solution)/shard_map/ppermute | solution.py:79
  56.6 8.4 %collective-permute-start.21 = (bf16[1,144,512]{2,1,0:T(8,128)(2,1)S(1)}, bf16[1,144,512]{2,1,0:T(8,128)(2,1)S(1)}, u32[]{:S(2)}, u32[]{:S(2)}) collective-permute-start(bf16[1,144,512]{2,1,0:T(8,128)(2,1)S(1)} %get-tuple-element.105), channel_id=1, source_target_pairs={{0,2},{1,3},{2,0},{3,1},{4,6},{5,7},{6,4},{7,5},{8,10},{9,11},{10,... | collective-permute-start | bytes 442376 | tf_op jit(solution)/shard_map/ppermute | solution.py:79
  62.0 12.8 %collective-permute-start.28 = (bf16[8,112,256]{2,1,0:T(8,128)(2,1)S(1)}, bf16[8,112,256]{2,1,0:T(8,128)(2,1)S(1)}, u32[]{:S(2)}, u32[]{:S(2)}) collective-permute-start(bf16[8,112,256]{2,1,0:T(8,128)(2,1)S(1)} %get-tuple-element.121), channel_id=1, source_target_pairs={{0,2},{1,3},{2,0},{3,1},{4,6},{5,7},{6,4},{7,5},{8,10},{9,11},{10,... | collective-permute-start | bytes 1376264 | tf_op jit(solution)/shard_map/ppermute | solution.py:89
  63.4 11.5 %collective-permute-start.27 = (bf16[8,176,256]{2,1,0:T(8,128)(2,1)S(1)}, bf16[8,176,256]{2,1,0:T(8,128)(2,1)S(1)}, u32[]{:S(2)}, u32[]{:S(2)}) collective-permute-start(bf16[8,176,256]{2,1,0:T(8,128)(2,1)S(1)} %get-tuple-element.111), channel_id=1, source_target_pairs={{0,8},{1,17},{2,10},{3,19},{4,12},{5,21},{6,14},{7,23},{8,0},{9,25... | collective-permute-start | bytes 2162696 | tf_op jit(solution)/shard_map/ppermute | solution.py:89
  65.0 1.6 %collective-permute-start.24 = (bf16[2,144,512]{2,1,0:T(8,128)(2,1)S(1)}, bf16[2,144,512]{2,1,0:T(8,128)(2,1)S(1)}, u32[]{:S(2)}, u32[]{:S(2)}) collective-permute-start(bf16[2,144,512]{2,1,0:T(8,128)(2,1)S(1)} %constant_dynamic-update-slice_fusion.2.refs_5_), channel_id=1, source_target_pairs={{0,1},{1,0},{2,3},{3,2},{4,5},{5,4},{6,7},{7,6},{8,9},{9,8},{10,11... | collective-permute-start | bytes 884744 | tf_op jit(solution)/shard_map/ppermute | solution.py:79
  75.2 12.4 %collective-permute-start.29 = (bf16[4,400,256]{2,1,0:T(8,128)(2,1)S(1)}, bf16[4,400,256]{2,1,0:T(8,128)(2,1)S(1)}, u32[]{:S(2)}, u32[]{:S(2)}) collective-permute-start(bf16[4,400,256]{2,1,0:T(8,128)(2,1)S(1)} %pad_maximum_fusion), channel_id=1, source_target_pairs={{0,16},{1,9},{2,18},{3,11},{4,20},{5,13},{6,22},{7,15},{8,24},{9,1... | collective-permute-start | bytes 2457608 | tf_op jit(solution)/shard_map/ppermute | solution.py:89
  78.3 17.8 %collective-permute-start.26 = (bf16[208,512]{1,0:T(8,128)(2,1)S(1)}, bf16[208,512]{1,0:T(8,128)(2,1)S(1)}, u32[]{:S(2)}, u32[]{:S(2)}) collective-permute-start(bf16[208,512]{1,0:T(8,128)(2,1)S(1)} %pad_maximum_fusion.8), channel_id=1, source_target_pairs={{0,4},{1,5},{2,6},{3,7},{4,0},{5,1},{6,2},{7,3},{8,12},{9,13},{10,... | collective-permute-start | bytes 638984 | tf_op jit(solution)/shard_map/ppermute | solution.py:79
  87.7 7.3 %collective-permute-start.30 = (bf16[2,176,256]{2,1,0:T(8,128)(2,1)S(1)}, bf16[2,176,256]{2,1,0:T(8,128)(2,1)S(1)}, u32[]{:S(2)}, u32[]{:S(2)}) collective-permute-start(bf16[2,176,256]{2,1,0:T(8,128)(2,1)S(1)} %get-tuple-element.153), channel_id=1, source_target_pairs={{0,2},{1,3},{2,0},{3,1},{4,6},{5,7},{6,4},{7,5},{8,10},{9,11},{10,... | collective-permute-start | bytes 540680 | tf_op jit(solution)/shard_map/ppermute | solution.py:89
  89.3 6.1 %collective-permute-start.31 = (bf16[2,224,256]{2,1,0:T(8,128)(2,1)S(1)}, bf16[2,224,256]{2,1,0:T(8,128)(2,1)S(1)}, u32[]{:S(2)}, u32[]{:S(2)}) collective-permute-start(bf16[2,224,256]{2,1,0:T(8,128)(2,1)S(1)} %get-tuple-element.151), channel_id=1, source_target_pairs={{0,8},{1,17},{2,10},{3,19},{4,12},{5,21},{6,14},{7,23},{8,0},{9,25... | collective-permute-start | bytes 688136 | tf_op jit(solution)/shard_map/ppermute | solution.py:89
  95.5 10.8 %collective-permute-start.32 = (bf16[1,400,256]{2,1,0:T(8,128)(2,1)S(1)}, bf16[1,400,256]{2,1,0:T(8,128)(2,1)S(1)}, u32[]{:S(2)}, u32[]{:S(2)}) collective-permute-start(bf16[1,400,256]{2,1,0:T(8,128)(2,1)S(1)} %pad_maximum_fusion.9), channel_id=1, source_target_pairs={{0,4},{1,5},{2,6},{3,7},{4,0},{5,1},{6,2},{7,3},{8,12},{9,13},{10,... | collective-permute-start | bytes 614408 | tf_op jit(solution)/shard_map/ppermute | solution.py:89
  (10 other events, 110.4 us)
